TPU v7x, 128 devices: a whole 4x4x4 slice. The times are simulated.
128 devices in a mesh: dp: 16 (over y, z_hi, core), ctx: 8 (over x, z_lo).
Axes of the slice: x: 4, y: 4, z: 4 (z_hi: 2, z_lo: 2; z = z_hi * 2 + z_lo), core: 2. Of those that a mesh axis runs over, the one named last changes fastest.
Arguments:
- hidden_in: bfloat16 [16, 1024, 768], P('dp', 'ctx'), may hold values from -6 to 6
- out_grad: bfloat16 [16, 1024, 768], P('dp', 'ctx'), may hold values from -6 to 6
- sequence_group: int32 [48], replicated, may hold values from 0 to 15, as said below
- sequence_start: int32 [48], replicated, may hold values from 0 to 992
- sequence_length: int32 [48], replicated, may hold values from 1 to 991
- norm_gain: bfloat16 [2, 2, 768], P(None, None, ('dp', 'ctx')), may hold values from 0.5 to 1.5
- norm_bias: bfloat16 [2, 2, 768], P(None, None, ('dp', 'ctx')), may hold values from -1.5 to 1.5
- input_weight: bfloat16 [2, 768, 2304], P(None, ('dp', 'ctx')), may hold values from -0.21875 to 0.21875
- input_bias: bfloat16 [2, 2, 768], P(None, None, ('dp', 'ctx')), may hold values from -1.5 to 1.5
- output_weight: bfloat16 [2, 768, 768], P(None, ('dp', 'ctx')), may hold values from -2.5 to 2.5
- branch_bias: bfloat16 [2, 2, 768], P(None, None, ('dp', 'ctx')), may hold values from -1.5 to 1.5
- up_weight: bfloat16 [2, 768, 3072], P(None, ('dp', 'ctx')), may hold values from -0.21875 to 0.21875
- up_bias: bfloat16 [2, 3072], P(None, ('dp', 'ctx')), may hold values from -1.5 to 1.5
- down_weight: bfloat16 [2, 3072, 768], P(None, ('dp', 'ctx')), may hold values from -0.109375 to 0.109375
Outputs:
- hidden_out: bfloat16 [16, 1024, 768], P('dp', 'ctx')
- grad_in: float32 [16, 1024, 768], P('dp', 'ctx')
- grad_norm_gain: float32 [2, 2, 768], P(None, None, ('dp', 'ctx'))
- grad_norm_bias: float32 [2, 2, 768], P(None, None, ('dp', 'ctx'))
- grad_input_weight: float32 [2, 768, 2304], P(None, ('dp', 'ctx'))
- grad_input_bias: float32 [2, 2, 768], P(None, None, ('dp', 'ctx'))
- grad_output_weight: float32 [2, 768, 768], P(None, ('dp', 'ctx'))
- grad_branch_bias: float32 [2, 2, 768], P(None, None, ('dp', 'ctx'))
- grad_up_weight: float32 [2, 768, 3072], P(None, ('dp', 'ctx'))
- grad_up_bias: float32 [2, 3072], P(None, ('dp', 'ctx'))
- grad_down_weight: float32 [2, 3072, 768], P(None, ('dp', 'ctx'))
Inputs may be any that keep to these rules, and one draw needn't show every extreme that they name: `sequence_group`: each group holds three sequences laid end to end from its first token slot; the slots after them are padding.
All inputs are finite; a program needn't handle non-finite values.
Results may differ from a plain program's by a relative error of at most 0.014.
Values may be sent and summed in bfloat16 or wider, within the bound.
No kernel may reach another device: no remote copies, remote signals or barrier semaphores. Data moves between devices by JAX's collectives and lax.ppermute only.
A program may use at most 256 MiB of HBM per device.

v0:
```python
import jax
import jax.numpy as jnp
from jax import lax
from jax.sharding import PartitionSpec as P

HEAD_DIM = 64
LAYERS = 2


norm_eps = 1e-05
score_scale = 0.125


def layer_norm(values, scales, offset):
    centre = values - jnp.mean(values, axis=-1, keepdims=True)
    spread = jnp.mean(centre * centre, axis=-1, keepdims=True)
    return centre * lax.rsqrt(spread + norm_eps) * scales + offset


def gelu_tanh(values):
    return (
        0.5
        * values
        * (1.0 + jnp.tanh(0.7978845608028654 * (values + 0.044715 * values * values * values)))
    )


def token_ids(group_index, positions, sequence_group, sequence_start, sequence_length):
    member = (
        (sequence_group[None, :] == group_index)
        & (sequence_start[None, :] <= positions[:, None])
        & (positions[:, None] < (sequence_start + sequence_length)[None, :])
    )
    numbers = jnp.arange(sequence_group.shape[0], dtype=jnp.int32) + 1
    located = jnp.sum(jnp.where(member, numbers[None, :], 0), axis=1)
    return jnp.where(located > 0, located - 1, -1 - positions)


def split_heads(values):
    return values.reshape(values.shape[0], values.shape[1] // HEAD_DIM, HEAD_DIM)


def outer_sum(left, right):
    return lax.dot_general(
        left, right, (((0,), (0,)), ((), ())), preferred_element_type=jnp.float32
    )


def back_product(left, matrix):
    return lax.dot_general(
        left, matrix, (((1,), (1,)), ((), ())), preferred_element_type=jnp.float32
    )


def column_sums(values):
    return jnp.sum(values.astype(jnp.float32), axis=0)


def attend(queries, key_all, value_all, visible):
    scores = (
        jnp.einsum(
            "qhd,khd->hqk",
            split_heads(queries),
            split_heads(key_all),
            preferred_element_type=jnp.float32,
        )
        * score_scale
    )
    scores = jnp.where(visible[None], scores, -1000000000.0)
    row_max = jnp.max(scores, axis=-1, keepdims=True)
    raised = jnp.exp(scores - row_max)
    totals = jnp.sum(raised, axis=-1, keepdims=True)
    soft_weights = (raised / totals).astype(jnp.bfloat16)
    mixture = jnp.einsum(
        "hqk,khd->qhd", soft_weights, split_heads(value_all), preferred_element_type=jnp.float32
    )
    return (mixture.reshape(queries.shape), row_max + jnp.log(totals))


def attend_back(queries, key_all, value_all, visible, log_total, mix_grad):
    query_heads = split_heads(queries)
    key_heads = split_heads(key_all)
    grad_heads = split_heads(mix_grad)
    scores = (
        jnp.einsum("qhd,khd->hqk", query_heads, key_heads, preferred_element_type=jnp.float32)
        * score_scale
    )
    soft_weights = jnp.where(visible[None], jnp.exp(scores - log_total), 0.0)
    weight_grad = jnp.einsum(
        "qhd,khd->hqk", grad_heads, split_heads(value_all), preferred_element_type=jnp.float32
    )
    centre = jnp.sum(soft_weights * weight_grad, axis=-1, keepdims=True)
    score_grad = (soft_weights * (weight_grad - centre)).astype(jnp.bfloat16)
    query_grad = (
        jnp.einsum("hqk,khd->qhd", score_grad, key_heads, preferred_element_type=jnp.float32)
        * score_scale
    )
    key_grad = (
        jnp.einsum("hqk,qhd->khd", score_grad, query_heads, preferred_element_type=jnp.float32)
        * score_scale
    )
    value_grad = jnp.einsum(
        "hqk,qhd->khd",
        soft_weights.astype(jnp.bfloat16),
        grad_heads,
        preferred_element_type=jnp.float32,
    )
    return (
        query_grad.reshape(queries.shape),
        key_grad.reshape(key_all.shape),
        value_grad.reshape(value_all.shape),
    )


def unpack(weights):
    (
        scales,
        offsets,
        joint_matrix,
        input_offsets,
        out_matrix,
        out_biases,
        up_matrix,
        up_offset,
        down_matrix,
    ) = weights
    return (
        scales.astype(jnp.float32),
        offsets.astype(jnp.float32),
        joint_matrix,
        input_offsets.astype(jnp.float32),
        out_matrix,
        out_biases.astype(jnp.float32),
        up_matrix,
        up_offset.astype(jnp.float32),
        down_matrix,
    )


def body(
    hidden_in,
    out_grad,
    sequence_group,
    sequence_start,
    sequence_length,
    norm_gain,
    norm_bias,
    input_weight,
    input_bias,
    output_weight,
    branch_bias,
    up_weight,
    up_bias,
    down_weight,
):
    local_rows = hidden_in.shape[1]
    model_width = hidden_in.shape[2]
    group_index = lax.axis_index("dp")
    block_index = lax.axis_index("ctx")
    group_rows = local_rows * lax.axis_size("ctx")
    my_positions = block_index * local_rows + jnp.arange(local_rows, dtype=jnp.int32)
    all_positions = jnp.arange(group_rows, dtype=jnp.int32)
    my_ids = token_ids(group_index, my_positions, sequence_group, sequence_start, sequence_length)
    all_ids = token_ids(group_index, all_positions, sequence_group, sequence_start, sequence_length)
    visible = (my_ids[:, None] == all_ids[None, :]) & (
        all_positions[None, :] <= my_positions[:, None]
    ) | (all_positions[None, :] == my_positions[:, None])
    hidden = hidden_in[0].astype(jnp.float32)
    stored = []
    for layer_index in range(LAYERS):
        weights = (
            lax.all_gather(norm_gain[layer_index], ("dp", "ctx"), axis=1, tiled=True),
            lax.all_gather(norm_bias[layer_index], ("dp", "ctx"), axis=1, tiled=True),
            lax.all_gather(input_weight[layer_index], ("dp", "ctx"), axis=0, tiled=True),
            lax.all_gather(input_bias[layer_index], ("dp", "ctx"), axis=1, tiled=True),
            lax.all_gather(output_weight[layer_index], ("dp", "ctx"), axis=0, tiled=True),
            lax.all_gather(branch_bias[layer_index], ("dp", "ctx"), axis=1, tiled=True),
            lax.all_gather(up_weight[layer_index], ("dp", "ctx"), axis=0, tiled=True),
            lax.all_gather(up_bias[layer_index], ("dp", "ctx"), axis=0, tiled=True),
            lax.all_gather(down_weight[layer_index], ("dp", "ctx"), axis=0, tiled=True),
        )
        (
            scales,
            offsets,
            joint_matrix,
            input_offsets,
            out_matrix,
            out_biases,
            up_matrix,
            up_offset,
            down_matrix,
        ) = unpack(weights)
        normed = layer_norm(hidden, scales[0], offsets[0]).astype(jnp.bfloat16)
        joined = jnp.dot(normed, joint_matrix, preferred_element_type=jnp.float32)
        queries = (joined[:, :model_width] + input_offsets[0]).astype(jnp.bfloat16)
        key_rows = joined[:, model_width : 2 * model_width].astype(jnp.bfloat16)
        value_rows = (joined[:, 2 * model_width :] + input_offsets[1]).astype(jnp.bfloat16)
        key_all, value_all = (
            lax.all_gather(key_rows, "ctx", axis=0, tiled=True),
            lax.all_gather(value_rows, "ctx", axis=0, tiled=True),
        )
        mixture, log_total = attend(queries, key_all, value_all, visible)
        mixed_low = mixture.astype(jnp.bfloat16)
        middle = (
            hidden
            + jnp.dot(mixed_low, out_matrix, preferred_element_type=jnp.float32)
            + out_biases[0]
        )
        second = layer_norm(middle, scales[1], offsets[1]).astype(jnp.bfloat16)
        pre_gelu = jnp.dot(second, up_matrix, preferred_element_type=jnp.float32) + up_offset
        activated = gelu_tanh(pre_gelu).astype(jnp.bfloat16)
        stored.append(
            (
                hidden,
                normed,
                queries,
                key_rows,
                value_rows,
                key_all,
                value_all,
                log_total,
                mixed_low,
                middle,
                second,
                pre_gelu,
                activated,
                weights,
            )
        )
        hidden = (
            middle
            + jnp.dot(activated, down_matrix, preferred_element_type=jnp.float32)
            + out_biases[1]
        )
    grad_hidden = out_grad[0].astype(jnp.float32)
    layer_grads = []
    for layer_index in reversed(range(LAYERS)):
        (
            layer_input,
            normed,
            queries,
            key_rows,
            value_rows,
            key_all,
            value_all,
            log_total,
            mixed_low,
            middle,
            second,
            pre_gelu,
            activated,
            weights,
        ) = stored[layer_index]
        again = (
            lax.all_gather(norm_gain[layer_index], ("dp", "ctx"), axis=1, tiled=True),
            lax.all_gather(norm_bias[layer_index], ("dp", "ctx"), axis=1, tiled=True),
            lax.all_gather(input_weight[layer_index], ("dp", "ctx"), axis=0, tiled=True),
            lax.all_gather(input_bias[layer_index], ("dp", "ctx"), axis=1, tiled=True),
            lax.all_gather(output_weight[layer_index], ("dp", "ctx"), axis=0, tiled=True),
            lax.all_gather(branch_bias[layer_index], ("dp", "ctx"), axis=1, tiled=True),
            lax.all_gather(up_weight[layer_index], ("dp", "ctx"), axis=0, tiled=True),
            lax.all_gather(up_bias[layer_index], ("dp", "ctx"), axis=0, tiled=True),
            lax.all_gather(down_weight[layer_index], ("dp", "ctx"), axis=0, tiled=True),
        )
        (
            scales,
            offsets,
            joint_matrix,
            input_offsets,
            out_matrix,
            out_biases,
            up_matrix,
            up_offset,
            down_matrix,
        ) = unpack(again)
        key_all, value_all = (
            lax.all_gather(key_rows, "ctx", axis=0, tiled=True),
            lax.all_gather(value_rows, "ctx", axis=0, tiled=True),
        )
        down_grad = grad_hidden.astype(jnp.bfloat16)
        grad_down = outer_sum(activated, down_grad)
        bias_down = column_sums(down_grad)
        gelu_grad = back_product(down_grad, down_matrix)
        pre_grad = jax.vjp(gelu_tanh, pre_gelu)[1](gelu_grad)[0].astype(jnp.bfloat16)
        grad_up = outer_sum(second, pre_grad)
        bias_up = column_sums(pre_grad)
        second_grad = back_product(pre_grad, up_matrix)
        middle_grad, scale_two, offset_two = jax.vjp(layer_norm, middle, scales[1], offsets[1])[1](
            second_grad
        )
        grad_middle = grad_hidden + middle_grad
        branch_grad = grad_middle.astype(jnp.bfloat16)
        grad_output = outer_sum(mixed_low, branch_grad)
        bias_out = column_sums(branch_grad)
        mix_grad = back_product(branch_grad, out_matrix).astype(jnp.bfloat16)
        query_grad, key_part, value_part = attend_back(
            queries, key_all, value_all, visible, log_total, mix_grad
        )
        key_grad, value_grad = (
            lax.psum_scatter(
                key_part.astype(jnp.bfloat16), "ctx", scatter_dimension=0, tiled=True
            ).astype(jnp.float32),
            lax.psum_scatter(
                value_part.astype(jnp.bfloat16), "ctx", scatter_dimension=0, tiled=True
            ).astype(jnp.float32),
        )
        joined_grad = jnp.concatenate(
            [
                query_grad.astype(jnp.bfloat16),
                key_grad.astype(jnp.bfloat16),
                value_grad.astype(jnp.bfloat16),
            ],
            axis=1,
        )
        grad_joint = outer_sum(normed, joined_grad)
        bias_query = column_sums(joined_grad[:, :model_width])
        bias_value = column_sums(joined_grad[:, 2 * model_width :])
        normed_grad = back_product(joined_grad, joint_matrix)
        input_grad, scale_one, offset_one = jax.vjp(layer_norm, layer_input, scales[0], offsets[0])[
            1
        ](normed_grad)
        grad_hidden = grad_middle + input_grad
        gain_terms = jnp.stack([scale_one, scale_two])
        offset_terms = jnp.stack([offset_one, offset_two])
        input_terms = jnp.stack([bias_query, bias_value])
        branch_terms = jnp.stack([bias_out, bias_down])
        summed = (
            lax.psum_scatter(gain_terms, ("dp", "ctx"), scatter_dimension=1, tiled=True),
            lax.psum_scatter(offset_terms, ("dp", "ctx"), scatter_dimension=1, tiled=True),
            lax.psum_scatter(grad_joint, ("dp", "ctx"), scatter_dimension=0, tiled=True),
            lax.psum_scatter(input_terms, ("dp", "ctx"), scatter_dimension=1, tiled=True),
            lax.psum_scatter(grad_output, ("dp", "ctx"), scatter_dimension=0, tiled=True),
            lax.psum_scatter(branch_terms, ("dp", "ctx"), scatter_dimension=1, tiled=True),
            lax.psum_scatter(grad_up, ("dp", "ctx"), scatter_dimension=0, tiled=True),
            lax.psum_scatter(bias_up, ("dp", "ctx"), scatter_dimension=0, tiled=True),
            lax.psum_scatter(grad_down, ("dp", "ctx"), scatter_dimension=0, tiled=True),
        )
        layer_grads.insert(0, summed)
    stacked = tuple(
        (
            jnp.stack([layer_entry[member_index] for layer_entry in layer_grads])
            for member_index in range(9)
        )
    )
    return (
        hidden.astype(jnp.bfloat16)[None],
        grad_hidden[None],
        stacked[0],
        stacked[1],
        stacked[2],
        stacked[3],
        stacked[4],
        stacked[5],
        stacked[6],
        stacked[7],
        stacked[8],
    )


def solution(mesh):
    placed = (
        P("dp", "ctx", None),
        P("dp", "ctx", None),
        P(),
        P(),
        P(),
        P(None, None, ("dp", "ctx")),
        P(None, None, ("dp", "ctx")),
        P(None, ("dp", "ctx"), None),
        P(None, None, ("dp", "ctx")),
        P(None, ("dp", "ctx"), None),
        P(None, None, ("dp", "ctx")),
        P(None, ("dp", "ctx"), None),
        P(None, ("dp", "ctx")),
        P(None, ("dp", "ctx"), None),
    )
    return jax.shard_map(
        body,
        mesh=mesh,
        in_specs=placed,
        out_specs=(
            P("dp", "ctx", None),
            P("dp", "ctx", None),
            P(None, None, ("dp", "ctx")),
            P(None, None, ("dp", "ctx")),
            P(None, ("dp", "ctx"), None),
            P(None, None, ("dp", "ctx")),
            P(None, ("dp", "ctx"), None),
            P(None, None, ("dp", "ctx")),
            P(None, ("dp", "ctx"), None),
            P(None, ("dp", "ctx")),
            P(None, ("dp", "ctx"), None),
        ),
        check_vma=False,
    )
```

profile of v0, /device:TPU:0, one launch (start us, length us, event | category | flops | bytes accessed | tf_op | source)
XLA Modules:
  0.0 5838.4 jit_solution(4293730717974979165)
XLA Ops:
  11.3 320.1 %all-gather = bf16[1,2,768]{1,0,2:T(2,128)(2,1)S(1)} all-gather(bf16[1,2,6]{1,0,2:T(2,128)(2,1)S(1)} %copy.148), channel_id=2, replica_groups=mesh['dp'=16,'ctx'=8] {'dp','ctx'}, dimensions={2}, use_global_device_ids=true | all-gather | bytes 3096 | tf_op jit(solution)/shard_map/all_gather | solution.py:172
  331.9 312.0 %all-gather.1 = bf16[1,2,768]{1,0,2:T(2,128)(2,1)S(1)} all-gather(bf16[1,2,6]{1,0,2:T(2,128)(2,1)S(1)} %copy.149), channel_id=3, replica_groups=mesh['dp'=16,'ctx'=8] {'dp','ctx'}, dimensions={2}, use_global_device_ids=true | all-gather | bytes 3096 | tf_op jit(solution)/shard_map/all_gather | solution.py:173
  644.2 314.2 %all-gather.3 = bf16[1,2,768]{1,0,2:T(2,128)(2,1)S(1)} all-gather(bf16[1,2,6]{1,0,2:T(2,128)(2,1)S(1)} %copy.150), channel_id=5, replica_groups=mesh['dp'=16,'ctx'=8] {'dp','ctx'}, dimensions={2}, use_global_device_ids=true | all-gather | bytes 3096 | tf_op jit(solution)/shard_map/all_gather | solution.py:175
  959.2 4.6 slice_reduce_fusion.10
  963.7 4.6 slice_reduce_fusion.9
  968.3 4.6 slice_reduce_fusion.12
  983.2 65.9 %all-reduce.25 = (bf16[3072]{0:T(1024)(128)(2,1)S(1)}, bf16[3072]{0:T(1024)(128)(2,1)}) all-reduce(bf16[3072]{0:T(1024)(128)(2,1)S(1)} %dynamic-update-slice, bf16[3072]{0:T(1024)(128)(2,1)S(1)} %dynamic-update-slice.1), channel_id=9, replica_groups=mesh['dp'=16,'ctx'=8] {'dp','ctx'}, use_global_device_ids=true, to_apply=%add | all-reduce | flops 6144 | bytes 24576
  1049.7 312.5 %all-gather.5 = bf16[1,2,768]{1,0,2:T(2,128)(2,1)S(1)} all-gather(bf16[1,2,6]{1,0,2:T(2,128)(2,1)S(1)} %copy.151), channel_id=7, replica_groups=mesh['dp'=16,'ctx'=8] {'dp','ctx'}, dimensions={2}, use_global_device_ids=true | all-gather | bytes 3096 | tf_op jit(solution)/shard_map/all_gather | solution.py:177
  1362.7 313.8 %all-gather.9 = bf16[1,2,768]{1,0,2:T(2,128)(2,1)S(1)} all-gather(bf16[1,2,6]{1,0,2:T(2,128)(2,1)S(1)} %copy.152), channel_id=11, replica_groups=mesh['dp'=16,'ctx'=8] {'dp','ctx'}, dimensions={2}, use_global_device_ids=true | all-gather | bytes 3096 | tf_op jit(solution)/shard_map/all_gather | solution.py:172
  1676.8 312.4 %all-gather.10 = bf16[1,2,768]{1,0,2:T(2,128)(2,1)S(1)} all-gather(bf16[1,2,6]{1,0,2:T(2,128)(2,1)S(1)} %copy.153), channel_id=12, replica_groups=mesh['dp'=16,'ctx'=8] {'dp','ctx'}, dimensions={2}, use_global_device_ids=true | all-gather | bytes 3096 | tf_op jit(solution)/shard_map/all_gather | solution.py:173
  1989.6 313.8 %all-gather.12 = bf16[1,2,768]{1,0,2:T(2,128)(2,1)S(1)} all-gather(bf16[1,2,6]{1,0,2:T(2,128)(2,1)S(1)} %copy.154), channel_id=14, replica_groups=mesh['dp'=16,'ctx'=8] {'dp','ctx'}, dimensions={2}, use_global_device_ids=true | all-gather | bytes 3096 | tf_op jit(solution)/shard_map/all_gather | solution.py:175
  2304.2 4.5 slice_reduce_fusion.8
  2308.8 4.6 slice_reduce_fusion.2
  2313.3 4.6 slice_reduce_fusion.1
  2317.9 4.8 slice_reduce_fusion.4
  2337.7 6.7 fusion.24
  2356.5 312.8 %all-gather.14 = bf16[1,2,768]{1,0,2:T(2,128)(2,1)S(1)} all-gather(bf16[1,2,6]{1,0,2:T(2,128)(2,1)S(1)} %copy.155), channel_id=16, replica_groups=mesh['dp'=16,'ctx'=8] {'dp','ctx'}, dimensions={2}, use_global_device_ids=true | all-gather | bytes 3096 | tf_op jit(solution)/shard_map/all_gather | solution.py:177
  2669.7 4.5 slice_reduce_fusion
  2684.6 53.7 all-gather.49.cloned.1.call-done
  2740.7 318.9 %all-gather.51.cloned.1.call-done = bf16[1,768,3072]{2,0,1:T(2,128)(2,1)} async-done(((bf16[1,6,3072]{2,0,1:T(2,128)(2,1)}), bf16[1,768,3072]{2,0,1:T(2,128)(2,1)}) %all-gather.51.cloned.1.call-update) | async-done | bytes 4718608 | tf_op jit(solution)/shard_map/all_gather | solution.py:178
  3059.6 5.5 fusion.27
  3065.1 305.0 %all-gather.53.cloned.1.call-done = bf16[1,3072,768]{2,1,0:T(8,128)(2,1)} async-done(((bf16[1,24,768]{2,1,0:T(8,128)(2,1)}), bf16[1,3072,768]{2,1,0:T(8,128)(2,1)}) %all-gather.53.cloned.1.call-update) | async-done | bytes 4718608 | tf_op jit(solution)/shard_map/all_gather | solution.py:180
  3370.1 5.4 convert_reduce_fusion
  3385.5 5.4 multiply_reduce_fusion.1
  3402.9 30.2 reduce-scatter.41.cloned.1.call-done
  3434.1 44.7 reduce-scatter.39.cloned.1.call-done
  3479.9 5.2 multiply_reduce_fusion.3
  3486.5 5.3 convert_reduce_fusion.1
  3491.9 6.5 multiply_reduce_fusion.4
  3507.1 5.4 multiply_reduce_fusion
  3528.9 21.9 reduce-scatter.45.cloned.1.call-done
  3552.0 44.5 reduce-scatter.43.cloned.1.call-done
  3597.7 4.7 fusion.183
  3605.1 5.2 fusion.145
  3611.9 5.1 fusion.167
  3619.3 5.1 fusion.182
  3630.5 5.1 fusion.181
  3639.7 1484.9 %fusion.184 = (f32[8,2304]{1,0:T(8,128)S(1)}, f32[8,2304]{1,0:T(8,128)S(1)}, f32[8,768]{1,0:T(8,128)S(1)}, f32[8,768]{1,0:T(8,128)S(1)}, f32[8,3072]{1,0:T(8,128)S(1)}, /*index=5*/f32[8,3072]{1,0:T(8,128)}) fusion(f32[768,2304]{1,0:T(8,128)} %fusion.144, f32[768,2304]{1,0:T(8,128)} %fusion.143, f32[768,768]{1,0:T(8,128)S(1)} %fusion.202, ...), kind=kCustom, calls=%all-reduce-scatter.6 | all-reduce-scatter fusion | flops 12582913 | bytes 38141952
  5137.7 5.5 collective-permute-start.123
  5151.2 7.2 collective-permute-start.118
  5203.3 4.9 collective-permute-start.99
  5229.7 4.7 collective-permute-start.86
  5310.7 4.6 collective-permute-start.54
  5319.4 5.2 collective-permute-start.51
  5336.0 4.7 collective-permute-start.44
  5340.7 4.6 collective-permute-start.43
  5384.6 4.6 fusion.117
  5393.5 4.7 collective-permute-start.22
  5414.2 7.1 concatenate.11
  5421.4 25.7 concatenate.10
  5455.2 5.7 collective-permute-start.11
  5478.1 5.8 collective-permute-start.3
  5490.2 4.6 collective-permute-start
  5543.8 6.1 collective-permute-start.171
  5553.9 7.8 collective-permute-start.168
  5572.8 5.1 collective-permute-start.163
  5600.2 7.0 collective-permute-start.151
  5611.1 5.4 collective-permute-start.148
  5628.3 32.6 concatenate.9
  5664.1 5.1 collective-permute-start.140
  5674.5 32.6 concatenate.8
  5723.5 4.9 collective-permute-start.131
  5739.5 33.3 concatenate.13
  5772.9 55.2 concatenate.12
  (1079 shorter events, 534.5 us)
Async XLA Ops:
  7.2 965.8 %all-gather.39.cloned.1.call-start = ((), (), s32[]{:S(2)}) async-start(), calls=%async_computation.12 | async-start | bytes 7133184 | tf_op jit(solution)/shard_map/all_gather | solution.py:174
  8.9 2314.9 %all-gather.31.cloned.1.call-start = ((), (), s32[]{:S(2)}) async-start(), calls=%async_computation.6 | async-start | bytes 1769472 | tf_op jit(solution)/shard_map/all_gather | solution.py:200
  977.9 1347.6 %all-gather.33.cloned.1.call-start = ((), (), s32[]{:S(2)}) async-start(), calls=%async_computation.7 | async-start | bytes 1769472 | tf_op jit(solution)/shard_map/all_gather | solution.py:199
  978.7 1356.0 %all-gather.41.cloned.1.call-start = ((), (), s32[]{:S(2)}) async-start(), calls=%async_computation.13 | async-start | bytes 2377728 | tf_op jit(solution)/shard_map/all_gather | solution.py:176
  979.4 1357.8 %all-gather.43.cloned.1.call-start = ((), (), s32[]{:S(2)}) async-start(), calls=%async_computation.14 | async-start | bytes 9510912 | tf_op jit(solution)/shard_map/all_gather | solution.py:178
  980.2 1364.2 %all-gather.45.cloned.1.call-start = ((), (), s32[]{:S(2)}) async-start(), calls=%async_computation.15 | async-start | bytes 4755456 | tf_op jit(solution)/shard_map/all_gather | solution.py:180
  981.0 1367.7 %all-gather.47.cloned.1.call-start = ((), (), s32[]{:S(2)}) async-start(), calls=%async_computation.16 | async-start | bytes 7133184 | tf_op jit(solution)/shard_map/all_gather | solution.py:174
  981.7 1692.7 %all-gather.35.cloned.1.call-start = ((), (), s32[]{:S(2)}) async-start(), calls=%async_computation.8 | async-start | bytes 1769472 | tf_op jit(solution)/shard_map/all_gather | solution.py:200
  2353.6 323.5 %all-gather.37.cloned.1.call-start = ((), (), s32[]{:S(2)}) async-start(), calls=%async_computation.9 | async-start | bytes 1769472 | tf_op jit(solution)/shard_map/all_gather | solution.py:199
  2354.4 383.9 %all-gather.49.cloned.1.call-start = ((), (), s32[]{:S(2)}) async-start(), calls=%async_computation.17 | async-start | bytes 2377728 | tf_op jit(solution)/shard_map/all_gather | solution.py:176
  2355.0 704.6 %all-gather.51.cloned.1.call-start = ((), (), s32[]{:S(2)}) async-start(), calls=%async_computation.18 | async-start | bytes 9510912 | tf_op jit(solution)/shard_map/all_gather | solution.py:178
  2355.7 1014.4 %all-gather.53.cloned.1.call-start = ((), (), s32[]{:S(2)}) async-start(), calls=%async_computation.19 | async-start | bytes 4755456 | tf_op jit(solution)/shard_map/all_gather | solution.py:180
  2356.3 1076.7 %reduce-scatter.41.cloned.1.call-start = ((), (), s32[]{:S(2)}) async-start(), calls=%async_computation.21 | async-start | bytes 1769472
  3385.5 93.3 %reduce-scatter.39.cloned.1.call-start = ((), (), s32[]{:S(2)}) async-start(), calls=%async_computation.20 | async-start | bytes 1769472
  3399.5 151.3 %reduce-scatter.45.cloned.1.call-start = ((), (), s32[]{:S(2)}) async-start(), calls=%async_computation.23 | async-start | bytes 1769472
  3506.8 89.7 %reduce-scatter.43.cloned.1.call-start = ((), (), s32[]{:S(2)}) async-start(), calls=%async_computation.22 | async-start | bytes 1769472
  3521.1 1979.7 %all-reduce.29.cloned.1.call-start = ((), (), s32[]{:S(2)}) async-start(), calls=%async_computation.24 | async-start | bytes 147456
  3605.1 2224.8 %reduce-scatter.37.cloned.1.call-start = ((), (), s32[]{:S(2)}) async-start(), calls=%async_computation.11 | async-start | bytes 9510912 | tf_op jit(solution)/shard_map/reduce_scatter | solution.py:336
  3610.4 2219.5 %reduce-scatter.35.cloned.1.call-start = ((), (), s32[]{:S(2)}) async-start(), calls=%async_computation.10 | async-start | bytes 9510912 | tf_op jit(solution)/shard_map/reduce_scatter | solution.py:336
  5126.0 18.6 collective-permute-start.126
  5128.9 18.2 collective-permute-start.125
  5130.2 18.9 collective-permute-start.124
  5278.7 26.4 collective-permute-start.62
  5280.1 22.4 collective-permute-start.31
  5281.4 22.4 collective-permute-start.63
  5307.8 16.9 collective-permute-start.55
  5310.7 17.1 collective-permute-start.54
  5336.0 16.7 collective-permute-start.44
  5400.1 47.1 collective-permute-start.20
  5403.1 45.4 collective-permute-start.19
  5405.5 45.5 collective-permute-start.18
  5407.4 45.0 collective-permute-start.17
  5409.6 45.6 collective-permute-start.16
  5476.3 18.5 collective-permute-start.4
  5478.1 18.0 collective-permute-start.3
  5511.9 16.7 collective-permute-start.183
  5540.5 21.2 collective-permute-start.172
  5543.8 19.2 collective-permute-start.171
  5551.9 17.6 collective-permute-start.169
  5553.9 18.8 collective-permute-start.168
  5563.1 18.0 collective-permute-start.166
  5566.1 17.4 collective-permute-start.165
  5569.5 18.0 collective-permute-start.164
  5572.8 16.9 collective-permute-start.163
  5598.3 19.0 collective-permute-start.152
  5600.2 19.2 collective-permute-start.151
  5617.2 43.8 collective-permute-start.147
  5619.4 43.2 collective-permute-start.146
  5621.3 42.7 collective-permute-start.145
  5623.3 45.9 collective-permute-start.144
  5625.6 46.2 collective-permute-start.143
  5661.1 46.1 collective-permute-start.142
  5662.6 46.5 collective-permute-start.141
  5664.1 47.7 collective-permute-start.140
  5669.2 44.2 collective-permute-start.139
  5671.8 45.7 collective-permute-start.138
  5711.8 16.7 collective-permute-start.135
  5713.5 17.4 collective-permute-start.134
  5717.5 16.7 collective-permute-start.133
  5720.5 52.3 collective-permute-start.132
  5723.5 49.4 collective-permute-start.131
  5728.4 44.4 collective-permute-start.130
  5730.9 42.0 collective-permute-start.129
  5734.9 38.0 collective-permute-start.128
  (393 other events, 20387.4 us)
Sparse Core Ops, SparseCore 0:
  10.3 312.1 all-gather.38
  978.0 37.2 all-gather.30
  1017.5 44.5 all-gather.32
  1063.7 301.8 all-gather.40
  1367.7 318.2 all-gather.42
  1687.5 309.0 all-gather.44
  1998.9 310.3 all-gather.46
  2353.7 37.8 all-gather.34
  2393.9 44.7 all-gather.36
  2440.2 298.1 all-gather.48
  2740.6 318.9 all-gather.50
  3061.7 308.3 all-gather.52
  3385.6 47.3 reduce-scatter.40
  3435.3 43.4 reduce-scatter.38
  3506.9 43.8 reduce-scatter.44
  3553.1 43.4 reduce-scatter.42
  3605.2 159.6 all-reduce.28
  3767.3 665.9 reduce-scatter.36
  4435.7 661.2 reduce-scatter.34
where the time goes:
time: 5860 us; the launch traced here: 5840 us
  blocking collectives  4060 us (69%)
  waiting for transfers between devices  823 us (14%)
  starting transfers between devices  496 us (8%)
  local copies, waits for them, and re-layouts  273 us (5%)
  matrix products  132 us (2%)
    unnamed x2, blocking collectives  1550 us
    all_gather x2, blocking collectives, body(): lax.all_gather(norm_gain[layer_index], ('dp', 'ctx'), axis=1, tiled=True)  634 us
    all_gather x2, blocking collectives, body(): lax.all_gather(input_bias[layer_index], ('dp', 'ctx'), axis=1, tiled=True)  628 us
    all_gather x2, blocking collectives, body(): lax.all_gather(branch_bias[layer_index], ('dp', 'ctx'), axis=1, tiled=True)  625 us
    all_gather x2, blocking collectives, body(): lax.all_gather(norm_bias[layer_index], ('dp', 'ctx'), axis=1, tiled=True)  624 us
    unnamed x197, starting transfers between devices  495 us
    all_gather x2, waiting for transfers between devices, body(): lax.all_gather(up_weight[layer_index], ('dp', 'ctx'), axis=0, tiled=True)  319 us
    all_gather x2, waiting for transfers between devices, body(): lax.all_gather(down_weight[layer_index], ('dp', 'ctx'), axis=0, tiled=True)  305 us
  transfers between devices with their start and end apart: 211, of which 8 were waited for; matrix products, arithmetic and copies ran while one was open for 32% of the time, Pallas kernels for 0%

commit v1 on v0

v1 whole, which is shorter than its diff:
```python
import jax
import jax.numpy as jnp
from jax import lax
from jax.sharding import Mesh, PartitionSpec as P

HEAD_DIM = 64
LAYERS = 2


norm_eps = 1e-05
score_scale = 0.125


def layer_norm(values, scales, offset):
    centre = values - jnp.mean(values, axis=-1, keepdims=True)
    spread = jnp.mean(centre * centre, axis=-1, keepdims=True)
    return centre * lax.rsqrt(spread + norm_eps) * scales + offset


def gelu_tanh(values):
    return (
        0.5
        * values
        * (1.0 + jnp.tanh(0.7978845608028654 * (values + 0.044715 * values * values * values)))
    )


def token_ids(group_index, positions, sequence_group, sequence_start, sequence_length):
    member = (
        (sequence_group[None, :] == group_index)
        & (sequence_start[None, :] <= positions[:, None])
        & (positions[:, None] < (sequence_start + sequence_length)[None, :])
    )
    numbers = jnp.arange(sequence_group.shape[0], dtype=jnp.int32) + 1
    located = jnp.sum(jnp.where(member, numbers[None, :], 0), axis=1)
    return jnp.where(located > 0, located - 1, -1 - positions)


DATA = ("y", "zh", "c")
CTX = ("x", "zl")
ALL = DATA + CTX
bf16 = jnp.bfloat16
f32 = jnp.float32


def outer_sum(left, right):
    return lax.dot_general(left, right, (((0,), (0,)), ((), ())), preferred_element_type=f32)


def back_product(left, matrix):
    return lax.dot_general(left, matrix, (((1,), (1,)), ((), ())), preferred_element_type=f32)


def column_sums(values):
    return jnp.sum(values.astype(f32), axis=0)


def spread(values, axes):
    count = lax.axis_size(axes)
    return lax.all_to_all(jnp.broadcast_to(values[None], (count,) + values.shape), axes, 0, 0)


def scores_of(q, k):
    return lax.dot_general(q, k, (((1,), (1,)), ((), ())), preferred_element_type=f32) * score_scale


def attend(q, k, v, visible):
    scores = jnp.where(visible, scores_of(q, k), -1000000000.0)
    row_max = jnp.max(scores, axis=-1, keepdims=True)
    raised = jnp.exp(scores - row_max)
    totals = jnp.sum(raised, axis=-1, keepdims=True)
    weights = (raised / totals).astype(bf16)
    mixed = jnp.dot(weights, v, preferred_element_type=f32)
    return mixed.astype(bf16), row_max + jnp.log(totals)


def attend_back(q, k, v, visible, log_total, mix_grad):
    weights = jnp.where(visible, jnp.exp(scores_of(q, k) - log_total), 0.0)
    weight_grad = lax.dot_general(mix_grad, v, (((1,), (1,)), ((), ())), preferred_element_type=f32)
    centre = jnp.sum(weights * weight_grad, axis=-1, keepdims=True)
    score_grad = (weights * (weight_grad - centre)).astype(bf16)
    q_grad = jnp.dot(score_grad, k, preferred_element_type=f32) * score_scale
    k_grad = outer_sum(score_grad, q) * score_scale
    v_grad = outer_sum(weights.astype(bf16), mix_grad)
    return q_grad.astype(bf16), k_grad.astype(bf16), v_grad.astype(bf16)


def to_heads(values, parts):
    pieces = []
    for x in range(4):
        for zl in range(2):
            own, shared = 3 * x + 2 * zl, 3 * x + 1
            for head in (own, shared):
                for v in values:
                    pieces.append(v[:, 64 * head : 64 * head + 64])
    width = 128 * len(values)
    return jnp.concatenate(pieces, axis=1).reshape(values[0].shape[0], 8, width).transpose(1, 0, 2)


def body(hidden_in, out_grad, sequence_group, sequence_start, sequence_length, norm_gain, norm_bias,
         input_weight, input_bias, output_weight, branch_bias, up_weight, up_bias, down_weight):
    width = hidden_in.shape[2]
    rows = hidden_in.shape[1]
    group_index = lax.axis_index(DATA)
    parity = lax.axis_index("zl")
    slots = rows * 8
    positions = jnp.arange(slots, dtype=jnp.int32)
    ids = token_ids(group_index, positions, sequence_group, sequence_start, sequence_length)
    visible = (ids[:, None] == ids[None, :]) & (positions[None, :] <= positions[:, None])

    def half_of(values):
        split = values.reshape((4, 2, rows) + values.shape[1:])
        return lax.dynamic_index_in_dim(split, parity, 1, keepdims=False).reshape((4 * rows,) + values.shape[1:])

    def pad_half(values):
        zero = jnp.zeros((4, 2, rows) + values.shape[1:], values.dtype)
        return lax.dynamic_update_index_in_dim(zero, values.reshape((4, rows) + values.shape[1:]), parity, 1).reshape(
            (8 * rows,) + values.shape[1:])

    visible_half = half_of(visible)

    smalls = jnp.concatenate([v.reshape(-1) for v in (norm_gain, norm_bias, input_bias, branch_bias, up_bias)])
    smalls = jnp.pad(smalls, (0, 2048 - smalls.shape[0])).reshape(16, 128)
    full = []
    for l in range(LAYERS):
        flat = [input_weight[l].reshape(-1, 128), output_weight[l].reshape(-1, 128), up_weight[l].reshape(-1, 128),
                down_weight[l].reshape(-1, 128)]
        if l == 0:
            flat.append(smalls)
        got = spread(jnp.concatenate(flat, axis=0), CTX)
        if l == 0:
            few = spread(got[:, 432:434], DATA).reshape(128, 256)
        own = (got[:, 0:108].reshape(48, 2304), got[:, 108:144].reshape(48, 768), got[:, 144:288].reshape(48, 3072),
               got[:, 288:432].reshape(192, 768))
        full.append([lax.all_gather(w, DATA, axis=0, tiled=True) for w in own])
    few = few.astype(f32)

    def vec(first):
        return few[:, first : first + 6].reshape(-1)

    gains = [[vec(12 * l + 6 * i) for i in range(2)] for l in range(2)]
    offsets = [[vec(24 + 12 * l + 6 * i) for i in range(2)] for l in range(2)]
    in_biases = [[vec(48 + 12 * l + 6 * i) for i in range(2)] for l in range(2)]
    out_biases = [[vec(72 + 12 * l + 6 * i) for i in range(2)] for l in range(2)]
    up_biases = [few[:, 96 + 24 * l : 120 + 24 * l].reshape(-1) for l in range(2)]

    hidden = hidden_in[0].astype(f32)
    stored = []
    for l in range(LAYERS):
        w_in, w_out, w_up, w_down = full[l]
        normed = layer_norm(hidden, gains[l][0], offsets[l][0]).astype(bf16)
        joined = jnp.dot(normed, w_in, preferred_element_type=f32)
        q = (joined[:, :width] + in_biases[l][0]).astype(bf16)
        k = joined[:, width : 2 * width].astype(bf16)
        v = (joined[:, 2 * width :] + in_biases[l][1]).astype(bf16)
        heads = lax.all_to_all(to_heads((q, k, v), 3), CTX, 0, 0).reshape(slots, 384)
        own = (heads[:, :64], heads[:, 64:128], heads[:, 128:192])
        shared = (half_of(heads[:, 192:256]), heads[:, 256:320], heads[:, 320:384])
        mix_own, log_own = attend(*own, visible)
        mix_shared, log_shared = attend(*shared, visible_half)
        back = lax.all_to_all(
            jnp.concatenate([mix_own, pad_half(mix_shared)], axis=1).reshape(8, rows, 128), CTX, 0, 0)
        mixed = []
        for x in range(4):
            mixed += [back[2 * x, :, :64], back[2 * x, :, 64:] + back[2 * x + 1, :, 64:], back[2 * x + 1, :, :64]]
        mixed = jnp.concatenate(mixed, axis=1)
        middle = hidden + jnp.dot(mixed, w_out, preferred_element_type=f32) + out_biases[l][0]
        second = layer_norm(middle, gains[l][1], offsets[l][1]).astype(bf16)
        pre_gelu = jnp.dot(second, w_up, preferred_element_type=f32) + up_biases[l]
        activated = gelu_tanh(pre_gelu).astype(bf16)
        stored.append((hidden, normed, own, shared, log_own, log_shared, mixed, middle, second, pre_gelu, activated))
        hidden = middle + jnp.dot(activated, w_down, preferred_element_type=f32) + out_biases[l][1]

    grad_hidden = out_grad[0].astype(f32)
    grads = [None, None]
    small_grads = [None, None]
    for l in reversed(range(LAYERS)):
        w_in, w_out, w_up, w_down = full[l]
        layer_input, normed, own, shared, log_own, log_shared, mixed, middle, second, pre_gelu, activated = stored[l]

        def scatter(grad):
            return lax.psum_scatter(grad.astype(bf16), DATA, scatter_dimension=0, tiled=True)

        down_grad = grad_hidden.astype(bf16)
        grad_down = scatter(outer_sum(activated, down_grad))
        bias_down = column_sums(down_grad)
        gelu_grad = back_product(down_grad, w_down)
        pre_grad = jax.vjp(gelu_tanh, pre_gelu)[1](gelu_grad)[0].astype(bf16)
        grad_up = scatter(outer_sum(second, pre_grad))
        bias_up = column_sums(pre_grad)
        second_grad = back_product(pre_grad, w_up)
        middle_grad, scale_two, offset_two = jax.vjp(layer_norm, middle, gains[l][1], offsets[l][1])[1](second_grad)
        grad_middle = grad_hidden + middle_grad
        branch_grad = grad_middle.astype(bf16)
        grad_output = scatter(outer_sum(mixed, branch_grad))
        bias_out = column_sums(branch_grad)
        mix_grad = back_product(branch_grad, w_out).astype(bf16)
        got = lax.all_to_all(to_heads((mix_grad,), 1), CTX, 0, 0).reshape(slots, 128)
        own_grads = attend_back(*own, visible, log_own, got[:, :64])
        shared_grads = attend_back(*shared, visible_half, log_shared, half_of(got[:, 64:]))
        shared_grads = (pad_half(shared_grads[0]),) + shared_grads[1:]
        back = lax.all_to_all(
            jnp.concatenate(own_grads + shared_grads, axis=1).reshape(8, rows, 384), CTX, 0, 0)
        joined_grad = []
        for part in range(3):
            for x in range(4):
                lo, hi = back[2 * x], back[2 * x + 1]
                a, b = 64 * part, 192 + 64 * part
                both = (lo[:, b : b + 64].astype(f32) + hi[:, b : b + 64].astype(f32)).astype(bf16)
                joined_grad += [lo[:, a : a + 64], both, hi[:, a : a + 64]]
        joined_grad = jnp.concatenate(joined_grad, axis=1)
        grad_joint = scatter(outer_sum(normed, joined_grad))
        bias_query = column_sums(joined_grad[:, :width])
        bias_value = column_sums(joined_grad[:, 2 * width :])
        normed_grad = back_product(joined_grad, w_in)
        input_grad, scale_one, offset_one = jax.vjp(layer_norm, layer_input, gains[l][0], offsets[l][0])[1](normed_grad)
        grad_hidden = grad_middle + input_grad
        flat = jnp.concatenate([grad_joint.reshape(8, 108, 128), grad_output.reshape(8, 36, 128),
                                grad_up.reshape(8, 144, 128), grad_down.reshape(8, 144, 128)], axis=1)
        flat = jnp.sum(lax.all_to_all(flat, CTX, 0, 0).astype(f32), axis=0)
        grads[l] = (flat[0:108].reshape(6, 2304), flat[108:144].reshape(6, 768), flat[144:288].reshape(6, 3072),
                    flat[288:432].reshape(24, 768))
        small_grads[l] = [t.reshape(128, -1) for t in (scale_one, scale_two, offset_one, offset_two, bias_query,
                                                       bias_value, bias_out, bias_down, bias_up)]
    few = jnp.concatenate(small_grads[0] + small_grads[1], axis=1)
    few = jnp.pad(few, ((0, 0), (0, 256 - 144)))
    few = jnp.sum(lax.all_to_all(few, ALL, 0, 0, tiled=True), axis=0)

    def pair(first):
        return jnp.stack([jnp.stack([few[72 * l + first + 6 * i : 72 * l + first + 6 * i + 6] for i in range(2)])
                          for l in range(2)])

    return (
        hidden.astype(bf16)[None],
        grad_hidden[None],
        pair(0),
        pair(12),
        jnp.stack([grads[0][0], grads[1][0]]),
        pair(24),
        jnp.stack([grads[0][1], grads[1][1]]),
        pair(36),
        jnp.stack([grads[0][2], grads[1][2]]),
        jnp.stack([few[48:72], few[120:144]]),
        jnp.stack([grads[0][3], grads[1][3]]),
    )


def solution(mesh):
    mesh = Mesh(mesh.devices.reshape(4, 2, 2, 4, 2), ALL)
    token = P(DATA, CTX, None)
    one = P(None, ALL)
    two = P(None, None, ALL)
    mat = P(None, ALL, None)
    return jax.shard_map(
        body,
        mesh=mesh,
        in_specs=(token, token, P(), P(), P(), two, two, mat, two, mat, two, mat, one, mat),
        out_specs=(token, token, two, two, mat, two, mat, two, mat, one, mat),
        check_vma=False,
    )
```

time: 5860 us -> 1240 us (0.21)
  blocking collectives: 4060 us -> 52.1 us
  starting transfers between devices: 496 us -> 52.1 us
  local copies, waits for them, and re-layouts: 273 us -> 146 us
    all_gather x8 -> x0, blocking collectives: 2510 us -> none  [the longest x2 634 us: body(): lax.all_gather(norm_gain[layer_index], ('dp', 'ctx'), axis=1, tiled=True)]
    unnamed x2 -> x0, blocking collectives: 1550 us -> none
    unnamed x197 -> x0, starting transfers between devices: 495 us -> none
    reduce_scatter x2 -> x8, waiting for transfers between devices: 0.01 us -> 447 us  [scatter(): lax.psum_scatter(grad.astype(bf16), DATA, scatter_dimension=0, tiled=True)]
    all_gather x12 -> x8, waiting for transfers between devices: 678 us -> 284 us  [body(): full.append([lax.all_gather(w, DATA, axis=0, tiled=True) for w in own])]
    unnamed x528 -> x322, local copies, waits for them, and re-layouts: 214 us -> 20.2 us
    unnamed x216 -> x16, waiting for transfers between devices: 145 us -> 0.26 us
    all_to_all x0 -> x11, waiting for transfers between devices: none -> 70 us  [the longest x2 19.1 us: body(): lax.all_to_all(jnp.concatenate(own_grads + shared_grads, axis=1).reshape(...]
  transfers between devices with their start and end apart: 211 -> 27, of which waited for: 8 -> 23; matrix products, arithmetic and copies ran while one was open for 32% -> 19% of each run, Pallas kernels for 0% -> 0%
where the time goes in v1:
time: 1240 us; the launch traced here: 1230 us
  waiting for transfers between devices  801 us (65%)
  local copies, waits for them, and re-layouts  146 us (12%)
  matrix products  121 us (10%)
  starting transfers between devices  52.1 us (4%)
  blocking collectives  52.1 us (4%)
  other arithmetic  41.3 us (3%)
  between operations  16.8 us (1%)
    reduce_scatter x8, waiting for transfers between devices, scatter(): lax.psum_scatter(grad.astype(bf16), DATA, scatter_dimension=0, tiled=True)  447 us
    all_gather x8, waiting for transfers between devices, body(): full.append([lax.all_gather(w, DATA, axis=0, tiled=True) for w in own])  284 us
    dot_general x16, matrix products, outer_sum(): lax.dot_general(left, right, (((0,), (0,)), ((), ())), preferred_element_...  42.4 us
    all_to_all x2, blocking collectives, spread(): lax.all_to_all(jnp.broadcast_to(values[None], (count,) + values.shape), a...  35 us
  transfers between devices with their start and end apart: 27, of which 23 were waited for; matrix products, arithmetic and copies ran while one was open for 19% of the time, Pallas kernels for 0%

profile of v1, /device:TPU:0, one launch (start us, length us, event | category | flops | bytes accessed | tf_op | source)
XLA Modules:
  0.0 1230.1 jit_solution(379790258873315613)
XLA Ops:
  15.8 19.7 %all_to_all.74 = bf16[8,448,128]{2,1,0:T(8,128)(2,1)S(1)} all-to-all(bf16[8,448,128]{2,1,0:T(8,128)(2,1)S(1)} %broadcast_in_dim.71), channel_id=1, replica_groups=mesh['y'=4,'zh'=2,'c'=2,'x'=4,'zl'=2] {'x','zl'}, dimensions={0} | all-to-all | bytes 1835008 | tf_op jit(solution)/shard_map/all_to_all | solution.py:60
  39.7 15.3 %all_to_all.75 = bf16[8,432,128]{2,1,0:T(8,128)(2,1)S(1)} all-to-all(bf16[8,432,128]{2,1,0:T(8,128)(2,1)S(1)} %broadcast_in_dim.136), channel_id=1, replica_groups=mesh['y'=4,'zh'=2,'c'=2,'x'=4,'zl'=2] {'x','zl'}, dimensions={0} | all-to-all | bytes 1769472 | tf_op jit(solution)/shard_map/all_to_all | solution.py:60
  59.2 7.6 all-to-all-start.1
  66.8 7.6 all-to-all-done.1
  76.1 18.4 %all-gather.9.cloned.1.call-done = bf16[768,2304]{1,0:T(8,128)(2,1)} async-done(((bf16[48,2304]{1,0:T(8,128)(2,1)}), bf16[768,2304]{1,0:T(8,128)(2,1)}) %all-gather.9.cloned.1.call-update) | async-done | bytes 3538960 | tf_op jit(solution)/shard_map/all_gather | solution.py:135
  94.5 2.7 fusion.177
  97.7 4.8 concatenate.110
  103.5 4.3 all-to-all-start.2
  111.2 9.6 all-to-all-done.2
  120.9 2.8 fusion.3
  128.8 3.5 fusion.1
  135.9 3.4 all-to-all-start.3
  143.3 2.8 all-to-all-done.3
  150.2 56.5 %all-gather.13.cloned.1.call-done = bf16[768,3072]{1,0:T(8,128)(2,1)} async-done(((bf16[48,3072]{1,0:T(8,128)(2,1)}), bf16[768,3072]{1,0:T(8,128)(2,1)}) %all-gather.13.cloned.1.call-update) | async-done | bytes 4718608 | tf_op jit(solution)/shard_map/all_gather | solution.py:135
  206.7 4.3 convolution_add_fusion.1
  211.0 55.1 %all-gather.15.cloned.1.call-done = bf16[3072,768]{1,0:T(8,128)(2,1)} async-done(((bf16[192,768]{1,0:T(8,128)(2,1)}), bf16[3072,768]{1,0:T(8,128)(2,1)}) %all-gather.15.cloned.1.call-update) | async-done | bytes 4718608 | tf_op jit(solution)/shard_map/all_gather | solution.py:135
  266.1 3.9 fusion.179
  270.3 50.5 %all-gather.17.cloned.1.call-done = bf16[768,2304]{1,0:T(8,128)(2,1)} async-done(((bf16[48,2304]{1,0:T(8,128)(2,1)}), bf16[768,2304]{1,0:T(8,128)(2,1)}) %all-gather.17.cloned.1.call-update) | async-done | bytes 3538960 | tf_op jit(solution)/shard_map/all_gather | solution.py:135
  320.8 2.7 fusion.180
  325.9 4.2 concatenate.116
  331.4 17.1 %all_to_all.76 = bf16[8,128,384]{2,1,0:T(8,128)(2,1)S(1)} all-to-all(bf16[8,128,384]{2,1,0:T(8,128)(2,1)S(1)} %bitcast.411), channel_id=1, replica_groups=mesh['y'=4,'zh'=2,'c'=2,'x'=4,'zl'=2] {'x','zl'}, dimensions={0} | all-to-all | bytes 1572864 | tf_op jit(solution)/shard_map/all_to_all | solution.py:156
  359.8 3.4 all-to-all-start.6
  367.2 2.9 all-to-all-done.6
  381.1 47.7 %all-gather.21.cloned.1.call-done = bf16[768,3072]{1,0:T(8,128)(2,1)} async-done(((bf16[48,3072]{1,0:T(8,128)(2,1)}), bf16[768,3072]{1,0:T(8,128)(2,1)}) %all-gather.21.cloned.1.call-update) | async-done | bytes 4718608 | tf_op jit(solution)/shard_map/all_gather | solution.py:135
  428.7 4.4 convolution_add_fusion
  433.1 54.6 %all-gather.23.cloned.1.call-done = bf16[3072,768]{1,0:T(8,128)(2,1)} async-done(((bf16[192,768]{1,0:T(8,128)(2,1)}), bf16[3072,768]{1,0:T(8,128)(2,1)}) %all-gather.23.cloned.1.call-update) | async-done | bytes 4718608 | tf_op jit(solution)/shard_map/all_gather | solution.py:135
  487.8 6.0 convert_reduce_fusion.2
  503.5 4.8 all-to-all-start.7
  510.9 4.8 all-to-all-done.7
  515.7 3.6 multiply_reduce_fusion.1
  524.1 2.7 fusion.40
  543.2 3.5 concatenate.128
  546.6 4.2 all-to-all-start.8
  550.9 2.5 convolution_convert_fusion.6
  553.4 8.9 all-to-all-done.8
  574.5 4.2 convolution_convert_fusion.2
  578.8 5.2 convolution_convert_fusion
  584.6 4.8 convolution_convert_fusion.1
  590.1 4.3 multiply_reduce_fusion.5
  595.8 5.7 convert_reduce_fusion.3
  611.0 4.3 all-to-all-start.9
  617.3 5.0 all-to-all-done.9
  624.1 3.6 multiply_reduce_fusion
  633.5 2.5 fusion.34
  636.8 3.3 fusion.43
  651.5 3.4 concatenate.137
  654.8 3.5 all-to-all-start.10
  660.0 10.2 all-to-all-done.10
  673.6 3.0 convolution_convert_fusion.5
  678.0 3.9 convolution_convert_fusion.3
  683.0 3.7 convolution_convert_fusion.4
  690.7 4.1 fusion.37
  717.2 2.5 fusion.138
  725.5 6.5 all-to-all-start.11
  733.0 8.3 all-to-all-done.11
  742.9 51.3 %reduce-scatter.23.cloned.1.call-done = bf16[192,768]{1,0:T(8,128)(2,1)} async-done(((bf16[3072,768]{1,0:T(8,128)(2,1)}), bf16[192,768]{1,0:T(8,128)(2,1)}) %reduce-scatter.23.cloned.1.call-update) | async-done | bytes 294928 | tf_op jit(solution)/shard_map/reduce_scatter | solution.py:182
  795.4 84.0 %reduce-scatter.21.cloned.1.call-done = bf16[48,3072]{1,0:T(8,128)(2,1)} async-done(((bf16[768,3072]{1,0:T(8,128)(2,1)}), bf16[48,3072]{1,0:T(8,128)(2,1)}) %reduce-scatter.21.cloned.1.call-update) | async-done | bytes 294928 | tf_op jit(solution)/shard_map/reduce_scatter | solution.py:182
  881.5 4.3 all-to-all-start.13
  886.6 63.2 %reduce-scatter.11.cloned.1.call-done = bf16[48,768]{1,0:T(8,128)(2,1)} async-done(((bf16[768,768]{1,0:T(8,128)(2,1)}), bf16[48,768]{1,0:T(8,128)(2,1)}) %reduce-scatter.11.cloned.1.call-update) | async-done | bytes 73744 | tf_op jit(solution)/shard_map/reduce_scatter | solution.py:182
  950.8 79.0 %reduce-scatter.9.cloned.1.call-done = bf16[48,2304]{1,0:T(8,128)(2,1)} async-done(((bf16[768,2304]{1,0:T(8,128)(2,1)}), bf16[48,2304]{1,0:T(8,128)(2,1)}) %reduce-scatter.9.cloned.1.call-update) | async-done | bytes 221200 | tf_op jit(solution)/shard_map/reduce_scatter | solution.py:182
  1031.0 84.2 %reduce-scatter.15.cloned.1.call-done = bf16[192,768]{1,0:T(8,128)(2,1)} async-done(((bf16[3072,768]{1,0:T(8,128)(2,1)}), bf16[192,768]{1,0:T(8,128)(2,1)}) %reduce-scatter.15.cloned.1.call-update) | async-done | bytes 294928 | tf_op jit(solution)/shard_map/reduce_scatter | solution.py:182
  1116.5 84.7 %reduce-scatter.13.cloned.1.call-done = bf16[48,3072]{1,0:T(8,128)(2,1)} async-done(((bf16[768,3072]{1,0:T(8,128)(2,1)}), bf16[48,3072]{1,0:T(8,128)(2,1)}) %reduce-scatter.13.cloned.1.call-update) | async-done | bytes 294928 | tf_op jit(solution)/shard_map/reduce_scatter | solution.py:182
  1203.3 4.4 all-to-all-start.12
  1210.2 9.9 all-to-all-done.12
  (665 shorter events, 205.5 us)
Async XLA Ops:
  7.2 87.3 %all-gather.9.cloned.1.call-start = ((), (), s32[]{:S(2)}) async-start(), calls=%async_computation.22 | async-start | bytes 3760128 | tf_op jit(solution)/shard_map/all_gather | solution.py:135
  36.4 111.2 %all-gather.11.cloned.1.call-start = ((), (), s32[]{:S(2)}) async-start(), calls=%async_computation.23 | async-start | bytes 1253376 | tf_op jit(solution)/shard_map/all_gather | solution.py:135
  37.3 169.4 %all-gather.13.cloned.1.call-start = ((), (), s32[]{:S(2)}) async-start(), calls=%async_computation.24 | async-start | bytes 5013504 | tf_op jit(solution)/shard_map/all_gather | solution.py:135
  38.3 227.9 %all-gather.15.cloned.1.call-start = ((), (), s32[]{:S(2)}) async-start(), calls=%async_computation.25 | async-start | bytes 5013504 | tf_op jit(solution)/shard_map/all_gather | solution.py:135
  39.3 281.5 %all-gather.17.cloned.1.call-start = ((), (), s32[]{:S(2)}) async-start(), calls=%async_computation.26 | async-start | bytes 3760128 | tf_op jit(solution)/shard_map/all_gather | solution.py:135
  56.1 321.3 %all-gather.19.cloned.1.call-start = ((), (), s32[]{:S(2)}) async-start(), calls=%async_computation.27 | async-start | bytes 1253376 | tf_op jit(solution)/shard_map/all_gather | solution.py:135
  56.9 371.8 %all-gather.21.cloned.1.call-start = ((), (), s32[]{:S(2)}) async-start(), calls=%async_computation.28 | async-start | bytes 5013504 | tf_op jit(solution)/shard_map/all_gather | solution.py:135
  58.3 38.9 %copy-start.108 = (f32[128]{0:T(128)}, f32[128]{0:T(128)S(1)}, u32[]{:S(2)}) copy-start(f32[128]{0:T(128)S(1)} %broadcast_multiply_fusion.3) | copy-start | bytes 1540
  58.5 16.0 %copy-start.140 = (f32[128]{0:T(128)}, f32[128]{0:T(128)S(1)}, u32[]{:S(2)}) copy-start(f32[128]{0:T(128)S(1)} %fusion.64) | copy-start | bytes 1540
  59.2 15.3 %all-to-all-start.1 = ((bf16[16,8,2,128]{3,1,2,0:T(8,128)(2,1)}), bf16[16,8,2,128]{3,1,2,0:T(8,128)(2,1)S(1)}, u32[]{:S(2)}, u32[]{:S(2)}) async-start(bf16[16,8,2,128]{3,1,2,0:T(8,128)(2,1)} %broadcast_in_dim.72), calls=%async_computation.1 | async-start | bytes 131072 | tf_op jit(solution)/shard_map/all_to_all | solution.py:60
  66.8 30.4 %copy-start.129 = (f32[128]{0:T(128)}, f32[128]{0:T(128)S(1)}, u32[]{:S(2)}) copy-start(f32[128]{0:T(128)S(1)} %fusion.116) | copy-start | bytes 1540
  75.7 21.5 %copy-start.94 = (f32[768]{0:T(1024)}, f32[768]{0:T(1024)S(1)}, u32[]{:S(2)}) copy-start(f32[768]{0:T(1024)S(1)} %add.458) | copy-start | bytes 9220
  75.8 21.4 %copy-start.89 = (f32[768]{0:T(1024)}, f32[768]{0:T(1024)S(1)}, u32[]{:S(2)}) copy-start(f32[768]{0:T(1024)S(1)} %mul.427) | copy-start | bytes 9220
  103.5 17.3 %all-to-all-start.2 = ((bf16[8,128,384]{2,1,0:T(8,128)(2,1)}), bf16[8,128,384]{2,1,0:T(8,128)(2,1)S(1)}, u32[]{:S(2)}, u32[]{:S(2)}) async-start(bf16[8,128,384]{2,1,0:T(8,128)(2,1)} %bitcast.386), calls=%async_computation.2 | async-start | bytes 1572864 | tf_op jit(solution)/shard_map/all_to_all | solution.py:156
  107.8 379.9 %all-gather.23.cloned.1.call-start = ((), (), s32[]{:S(2)}) async-start(), calls=%async_computation.29 | async-start | bytes 5013504 | tf_op jit(solution)/shard_map/all_gather | solution.py:135
  123.7 8.5 copy-start.117
  132.9 9.7 copy-start.85
  135.0 7.9 copy-start.83
  135.0 8.0 copy-start.82
  135.9 10.3 all-to-all-start.3
  142.7 64.0 %copy-start.93 = (f32[3072]{0:T(1024)S(1)}, f32[3072]{0:T(1024)}, u32[]{:S(2)}) copy-start(f32[3072]{0:T(1024)} %add.484) | copy-start | bytes 36868
  142.8 177.9 %copy-start.96 = (f32[768]{0:T(1024)}, f32[768]{0:T(1024)S(1)}, u32[]{:S(2)}) copy-start(f32[768]{0:T(1024)S(1)} %add.494) | copy-start | bytes 9220
  143.0 177.8 %copy-start.91 = (f32[768]{0:T(1024)}, f32[768]{0:T(1024)S(1)}, u32[]{:S(2)}) copy-start(f32[768]{0:T(1024)S(1)} %mul.447) | copy-start | bytes 9220
  146.3 64.7 %copy-start.48 = (bf16[128,768]{0,1:T(8,128)(2,1)}, bf16[128,768]{0,1:T(8,128)(2,1)S(1)}, u32[]{:S(2)}) copy-start(bf16[128,768]{0,1:T(8,128)(2,1)S(1)} %constant_dynamic-update-slice_fusion) | copy-start | bytes 589828
  149.4 61.6 %copy-start.100 = (f32[128]{0:T(128)}, f32[128]{0:T(128)S(1)}, u32[]{:S(2)}) copy-start(f32[128]{0:T(128)S(1)} %broadcast_multiply_fusion.2) | copy-start | bytes 1540
  150.2 60.8 %copy-start.121 = (f32[128]{0:T(128)}, f32[128]{0:T(128)S(1)}, u32[]{:S(2)}) copy-start(f32[128]{0:T(128)S(1)} %fusion.117) | copy-start | bytes 1540
  150.2 115.9 %copy-start.135 = (f32[768]{0:T(1024)S(1)}, f32[768]{0:T(1024)}, u32[]{:S(2)}) copy-start(f32[768]{0:T(1024)} %add.490) | copy-start | bytes 9220
  270.1 53.4 %copy-start.10 = (f32[128,768]{1,0:T(8,128)}, f32[128,768]{1,0:T(8,128)S(1)}, u32[]{:S(2)}) copy-start(f32[128,768]{1,0:T(8,128)S(1)} %get-tuple-element.318) | copy-start | bytes 1179652
  270.1 53.4 %copy-start.124 = (f32[128]{0:T(128)}, f32[128]{0:T(128)S(1)}, u32[]{:S(2)}) copy-start(f32[128]{0:T(128)S(1)} %broadcast_multiply_fusion.1) | copy-start | bytes 1540
  270.3 53.2 %copy-start.144 = (f32[128]{0:T(128)}, f32[128]{0:T(128)S(1)}, u32[]{:S(2)}) copy-start(f32[128]{0:T(128)S(1)} %multiply_reduce_fusion.11) | copy-start | bytes 1540
  270.3 53.2 %copy-start.132 = (f32[128]{0:T(128)}, f32[128]{0:T(128)S(1)}, u32[]{:S(2)}) copy-start(f32[128]{0:T(128)S(1)} %fusion.118) | copy-start | bytes 1540
  356.8 9.5 copy-start.81
  356.9 10.2 copy-start.80
  359.8 10.3 all-to-all-start.6
  503.5 12.2 all-to-all-start.7
  546.6 15.7 %all-to-all-start.8 = ((bf16[8,128,384]{2,1,0:T(8,128)(2,1)}), bf16[8,128,384]{2,1,0:T(8,128)(2,1)}, u32[]{:S(2)}, u32[]{:S(2)}) async-start(bf16[8,128,384]{2,1,0:T(8,128)(2,1)} %concatenate.128), calls=%async_computation.8 | async-start | bytes 1572864 | tf_op jit(solution)/shard_map/all_to_all | solution.py:202
  550.9 161.2 %reduce-scatter.19.cloned.1.call-start = ((), (), s32[]{:S(2)}) async-start(), calls=%async_computation.35 | async-start | bytes 1253376 | tf_op jit(solution)/shard_map/reduce_scatter | solution.py:182
  553.4 188.3 %reduce-scatter.17.cloned.1.call-start = ((), (), s32[]{:S(2)}) async-start(), calls=%async_computation.34 | async-start | bytes 3760128 | tf_op jit(solution)/shard_map/reduce_scatter | solution.py:182
  569.9 8.8 copy-start.51
  569.9 8.8 copy-start.54
  570.6 8.0 copy-start.52
  578.7 215.5 %reduce-scatter.23.cloned.1.call-start = ((), (), s32[]{:S(2)}) async-start(), calls=%async_computation.37 | async-start | bytes 5013504 | tf_op jit(solution)/shard_map/reduce_scatter | solution.py:182
  584.0 295.5 %reduce-scatter.21.cloned.1.call-start = ((), (), s32[]{:S(2)}) async-start(), calls=%async_computation.36 | async-start | bytes 5013504 | tf_op jit(solution)/shard_map/reduce_scatter | solution.py:182
  595.5 8.7 copy-start.24
  605.4 9.9 copy-start.98
  611.0 11.2 all-to-all-start.9
  654.8 15.4 %all-to-all-start.10 = ((bf16[8,128,384]{2,1,0:T(8,128)(2,1)}), bf16[8,128,384]{2,1,0:T(8,128)(2,1)S(1)}, u32[]{:S(2)}, u32[]{:S(2)}) async-start(bf16[8,128,384]{2,1,0:T(8,128)(2,1)} %concatenate.137), calls=%async_computation.10 | async-start | bytes 1572864 | tf_op jit(solution)/shard_map/all_to_all | solution.py:202
  658.4 291.4 %reduce-scatter.11.cloned.1.call-start = ((), (), s32[]{:S(2)}) async-start(), calls=%async_computation.31 | async-start | bytes 1253376 | tf_op jit(solution)/shard_map/reduce_scatter | solution.py:182
  660.0 369.8 %reduce-scatter.9.cloned.1.call-start = ((), (), s32[]{:S(2)}) async-start(), calls=%async_computation.30 | async-start | bytes 3760128 | tf_op jit(solution)/shard_map/reduce_scatter | solution.py:182
  676.6 438.7 %reduce-scatter.15.cloned.1.call-start = ((), (), s32[]{:S(2)}) async-start(), calls=%async_computation.33 | async-start | bytes 5013504 | tf_op jit(solution)/shard_map/reduce_scatter | solution.py:182
  681.9 519.3 %reduce-scatter.13.cloned.1.call-start = ((), (), s32[]{:S(2)}) async-start(), calls=%async_computation.32 | async-start | bytes 5013504 | tf_op jit(solution)/shard_map/reduce_scatter | solution.py:182
  690.7 14.9 %copy-start.116 = (f32[768]{0:T(1024)S(1)}, f32[768]{0:T(1024)}, u32[]{:S(2)}) copy-start(f32[768]{0:T(1024)} %get-tuple-element.46) | copy-start | bytes 9220
  690.7 15.7 %copy-start.115 = (f32[768]{0:T(1024)S(1)}, f32[768]{0:T(1024)}, u32[]{:S(2)}) copy-start(f32[768]{0:T(1024)} %get-tuple-element.53) | copy-start | bytes 9220
  694.8 22.4 %copy-start.12 = (bf16[768,2304]{1,0:T(8,128)(2,1)S(1)}, bf16[768,2304]{1,0:T(8,128)(2,1)}, u32[]{:S(2)}) copy-start(bf16[768,2304]{1,0:T(8,128)(2,1)} %all-gather.9.cloned.1.call-done) | copy-start | bytes 10616836
  694.8 22.4 %copy-start.110 = (f32[128]{0:T(128)S(1)}, f32[128]{0:T(128)}, u32[]{:S(2)}) copy-start(f32[128]{0:T(128)} %copy-done.108) | copy-start | bytes 1540
  719.8 12.3 copy-start.16
  719.8 12.3 copy-start.26
  719.8 12.3 copy-start.31
  719.8 12.3 copy-start.137
  720.5 11.6 copy-start.35
  724.7 155.9 %copy-start.50 = (bf16[8,36,128]{2,1,0:T(8,128)(2,1)S(1)}, bf16[8,36,128]{2,1,0:T(8,128)(2,1)}, u32[]{:S(2)}) copy-start(bf16[8,36,128]{2,1,0:T(8,128)(2,1)} %reshape.554) | copy-start | bytes 221188
  725.5 15.8 %all-to-all-start.11 = ((f32[128,1,256]{2,1,0:T(1,128)}), f32[128,1,256]{2,1,0:T(1,128)S(1)}, u32[]{:S(2)}, u32[]{:S(2)}) async-start(f32[128,1,256]{2,1,0:T(1,128)} %copy.153), calls=%async_computation.11 | async-start | bytes 262144 | tf_op jit(solution)/shard_map/all_to_all | solution.py:227
  881.5 321.8 %all-to-all-start.13 = ((bf16[8,432,128]{2,1,0:T(8,128)(2,1)}), bf16[8,432,128]{2,1,0:T(8,128)(2,1)S(1)}, u32[]{:S(2)}, u32[]{:S(2)}) async-start(bf16[8,432,128]{2,1,0:T(8,128)(2,1)} %pad_maximum_fusion.1), calls=%async_computation.21 | async-start | bytes 1769472 | tf_op jit(solution)/shard_map/all_to_all | solution.py:220
  1203.3 16.7 %all-to-all-start.12 = ((bf16[8,432,128]{2,1,0:T(8,128)(2,1)}), bf16[8,432,128]{2,1,0:T(8,128)(2,1)S(1)}, u32[]{:S(2)}, u32[]{:S(2)}) async-start(bf16[8,432,128]{2,1,0:T(8,128)(2,1)} %pad_maximum_fusion), calls=%async_computation.16 | async-start | bytes 1769472 | tf_op jit(solution)/shard_map/all_to_all | solution.py:220
  (116 other events, 303.7 us)
Sparse Core Ops, SparseCore 0:
  36.6 57.8 all-gather.8
  97.5 50.1 all-gather.10
  150.1 56.5 all-gather.12
  209.5 56.5 all-gather.14
  268.4 52.3 all-gather.16
  323.6 46.0 all-gather.18
  372.1 56.5 all-gather.20
  431.1 56.5 all-gather.22
  555.5 67.2 reduce-scatter.18
  627.3 80.6 reduce-scatter.16
  712.7 81.4 reduce-scatter.22
  798.1 81.2 reduce-scatter.20
  883.7 66.0 reduce-scatter.10
  953.7 76.0 reduce-scatter.8
  1033.7 81.5 reduce-scatter.14
  1119.7 81.4 reduce-scatter.12

commit v2 on v1

v2 whole, which is shorter than its diff:
```python
import functools

import jax
import jax.numpy as jnp
from jax import lax
from jax.experimental import pallas as pl
from jax.experimental.pallas import tpu as pltpu
from jax.sharding import Mesh, PartitionSpec as P

LAYERS = 2
D = 768
TOK = 128
CTX_DEV = 8
SLOTS = TOK * CTX_DEV
DATA = ("y", "zh", "c")
CTX = ("x", "zl")
ALL = DATA + CTX
bf16 = jnp.bfloat16
f32 = jnp.float32
norm_eps = 1e-05
score_scale = 0.125
hidden_value = -1000000000.0


def coord(bit_b, bit_a, core):
    return core * (2 * bit_b + bit_a) + (1 - core) * (3 * bit_a + bit_b * (1 - 2 * bit_a))


def place(n, core):
    y = coord((n >> 5) & 1, (n >> 2) & 1, core)
    z = coord((n >> 4) & 1, (n >> 1) & 1, core)
    x = coord((n >> 3) & 1, n & 1, core)
    return (y * 2 + (z >> 1)) * 2 + core, x * 2 + (z & 1)


SLOT_OF = {(c,) + place(n, c): n for c in range(2) for n in range(64)}


def device_id(y, z, core, x):
    return y * 32 + (z >> 1) * 16 + core * 8 + x * 2 + (z & 1)


def cube_groups(level):
    found = {}
    for core in range(2):
        for n in range(64):
            bits = [(n >> s) & 1 for s in range(6)]
            y, z, x = (coord(bits[3 + s], bits[s], core) for s in (2, 1, 0))
            if level == 1:
                key = (core,) + tuple(coord(bits[3 + s], 0, core) for s in (2, 1, 0))
                slot = n & 7
            else:
                pair = [coord(bits[3 + s], bits[s], core) for s in (2, 1, 0)]
                pair = [(v // 2 if core == 0 else ((v + 1) // 2) % 2) for v in pair]
                key = (core,) + tuple(pair)
                slot = n >> 3
            found.setdefault(key, [None] * 8)[slot] = device_id(y, z, core, x)
    return [found[k] for k in sorted(found)]


GROUPS_A = cube_groups(1)
GROUPS_B = cube_groups(0)


def fetch(core_ref, mine, theirs, w, sem, low, high):
    core = core_ref[0]

    def step(n, carry):
        for src, own in ((mine, core), (theirs, 1 - core)):
            row, triple = place(n, own)

            @pl.when((triple >= low) & (triple < high))
            def _():
                pltpu.make_async_copy(src.at[n], w.at[row, pl.ds((triple - low) * 3, 3)], sem).start()

        return carry

    lax.fori_loop(0, 64, step, 0)


def arrived(w, sem):
    pltpu.make_async_copy(w, w, sem).wait()


def units(w, first, count):
    parts = [w[:, first + i].reshape(D, 128) for i in range(count)]
    return parts[0] if count == 1 else jnp.concatenate(parts, axis=1)


def tall_units(w, cb):
    return w[:, 4 * cb : 4 * cb + 4].reshape(4 * D, 128)


def mul(a, b):
    return jnp.dot(a, b, preferred_element_type=f32)


def mul_t(a, b):
    return lax.dot_general(a, b, (((1,), (1,)), ((), ())), preferred_element_type=f32)


def t_mul(a, b):
    return lax.dot_general(a, b, (((0,), (0,)), ((), ())), preferred_element_type=f32)


def norm_parts(values):
    centre = values - jnp.mean(values, axis=-1, keepdims=True)
    var = jnp.mean(centre * centre, axis=-1, keepdims=True)
    r = lax.rsqrt(var + norm_eps)
    return centre * r, r


def norm_back(cot, gain, xh, r):
    cg = cot * gain
    return r * (cg - jnp.mean(cg, axis=-1, keepdims=True) - xh * jnp.mean(cg * xh, axis=-1, keepdims=True))


def rows_sum(values):
    return jnp.sum(values, axis=0, keepdims=True)


def windows(values):
    out = []
    for x in range(4):
        for zl in range(2):
            own, shared = 3 * x + 2 * zl, 3 * x + 1
            out.append(jnp.concatenate([values[:, 64 * own : 64 * own + 64],
                                        values[:, 64 * shared : 64 * shared + 64]], axis=1))
    return out


def unwindow(get):
    parts = []
    for x in range(4):
        lo, hi = get(2 * x), get(2 * x + 1)
        parts += [lo[:, :64], lo[:, 64:] + hi[:, 64:], hi[:, :64]]
    return jnp.concatenate(parts, axis=1)


def gelu_both(u):
    k = 0.7978845608028654
    t = jnp.tanh(k * (u + 0.044715 * u * u * u))
    half = 0.5 * (1.0 + t)
    return u * half, half + 0.5 * u * (1.0 - t * t) * (k * (1.0 + 3 * 0.044715 * u * u))


def project_kernel(core, h_ref, vec, mine, theirs, a1_ref, pay_ref, w, sem):
    fetch(core, mine, theirs, w, sem, 0, 6)
    xh, _ = norm_parts(h_ref[...].astype(f32))
    a1 = (xh * vec[0:1] + vec[1:2]).astype(bf16)
    a1_ref[...] = a1
    arrived(w, sem)
    for part in range(3):
        cols = [mul(a1, units(w, 6 * part + 2 * j, 2)) for j in range(3)]
        got = jnp.concatenate(cols, axis=1)
        if part != 1:
            got = got + vec[2 + part // 2 : 3 + part // 2]
        got = got.astype(bf16).astype(f32)
        for d, win in enumerate(windows(got)):
            pay_ref[d, :, 128 * part : 128 * part + 128] = win.astype(bf16)


def visible_of(block, count, idc_ref, idr_ref):
    n = count * TOK
    qpos = block * TOK + lax.broadcasted_iota(jnp.int32, (TOK, n), 0)
    kpos = lax.broadcasted_iota(jnp.int32, (TOK, n), 1)
    return (idc_ref[block] == idr_ref[:, 0:n]) & (kpos <= qpos)


def head_blocks(par):
    for i in range(4):
        yield i, ((0, 2 * i, 2 * i + 1), (0, 2 * i + 1, 2 * i + 2), (1, 2 * i + par, 2 * i + 2))


def half(values, head):
    return values[:, 64 * head : 64 * head + 64]


def store_pair(out, lanes, i, par, parts):
    for k in range(2):
        shared = jnp.where(par == k, parts[2], 0.0)
        out[2 * i + k, :, lanes] = jnp.concatenate([parts[k], shared], axis=1).astype(bf16)


def weights_of(q, key, seen):
    s = jnp.where(seen, mul_t(q, key) * score_scale, hidden_value)
    e = jnp.exp(s - jnp.max(s, axis=1, keepdims=True))
    return e / jnp.sum(e, axis=1, keepdims=True)


def attend_kernel(par_ref, heads, idc, idr, out):
    par = par_ref[0]
    key = heads[:, :, 128:256].reshape(SLOTS, 128)
    val = heads[:, :, 256:384].reshape(SLOTS, 128)
    keys, vals = [half(key, h) for h in range(2)], [half(val, h) for h in range(2)]
    for i, blocks in head_blocks(par):
        parts = []
        for head, block, count in blocks:
            n = count * TOK
            q = half(heads[block, :, 0:128], head)
            p = weights_of(q, keys[head][:n], visible_of(block, count, idc, idr)).astype(bf16)
            parts.append(mul(p, vals[head][:n]))
        store_pair(out, slice(0, 128), i, par, parts)


def attend_back_kernel(par_ref, heads, cot, idc, idr, out, dk_acc, dv_acc):
    par = par_ref[0]
    key = heads[:, :, 128:256].reshape(SLOTS, 128)
    val = heads[:, :, 256:384].reshape(SLOTS, 128)
    keys, vals = [half(key, h) for h in range(2)], [half(val, h) for h in range(2)]
    dk_acc[...] = jnp.zeros_like(dk_acc)
    dv_acc[...] = jnp.zeros_like(dv_acc)
    for i, blocks in head_blocks(par):
        parts = []
        for head, block, count in blocks:
            n = count * TOK
            q = half(heads[block, :, 0:128], head)
            g = half(cot[block], head)
            p = weights_of(q, keys[head][:n], visible_of(block, count, idc, idr))
            dp = mul_t(g, vals[head][:n])
            ds = (p * (dp - jnp.sum(p * dp, axis=1, keepdims=True))).astype(bf16)
            parts.append(mul(ds, keys[head][:n]) * score_scale)
            dk_acc[head, 0:n] += t_mul(ds, q)
            dv_acc[head, 0:n] += t_mul(p.astype(bf16), g)
        store_pair(out, slice(0, 128), i, par, parts)
    dk = jnp.concatenate([dk_acc[0], dk_acc[1]], axis=1) * score_scale
    dv = jnp.concatenate([dv_acc[0], dv_acc[1]], axis=1)
    out[:, :, 128:256] = dk.astype(bf16).reshape(8, TOK, 128)
    out[:, :, 256:384] = dv.astype(bf16).reshape(8, TOK, 128)


def forward_kernel(core, h_ref, back, vec, upb, me, te, mu, tu, md, td,
                   o_ref, h1_ref, a2_ref, u_ref, next_ref, wo, wu, wd, sems):
    fetch(core, me, te, wo, sems.at[0], 6, 8)
    fetch(core, mu, tu, wu, sems.at[1], 0, 8)
    fetch(core, md, td, wd, sems.at[2], 0, 8)
    o = unwindow(lambda d: back[d].astype(f32)).astype(bf16)
    o_ref[...] = o
    arrived(wo, sems.at[0])
    got = jnp.concatenate([mul(o, units(wo, 2 * j, 2)) for j in range(3)], axis=1)
    h1 = h_ref[...].astype(f32) + got + vec[2:3]
    h1_ref[...] = h1
    xh, _ = norm_parts(h1)
    a2 = (xh * vec[0:1] + vec[1:2]).astype(bf16)
    a2_ref[...] = a2
    arrived(wu, sems.at[1])
    acts = []
    for j in range(12):
        u = mul(a2, units(wu, 2 * j, 2)) + upb[:, 256 * j : 256 * j + 256]
        u_ref[:, 256 * j : 256 * j + 256] = u
        acts.append(gelu_both(u)[0].astype(bf16))
    f = jnp.concatenate(acts, axis=1)
    arrived(wd, sems.at[2])
    for j in range(3):
        w = jnp.concatenate([tall_units(wd, 2 * j), tall_units(wd, 2 * j + 1)], axis=1)
        c = slice(256 * j, 256 * j + 256)
        next_ref[:, c] = (h1[:, c] + mul(f, w) + vec[3:4, c]).astype(next_ref.dtype)


def backward_kernel(core, e_ref, u_ref, h1_ref, vec, me, te, mu, tu, md, td,
                    f_ref, du_ref, e1_ref, pay_ref, small_ref, upb_ref, wo, wu, wd, sems):
    fetch(core, md, td, wd, sems.at[2], 0, 8)
    fetch(core, mu, tu, wu, sems.at[1], 0, 8)
    fetch(core, me, te, wo, sems.at[0], 6, 8)
    e = e_ref[...].astype(f32)
    e2 = e.astype(bf16)
    arrived(wd, sems.at[2])
    df = jnp.zeros((TOK, 4 * D), f32)
    for j in range(3):
        w = jnp.concatenate([tall_units(wd, 2 * j), tall_units(wd, 2 * j + 1)], axis=1)
        df = df + mul_t(e2[:, 256 * j : 256 * j + 256], w)
    arrived(wu, sems.at[1])
    cot = jnp.zeros((TOK, D), f32)
    for j in range(12):
        c = slice(256 * j, 256 * j + 256)
        f, slope = gelu_both(u_ref[:, c])
        f_ref[:, c] = f.astype(bf16)
        du = (df[:, c] * slope).astype(bf16)
        du_ref[:, c] = du
        upb_ref[:, c] = rows_sum(du.astype(f32))
        cot = cot + mul_t(du, units(wu, 2 * j, 2))
    xh, r = norm_parts(h1_ref[...])
    e1 = e + norm_back(cot, vec[0:1], xh, r)
    e1_ref[...] = e1
    b1 = e1.astype(bf16)
    small_ref[0:1] = rows_sum(cot * xh)
    small_ref[1:2] = rows_sum(cot)
    small_ref[2:3] = rows_sum(b1.astype(f32))
    small_ref[3:4] = rows_sum(e2.astype(f32))
    arrived(wo, sems.at[0])
    do = jnp.zeros((TOK, D), f32)
    for j in range(3):
        do = do + mul_t(b1[:, 256 * j : 256 * j + 256], units(wo, 2 * j, 2))
    do = do.astype(bf16).astype(f32)
    for d, win in enumerate(windows(do)):
        pay_ref[d] = win.astype(bf16)


def back_project_kernel(core, back, e1_ref, h_ref, vec, mine, theirs, g_ref, e_ref, small_ref, w, sem):
    fetch(core, mine, theirs, w, sem, 0, 6)
    for part in range(3):
        got = unwindow(lambda d: back[d, :, 128 * part : 128 * part + 128].astype(f32)).astype(bf16)
        g_ref[:, D * part : D * part + D] = got
        if part != 1:
            small_ref[2 + part // 2 : 3 + part // 2] = rows_sum(got.astype(f32))
    arrived(w, sem)
    cot = jnp.zeros((TOK, D), f32)
    for j in range(9):
        cot = cot + mul_t(g_ref[:, 256 * j : 256 * j + 256], units(w, 2 * j, 2))
    xh, r = norm_parts(h_ref[...].astype(f32))
    small_ref[0:1] = rows_sum(cot * xh)
    small_ref[1:2] = rows_sum(cot)
    e_ref[...] = e1_ref[...] + norm_back(cot, vec[0:1], xh, r)


def store_grad(core, out, wide, first):
    for i in range(wide.shape[1] // 128):
        rows = wide[:, 128 * i : 128 * i + 128].astype(bf16).reshape(16, 48, 128)
        triple, k = divmod(first + i, 3)
        for row in range(16):
            target = row & 1
            out[core ^ target, SLOT_OF[(target, row, triple)], k] = rows[row]


def grad_wide_kernel(core_ref, a_ref, b_ref, out):
    core = core_ref[0]
    at = a_ref[...].T
    for j in range(4):
        store_grad(core, out, mul(at, b_ref[:, D * j : D * j + D]), 6 * j)


def grad_tall_kernel(core_ref, f_ref, e_ref, out):
    core = core_ref[0]
    ft = f_ref[...].T
    e2 = e_ref[...].astype(f32).astype(bf16)
    for j in range(3):
        wide = mul(ft, e2[:, 256 * j : 256 * j + 256]).astype(bf16)
        for half in range(2):
            rows = wide[:, 128 * half : 128 * half + 128].reshape(16, 4, 48, 128)
            for q in range(4):
                triple, k = divmod(4 * (2 * j + half) + q, 3)
                for row in range(16):
                    target = row & 1
                    out[core ^ target, SLOT_OF[(target, row, triple)], k] = rows[row, q]


def grad_joint_kernel(core_ref, a_ref, g_ref, o_ref, e1_ref, out):
    core = core_ref[0]
    at = a_ref[...].T
    for j in range(3):
        store_grad(core, out, mul(at, g_ref[:, D * j : D * j + D]), 6 * j)
    store_grad(core, out, mul(o_ref[...].T, e1_ref[...].astype(bf16)), 18)


def call(kernel, outs, ins, scratch=(), flops=0, bytes_accessed=0):
    spaces = {"s": pltpu.SMEM, "v": pltpu.VMEM, "a": pl.ANY}
    return pl.pallas_call(
        kernel,
        out_shape=[jax.ShapeDtypeStruct(*o) for o in outs],
        in_specs=[pl.BlockSpec(memory_space=spaces[m]) for _, m in ins],
        out_specs=[pl.BlockSpec(memory_space=pltpu.VMEM)] * len(outs),
        scratch_shapes=list(scratch),
        compiler_params=pltpu.CompilerParams(vmem_limit_bytes=56 * 1024 * 1024),
        cost_estimate=pl.CostEstimate(flops=flops, bytes_accessed=bytes_accessed, transcendentals=0),
    )(*[a for a, _ in ins])


def w_scratch(count):
    return pltpu.VMEM((16, count, 48, 128), bf16)


DMA = pltpu.SemaphoreType.DMA


def copies(values, groups):
    many = jnp.broadcast_to(values[None], (8,) + values.shape)
    return lax.all_to_all(many, ALL, 0, 0, axis_index_groups=groups)


def sum_first(values):
    return jnp.sum(values.astype(f32), axis=0)


def swap_core(values):
    return lax.ppermute(values, "c", [(0, 1), (1, 0)])


def spread(shard):
    rows = shard.shape[1]
    mine = copies(shard.reshape(8 * rows, 128), GROUPS_B).reshape(64, rows // 48, 48, 128)
    return mine, swap_core(mine)


def ff_in(values):
    lead = values.shape[:-1]
    return jnp.swapaxes(values.reshape(lead + (16, 8, 4, 6)), -3, -2).reshape(lead + (4 * D,))


def ff_out(values):
    lead = values.shape[:-1]
    return jnp.swapaxes(values.reshape(lead + (16, 4, 8, 6)), -3, -2).reshape(lead + (4 * D,))


def to_units(values):
    return jnp.swapaxes(values.reshape(6, -1, 128), 0, 1)


def from_units(values):
    return jnp.swapaxes(values, 0, 1).reshape(6, -1)


def token_ids(group_index, positions, sequence_group, sequence_start, sequence_length):
    member = (
        (sequence_group[None, :] == group_index)
        & (sequence_start[None, :] <= positions[:, None])
        & (positions[:, None] < (sequence_start + sequence_length)[None, :])
    )
    numbers = jnp.arange(sequence_group.shape[0], dtype=jnp.int32) + 1
    located = jnp.sum(jnp.where(member, numbers[None, :], 0), axis=1)
    return jnp.where(located > 0, located - 1, -1 - positions)


def body(hidden_in, out_grad, sequence_group, sequence_start, sequence_length, norm_gain, norm_bias,
         input_weight, input_bias, output_weight, branch_bias, up_weight, up_bias, down_weight):
    core = lax.axis_index("c").astype(jnp.int32).reshape(1)
    par = lax.axis_index("zl").astype(jnp.int32).reshape(1)
    positions = jnp.arange(SLOTS, dtype=jnp.int32)
    ids = token_ids(lax.axis_index(DATA), positions, sequence_group, sequence_start, sequence_length)
    idc, idr = ids.reshape(CTX_DEV, TOK, 1), ids.reshape(1, SLOTS)

    parts = []
    for l in range(LAYERS):
        parts.append(to_units(input_weight[l]))
        parts.append(to_units(output_weight[l]))
        parts.append(to_units(ff_in(up_weight[l])))
        down = down_weight[l].reshape(4, 6, 6, 128)
        parts.append(down.transpose(2, 0, 1, 3).reshape(24, 6, 128))
    packed = jnp.concatenate(parts, axis=0).reshape(2, 3, 8, 3, 6, 128)
    packed = packed.transpose(2, 0, 1, 3, 4, 5).reshape(8, 18, 6, 128)
    got = lax.all_to_all(packed, CTX, 0, 0)
    got = got.transpose(1, 0, 2, 3).reshape(2, 3, 144, 128)

    smalls = jnp.concatenate([v.reshape(-1) for v in (norm_gain, norm_bias, input_bias, branch_bias, up_bias)])
    smalls = jnp.pad(smalls, (0, 256 - 144)).reshape(1, 2, 128)
    few = lax.all_to_all(jnp.broadcast_to(smalls, (128, 2, 128)), ALL, 0, 0).reshape(128, 256).astype(f32)
    vecs = few[:, :96].reshape(128, 16, 6).transpose(1, 0, 2).reshape(16, D)
    ups = few[:, 96:144].reshape(16, 8, 2, 4, 6).transpose(2, 0, 3, 1, 4).reshape(2, 4 * D)

    first = copies(got[0, 0], GROUPS_A)
    rest = copies(got.reshape(6 * 144, 128)[144:], GROUPS_A).reshape(8, 5, 144, 128)
    weights = [[spread(first), spread(rest[:, 0]), spread(rest[:, 1])],
               [spread(rest[:, 2]), spread(rest[:, 3]), spread(rest[:, 4])]]

    def vec(*index):
        return jnp.concatenate([vecs[i : i + 1] for i in index], axis=0)

    hidden = hidden_in[0]
    stored = []
    for l in range(LAYERS):
        group_e, group_u, group_d = weights[l]
        a1, pay = call(
            project_kernel,
            [((TOK, D), bf16), ((8, TOK, 384), bf16)],
            [(core, "s"), (hidden, "v"), (vec(2 * l, 4 + 2 * l, 8 + 2 * l, 9 + 2 * l), "v"),
             (group_e[0], "a"), (group_e[1], "a")],
            [w_scratch(18), DMA],
            flops=2 * TOK * D * 3 * D, bytes_accessed=4 * 2**20)
        heads = lax.all_to_all(pay, CTX, 0, 0)
        (mix,) = call(
            attend_kernel,
            [((8, TOK, 128), bf16)],
            [(par, "s"), (heads, "v"), (idc, "v"), (idr, "v")],
            flops=2 * 2 * 64 * 56 * 128 * 128, bytes_accessed=2**20)
        back = lax.all_to_all(mix, CTX, 0, 0)
        o, h1, a2, u, following = call(
            forward_kernel,
            [((TOK, D), bf16), ((TOK, D), f32), ((TOK, D), bf16), ((TOK, 4 * D), f32),
             ((TOK, D), f32 if l == 0 else bf16)],
            [(core, "s"), (hidden, "v"), (back, "v"), (vec(2 * l + 1, 5 + 2 * l, 12 + 2 * l, 13 + 2 * l), "v"),
             (ups[l : l + 1], "v")] + [(w, "a") for pair in weights[l] for w in pair],
            [w_scratch(6), w_scratch(24), w_scratch(24), DMA((3,))],
            flops=2 * TOK * D * 9 * D, bytes_accessed=12 * 2**20)
        stored.append((hidden, a1, heads, o, h1, a2, u))
        hidden = following

    grad = out_grad[0]
    sums = []
    few_rows, few_up = [None] * 2, [None] * 2
    for l in reversed(range(LAYERS)):
        layer_in, a1, heads, o, h1, a2, u = stored[l]
        f, du, e1, pay, small_b, small_u = call(
            backward_kernel,
            [((TOK, 4 * D), bf16), ((TOK, 4 * D), bf16), ((TOK, D), f32), ((8, TOK, 128), bf16),
             ((4, D), f32), ((1, 4 * D), f32)],
            [(core, "s"), (grad, "v"), (u, "v"), (h1, "v"), (vec(2 * l + 1), "v")]
            + [(w, "a") for pair in weights[l] for w in pair],
            [w_scratch(6), w_scratch(24), w_scratch(24), DMA((3,))],
            flops=2 * TOK * D * 9 * D, bytes_accessed=12 * 2**20)
        cot = lax.all_to_all(pay, CTX, 0, 0)
        (grad_d,) = call(grad_tall_kernel, [((2, 64, 3, 48, 128), bf16)], [(core, "s"), (f, "v"), (grad, "v")],
                         flops=2 * TOK * D * 4 * D, bytes_accessed=6 * 2**20)
        (grad_u,) = call(grad_wide_kernel, [((2, 64, 3, 48, 128), bf16)], [(core, "s"), (a2, "v"), (du, "v")],
                         flops=2 * TOK * D * 4 * D, bytes_accessed=6 * 2**20)
        (pay2,) = call(
            attend_back_kernel,
            [((8, TOK, 384), bf16)],
            [(par, "s"), (heads, "v"), (cot, "v"), (idc, "v"), (idr, "v")],
            [pltpu.VMEM((2, SLOTS, 64), f32)] * 2,
            flops=5 * 2 * 64 * 56 * 128 * 128, bytes_accessed=2**21)
        back2 = lax.all_to_all(pay2, CTX, 0, 0)
        g, grad, small_a = call(
            back_project_kernel,
            [((TOK, 3 * D), bf16), ((TOK, D), f32), ((4, D), f32)],
            [(core, "s"), (back2, "v"), (e1, "v"), (layer_in, "v"), (vec(2 * l), "v"),
             (weights[l][0][0], "a"), (weights[l][0][1], "a")],
            [w_scratch(18), DMA],
            flops=2 * TOK * D * 3 * D, bytes_accessed=4 * 2**20)
        (grad_e,) = call(grad_joint_kernel, [((2, 64, 3, 48, 128), bf16)],
                         [(core, "s"), (a1, "v"), (g, "v"), (o, "v"), (e1, "v")],
                         flops=2 * TOK * D * 4 * D, bytes_accessed=6 * 2**20)
        layer_sums = []
        for both in (grad_e, grad_u, grad_d):
            part = (both[0].astype(f32) + swap_core(both[1]).astype(f32)).astype(bf16).reshape(8, 8 * 144, 128)
            part = sum_first(lax.all_to_all(part, ALL, 0, 0, axis_index_groups=GROUPS_B)).astype(bf16)
            layer_sums.append(part.reshape(8, 144, 128))
        sums.append(layer_sums)
        few_rows[l] = jnp.concatenate([small_a[0:1], small_b[0:1], small_a[1:2], small_b[1:2], small_a[2:4],
                                       small_b[2:4]], axis=0)
        few_up[l] = small_u

    def finish(values):
        n = values.shape[1] // 144
        part = sum_first(lax.all_to_all(values, ALL, 0, 0, axis_index_groups=GROUPS_A))
        part = part.reshape(n * 3, 8, 6, 128).transpose(1, 0, 2, 3)
        part = lax.all_to_all(part, CTX, 0, 0)
        return part.reshape(8, n, 3, 6, 128).transpose(1, 0, 2, 3, 4).reshape(n, 24, 6, 128)

    (e_hi, u_hi, d_hi), (e_lo, u_lo, d_lo) = sums
    early = finish(jnp.concatenate([e_hi, u_hi, d_hi, u_lo, d_lo], axis=1))
    late = finish(e_lo)
    group_e, group_u, group_d = (late[0], early[0]), (early[3], early[1]), (early[4], early[2])

    few = jnp.concatenate([r.reshape(8, 128, 6).transpose(1, 0, 2).reshape(128, 48) for r in few_rows]
                          + [r.reshape(16, 4, 8, 6).transpose(0, 2, 1, 3).reshape(128, 24) for r in few_up], axis=1)
    few = jnp.pad(few, ((0, 0), (0, 256 - 144))).reshape(128, 2, 128)
    few = jnp.sum(lax.all_to_all(few, ALL, 0, 0), axis=0).reshape(256)
    few_l = [few[48 * l : 48 * l + 48].reshape(4, 2, 6) for l in range(2)]

    def pair(k):
        return jnp.stack([few_l[0][k], few_l[1][k]])

    return (
        hidden[None],
        grad[None],
        pair(0),
        pair(1),
        jnp.stack([from_units(v[:18]) for v in group_e]),
        pair(2),
        jnp.stack([from_units(v[18:]) for v in group_e]),
        pair(3),
        jnp.stack([ff_out(from_units(v)) for v in group_u]),
        few[96:144].reshape(2, 24),
        jnp.stack([v.reshape(6, 4, 6, 128).transpose(1, 2, 0, 3).reshape(24, D) for v in group_d]),
    )


def solution(mesh):
    mesh = Mesh(mesh.devices.reshape(4, 2, 2, 4, 2), ALL)
    token = P(DATA, CTX, None)
    one = P(None, ALL)
    two = P(None, None, ALL)
    mat = P(None, ALL, None)
    return jax.shard_map(
        body,
        mesh=mesh,
        in_specs=(token, token, P(), P(), P(), two, two, mat, two, mat, two, mat, one, mat),
        out_specs=(token, token, two, two, mat, two, mat, two, mat, one, mat),
        check_vma=False,
    )
```

time: 1240 us -> 684 us (0.55)
  waiting for transfers between devices: 801 us -> 164 us
  Pallas kernels: 0 us -> 131 us
  matrix products: 121 us -> 0 us
  starting transfers between devices: 52.1 us -> 136 us
  local copies, waits for them, and re-layouts: 146 us -> 91.9 us
  blocking collectives: 52.1 us -> 103 us
  between operations: 16.8 us -> 2.39 us
    reduce_scatter x8 -> x0, waiting for transfers between devices: 447 us -> none  [scatter(): lax.psum_scatter(grad.astype(bf16), DATA, scatter_dimension=0, tiled=True)]
    all_gather x8 -> x0, waiting for transfers between devices: 284 us -> none  [body(): full.append([lax.all_gather(w, DATA, axis=0, tiled=True) for w in own])]
    pallas_call x0 -> x18, Pallas kernels: none -> 131 us  [call(): pl.pallas_call(kernel, out_shape=[jax.ShapeDtypeStruct(*o) for o in outs]...]
    dot_general x48 -> x0, matrix products: 121 us -> none  [the longest x16 42.4 us: outer_sum(): lax.dot_general(left, right, (((0,), (0,)), ((), ())), preferred_element_...]
    all_to_all x11 -> x24, waiting for transfers between devices: 70 us -> 164 us  [the longest x4 56.2 us: copies(): return lax.all_to_all(many, ALL, 0, 0, axis_index_groups=groups)]
    all_to_all x11 -> x24, starting transfers between devices: 50.8 us -> 114 us  [the longest x6 28.7 us: body(): lax.all_to_all(part, ALL, 0, 0, axis_index_groups=GROUPS_B)]
    all_to_all x3 -> x5, blocking collectives: 52.1 us -> 103 us  [the longest x4 86.1 us: copies(): return lax.all_to_all(many, ALL, 0, 0, axis_index_groups=groups)]
    concatenate x28 -> x4, local copies, waits for them, and re-layouts: 43.7 us -> 1.01 us  [the longest x1 0.78 us: body(): early = finish(jnp.concatenate([e_hi, u_hi, d_hi, u_lo, d_lo], axis=1))]
  transfers between devices with their start and end apart: 27 -> 36, of which waited for: 23 -> 21; matrix products, arithmetic and copies ran while one was open for 19% -> 15% of each run, Pallas kernels for 0% -> 15%
where the time goes in v2:
time: 684 us; the launch traced here: 672 us
  waiting for transfers between devices  164 us (24%)
  starting transfers between devices  136 us (20%)
  Pallas kernels  131 us (19%)
  blocking collectives  103 us (15%)
  local copies, waits for them, and re-layouts  91.9 us (13%)
  other arithmetic  43.4 us (6%)
    pallas_call x18, Pallas kernels, call(): pl.pallas_call(kernel, out_shape=[jax.ShapeDtypeStruct(*o) for o in outs]...  131 us
    all_to_all x4, blocking collectives, copies(): return lax.all_to_all(many, ALL, 0, 0, axis_index_groups=groups)  86.1 us
    all_to_all x4, waiting for transfers between devices, copies(): return lax.all_to_all(many, ALL, 0, 0, axis_index_groups=groups)  56.2 us
    all_to_all x6, waiting for transfers between devices, body(): lax.all_to_all(part, ALL, 0, 0, axis_index_groups=GROUPS_B)  33.5 us
    all_to_all x6, starting transfers between devices, body(): lax.all_to_all(part, ALL, 0, 0, axis_index_groups=GROUPS_B)  28.7 us
    convert_element_type x6, other arithmetic, body(): (both[0].astype(f32) + swap_core(both[1]).astype(f32)).astype(bf16)  22.9 us
    ppermute x12, starting transfers between devices, swap_core(): return lax.ppermute(values, 'c', [(0, 1), (1, 0)])  22.2 us
    squeeze x6, local copies, waits for them, and re-layouts, body(): both[1]  21.1 us
  transfers between devices with their start and end apart: 36, of which 21 were waited for; matrix products, arithmetic and copies ran while one was open for 15% of the time, Pallas kernels for 15%

profile of v2, /device:TPU:0, one launch (start us, length us, event | category | flops | bytes accessed | tf_op | source)
XLA Modules:
  0.0 671.8 jit_solution(8535555670379069387)
XLA Ops:
  10.6 5.7 all-to-all-start.1
  16.9 6.9 %all-to-all-done.1 = bf16[8,18,6,128]{3,2,1,0:T(8,128)(2,1)S(1)} async-done(((bf16[8,18,6,128]{3,2,1,0:T(8,128)(2,1)}), bf16[8,18,6,128]{3,2,1,0:T(8,128)(2,1)S(1)}, u32[]{:S(2)}, u32[]{:S(2)}) %all-to-all-start.1) | async-done | bytes 221216 | tf_op jit(solution)/shard_map/all_to_all | solution.py:440
  24.4 8.8 %all-to-all-start = ((bf16[128,2,128]{2,1,0:T(2,128)(2,1)}), bf16[128,2,128]{2,1,0:T(2,128)(2,1)S(1)}, u32[]{:S(2)}, u32[]{:S(2)}) async-start(bf16[128,2,128]{2,1,0:T(2,128)(2,1)} %broadcast_in_dim.89), calls=%async_computation | async-start | bytes 131072 | tf_op jit(solution)/shard_map/all_to_all | solution.py:445
  33.4 9.0 %all-to-all-done = bf16[128,2,128]{2,1,0:T(2,128)(2,1)S(1)} async-done(((bf16[128,2,128]{2,1,0:T(2,128)(2,1)}), bf16[128,2,128]{2,1,0:T(2,128)(2,1)S(1)}, u32[]{:S(2)}, u32[]{:S(2)}) %all-to-all-start) | async-done | bytes 65568 | tf_op jit(solution)/shard_map/all_to_all | solution.py:445
  46.8 10.5 %all-to-all-done.2 = bf16[8,144,128]{2,1,0:T(8,128)(2,1)S(1)} async-done(((bf16[8,144,128]{2,1,0:T(8,128)(2,1)}), bf16[8,144,128]{2,1,0:T(8,128)(2,1)S(1)}, u32[]{:S(2)}, u32[]{:S(2)}) %all-to-all-start.2) | async-done | bytes 294944 | tf_op jit(solution)/shard_map/all_to_all | solution.py:377
  57.5 20.2 %all_to_all.145 = bf16[8,720,128]{2,1,0:T(8,128)(2,1)} all-to-all(bf16[8,720,128]{2,1,0:T(8,128)(2,1)S(1)} %broadcast_in_dim.97), channel_id=1, replica_groups={{0,6,17,23,96,102,113,119},{2,4,19,21,98,100,115,117},{1,7,16,22,97,103..., dimensions={0} | all-to-all | bytes 2949120 | tf_op jit(solution)/shard_map/all_to_all | solution.py:377
  85.2 16.0 %all-to-all-done.3 = bf16[8,1152,128]{2,1,0:T(8,128)(2,1)S(1)} async-done(((bf16[8,1152,128]{2,1,0:T(8,128)(2,1)}), bf16[8,1152,128]{2,1,0:T(8,128)(2,1)S(1)}, u32[]{:S(2)}, u32[]{:S(2)}) %all-to-all-start.3) | async-done | bytes 2359328 | tf_op jit(solution)/shard_map/all_to_all | solution.py:377
  102.7 23.1 %all_to_all.146 = bf16[8,1152,128]{2,1,0:T(8,128)(2,1)} all-to-all(bf16[8,1152,128]{2,1,0:T(8,128)(2,1)S(1)} %broadcast_in_dim.99), channel_id=1, replica_groups={{0,2,1,3,32,34,33,35},{6,4,7,5,38,36,39,37},{17,19,16,18,49,51,48,50},{..., dimensions={0} | all-to-all | bytes 4718592 | tf_op jit(solution)/shard_map/all_to_all | solution.py:377
  126.1 21.4 %all_to_all.147 = bf16[8,1152,128]{2,1,0:T(8,128)(2,1)} all-to-all(bf16[8,1152,128]{2,1,0:T(8,128)(2,1)S(1)} %broadcast_in_dim.101), channel_id=1, replica_groups={{0,2,1,3,32,34,33,35},{6,4,7,5,38,36,39,37},{17,19,16,18,49,51,48,50},{..., dimensions={0} | all-to-all | bytes 4718592 | tf_op jit(solution)/shard_map/all_to_all | solution.py:377
  147.9 21.4 %all_to_all.148 = bf16[8,1152,128]{2,1,0:T(8,128)(2,1)} all-to-all(bf16[8,1152,128]{2,1,0:T(8,128)(2,1)S(1)} %broadcast_in_dim.103), channel_id=1, replica_groups={{0,2,1,3,32,34,33,35},{6,4,7,5,38,36,39,37},{17,19,16,18,49,51,48,50},{..., dimensions={0} | all-to-all | bytes 4718592 | tf_op jit(solution)/shard_map/all_to_all | solution.py:377
  171.0 4.4 all-to-all-start.12
  175.7 17.9 %all-to-all-done.12 = bf16[8,1152,128]{2,1,0:T(8,128)(2,1)} async-done(((bf16[8,1152,128]{2,1,0:T(8,128)(2,1)}), bf16[8,1152,128]{2,1,0:T(8,128)(2,1)}, u32[]{:S(2)}, u32[]{:S(2)}) %all-to-all-start.12) | async-done | bytes 2359328 | tf_op jit(solution)/shard_map/all_to_all | solution.py:377
  195.4 5.1 all-to-all-start.13
  207.2 11.7 %all-to-all-done.13 = bf16[8,1152,128]{2,1,0:T(8,128)(2,1)} async-done(((bf16[8,1152,128]{2,1,0:T(8,128)(2,1)}), bf16[8,1152,128]{2,1,0:T(8,128)(2,1)}, u32[]{:S(2)}, u32[]{:S(2)}) %all-to-all-start.13) | async-done | bytes 2359328 | tf_op jit(solution)/shard_map/all_to_all | solution.py:377
  218.9 4.9 collective-permute-start.5
  224.4 5.0 shard_map.221
  237.1 8.8 %all-to-all-done.4.heads = bf16[8,128,384]{2,1,0:T(8,128)(2,1)S(1)} async-done(((bf16[8,128,384]{2,1,0:T(8,128)(2,1)}), bf16[8,128,384]{2,1,0:T(8,128)(2,1)S(1)}, u32[]{:S(2)}, u32[]{:S(2)}) %all-to-all-start.4) | async-done | bytes 786464 | tf_op jit(solution)/shard_map/all_to_all | solution.py:468
  246.8 7.0 %shard_map.222 = bf16[8,128,128]{2,1,0:T(8,128)(2,1)} custom-call(s32[1]{0:T(128)} %bitcast.2.par_ref, bf16[8,128,384]{2,1,0:T(8,128)(2,1)} %copy-done.2, s32[8,128,1]{2,1,0:T(8,128)} %subtract_select_fusion.idc, s32[1,1024]{1,0:T(1,128)} %reshape_select_fusion.idr), custom_call_target="tpu_custom_call" | custom-call | flops 234881024 | bytes 1048576 | tf_op jit(solution)/shard_map/pallas_call | solution.py:357
  253.8 4.1 all-to-all-start.5
  267.5 9.2 %shard_map.223 = (bf16[128,768]{1,0:T(8,128)(2,1)}, f32[128,768]{1,0:T(8,128)}, bf16[128,768]{1,0:T(8,128)(2,1)}, f32[128,3072]{1,0:T(8,128)}, f32[128,768]{1,0:T(8,128)}) custom-call(s32[1]{0:T(128)} %bitcast.core.core_ref, bf16[128,768]{1,0:T(8,128)(2,1)} %bitcast.207, bf16[8,128,128]{2,1,0:T(8,128)(2,1)} %copy-done.5, f32[4,768]{1,0:T(4,128)} %pad_maximum_fusion.5.vec, ...), custom_call_target="tpu_custom_call" | custom-call | flops 1358954496 | bytes 12582912 | tf_op jit(solution)/shard_map/pallas_call | solution.py:357
  276.6 5.0 shard_map.224
  281.7 17.4 %all_to_all.149.heads = bf16[8,128,384]{2,1,0:T(8,128)(2,1)} all-to-all(bf16[8,128,384]{2,1,0:T(8,128)(2,1)} %get-tuple-element.45), channel_id=1, replica_groups=mesh['y'=4,'zh'=2,'c'=2,'x'=4,'zl'=2] {'x','zl'}, dimensions={0} | all-to-all | bytes 1572864 | tf_op jit(solution)/shard_map/all_to_all | solution.py:468
  299.1 7.0 %shard_map.225 = bf16[8,128,128]{2,1,0:T(8,128)(2,1)} custom-call(s32[1]{0:T(128)} %bitcast.2.par_ref, bf16[8,128,384]{2,1,0:T(8,128)(2,1)} %all_to_all.149.heads, s32[8,128,1]{2,1,0:T(8,128)} %subtract_select_fusion.idc, s32[1,1024]{1,0:T(1,128)} %reshape_select_fusion.idr), custom_call_target="tpu_custom_call" | custom-call | flops 234881024 | bytes 1048576 | tf_op jit(solution)/shard_map/pallas_call | solution.py:357
  312.6 3.9 all-to-all-done.11.back
  317.2 9.1 %shard_map.226 = (bf16[128,768]{1,0:T(8,128)(2,1)}, f32[128,768]{1,0:T(8,128)}, bf16[128,768]{1,0:T(8,128)(2,1)}, f32[128,3072]{1,0:T(8,128)}, bf16[128,768]{1,0:T(8,128)(2,1)}) custom-call(s32[1]{0:T(128)} %bitcast.core.core_ref, f32[128,768]{1,0:T(8,128)} %get-tuple-element.44.h_ref, bf16[8,128,128]{2,1,0:T(8,128)(2,1)} %copy-done.6, ...), custom_call_target="tpu_custom_call" | custom-call | flops 1358954496 | bytes 12582912 | tf_op jit(solution)/shard_map/pallas_call | solution.py:357
  326.4 12.5 %shard_map.227 = (bf16[128,3072]{1,0:T(8,128)(2,1)}, bf16[128,3072]{1,0:T(8,128)(2,1)}, f32[128,768]{1,0:T(8,128)}, bf16[8,128,128]{2,1,0:T(8,128)(2,1)}, f32[4,768]{1,0:T(4,128)}, /*index=5*/f32[1,3072]{1,0:T(1,128)}) custom-call(s32[1]{0:T(128)} %bitcast.core.core_ref, bf16[128,768]{1,0:T(8,128)(2,1)} %bitcast.227, f32[128,3072]{1,0:T(8,128)} %get-tuple-element.47.u_ref, ...), custom_call_target="tpu_custom_call" | custom-call | flops 1358954496 | bytes 12582912 | tf_op jit(solution)/shard_map/pallas_call | solution.py:357
  342.5 5.1 shard_map.236
  350.1 10.1 %shard_map.228 = bf16[8,128,384]{2,1,0:T(8,128)(2,1)} custom-call(s32[1]{0:T(128)} %bitcast.2.par_ref, bf16[8,128,384]{2,1,0:T(8,128)(2,1)} %all_to_all.149.heads, bf16[8,128,128]{2,1,0:T(8,128)(2,1)} %copy-done.8, s32[8,128,1]{2,1,0:T(8,128)} %subtract_select_fusion.idc, s32[1,1024]{1,0:T(1,128)} %reshape_select_fusion.idr), custom_call_target="tpu_custom_call" | custom-call | flops 587202560 | bytes 2097152 | tf_op jit(solution)/shard_map/pallas_call | solution.py:357
  360.1 3.9 all-to-all-start.15
  367.6 6.1 all-to-all-done.15.back
  374.5 6.0 shard_map.229
  380.6 12.5 %shard_map.230 = (bf16[128,3072]{1,0:T(8,128)(2,1)}, bf16[128,3072]{1,0:T(8,128)(2,1)}, f32[128,768]{1,0:T(8,128)}, bf16[8,128,128]{2,1,0:T(8,128)(2,1)}, f32[4,768]{1,0:T(4,128)}, /*index=5*/f32[1,3072]{1,0:T(1,128)}) custom-call(s32[1]{0:T(128)} %bitcast.core.core_ref, f32[128,768]{1,0:T(8,128)} %get-tuple-element.51.e_ref, ...), custom_call_target="tpu_custom_call" | custom-call | flops 1358954496 | bytes 12582912 | tf_op jit(solution)/shard_map/pallas_call | solution.py:357
  393.1 3.8 all-to-all-start.16
  397.0 5.2 shard_map.235
  404.5 10.1 %shard_map.231 = bf16[8,128,384]{2,1,0:T(8,128)(2,1)} custom-call(s32[1]{0:T(128)} %bitcast.2.par_ref, bf16[8,128,384]{2,1,0:T(8,128)(2,1)} %copy-done.2, bf16[8,128,128]{2,1,0:T(8,128)(2,1)} %copy-done.7, s32[8,128,1]{2,1,0:T(8,128)} %subtract_select_fusion.idc, s32[1,1024]{1,0:T(1,128)} %reshape_select_fusion.idr), custom_call_target="tpu_custom_call" | custom-call | flops 587202560 | bytes 2097152 | tf_op jit(solution)/shard_map/pallas_call | solution.py:357
  414.6 4.0 all-to-all-start.17
  432.4 6.0 shard_map.232
  441.4 7.5 %all-to-all-start.18 = ((f32[128,2,128]{2,1,0:T(2,128)}), f32[128,2,128]{2,1,0:T(2,128)S(1)}, u32[]{:S(2)}, u32[]{:S(2)}) async-start(f32[128,2,128]{2,1,0:T(2,128)} %copy.200), calls=%async_computation.18 | async-start | bytes 262144 | tf_op jit(solution)/shard_map/all_to_all | solution.py:546
  452.6 5.6 all-to-all-done.18
  458.2 3.7 all-to-all-start.24
  461.9 5.4 shard_map.238
  471.0 3.7 fusion.3
  474.7 5.4 all-to-all-done.24
  480.1 5.1 all-to-all-start.23
  485.2 5.3 shard_map.234
  503.6 5.1 all-to-all-start.26
  508.7 5.4 shard_map.233
  517.6 4.5 collective-permute-start.6
  527.1 5.4 all-to-all-start.22
  532.5 5.2 shard_map.237
  541.2 6.7 collective-permute-start.10
  547.9 3.8 fusion.5
  551.7 4.4 all-to-all-start.19
  556.1 4.4 fusion.1
  560.4 13.9 %all-to-all-done.19 = bf16[8,1152,128]{2,1,0:T(8,128)(2,1)} async-done(((bf16[8,1152,128]{2,1,0:T(8,128)(2,1)}), bf16[8,1152,128]{2,1,0:T(8,128)(2,1)}, u32[]{:S(2)}, u32[]{:S(2)}) %all-to-all-start.19) | async-done | bytes 2359328 | tf_op jit(solution)/shard_map/all_to_all | solution.py:524
  574.3 5.0 all-to-all-start.25
  588.3 9.3 %all-to-all-done.25 = bf16[8,1152,128]{2,1,0:T(8,128)(2,1)} async-done(((bf16[8,1152,128]{2,1,0:T(8,128)(2,1)}), bf16[8,1152,128]{2,1,0:T(8,128)(2,1)}, u32[]{:S(2)}, u32[]{:S(2)}) %all-to-all-start.25) | async-done | bytes 2359328 | tf_op jit(solution)/shard_map/all_to_all | solution.py:524
  597.7 8.5 %all-to-all-start.20 = ((bf16[8,144,128]{2,1,0:T(8,128)(2,1)}), bf16[8,144,128]{2,1,0:T(8,128)(2,1)S(1)}, u32[]{:S(2)}, u32[]{:S(2)}) async-start(bf16[8,144,128]{2,1,0:T(8,128)(2,1)} %bitcast.52), calls=%async_computation.20 | async-start | bytes 589824 | tf_op jit(solution)/shard_map/all_to_all | solution.py:533
  612.7 4.2 all-to-all-done.20
  616.9 4.5 all-to-all-start.27
  622.3 16.2 %all-to-all-done.27 = bf16[8,720,128]{2,1,0:T(8,128)(2,1)S(1)} async-done(((bf16[8,720,128]{2,1,0:T(8,128)(2,1)}), bf16[8,720,128]{2,1,0:T(8,128)(2,1)S(1)}, u32[]{:S(2)}, u32[]{:S(2)}) %all-to-all-start.27) | async-done | bytes 1474592 | tf_op jit(solution)/shard_map/all_to_all | solution.py:533
  643.1 5.0 all-to-all-done.21
  648.1 3.7 all-to-all-start.28
  654.4 4.8 all-to-all-done.28
  (336 shorter events, 159.0 us)
Async XLA Ops:
  7.1 9.2 %copy-start.32 = (bf16[2,2,6]{2,1,0:T(2,128)(2,1)S(1)}, bf16[2,2,6]{2,1,0:T(2,128)(2,1)}, u32[]{:S(2)}) copy-start(bf16[2,2,6]{2,1,0:T(2,128)(2,1)} %param.19) | copy-start | bytes 148
  7.1 9.3 %copy-start.33 = (bf16[2,2,6]{2,1,0:T(2,128)(2,1)S(1)}, bf16[2,2,6]{2,1,0:T(2,128)(2,1)}, u32[]{:S(2)}) copy-start(bf16[2,2,6]{2,1,0:T(2,128)(2,1)} %param.20) | copy-start | bytes 148
  7.1 9.4 %copy-start.34 = (bf16[2,2,6]{2,1,0:T(2,128)(2,1)S(1)}, bf16[2,2,6]{2,1,0:T(2,128)(2,1)}, u32[]{:S(2)}) copy-start(bf16[2,2,6]{2,1,0:T(2,128)(2,1)} %param.22) | copy-start | bytes 148
  7.2 9.4 %copy-start.35 = (bf16[2,2,6]{2,1,0:T(2,128)(2,1)S(1)}, bf16[2,2,6]{2,1,0:T(2,128)(2,1)}, u32[]{:S(2)}) copy-start(bf16[2,2,6]{2,1,0:T(2,128)(2,1)} %param.24) | copy-start | bytes 148
  7.2 9.5 %copy-start.36 = (bf16[2,24]{1,0:T(2,128)(2,1)S(1)}, bf16[2,24]{1,0:T(2,128)(2,1)}, u32[]{:S(2)}) copy-start(bf16[2,24]{1,0:T(2,128)(2,1)} %param.26) | copy-start | bytes 292
  10.6 13.2 %all-to-all-start.1 = ((bf16[8,18,6,128]{3,2,1,0:T(8,128)(2,1)}), bf16[8,18,6,128]{3,2,1,0:T(8,128)(2,1)S(1)}, u32[]{:S(2)}, u32[]{:S(2)}) async-start(bf16[8,18,6,128]{3,2,1,0:T(8,128)(2,1)} %bitcast.20), calls=%async_computation.1 | async-start | bytes 589824 | tf_op jit(solution)/shard_map/all_to_all | solution.py:440
  24.4 18.0 %all-to-all-start = ((bf16[128,2,128]{2,1,0:T(2,128)(2,1)}), bf16[128,2,128]{2,1,0:T(2,128)(2,1)S(1)}, u32[]{:S(2)}, u32[]{:S(2)}) async-start(bf16[128,2,128]{2,1,0:T(2,128)(2,1)} %broadcast_in_dim.89), calls=%async_computation | async-start | bytes 131072 | tf_op jit(solution)/shard_map/all_to_all | solution.py:445
  42.4 35.3 %copy-start.12 = (bf16[128,2,128]{2,1,0:T(2,128)(2,1)}, bf16[128,2,128]{2,1,0:T(2,128)(2,1)S(1)}, u32[]{:S(2)}) copy-start(bf16[128,2,128]{2,1,0:T(2,128)(2,1)S(1)} %all-to-all-done) | copy-start | bytes 196612
  43.2 14.1 %all-to-all-start.2 = ((bf16[8,144,128]{2,1,0:T(8,128)(2,1)}), bf16[8,144,128]{2,1,0:T(8,128)(2,1)S(1)}, u32[]{:S(2)}, u32[]{:S(2)}) async-start(bf16[8,144,128]{2,1,0:T(8,128)(2,1)} %broadcast_in_dim.91), calls=%async_computation.2 | async-start | bytes 589824 | tf_op jit(solution)/shard_map/all_to_all | solution.py:377
  79.5 21.8 %all-to-all-start.3 = ((bf16[8,1152,128]{2,1,0:T(8,128)(2,1)}), bf16[8,1152,128]{2,1,0:T(8,128)(2,1)S(1)}, u32[]{:S(2)}, u32[]{:S(2)}) async-start(bf16[8,1152,128]{2,1,0:T(8,128)(2,1)} %broadcast_in_dim.93), calls=%async_computation.3 | async-start | bytes 4718592 | tf_op jit(solution)/shard_map/all_to_all | solution.py:377
  101.3 74.1 %copy-start = (bf16[8,1152,128]{2,1,0:T(8,128)(2,1)}, bf16[8,1152,128]{2,1,0:T(8,128)(2,1)S(1)}, u32[]{:S(2)}) copy-start(bf16[8,1152,128]{2,1,0:T(8,128)(2,1)S(1)} %all-to-all-done.3) | copy-start | bytes 7077892
  171.0 22.6 %all-to-all-start.12 = ((bf16[8,1152,128]{2,1,0:T(8,128)(2,1)}), bf16[8,1152,128]{2,1,0:T(8,128)(2,1)}, u32[]{:S(2)}, u32[]{:S(2)}) async-start(bf16[8,1152,128]{2,1,0:T(8,128)(2,1)} %broadcast_in_dim.105), calls=%async_computation.12 | async-start | bytes 4718592 | tf_op jit(solution)/shard_map/all_to_all | solution.py:377
  175.4 43.5 %collective-permute-start = (bf16[64,3,48,128]{3,2,1,0:T(8,128)(2,1)S(1)}, bf16[64,3,48,128]{3,2,1,0:T(8,128)(2,1)}, u32[]{:S(2)}, u32[]{:S(2)}) collective-permute-start(bf16[64,3,48,128]{3,2,1,0:T(8,128)(2,1)S(1)} %bitcast.172), channel_id=1, source_target_pairs={{0,8},{8,0},{1,9},{9,1},{2,10},{10,2},{3,11},{11,3},{4,12},{12,4},... | collective-permute-start | bytes 7077896 | tf_op jit(solution)/shard_map/ppermute | solution.py:385
  195.4 7.8 %copy-start.38 = (s32[48]{0:T(128)S(1)}, s32[48]{0:T(128)}, u32[]{:S(2)}) copy-start(s32[48]{0:T(128)} %param.18) | copy-start | bytes 580
  195.4 9.8 %copy-start.13 = (bf16[128,2,128]{2,1,0:T(2,128)(2,1)S(1)}, bf16[128,2,128]{2,1,0:T(2,128)(2,1)}, u32[]{:S(2)}) copy-start(bf16[128,2,128]{2,1,0:T(2,128)(2,1)} %copy-done.12) | copy-start | bytes 196612
  195.4 23.5 %all-to-all-start.13 = ((bf16[8,1152,128]{2,1,0:T(8,128)(2,1)}), bf16[8,1152,128]{2,1,0:T(8,128)(2,1)}, u32[]{:S(2)}, u32[]{:S(2)}) async-start(bf16[8,1152,128]{2,1,0:T(8,128)(2,1)} %broadcast_in_dim.107), calls=%async_computation.13 | async-start | bytes 4718592 | tf_op jit(solution)/shard_map/all_to_all | solution.py:377
  200.5 66.3 %collective-permute-start.1 = (bf16[64,3,48,128]{3,2,1,0:T(8,128)(2,1)}, bf16[64,3,48,128]{3,2,1,0:T(8,128)(2,1)}, u32[]{:S(2)}, u32[]{:S(2)}) collective-permute-start(bf16[64,3,48,128]{3,2,1,0:T(8,128)(2,1)} %bitcast.182), channel_id=1, source_target_pairs={{0,8},{8,0},{1,9},{9,1},{2,10},{10,2},{3,11},{11,3},{4,12},{12,4},... | collective-permute-start | bytes 7077896 | tf_op jit(solution)/shard_map/ppermute | solution.py:385
  203.0 63.7 %collective-permute-start.2 = (bf16[64,3,48,128]{3,2,1,0:T(8,128)(2,1)}, bf16[64,3,48,128]{3,2,1,0:T(8,128)(2,1)}, u32[]{:S(2)}, u32[]{:S(2)}) collective-permute-start(bf16[64,3,48,128]{3,2,1,0:T(8,128)(2,1)} %bitcast.185), channel_id=1, source_target_pairs={{0,8},{8,0},{1,9},{9,1},{2,10},{10,2},{3,11},{11,3},{4,12},{12,4},... | collective-permute-start | bytes 7077896 | tf_op jit(solution)/shard_map/ppermute | solution.py:385
  203.2 73.5 %collective-permute-start.3 = (bf16[64,3,48,128]{3,2,1,0:T(8,128)(2,1)}, bf16[64,3,48,128]{3,2,1,0:T(8,128)(2,1)}, u32[]{:S(2)}, u32[]{:S(2)}) collective-permute-start(bf16[64,3,48,128]{3,2,1,0:T(8,128)(2,1)} %bitcast.177), channel_id=1, source_target_pairs={{0,8},{8,0},{1,9},{9,1},{2,10},{10,2},{3,11},{11,3},{4,12},{12,4},... | collective-permute-start | bytes 7077896 | tf_op jit(solution)/shard_map/ppermute | solution.py:385
  206.2 23.2 %copy-start.17 = (f32[1,768]{1,0:T(1,128)}, f32[1,768]{1,0:T(1,128)S(1)}, u32[]{:S(2)}) copy-start(f32[1,768]{1,0:T(1,128)S(1)} %slice.359.vec) | copy-start | bytes 9220
  207.0 105.6 %collective-permute-start.4 = (bf16[64,3,48,128]{3,2,1,0:T(8,128)(2,1)}, bf16[64,3,48,128]{3,2,1,0:T(8,128)(2,1)}, u32[]{:S(2)}, u32[]{:S(2)}) collective-permute-start(bf16[64,3,48,128]{3,2,1,0:T(8,128)(2,1)} %bitcast.37.mu), channel_id=1, source_target_pairs={{0,8},{8,0},{1,9},{9,1},{2,10},{10,2},{3,11},{11,3},{4,12},{12,4},... | collective-permute-start | bytes 7077896 | tf_op jit(solution)/shard_map/ppermute | solution.py:385
  218.9 93.7 %collective-permute-start.5 = (bf16[64,3,48,128]{3,2,1,0:T(8,128)(2,1)}, bf16[64,3,48,128]{3,2,1,0:T(8,128)(2,1)S(1)}, u32[]{:S(2)}, u32[]{:S(2)}) collective-permute-start(bf16[64,3,48,128]{3,2,1,0:T(8,128)(2,1)} %bitcast.39.md), channel_id=1, source_target_pairs={{0,8},{8,0},{1,9},{9,1},{2,10},{10,2},{3,11},{11,3},{4,12},{12,4},... | collective-permute-start | bytes 7077896 | tf_op jit(solution)/shard_map/ppermute | solution.py:385
  229.4 16.5 %all-to-all-start.4 = ((bf16[8,128,384]{2,1,0:T(8,128)(2,1)}), bf16[8,128,384]{2,1,0:T(8,128)(2,1)S(1)}, u32[]{:S(2)}, u32[]{:S(2)}) async-start(bf16[8,128,384]{2,1,0:T(8,128)(2,1)} %get-tuple-element.43), calls=%async_computation.4 | async-start | bytes 1572864 | tf_op jit(solution)/shard_map/all_to_all | solution.py:468
  237.1 28.2 %copy-start.22 = (f32[1,128,6]{1,2,0:T(8,128)S(1)}, f32[1,128,6]{1,2,0:T(8,128)}, u32[]{:S(2)}) copy-start(f32[1,128,6]{1,2,0:T(8,128)} %get-tuple-element.142) | copy-start | bytes 9220
  253.8 10.7 %copy-start.25 = (f32[1,128,6]{1,2,0:T(8,128)S(1)}, f32[1,128,6]{1,2,0:T(8,128)}, u32[]{:S(2)}) copy-start(f32[1,128,6]{1,2,0:T(8,128)} %get-tuple-element.145) | copy-start | bytes 9220
  253.8 11.0 %copy-start.24 = (f32[1,128,6]{1,2,0:T(8,128)S(1)}, f32[1,128,6]{1,2,0:T(8,128)}, u32[]{:S(2)}) copy-start(f32[1,128,6]{1,2,0:T(8,128)} %get-tuple-element.144) | copy-start | bytes 9220
  253.8 11.2 %copy-start.23 = (f32[1,128,6]{1,2,0:T(8,128)S(1)}, f32[1,128,6]{1,2,0:T(8,128)}, u32[]{:S(2)}) copy-start(f32[1,128,6]{1,2,0:T(8,128)} %get-tuple-element.143) | copy-start | bytes 9220
  253.8 13.0 %all-to-all-start.5 = ((bf16[8,128,128]{2,1,0:T(8,128)(2,1)}), bf16[8,128,128]{2,1,0:T(8,128)(2,1)S(1)}, u32[]{:S(2)}, u32[]{:S(2)}) async-start(bf16[8,128,128]{2,1,0:T(8,128)(2,1)} %shard_map.222), calls=%async_computation.5 | async-start | bytes 524288 | tf_op jit(solution)/shard_map/all_to_all | solution.py:474
  259.5 17.1 %copy-start.19 = (f32[1,768]{1,0:T(1,128)}, f32[1,768]{1,0:T(1,128)S(1)}, u32[]{:S(2)}) copy-start(f32[1,768]{1,0:T(1,128)S(1)} %slice.376.vec) | copy-start | bytes 9220
  264.7 11.9 %copy-start.18 = (f32[1,768]{1,0:T(1,128)}, f32[1,768]{1,0:T(1,128)S(1)}, u32[]{:S(2)}) copy-start(f32[1,768]{1,0:T(1,128)S(1)} %slice.390.vec) | copy-start | bytes 9220
  281.7 27.9 %copy-start.21 = (f32[1,128,6]{1,2,0:T(8,128)S(1)}, f32[1,128,6]{1,2,0:T(8,128)}, u32[]{:S(2)}) copy-start(f32[1,128,6]{1,2,0:T(8,128)} %get-tuple-element.138) | copy-start | bytes 9220
  306.1 10.5 %all-to-all-start.11 = ((bf16[8,128,128]{2,1,0:T(8,128)(2,1)}), bf16[8,128,128]{2,1,0:T(8,128)(2,1)S(1)}, u32[]{:S(2)}, u32[]{:S(2)}) async-start(bf16[8,128,128]{2,1,0:T(8,128)(2,1)} %shard_map.225), calls=%async_computation.11 | async-start | bytes 524288 | tf_op jit(solution)/shard_map/all_to_all | solution.py:474
  309.9 16.4 %copy-start.20 = (f32[1,768]{1,0:T(1,128)}, f32[1,768]{1,0:T(1,128)S(1)}, u32[]{:S(2)}) copy-start(f32[1,768]{1,0:T(1,128)S(1)} %slice.399.vec) | copy-start | bytes 9220
  338.9 10.5 %all-to-all-start.14 = ((bf16[8,128,128]{2,1,0:T(8,128)(2,1)}), bf16[8,128,128]{2,1,0:T(8,128)(2,1)S(1)}, u32[]{:S(2)}, u32[]{:S(2)}) async-start(bf16[8,128,128]{2,1,0:T(8,128)(2,1)} %get-tuple-element.49), calls=%async_computation.14 | async-start | bytes 524288 | tf_op jit(solution)/shard_map/all_to_all | solution.py:499
  360.1 13.5 %all-to-all-start.15 = ((bf16[8,128,384]{2,1,0:T(8,128)(2,1)}), bf16[8,128,384]{2,1,0:T(8,128)(2,1)S(1)}, u32[]{:S(2)}, u32[]{:S(2)}) async-start(bf16[8,128,384]{2,1,0:T(8,128)(2,1)} %shard_map.228), calls=%async_computation.15 | async-start | bytes 1572864 | tf_op jit(solution)/shard_map/all_to_all | solution.py:510
  367.6 81.3 %collective-permute-start.9 = (bf16[64,3,48,128]{3,2,1,0:T(8,128)(2,1)}, bf16[64,3,48,128]{3,2,1,0:T(8,128)(2,1)S(1)}, u32[]{:S(2)}, u32[]{:S(2)}) collective-permute-start(bf16[64,3,48,128]{3,2,1,0:T(8,128)(2,1)} %slice_bitcast_fusion.4), channel_id=1, source_target_pairs={{0,8},{8,0},{1,9},{9,1},{2,10},{10,2},{3,11},{11,3},{4,12},{12,4},... | collective-permute-start | bytes 7077896 | tf_op jit(solution)/shard_map/ppermute | solution.py:385
  393.1 10.7 %all-to-all-start.16 = ((bf16[8,128,128]{2,1,0:T(8,128)(2,1)}), bf16[8,128,128]{2,1,0:T(8,128)(2,1)S(1)}, u32[]{:S(2)}, u32[]{:S(2)}) async-start(bf16[8,128,128]{2,1,0:T(8,128)(2,1)} %get-tuple-element.54), calls=%async_computation.16 | async-start | bytes 524288 | tf_op jit(solution)/shard_map/all_to_all | solution.py:499
  414.6 16.9 %all-to-all-start.17 = ((bf16[8,128,384]{2,1,0:T(8,128)(2,1)}), bf16[8,128,384]{2,1,0:T(8,128)(2,1)S(1)}, u32[]{:S(2)}, u32[]{:S(2)}) async-start(bf16[8,128,384]{2,1,0:T(8,128)(2,1)} %shard_map.231), calls=%async_computation.17 | async-start | bytes 1572864 | tf_op jit(solution)/shard_map/all_to_all | solution.py:510
  418.6 9.8 %copy-start.29 = (f32[1,3072]{1,0:T(1,128)S(1)}, f32[1,3072]{1,0:T(1,128)}, u32[]{:S(2)}) copy-start(f32[1,3072]{1,0:T(1,128)} %get-tuple-element.61) | copy-start | bytes 36868
  422.1 48.9 %collective-permute-start.8 = (bf16[64,3,48,128]{3,2,1,0:T(8,128)(2,1)}, bf16[64,3,48,128]{3,2,1,0:T(8,128)(2,1)}, u32[]{:S(2)}, u32[]{:S(2)}) collective-permute-start(bf16[64,3,48,128]{3,2,1,0:T(8,128)(2,1)} %slice_bitcast_fusion.6), channel_id=1, source_target_pairs={{0,8},{8,0},{1,9},{9,1},{2,10},{10,2},{3,11},{11,3},{4,12},{12,4},... | collective-permute-start | bytes 7077896 | tf_op jit(solution)/shard_map/ppermute | solution.py:385
  441.4 16.8 %all-to-all-start.18 = ((f32[128,2,128]{2,1,0:T(2,128)}), f32[128,2,128]{2,1,0:T(2,128)S(1)}, u32[]{:S(2)}, u32[]{:S(2)}) async-start(f32[128,2,128]{2,1,0:T(2,128)} %copy.200), calls=%async_computation.18 | async-start | bytes 262144 | tf_op jit(solution)/shard_map/all_to_all | solution.py:546
  458.2 12.8 %slice-start = ((s8[4718592]{0:T(1024)(128)(4,1)}), s8[524288]{0:T(1024)(128)(4,1)S(1)}, s32[]{:S(2)}) async-start(s8[4718592]{0:T(1024)(128)(4,1)} %bitcast.188), calls=%async_computation.29 | async-start | bytes 1048576
  458.2 21.9 %all-to-all-start.24 = ((bf16[8,1152,128]{2,1,0:T(8,128)(2,1)}), bf16[8,1152,128]{2,1,0:T(8,128)(2,1)S(1)}, u32[]{:S(2)}, u32[]{:S(2)}) async-start(bf16[8,1152,128]{2,1,0:T(8,128)(2,1)} %bitcast.67), calls=%async_computation.24 | async-start | bytes 4718592 | tf_op jit(solution)/shard_map/all_to_all | solution.py:524
  461.9 9.0 %slice-start.1 = ((s8[4718592]{0:T(1024)(128)(4,1)}), s8[4194304]{0:T(1024)(128)(4,1)S(1)}, s32[]{:S(2)}) async-start(s8[4718592]{0:T(1024)(128)(4,1)} %bitcast.188), calls=%async_computation.30 | async-start | bytes 8388608
  470.8 25.5 %collective-permute-start.11 = (bf16[64,3,48,128]{3,2,1,0:T(8,128)(2,1)}, bf16[64,3,48,128]{3,2,1,0:T(8,128)(2,1)}, u32[]{:S(2)}, u32[]{:S(2)}) collective-permute-start(bf16[64,3,48,128]{3,2,1,0:T(8,128)(2,1)} %slice_bitcast_fusion), channel_id=1, source_target_pairs={{0,8},{8,0},{1,9},{9,1},{2,10},{10,2},{3,11},{11,3},{4,12},{12,4},... | collective-permute-start | bytes 7077896 | tf_op jit(solution)/shard_map/ppermute | solution.py:385
  480.1 16.2 %slice-start.6 = ((s8[4718592]{0:T(1024)(128)(4,1)}), s8[524288]{0:T(1024)(128)(4,1)S(1)}, s32[]{:S(2)}) async-start(s8[4718592]{0:T(1024)(128)(4,1)} %bitcast.194), calls=%async_computation.35 | async-start | bytes 1048576
  480.1 23.5 %all-to-all-start.23 = ((bf16[8,1152,128]{2,1,0:T(8,128)(2,1)}), bf16[8,1152,128]{2,1,0:T(8,128)(2,1)}, u32[]{:S(2)}, u32[]{:S(2)}) async-start(bf16[8,1152,128]{2,1,0:T(8,128)(2,1)} %bitcast.63), calls=%async_computation.23 | async-start | bytes 4718592 | tf_op jit(solution)/shard_map/all_to_all | solution.py:524
  485.2 11.1 %slice-start.7 = ((s8[4718592]{0:T(1024)(128)(4,1)}), s8[4194304]{0:T(1024)(128)(4,1)S(1)}, s32[]{:S(2)}) async-start(s8[4718592]{0:T(1024)(128)(4,1)} %bitcast.194), calls=%async_computation.36 | async-start | bytes 8388608
  494.0 28.1 %collective-permute-start.7 = (bf16[64,3,48,128]{3,2,1,0:T(8,128)(2,1)}, bf16[64,3,48,128]{3,2,1,0:T(8,128)(2,1)}, u32[]{:S(2)}, u32[]{:S(2)}) collective-permute-start(bf16[64,3,48,128]{3,2,1,0:T(8,128)(2,1)} %slice_bitcast_fusion.8), channel_id=1, source_target_pairs={{0,8},{8,0},{1,9},{9,1},{2,10},{10,2},{3,11},{11,3},{4,12},{12,4},... | collective-permute-start | bytes 7077896 | tf_op jit(solution)/shard_map/ppermute | solution.py:385
  503.6 18.6 %slice-start.2 = ((s8[4718592]{0:T(1024)(128)(4,1)}), s8[524288]{0:T(1024)(128)(4,1)S(1)}, s32[]{:S(2)}) async-start(s8[4718592]{0:T(1024)(128)(4,1)} %bitcast.190), calls=%async_computation.31 | async-start | bytes 1048576
  503.6 23.5 %all-to-all-start.26 = ((bf16[8,1152,128]{2,1,0:T(8,128)(2,1)}), bf16[8,1152,128]{2,1,0:T(8,128)(2,1)}, u32[]{:S(2)}, u32[]{:S(2)}) async-start(bf16[8,1152,128]{2,1,0:T(8,128)(2,1)} %bitcast.75), calls=%async_computation.26 | async-start | bytes 4718592 | tf_op jit(solution)/shard_map/all_to_all | solution.py:524
  508.7 13.4 %slice-start.3 = ((s8[4718592]{0:T(1024)(128)(4,1)}), s8[4194304]{0:T(1024)(128)(4,1)S(1)}, s32[]{:S(2)}) async-start(s8[4718592]{0:T(1024)(128)(4,1)} %bitcast.190), calls=%async_computation.32 | async-start | bytes 8388608
  517.6 30.3 %collective-permute-start.6 = (bf16[64,3,48,128]{3,2,1,0:T(8,128)(2,1)}, bf16[64,3,48,128]{3,2,1,0:T(8,128)(2,1)}, u32[]{:S(2)}, u32[]{:S(2)}) collective-permute-start(bf16[64,3,48,128]{3,2,1,0:T(8,128)(2,1)} %slice_bitcast_fusion.10), channel_id=1, source_target_pairs={{0,8},{8,0},{1,9},{9,1},{2,10},{10,2},{3,11},{11,3},{4,12},{12,4},... | collective-permute-start | bytes 7077896 | tf_op jit(solution)/shard_map/ppermute | solution.py:385
  527.1 20.8 %slice-start.4 = ((s8[4718592]{0:T(1024)(128)(4,1)}), s8[524288]{0:T(1024)(128)(4,1)S(1)}, s32[]{:S(2)}) async-start(s8[4718592]{0:T(1024)(128)(4,1)} %bitcast.192), calls=%async_computation.33 | async-start | bytes 1048576
  527.1 24.6 %all-to-all-start.22 = ((bf16[8,1152,128]{2,1,0:T(8,128)(2,1)}), bf16[8,1152,128]{2,1,0:T(8,128)(2,1)}, u32[]{:S(2)}, u32[]{:S(2)}) async-start(bf16[8,1152,128]{2,1,0:T(8,128)(2,1)} %bitcast.59), calls=%async_computation.22 | async-start | bytes 4718592 | tf_op jit(solution)/shard_map/all_to_all | solution.py:524
  532.5 15.4 %slice-start.5 = ((s8[4718592]{0:T(1024)(128)(4,1)}), s8[4194304]{0:T(1024)(128)(4,1)S(1)}, s32[]{:S(2)}) async-start(s8[4718592]{0:T(1024)(128)(4,1)} %bitcast.192), calls=%async_computation.34 | async-start | bytes 8388608
  541.2 14.9 %collective-permute-start.10 = (bf16[64,3,48,128]{3,2,1,0:T(8,128)(2,1)}, bf16[64,3,48,128]{3,2,1,0:T(8,128)(2,1)}, u32[]{:S(2)}, u32[]{:S(2)}) collective-permute-start(bf16[64,3,48,128]{3,2,1,0:T(8,128)(2,1)} %slice_bitcast_fusion.2), channel_id=1, source_target_pairs={{0,8},{8,0},{1,9},{9,1},{2,10},{10,2},{3,11},{11,3},{4,12},{12,4},... | collective-permute-start | bytes 7077896 | tf_op jit(solution)/shard_map/ppermute | solution.py:385
  551.7 22.6 %all-to-all-start.19 = ((bf16[8,1152,128]{2,1,0:T(8,128)(2,1)}), bf16[8,1152,128]{2,1,0:T(8,128)(2,1)}, u32[]{:S(2)}, u32[]{:S(2)}) async-start(bf16[8,1152,128]{2,1,0:T(8,128)(2,1)} %bitcast.51), calls=%async_computation.19 | async-start | bytes 4718592 | tf_op jit(solution)/shard_map/all_to_all | solution.py:524
  574.3 23.3 %all-to-all-start.25 = ((bf16[8,1152,128]{2,1,0:T(8,128)(2,1)}), bf16[8,1152,128]{2,1,0:T(8,128)(2,1)}, u32[]{:S(2)}, u32[]{:S(2)}) async-start(bf16[8,1152,128]{2,1,0:T(8,128)(2,1)} %bitcast.71), calls=%async_computation.25 | async-start | bytes 4718592 | tf_op jit(solution)/shard_map/all_to_all | solution.py:524
  597.7 19.2 %all-to-all-start.20 = ((bf16[8,144,128]{2,1,0:T(8,128)(2,1)}), bf16[8,144,128]{2,1,0:T(8,128)(2,1)S(1)}, u32[]{:S(2)}, u32[]{:S(2)}) async-start(bf16[8,144,128]{2,1,0:T(8,128)(2,1)} %bitcast.52), calls=%async_computation.20 | async-start | bytes 589824 | tf_op jit(solution)/shard_map/all_to_all | solution.py:533
  616.9 21.6 %all-to-all-start.27 = ((bf16[8,720,128]{2,1,0:T(8,128)(2,1)}), bf16[8,720,128]{2,1,0:T(8,128)(2,1)S(1)}, u32[]{:S(2)}, u32[]{:S(2)}) async-start(bf16[8,720,128]{2,1,0:T(8,128)(2,1)} %constant_dynamic-update-slice_fusion), calls=%async_computation.27 | async-start | bytes 2949120 | tf_op jit(solution)/shard_map/all_to_all | solution.py:533
  638.5 9.6 %all-to-all-start.21 = ((f32[8,3,6,128]{3,2,1,0:T(8,128)}), f32[8,3,6,128]{3,2,1,0:T(8,128)S(1)}, u32[]{:S(2)}, u32[]{:S(2)}) async-start(f32[8,3,6,128]{3,2,1,0:T(8,128)} %copy.201), calls=%async_computation.21 | async-start | bytes 196608 | tf_op jit(solution)/shard_map/all_to_all | solution.py:535
  648.1 14.7 %copy-start.9 = (f32[8,3,6,128]{3,2,1,0:T(8,128)}, f32[8,3,6,128]{3,2,1,0:T(8,128)S(1)}, u32[]{:S(2)}) copy-start(f32[8,3,6,128]{3,2,1,0:T(8,128)S(1)} %all-to-all-done.21) | copy-start | bytes 221188
  648.1 11.2 %all-to-all-start.28 = ((f32[8,15,6,128]{3,1,2,0:T(8,128)}), f32[8,15,6,128]{3,1,2,0:T(8,128)S(1)}, u32[]{:S(2)}, u32[]{:S(2)}) async-start(f32[8,15,6,128]{3,1,2,0:T(8,128)} %copy.202), calls=%async_computation.28 | async-start | bytes 786432 | tf_op jit(solution)/shard_map/all_to_all | solution.py:535
  (21 other events, 75.7 us)

commit v3 on v2

--- a/solution.py
+++ b/solution.py
@@ -2,6 +2,7 @@
 
 import jax
 import jax.numpy as jnp
+import numpy as np
 from jax import lax
 from jax.experimental import pallas as pl
 from jax.experimental.pallas import tpu as pltpu
@@ -34,6 +35,16 @@
 
 
 SLOT_OF = {(c,) + place(n, c): n for c in range(2) for n in range(64)}
+
+
+def tail_order():
+    table = np.zeros((128, 128), np.float32)
+    for (c, row, triple), n in SLOT_OF.items():
+        table[row * 8 + triple, 64 * c + n] = 1.0
+    return table
+
+
+TAIL_ORDER = tail_order()
 
 
 def device_id(y, z, core, x):
@@ -62,7 +73,18 @@
 GROUPS_B = cube_groups(0)
 
 
-def fetch(core_ref, mine, theirs, w, sem, low, high):
+def ff_order():
+    used = np.arange(384)
+    block, q, ctx, r = used // 192, used // 48 % 4, used // 6 % 8, used % 6
+    table = np.zeros((384, 384), np.float32)
+    table[block * 192 + ctx * 24 + q * 6 + r, used] = 1.0
+    return table
+
+
+FF_ORDER = ff_order()
+
+
+def fetch_cube(core_ref, mine, theirs, offset, w, sem, low, high):
     core = core_ref[0]
 
     def step(n, carry):
@@ -71,11 +93,34 @@
 
             @pl.when((triple >= low) & (triple < high))
             def _():
-                pltpu.make_async_copy(src.at[n], w.at[row, pl.ds((triple - low) * 3, 3)], sem).start()
+                pltpu.make_async_copy(
+                    src.at[n, pl.ds(offset, 9)], w.at[row, pl.ds((triple - low) * 9, 9)], sem).start()
 
         return carry
 
     lax.fori_loop(0, 64, step, 0)
+
+
+COMES = {(0, 0): ("cube", 0), (0, 1): ("cube", 0), (0, 2): ("plain", 0),
+         (1, 0): ("cube", 9), (1, 1): ("plain", 0), (1, 2): ("plain", 72)}
+
+
+def fetch(layer, group, core_ref, sources, w, sem, low, high):
+    kind, first = COMES[layer, group]
+    if kind == "cube":
+        fetch_cube(core_ref, sources[0], sources[1], first, w, sem, low, high)
+    else:
+        tiles = pl.ds(first + 9 * low, 9 * (high - low))
+        pltpu.make_async_copy(sources[0].at[:, tiles], w, sem).start()
+
+
+def sources_of(layer, groups, refs):
+    out, at = {}, 0
+    for group in groups:
+        n = 2 if COMES[layer, group][0] == "cube" else 1
+        out[group] = refs[at : at + n]
+        at += n
+    return out, refs[at:]
 
 
 def arrived(w, sem):
@@ -83,12 +128,12 @@
 
 
 def units(w, first, count):
-    parts = [w[:, first + i].reshape(D, 128) for i in range(count)]
+    parts = [w[:, 3 * (first + i) : 3 * (first + i) + 3].reshape(D, 128) for i in range(count)]
     return parts[0] if count == 1 else jnp.concatenate(parts, axis=1)
 
 
 def tall_units(w, cb):
-    return w[:, 4 * cb : 4 * cb + 4].reshape(4 * D, 128)
+    return w[:, 12 * cb : 12 * cb + 12].reshape(4 * D, 128)
 
 
 def mul(a, b):
@@ -144,8 +189,9 @@
     return u * half, half + 0.5 * u * (1.0 - t * t) * (k * (1.0 + 3 * 0.044715 * u * u))
 
 
-def project_kernel(core, h_ref, vec, mine, theirs, a1_ref, pay_ref, w, sem):
-    fetch(core, mine, theirs, w, sem, 0, 6)
+def project_kernel(layer, core, h_ref, vec, *refs):
+    src, (a1_ref, pay_ref, w, sem) = sources_of(layer, (0,), refs)
+    fetch(layer, 0, core, src[0], w, sem, 0, 6)
     xh, _ = norm_parts(h_ref[...].astype(f32))
     a1 = (xh * vec[0:1] + vec[1:2]).astype(bf16)
     a1_ref[...] = a1
@@ -229,11 +275,11 @@
     out[:, :, 256:384] = dv.astype(bf16).reshape(8, TOK, 128)
 
 
-def forward_kernel(core, h_ref, back, vec, upb, me, te, mu, tu, md, td,
-                   o_ref, h1_ref, a2_ref, u_ref, next_ref, wo, wu, wd, sems):
-    fetch(core, me, te, wo, sems.at[0], 6, 8)
-    fetch(core, mu, tu, wu, sems.at[1], 0, 8)
-    fetch(core, md, td, wd, sems.at[2], 0, 8)
+def forward_kernel(layer, core, h_ref, back, vec, upb, *refs):
+    src, (o_ref, h1_ref, a2_ref, u_ref, next_ref, wo, wu, wd, sems) = sources_of(layer, (0, 1, 2), refs)
+    fetch(layer, 0, core, src[0], wo, sems.at[0], 6, 8)
+    fetch(layer, 1, core, src[1], wu, sems.at[1], 0, 8)
+    fetch(layer, 2, core, src[2], wd, sems.at[2], 0, 8)
     o = unwindow(lambda d: back[d].astype(f32)).astype(bf16)
     o_ref[...] = o
     arrived(wo, sems.at[0])
@@ -257,11 +303,11 @@
         next_ref[:, c] = (h1[:, c] + mul(f, w) + vec[3:4, c]).astype(next_ref.dtype)
 
 
-def backward_kernel(core, e_ref, u_ref, h1_ref, vec, me, te, mu, tu, md, td,
-                    f_ref, du_ref, e1_ref, pay_ref, small_ref, upb_ref, wo, wu, wd, sems):
-    fetch(core, md, td, wd, sems.at[2], 0, 8)
-    fetch(core, mu, tu, wu, sems.at[1], 0, 8)
-    fetch(core, me, te, wo, sems.at[0], 6, 8)
+def backward_kernel(layer, core, e_ref, u_ref, h1_ref, vec, *refs):
+    src, (f_ref, du_ref, e1_ref, pay_ref, small_ref, upb_ref, wo, wu, wd, sems) = sources_of(layer, (0, 1, 2), refs)
+    fetch(layer, 2, core, src[2], wd, sems.at[2], 0, 8)
+    fetch(layer, 1, core, src[1], wu, sems.at[1], 0, 8)
+    fetch(layer, 0, core, src[0], wo, sems.at[0], 6, 8)
     e = e_ref[...].astype(f32)
     e2 = e.astype(bf16)
     arrived(wd, sems.at[2])
@@ -296,8 +342,9 @@
         pay_ref[d] = win.astype(bf16)
 
 
-def back_project_kernel(core, back, e1_ref, h_ref, vec, mine, theirs, g_ref, e_ref, small_ref, w, sem):
-    fetch(core, mine, theirs, w, sem, 0, 6)
+def back_project_kernel(layer, core, back, e1_ref, h_ref, vec, *refs):
+    src, (g_ref, e_ref, small_ref, w, sem) = sources_of(layer, (0,), refs)
+    fetch(layer, 0, core, src[0], w, sem, 0, 6)
     for part in range(3):
         got = unwindow(lambda d: back[d, :, 128 * part : 128 * part + 128].astype(f32)).astype(bf16)
         g_ref[:, D * part : D * part + D] = got
@@ -313,63 +360,215 @@
     e_ref[...] = e1_ref[...] + norm_back(cot, vec[0:1], xh, r)
 
 
-def store_grad(core, out, wide, first):
-    for i in range(wide.shape[1] // 128):
-        rows = wide[:, 128 * i : 128 * i + 128].astype(bf16).reshape(16, 48, 128)
-        triple, k = divmod(first + i, 3)
-        for row in range(16):
-            target = row & 1
-            out[core ^ target, SLOT_OF[(target, row, triple)], k] = rows[row]
-
-
-def grad_wide_kernel(core_ref, a_ref, b_ref, out):
+def cube_store(core, stage, first_tile, triple, k, rows):
+    for row in range(16):
+        target = row & 1
+        tile = first_tile + 3 * k
+        stage[core ^ target, SLOT_OF[(target, row, triple)], tile : tile + 3] = rows[row].reshape(3, 16, 128)
+
+
+def plain_store(stage, unit, rows):
+    stage[:, 3 * unit : 3 * unit + 3] = rows.reshape(16, 3, 16, 128)
+
+
+def wide_grad(at, b, first, store):
+    for j in range(b.shape[1] // D):
+        wide = mul(at, b[:, D * j : D * j + D])
+        for i in range(6):
+            store(first + 6 * j + i, wide[:, 128 * i : 128 * i + 128].astype(bf16).reshape(16, 48, 128))
+
+
+def tall_grad(ft, b, store):
+    for j in range(3):
+        wide = mul(ft, b[:, 256 * j : 256 * j + 256])
+        for i in range(2):
+            rows = wide[:, 128 * i : 128 * i + 128].astype(bf16).reshape(16, 4, 48, 128)
+            for q in range(4):
+                store(4 * (2 * j + i) + q, rows[:, q])
+
+
+def low(ref):
+    return ref[...].astype(f32).astype(bf16)
+
+
+def ship(pairs, sem):
+    copies = [pltpu.make_async_copy(src, dst, sem.at[k]) for k, (src, dst) in enumerate(pairs)]
+    for copy in copies:
+        copy.start()
+    for copy in copies:
+        copy.wait()
+
+
+def grad_mlp_cube(core_ref, f_ref, e_ref, a2_ref, du_ref, keep, send, stage, sem):
     core = core_ref[0]
-    at = a_ref[...].T
-    for j in range(4):
-        store_grad(core, out, mul(at, b_ref[:, D * j : D * j + D]), 6 * j)
-
-
-def grad_tall_kernel(core_ref, f_ref, e_ref, out):
+    tall_grad(f_ref[...].T, low(e_ref), lambda u, rows: cube_store(core, stage, 9, u // 3, u % 3, rows))
+    wide_grad(a2_ref[...].T, du_ref[...], 0, lambda u, rows: cube_store(core, stage, 0, u // 3, u % 3, rows))
+    ship(((stage.at[0], keep), (stage.at[1], send)), sem)
+
+
+def grad_joint_cube(core_ref, a_ref, g_ref, o_ref, e1_ref, keep, send, stage, sem):
     core = core_ref[0]
-    ft = f_ref[...].T
-    e2 = e_ref[...].astype(f32).astype(bf16)
-    for j in range(3):
-        wide = mul(ft, e2[:, 256 * j : 256 * j + 256]).astype(bf16)
-        for half in range(2):
-            rows = wide[:, 128 * half : 128 * half + 128].reshape(16, 4, 48, 128)
-            for q in range(4):
-                triple, k = divmod(4 * (2 * j + half) + q, 3)
-                for row in range(16):
-                    target = row & 1
-                    out[core ^ target, SLOT_OF[(target, row, triple)], k] = rows[row, q]
-
-
-def grad_joint_kernel(core_ref, a_ref, g_ref, o_ref, e1_ref, out):
+    put = lambda u, rows: cube_store(core, stage, 0, u // 3, u % 3, rows)
+    wide_grad(a_ref[...].T, g_ref[...], 0, put)
+    wide_grad(o_ref[...].T, low(e1_ref), 18, put)
+    ship(((stage.at[0], keep), (stage.at[1], send)), sem)
+
+
+def grad_down_plain(f_ref, e_ref, out, stage, sem):
+    tall_grad(f_ref[...].T, low(e_ref), lambda u, rows: plain_store(stage, u, rows))
+    ship(((stage, out),), sem)
+
+
+def grad_up_cube(core_ref, a2_ref, du_ref, keep, send, stage, sem):
     core = core_ref[0]
-    at = a_ref[...].T
-    for j in range(3):
-        store_grad(core, out, mul(at, g_ref[:, D * j : D * j + D]), 6 * j)
-    store_grad(core, out, mul(o_ref[...].T, e1_ref[...].astype(bf16)), 18)
-
-
-def call(kernel, outs, ins, scratch=(), flops=0, bytes_accessed=0):
+    wide_grad(a2_ref[...].T, du_ref[...], 0, lambda u, rows: cube_store(core, stage, 0, u // 3, u % 3, rows))
+    ship(((stage.at[0], keep), (stage.at[1], send)), sem)
+
+
+CUBE_IN, PLAIN_IN = ((0, 0), (0, 1), (1, 0)), ((0, 2), (1, 1), (1, 2))
+CUBE_OUT = ((0, 0), (0, 1), (0, 2), (1, 0), (1, 1))
+
+
+def pack_kernel(win, wout, wup, wdown, order, pay):
+    ups = []
+    for l in range(LAYERS):
+        up = [mul(wup[l, :, 384 * m : 384 * m + 384], order[...]) for m in range(8)]
+        ups.append(jnp.concatenate(up, axis=1).astype(bf16))
+
+    def get(l, group, u):
+        if group == 0:
+            return win[l, :, 128 * u : 128 * u + 128] if u < 18 else wout[l, :, 128 * (u - 18) : 128 * (u - 17)]
+        if group == 1:
+            return ups[l][:, 128 * u : 128 * u + 128]
+        cb, q = divmod(u, 4)
+        return wdown[l, 6 * q : 6 * q + 6, 128 * cb : 128 * cb + 128]
+
+    for u in range(24):
+        for k, key in enumerate(CUBE_IN):
+            pay[u // 3, 3 * k + u % 3, 0:6] = get(*key, u)
+        for k, key in enumerate(PLAIN_IN):
+            rows = get(*key, u)
+            for d in range(8):
+                pay[d, 9 + 24 * k + u, 0:6] = rows
+
+
+def join_rows(got, u):
+    rows = jnp.concatenate([got[d, u].astype(f32)[0:6] for d in range(8)], axis=0)
+    return rows.astype(bf16).reshape(3, 16, 128)
+
+
+def regroup_kernel(got, smalls, first, third, fourth):
+    for u in range(3):
+        first[3 * u : 3 * u + 3] = join_rows(got, u)
+    first[9] = smalls[...]
+    for u in range(3, 9):
+        first[3 * u + 1 : 3 * u + 4] = join_rows(got, u)
+    for u in range(24):
+        third[3 * u : 3 * u + 3] = join_rows(got, 9 + u)
+    for u in range(48):
+        fourth[3 * u : 3 * u + 3] = join_rows(got, 33 + u)
+
+
+def smalls_kernel(core_ref, mine, theirs, vecs, few, buf, sem):
+    core = core_ref[0]
+
+    def step(n, carry):
+        for src, own in ((mine, core), (theirs, 1 - core)):
+            row, triple = place(n, own)
+            pltpu.make_async_copy(src.at[n, 9], buf.at[row * 8 + triple], sem).start()
+        return carry
+
+    lax.fori_loop(0, 64, step, 0)
+    pltpu.make_async_copy(buf, buf, sem).wait()
+    rows = buf[...].astype(f32)
+    low_part, high_part = rows[:, 0], rows[:, 1]
+    few[:, 0:128] = low_part
+    few[:, 128:256] = high_part
+    low_part = low_part.astype(bf16)
+    value = lax.broadcasted_iota(jnp.int32, (128, 16), 0) - 6 * lax.broadcasted_iota(jnp.int32, (128, 16), 1)
+    place_in = lax.broadcasted_iota(jnp.int32, (128, D), 1) - 6 * lax.broadcasted_iota(jnp.int32, (128, D), 0)
+    total = jnp.zeros((16, D), f32)
+    for i in range(6):
+        picked = mul(low_part, (value == i).astype(f32).astype(bf16)).astype(bf16)
+        total = total + t_mul(picked, (place_in == i).astype(f32).astype(bf16))
+    vecs[...] = total
+
+
+def split_rows(out, u, rows):
+    for d in range(8):
+        part = jnp.concatenate([rows[6 * d : 6 * d + 6], jnp.zeros((2, 128), f32)], axis=0)
+        out[d, u] = part.astype(bf16)
+
+
+def finish_kernel(parts, total, out, few):
+    small = jnp.zeros((2, 128), f32)
+    for k in range(8):
+        small = small + parts[k, 9].astype(f32)[0:2]
+    few[...] = small
+    for u in range(24):
+        split_rows(out, 15 + u, total[3 * u : 3 * u + 3].reshape(48, 128).astype(f32))
+    for u in range(15):
+        tile = 3 * u if u < 3 else 3 * u + 1
+        rows = jnp.zeros((48, 128), f32)
+        for k in range(8):
+            rows = rows + parts[k, tile : tile + 3].reshape(48, 128).astype(f32)
+        split_rows(out, u, rows)
+
+
+def unpack_kernel(got, order, g_in, g_out, g_up, g_down):
+    for l in range(LAYERS):
+        for group in range(3):
+            ups = []
+            for u in range(24):
+                if (l, group) in CUBE_OUT:
+                    rows = got[u // 3, 3 * CUBE_OUT.index((l, group)) + u % 3].astype(f32)
+                else:
+                    rows = got[0, 15 + u].astype(f32)
+                    for d in range(1, 8):
+                        rows = rows + got[d, 15 + u].astype(f32)
+                rows = rows[0:6]
+                if group == 0 and u < 18:
+                    g_in[l, :, 128 * u : 128 * u + 128] = rows
+                elif group == 0:
+                    g_out[l, :, 128 * (u - 18) : 128 * (u - 17)] = rows
+                elif group == 1:
+                    ups.append(rows)
+                else:
+                    cb, q = divmod(u, 4)
+                    g_down[l, 6 * q : 6 * q + 6, 128 * cb : 128 * cb + 128] = rows
+            for m in range(len(ups) // 3):
+                left = jnp.concatenate(ups[3 * m : 3 * m + 3], axis=1)
+                wide = jnp.zeros((6, 384), f32)
+                for _ in range(3):
+                    term = left.astype(bf16)
+                    left = left - term.astype(f32)
+                    wide = wide + mul_t(term, order[...])
+                g_up[l, :, 384 * m : 384 * m + 384] = wide
+
+
+def call(kernel, outs, ins, scratch=(), us=3, out_spaces=None, aliases=None):
     spaces = {"s": pltpu.SMEM, "v": pltpu.VMEM, "a": pl.ANY}
     return pl.pallas_call(
         kernel,
         out_shape=[jax.ShapeDtypeStruct(*o) for o in outs],
         in_specs=[pl.BlockSpec(memory_space=spaces[m]) for _, m in ins],
-        out_specs=[pl.BlockSpec(memory_space=pltpu.VMEM)] * len(outs),
+        out_specs=[pl.BlockSpec(memory_space=spaces[m]) for m in (out_spaces or "v" * len(outs))],
         scratch_shapes=list(scratch),
+        input_output_aliases=aliases or {},
         compiler_params=pltpu.CompilerParams(vmem_limit_bytes=56 * 1024 * 1024),
-        cost_estimate=pl.CostEstimate(flops=flops, bytes_accessed=bytes_accessed, transcendentals=0),
+        cost_estimate=pl.CostEstimate(flops=0, bytes_accessed=us * 3690000, transcendentals=0),
     )(*[a for a, _ in ins])
 
 
 def w_scratch(count):
-    return pltpu.VMEM((16, count, 48, 128), bf16)
+    return pltpu.VMEM((16, 3 * count, 16, 128), bf16)
 
 
 DMA = pltpu.SemaphoreType.DMA
+
+
+def after(values, *others):
+    return lax.optimization_barrier((values,) + others)[0]
 
 
 def copies(values, groups):
@@ -385,28 +584,48 @@
     return lax.ppermute(values, "c", [(0, 1), (1, 0)])
 
 
-def spread(shard):
-    rows = shard.shape[1]
-    mine = copies(shard.reshape(8 * rows, 128), GROUPS_B).reshape(64, rows // 48, 48, 128)
+def cube_copies(shards):
+    return copies(shards, GROUPS_B).reshape((64,) + shards.shape[1:])
+
+
+def spread(shards):
+    mine = cube_copies(shards)
     return mine, swap_core(mine)
 
 
-def ff_in(values):
-    lead = values.shape[:-1]
-    return jnp.swapaxes(values.reshape(lead + (16, 8, 4, 6)), -3, -2).reshape(lead + (4 * D,))
-
-
-def ff_out(values):
-    lead = values.shape[:-1]
-    return jnp.swapaxes(values.reshape(lead + (16, 4, 8, 6)), -3, -2).reshape(lead + (4 * D,))
-
-
-def to_units(values):
-    return jnp.swapaxes(values.reshape(6, -1, 128), 0, 1)
-
-
-def from_units(values):
-    return jnp.swapaxes(values, 0, 1).reshape(6, -1)
+def add_kernel(*refs):
+    out, first = refs[-1], 0
+    for keep, got in zip(refs[0:-1:2], refs[1:-1:2]):
+        n = keep.shape[1]
+        out[:, first : first + n] = (keep[...].astype(f32) + got[...].astype(f32)).astype(bf16)
+        first += n
+
+
+def add_pairs(pairs):
+    total = sum(a.shape[1] for a, _ in pairs)
+    flat = [v for pair in pairs for v in pair]
+
+    def spec(t):
+        return pl.BlockSpec((8, t, 16, 128), lambda i: (i, 0, 0, 0))
+
+    return pl.pallas_call(
+        add_kernel,
+        grid=(8,),
+        out_shape=jax.ShapeDtypeStruct((64, total, 16, 128), bf16),
+        in_specs=[spec(v.shape[1]) for v in flat],
+        out_specs=spec(total),
+        compiler_params=pltpu.CompilerParams(vmem_limit_bytes=56 * 1024 * 1024),
+        cost_estimate=pl.CostEstimate(flops=2**22, bytes_accessed=3 * 64 * total * 4096, transcendentals=0),
+    )(*flat)
+
+
+def core_sums(pairs):
+    return add_pairs([(keep, swap_core(send)) for keep, send in pairs])
+
+
+def gather_sums(part):
+    part = part.reshape((8, 8) + part.shape[1:])
+    return sum_first(lax.all_to_all(part, ALL, 0, 0, axis_index_groups=GROUPS_B)).astype(bf16)
 
 
 def token_ids(group_index, positions, sequence_group, sequence_start, sequence_length):
@@ -428,122 +647,159 @@
     ids = token_ids(lax.axis_index(DATA), positions, sequence_group, sequence_start, sequence_length)
     idc, idr = ids.reshape(CTX_DEV, TOK, 1), ids.reshape(1, SLOTS)
 
-    parts = []
-    for l in range(LAYERS):
-        parts.append(to_units(input_weight[l]))
-        parts.append(to_units(output_weight[l]))
-        parts.append(to_units(ff_in(up_weight[l])))
-        down = down_weight[l].reshape(4, 6, 6, 128)
-        parts.append(down.transpose(2, 0, 1, 3).reshape(24, 6, 128))
-    packed = jnp.concatenate(parts, axis=0).reshape(2, 3, 8, 3, 6, 128)
-    packed = packed.transpose(2, 0, 1, 3, 4, 5).reshape(8, 18, 6, 128)
-    got = lax.all_to_all(packed, CTX, 0, 0)
-    got = got.transpose(1, 0, 2, 3).reshape(2, 3, 144, 128)
-
+    order = jnp.asarray(FF_ORDER, bf16)
     smalls = jnp.concatenate([v.reshape(-1) for v in (norm_gain, norm_bias, input_bias, branch_bias, up_bias)])
-    smalls = jnp.pad(smalls, (0, 256 - 144)).reshape(1, 2, 128)
-    few = lax.all_to_all(jnp.broadcast_to(smalls, (128, 2, 128)), ALL, 0, 0).reshape(128, 256).astype(f32)
-    vecs = few[:, :96].reshape(128, 16, 6).transpose(1, 0, 2).reshape(16, D)
+    smalls = jnp.pad(smalls, (0, 2048 - 144)).reshape(16, 128)
+    (pay,) = call(pack_kernel, [((8, 81, 8, 128), bf16)],
+                  [(input_weight, "v"), (output_weight, "v"), (up_weight, "v"), (down_weight, "v"), (order, "v")])
+    got = lax.all_to_all(pay, CTX, 0, 0)
+    first, third, fourth = call(
+        regroup_kernel,
+        [((28, 16, 128), bf16), ((72, 16, 128), bf16), ((144, 16, 128), bf16)],
+        [(got, "v"), (smalls, "v")])
+    down_0 = lax.all_gather(third, DATA, axis=0, tiled=False)
+    shards = copies(first, GROUPS_A)
+    group_e, shards = spread(shards[:, :10]), shards[:, 10:]
+    sources = {(0, 0): group_e, (0, 2): (down_0,)}
+
+    vecs, few = call(
+        smalls_kernel, [((16, D), f32), ((128, 256), f32)],
+        [(core, "s"), (group_e[0], "a"), (group_e[1], "a")],
+        [pltpu.VMEM((128, 16, 128), bf16), DMA], us=2)
     ups = few[:, 96:144].reshape(16, 8, 2, 4, 6).transpose(2, 0, 3, 1, 4).reshape(2, 4 * D)
-
-    first = copies(got[0, 0], GROUPS_A)
-    rest = copies(got.reshape(6 * 144, 128)[144:], GROUPS_A).reshape(8, 5, 144, 128)
-    weights = [[spread(first), spread(rest[:, 0]), spread(rest[:, 1])],
-               [spread(rest[:, 2]), spread(rest[:, 3]), spread(rest[:, 4])]]
 
     def vec(*index):
         return jnp.concatenate([vecs[i : i + 1] for i in index], axis=0)
+
+    def weights(l, all_groups):
+        return [(w, "a") for group in range(3 if all_groups else 1) for w in sources[l, group]]
 
     hidden = hidden_in[0]
     stored = []
     for l in range(LAYERS):
-        group_e, group_u, group_d = weights[l]
         a1, pay = call(
-            project_kernel,
+            functools.partial(project_kernel, l),
             [((TOK, D), bf16), ((8, TOK, 384), bf16)],
-            [(core, "s"), (hidden, "v"), (vec(2 * l, 4 + 2 * l, 8 + 2 * l, 9 + 2 * l), "v"),
-             (group_e[0], "a"), (group_e[1], "a")],
+            [(core, "s"), (hidden, "v"), (vec(2 * l, 4 + 2 * l, 8 + 2 * l, 9 + 2 * l), "v")] + weights(l, False),
             [w_scratch(18), DMA],
-            flops=2 * TOK * D * 3 * D, bytes_accessed=4 * 2**20)
+            us=5)
+        if l == 0:
+            both_1 = lax.all_gather(after(fourth, a1), DATA, axis=0, tiled=False)
+            sources[1, 1] = sources[1, 2] = (both_1,)
         heads = lax.all_to_all(pay, CTX, 0, 0)
+        if l == 0:
+            mine = cube_copies(after(shards, heads, down_0))
         (mix,) = call(
             attend_kernel,
             [((8, TOK, 128), bf16)],
             [(par, "s"), (heads, "v"), (idc, "v"), (idr, "v")],
-            flops=2 * 2 * 64 * 56 * 128 * 128, bytes_accessed=2**20)
+            us=7)
+        if l == 0:
+            theirs = swap_core(after(mine, mix))
+            for key in CUBE_IN[1:]:
+                sources[key] = (mine, theirs)
+        mix = after(mix, mine if l == 0 else both_1)
         back = lax.all_to_all(mix, CTX, 0, 0)
         o, h1, a2, u, following = call(
-            forward_kernel,
+            functools.partial(forward_kernel, l),
             [((TOK, D), bf16), ((TOK, D), f32), ((TOK, D), bf16), ((TOK, 4 * D), f32),
              ((TOK, D), f32 if l == 0 else bf16)],
             [(core, "s"), (hidden, "v"), (back, "v"), (vec(2 * l + 1, 5 + 2 * l, 12 + 2 * l, 13 + 2 * l), "v"),
-             (ups[l : l + 1], "v")] + [(w, "a") for pair in weights[l] for w in pair],
+             (ups[l : l + 1], "v")] + weights(l, True),
             [w_scratch(6), w_scratch(24), w_scratch(24), DMA((3,))],
-            flops=2 * TOK * D * 9 * D, bytes_accessed=12 * 2**20)
+            us=8)
         stored.append((hidden, a1, heads, o, h1, a2, u))
         hidden = following
 
+    def grad_joint(g, a1, o, e1):
+        return call(
+            grad_joint_cube, [((64, 9, 16, 128), bf16)] * 2,
+            [(core, "s"), (a1, "v"), (g, "v"), (o, "v"), (e1, "v")],
+            [pltpu.VMEM((2, 64, 9, 16, 128), bf16), DMA((2,))], us=5, out_spaces="aa")
+
     grad = out_grad[0]
-    sums = []
     few_rows, few_up = [None] * 2, [None] * 2
     for l in reversed(range(LAYERS)):
         layer_in, a1, heads, o, h1, a2, u = stored[l]
         f, du, e1, pay, small_b, small_u = call(
-            backward_kernel,
+            functools.partial(backward_kernel, l),
             [((TOK, 4 * D), bf16), ((TOK, 4 * D), bf16), ((TOK, D), f32), ((8, TOK, 128), bf16),
              ((4, D), f32), ((1, 4 * D), f32)],
-            [(core, "s"), (grad, "v"), (u, "v"), (h1, "v"), (vec(2 * l + 1), "v")]
-            + [(w, "a") for pair in weights[l] for w in pair],
+            [(core, "s"), (grad, "v"), (u, "v"), (h1, "v"), (vec(2 * l + 1), "v")] + weights(l, True),
             [w_scratch(6), w_scratch(24), w_scratch(24), DMA((3,))],
-            flops=2 * TOK * D * 9 * D, bytes_accessed=12 * 2**20)
+            us=10)
+        if l == 0:
+            sums_up = gather_sums(after(up_1, back2))
+            pay = after(pay, sums_up)
+            f = after(f, sums_up)
         cot = lax.all_to_all(pay, CTX, 0, 0)
-        (grad_d,) = call(grad_tall_kernel, [((2, 64, 3, 48, 128), bf16)], [(core, "s"), (f, "v"), (grad, "v")],
-                         flops=2 * TOK * D * 4 * D, bytes_accessed=6 * 2**20)
-        (grad_u,) = call(grad_wide_kernel, [((2, 64, 3, 48, 128), bf16)], [(core, "s"), (a2, "v"), (du, "v")],
-                         flops=2 * TOK * D * 4 * D, bytes_accessed=6 * 2**20)
+        if l == 1:
+            (down_1,) = call(
+                grad_down_plain, [((16, 72, 16, 128), bf16)], [(f, "v"), (grad, "v")],
+                [w_scratch(24), DMA((1,))], us=5, out_spaces="a")
+            up_1 = call(
+                grad_up_cube, [((64, 9, 16, 128), bf16)] * 2, [(core, "s"), (a2, "v"), (du, "v")],
+                [pltpu.VMEM((2, 64, 9, 16, 128), bf16), DMA((2,))], us=5, out_spaces="aa")
+        else:
+            keep_ud, send_ud = call(
+                grad_mlp_cube, [((64, 18, 16, 128), bf16)] * 2,
+                [(core, "s"), (f, "v"), (grad, "v"), (a2, "v"), (du, "v")],
+                [pltpu.VMEM((2, 64, 18, 16, 128), bf16), DMA((2,))],
+                us=9, out_spaces="aa")
+        if l == 0:
+            send_ud = after(send_ud, cot)
+            joint_1 = grad_joint(after(saved[0], cot), *saved[1:])
+        else:
+            scattered = lax.psum_scatter(after(down_1, cot), DATA, scatter_dimension=0, tiled=False)
+        cot = after(cot, down_1 if l == 1 else keep_ud)
         (pay2,) = call(
             attend_back_kernel,
             [((8, TOK, 384), bf16)],
             [(par, "s"), (heads, "v"), (cot, "v"), (idc, "v"), (idr, "v")],
             [pltpu.VMEM((2, SLOTS, 64), f32)] * 2,
-            flops=5 * 2 * 64 * 56 * 128 * 128, bytes_accessed=2**21)
+            us=10)
+        if l == 0:
+            pay2 = after(pay2, scattered)
         back2 = lax.all_to_all(pay2, CTX, 0, 0)
+        if l == 1:
+            up_1 = core_sums([up_1])
+            back2 = after(back2, up_1)
+        else:
+            middle = core_sums([(keep_ud, send_ud), joint_1])
+            back2 = after(back2, middle)
         g, grad, small_a = call(
-            back_project_kernel,
+            functools.partial(back_project_kernel, l),
             [((TOK, 3 * D), bf16), ((TOK, D), f32), ((4, D), f32)],
-            [(core, "s"), (back2, "v"), (e1, "v"), (layer_in, "v"), (vec(2 * l), "v"),
-             (weights[l][0][0], "a"), (weights[l][0][1], "a")],
+            [(core, "s"), (back2, "v"), (e1, "v"), (layer_in, "v"), (vec(2 * l), "v")] + weights(l, False),
             [w_scratch(18), DMA],
-            flops=2 * TOK * D * 3 * D, bytes_accessed=4 * 2**20)
-        (grad_e,) = call(grad_joint_kernel, [((2, 64, 3, 48, 128), bf16)],
-                         [(core, "s"), (a1, "v"), (g, "v"), (o, "v"), (e1, "v")],
-                         flops=2 * TOK * D * 4 * D, bytes_accessed=6 * 2**20)
-        layer_sums = []
-        for both in (grad_e, grad_u, grad_d):
-            part = (both[0].astype(f32) + swap_core(both[1]).astype(f32)).astype(bf16).reshape(8, 8 * 144, 128)
-            part = sum_first(lax.all_to_all(part, ALL, 0, 0, axis_index_groups=GROUPS_B)).astype(bf16)
-            layer_sums.append(part.reshape(8, 144, 128))
-        sums.append(layer_sums)
+            us=6)
+        if l == 1:
+            saved = (g, a1, o, e1)
+        else:
+            joint_0 = grad_joint(g, a1, o, e1)
         few_rows[l] = jnp.concatenate([small_a[0:1], small_b[0:1], small_a[1:2], small_b[1:2], small_a[2:4],
                                        small_b[2:4]], axis=0)
         few_up[l] = small_u
 
-    def finish(values):
-        n = values.shape[1] // 144
-        part = sum_first(lax.all_to_all(values, ALL, 0, 0, axis_index_groups=GROUPS_A))
-        part = part.reshape(n * 3, 8, 6, 128).transpose(1, 0, 2, 3)
-        part = lax.all_to_all(part, CTX, 0, 0)
-        return part.reshape(8, n, 3, 6, 128).transpose(1, 0, 2, 3, 4).reshape(n, 24, 6, 128)
-
-    (e_hi, u_hi, d_hi), (e_lo, u_lo, d_lo) = sums
-    early = finish(jnp.concatenate([e_hi, u_hi, d_hi, u_lo, d_lo], axis=1))
-    late = finish(e_lo)
-    group_e, group_u, group_d = (late[0], early[0]), (early[3], early[1]), (early[4], early[2])
-
     few = jnp.concatenate([r.reshape(8, 128, 6).transpose(1, 0, 2).reshape(128, 48) for r in few_rows]
                           + [r.reshape(16, 4, 8, 6).transpose(0, 2, 1, 3).reshape(128, 24) for r in few_up], axis=1)
-    few = jnp.pad(few, ((0, 0), (0, 256 - 144))).reshape(128, 2, 128)
-    few = jnp.sum(lax.all_to_all(few, ALL, 0, 0), axis=0).reshape(256)
+    few = jnp.pad(few, ((0, 0), (0, 256 - 144))).astype(bf16)
+    few = jnp.dot(jnp.asarray(TAIL_ORDER.T, bf16), few, preferred_element_type=f32).astype(bf16)
+    few = jnp.pad(few.reshape(2, 64, 1, 2, 128), ((0, 0),) * 3 + ((0, 14), (0, 0)))
+    few = [jnp.where(core[0] == k, few[0], few[1]) for k in range(2)]
+
+    middle = gather_sums(middle)
+    last = gather_sums(after(core_sums([joint_0, few]), middle))
+    sums = jnp.concatenate([last, middle, sums_up], axis=1)
+    sums = lax.all_to_all(sums, ALL, 0, 0, axis_index_groups=GROUPS_A)
+    sums, few = call(finish_kernel, [((8, 39, 8, 128), bf16), ((2, 128), f32)],
+                     [(sums, "v"), (scattered, "v")])
+    got = lax.all_to_all(sums, CTX, 0, 0)
+    grad_in, grad_out, grad_up, grad_down = call(
+        unpack_kernel,
+        [((2, 6, 3 * D), f32), ((2, 6, D), f32), ((2, 6, 4 * D), f32), ((2, 24, D), f32)],
+        [(got, "v"), (order, "v")])
+    few = few.reshape(256)
     few_l = [few[48 * l : 48 * l + 48].reshape(4, 2, 6) for l in range(2)]
 
     def pair(k):
@@ -554,13 +810,13 @@
         grad[None],
         pair(0),
         pair(1),
-        jnp.stack([from_units(v[:18]) for v in group_e]),
+        grad_in,
         pair(2),
-        jnp.stack([from_units(v[18:]) for v in group_e]),
+        grad_out,
         pair(3),
-        jnp.stack([ff_out(from_units(v)) for v in group_u]),
+        grad_up,
         few[96:144].reshape(2, 24),
-        jnp.stack([v.reshape(6, 4, 6, 128).transpose(1, 2, 0, 3).reshape(24, D) for v in group_d]),
+        grad_down,
     )
 
 

time: 684 us -> 528 us (0.77)
  starting transfers between devices: 136 us -> 56.9 us
  local copies, waits for them, and re-layouts: 91.9 us -> 37.6 us
  waiting for transfers between devices: 164 us -> 119 us
  Pallas kernels: 131 us -> 162 us
  other arithmetic: 43.4 us -> 15.1 us
  between operations: 2.39 us -> 15 us
  blocking collectives: 103 us -> 112 us
    all_to_all x13 -> x4, starting transfers between devices: 70.8 us -> 18.4 us  [the longest x2 9.16 us: gather_sums(): lax.all_to_all(part, ALL, 0, 0, axis_index_groups=GROUPS_B)]
    all_to_all x0 -> x2, blocking collectives: none -> 51.4 us  [the longest x1 26.6 us: gather_sums(): lax.all_to_all(part, ALL, 0, 0, axis_index_groups=GROUPS_B)]
    all_to_all x4 -> x2, blocking collectives: 86.1 us -> 43.9 us  [copies(): return lax.all_to_all(many, ALL, 0, 0, axis_index_groups=groups)]
    all_to_all x13 -> x4, waiting for transfers between devices: 85.2 us -> 50 us  [the longest x2 27.7 us: gather_sums(): lax.all_to_all(part, ALL, 0, 0, axis_index_groups=GROUPS_B)]
    all_to_all x4 -> x1, waiting for transfers between devices: 56.2 us -> 22.6 us  [copies(): return lax.all_to_all(many, ALL, 0, 0, axis_index_groups=groups)]
    pallas_call x0 -> x3, Pallas kernels: none -> 23.1 us  [add_pairs(): pl.pallas_call(add_kernel, grid=(8,), out_shape=jax.ShapeDtypeStruct((64,...]
    convert_element_type x6 -> x0, other arithmetic: 22.9 us -> none  [body(): (both[0].astype(f32) + swap_core(both[1]).astype(f32)).astype(bf16)]
    squeeze x8 -> x0, local copies, waits for them, and re-layouts: 21.1 us -> none  [the longest x6 21.1 us: body(): both[1]]
  transfers between devices with their start and end apart: 36 -> 22, of which waited for: 21 -> 13; matrix products, arithmetic and copies ran while one was open for 15% -> 5% of each run, Pallas kernels for 15% -> 24%
where the time goes in v3:
time: 528 us; the launch traced here: 518 us
  Pallas kernels  162 us (31%)
  waiting for transfers between devices  119 us (23%)
  blocking collectives  112 us (21%)
  starting transfers between devices  56.9 us (11%)
  local copies, waits for them, and re-layouts  37.6 us (7%)
  other arithmetic  15.1 us (3%)
  between operations  15 us (3%)
    pallas_call x22, Pallas kernels, call(): pl.pallas_call(kernel, out_shape=[jax.ShapeDtypeStruct(*o) for o in outs]...  139 us
    all_to_all x2, blocking collectives, copies(): return lax.all_to_all(many, ALL, 0, 0, axis_index_groups=groups)  43.9 us
    all_to_all x2, waiting for transfers between devices, gather_sums(): lax.all_to_all(part, ALL, 0, 0, axis_index_groups=GROUPS_B)  27.7 us
    all_to_all x1, blocking collectives, gather_sums(): lax.all_to_all(part, ALL, 0, 0, axis_index_groups=GROUPS_B)  26.6 us
    all_to_all x1, blocking collectives, body(): sums = lax.all_to_all(sums, ALL, 0, 0, axis_index_groups=GROUPS_A)  24.8 us
    pallas_call x3, Pallas kernels, add_pairs(): pl.pallas_call(add_kernel, grid=(8,), out_shape=jax.ShapeDtypeStruct((64,...  23.1 us
    all_to_all x1, waiting for transfers between devices, copies(): return lax.all_to_all(many, ALL, 0, 0, axis_index_groups=groups)  22.6 us
    unnamed x76, local copies, waits for them, and re-layouts  20.3 us
  transfers between devices with their start and end apart: 22, of which 13 were waited for; matrix products, arithmetic and copies ran while one was open for 5% of the time, Pallas kernels for 24%

profile of v3, /device:TPU:0, one launch (start us, length us, event | category | flops | bytes accessed | tf_op | source)
XLA Modules:
  0.0 517.8 jit_solution(15833935187536545853)
XLA Ops:
  7.2 1.5 copy.72.wup
  8.7 1.5 copy.70.win
  10.3 1.3 copy.71.wout
  11.6 3.0 shard_map.239
  14.6 5.7 %all-to-all-start = ((bf16[8,81,8,128]{3,2,1,0:T(8,128)(2,1)}), bf16[8,81,8,128]{3,2,1,0:T(8,128)(2,1)S(1)}, u32[]{:S(2)}, u32[]{:S(2)}) async-start(bf16[8,81,8,128]{3,2,1,0:T(8,128)(2,1)} %shard_map.239), calls=%async_computation | async-start | bytes 2654208 | tf_op jit(solution)/shard_map/all_to_all | solution.py:655
  21.5 19.0 %all-to-all-done.got = bf16[8,81,8,128]{3,2,1,0:T(8,128)(2,1)S(1)} async-done(((bf16[8,81,8,128]{3,2,1,0:T(8,128)(2,1)}), bf16[8,81,8,128]{3,2,1,0:T(8,128)(2,1)S(1)}, u32[]{:S(2)}, u32[]{:S(2)}) %all-to-all-start) | async-done | bytes 1327136 | tf_op jit(solution)/shard_map/all_to_all | solution.py:655
  41.6 2.4 shard_map.240
  45.1 19.9 %all_to_all.85 = bf16[8,28,16,128]{3,2,1,0:T(8,128)(2,1)S(1)} all-to-all(bf16[8,28,16,128]{3,2,1,0:T(8,128)(2,1)S(1)} %broadcast_in_dim.22), channel_id=1, replica_groups={{0,6,17,23,96,102,113,119},{2,4,19,21,98,100,115,117},{1,7,16,22,97,103..., dimensions={0} | all-to-all | bytes 1835008 | tf_op jit(solution)/shard_map/all_to_all | solution.py:576
  66.3 24.1 %all_to_all.86 = bf16[8,8,10,16,128]{4,3,2,1,0:T(8,128)(2,1)S(1)} all-to-all(bf16[8,8,10,16,128]{4,3,2,1,0:T(8,128)(2,1)S(1)} %broadcast_in_dim.23), channel_id=1, replica_groups={{0,2,1,3,32,34,33,35},{6,4,7,5,38,36,39,37},{17,19,16,18,49,51,48,50},{..., dimensions={0} | all-to-all | bytes 5242880 | tf_op jit(solution)/shard_map/all_to_all | solution.py:576
  90.4 5.0 collective-permute-done.theirs.refs_1_
  95.4 4.1 shard_map.241
  102.2 5.0 shard_map.242
  107.3 5.1 all-to-all-start.3
  112.4 12.7 %all-to-all-done.3.heads = bf16[8,128,384]{2,1,0:T(8,128)(2,1)S(1)} async-done(((bf16[8,128,384]{2,1,0:T(8,128)(2,1)}), bf16[8,128,384]{2,1,0:T(8,128)(2,1)S(1)}, u32[]{:S(2)}, u32[]{:S(2)}) %all-to-all-start.3) | async-done | bytes 786464 | tf_op jit(solution)/shard_map/all_to_all | solution.py:689
  125.1 2.9 broadcast_in_dim.26
  128.0 4.8 all-to-all-start.4
  135.1 7.0 %shard_map.243 = bf16[8,128,128]{2,1,0:T(8,128)(2,1)} custom-call(s32[1]{0:T(128)} %bitcast.2.par_ref, bf16[8,128,384]{2,1,0:T(8,128)(2,1)} %copy-done.1, s32[8,128,1]{2,1,0:T(8,128)} %subtract_select_fusion.idc, s32[1,1024]{1,0:T(1,128)} %reshape_select_fusion.idr), custom_call_target="tpu_custom_call" | custom-call | bytes 25830000 | tf_op jit(solution)/shard_map/pallas_call | solution.py:551
  142.1 22.6 %all-to-all-done.4 = bf16[8,8,18,16,128]{4,3,2,1,0:T(8,128)(2,1)} async-done(((bf16[8,8,18,16,128]{4,3,2,1,0:T(8,128)(2,1)}), bf16[8,8,18,16,128]{4,3,2,1,0:T(8,128)(2,1)}, u32[]{:S(2)}, u32[]{:S(2)}) %all-to-all-start.4) | async-done | bytes 4718624 | tf_op jit(solution)/shard_map/all_to_all | solution.py:576
  165.8 6.3 %all-to-all-start.5 = ((bf16[8,128,128]{2,1,0:T(8,128)(2,1)}), bf16[8,128,128]{2,1,0:T(8,128)(2,1)S(1)}, u32[]{:S(2)}, u32[]{:S(2)}) async-start(bf16[8,128,128]{2,1,0:T(8,128)(2,1)} %shard_map.243), calls=%async_computation.5 | async-start | bytes 524288 | tf_op jit(solution)/shard_map/all_to_all | solution.py:702
  174.6 5.1 all-to-all-done.5.back
  180.3 8.2 %shard_map.244 = (bf16[128,768]{1,0:T(8,128)(2,1)}, f32[128,768]{1,0:T(8,128)}, bf16[128,768]{1,0:T(8,128)(2,1)}, f32[128,3072]{1,0:T(8,128)}, f32[128,768]{1,0:T(8,128)}) custom-call(s32[1]{0:T(128)} %bitcast.core_ref.core, bf16[128,768]{1,0:T(8,128)(2,1)} %bitcast.70, bf16[8,128,128]{2,1,0:T(8,128)(2,1)} %copy-done.10, f32[4,768]{1,0:T(4,128)} %pad_maximum_fusion.2.vec, ...), custom_call_target="tpu_custom_call" | custom-call | bytes 29520000 | tf_op jit(solution)/shard_map/pallas_call | solution.py:551
  188.6 5.0 shard_map.245
  193.6 16.8 %all_to_all.87.heads = bf16[8,128,384]{2,1,0:T(8,128)(2,1)} all-to-all(bf16[8,128,384]{2,1,0:T(8,128)(2,1)} %get-tuple-element.88), channel_id=1, replica_groups=mesh['y'=4,'zh'=2,'c'=2,'x'=4,'zl'=2] {'x','zl'}, dimensions={0} | all-to-all | bytes 1572864 | tf_op jit(solution)/shard_map/all_to_all | solution.py:689
  210.4 7.0 %shard_map.246 = bf16[8,128,128]{2,1,0:T(8,128)(2,1)} custom-call(s32[1]{0:T(128)} %bitcast.2.par_ref, bf16[8,128,384]{2,1,0:T(8,128)(2,1)} %all_to_all.87.heads, s32[8,128,1]{2,1,0:T(8,128)} %subtract_select_fusion.idc, s32[1,1024]{1,0:T(1,128)} %reshape_select_fusion.idr), custom_call_target="tpu_custom_call" | custom-call | bytes 25830000 | tf_op jit(solution)/shard_map/pallas_call | solution.py:551
  217.4 3.7 all-to-all-start.7
  222.9 5.0 all-to-all-done.7.back
  228.6 7.6 %shard_map.247 = (bf16[128,768]{1,0:T(8,128)(2,1)}, f32[128,768]{1,0:T(8,128)}, bf16[128,768]{1,0:T(8,128)(2,1)}, f32[128,3072]{1,0:T(8,128)}, bf16[128,768]{1,0:T(8,128)(2,1)}) custom-call(s32[1]{0:T(128)} %bitcast.core_ref.core, f32[128,768]{1,0:T(8,128)} %get-tuple-element.87.h_ref, bf16[8,128,128]{2,1,0:T(8,128)(2,1)} %copy-done.11, ...), custom_call_target="tpu_custom_call" | custom-call | bytes 29520000 | tf_op jit(solution)/shard_map/pallas_call | solution.py:551
  236.2 9.5 %shard_map.248 = (bf16[128,3072]{1,0:T(8,128)(2,1)}, bf16[128,3072]{1,0:T(8,128)(2,1)}, f32[128,768]{1,0:T(8,128)}, bf16[8,128,128]{2,1,0:T(8,128)(2,1)}, f32[4,768]{1,0:T(4,128)}, /*index=5*/f32[1,3072]{1,0:T(1,128)}) custom-call(s32[1]{0:T(128)} %bitcast.core_ref.core, bf16[128,768]{1,0:T(8,128)(2,1)} %bitcast.75, f32[128,3072]{1,0:T(8,128)} %get-tuple-element.94.u_ref, ...), custom_call_target="tpu_custom_call" | custom-call | bytes 36900000 | tf_op jit(solution)/shard_map/pallas_call | solution.py:551
  245.8 5.1 shard_map.251
  250.9 3.4 all-to-all-start.8
  254.9 4.8 shard_map.249
  259.7 2.3 all-to-all-done.8.cot
  262.6 10.1 %shard_map.250 = bf16[8,128,384]{2,1,0:T(8,128)(2,1)} custom-call(s32[1]{0:T(128)} %bitcast.2.par_ref, bf16[8,128,384]{2,1,0:T(8,128)(2,1)} %all_to_all.87.heads, bf16[8,128,128]{2,1,0:T(8,128)(2,1)} %copy-done.13, s32[8,128,1]{2,1,0:T(8,128)} %subtract_select_fusion.idc, s32[1,1024]{1,0:T(1,128)} %reshape_select_fusion.idr), custom_call_target="tpu_custom_call" | custom-call | bytes 36900000 | tf_op jit(solution)/shard_map/pallas_call | solution.py:551
  272.7 3.6 all-to-all-start.9
  276.3 1.4 copy-done.7
  277.7 6.5 %shard_map.252 = bf16[64,9,16,128]{3,2,1,0:T(8,128)(2,1)} custom-call(bf16[64,9,16,128]{3,2,1,0:T(8,128)(2,1)} %get-tuple-element.101.refs_0_, bf16[64,9,16,128]{3,2,1,0:T(8,128)(2,1)} %copy-done.7), custom_call_target="tpu_custom_call" | custom-call | flops 4194304 | bytes 7077888 | tf_op jit(solution)/shard_map/pallas_call | solution.py:611
  284.2 4.6 all-to-all-done.9.back
  289.7 4.3 all-to-all-start.10
  294.0 6.2 %shard_map.253 = (bf16[128,2304]{1,0:T(8,128)(2,1)}, f32[128,768]{1,0:T(8,128)}, f32[4,768]{1,0:T(4,128)}) custom-call(s32[1]{0:T(128)} %bitcast.core_ref.core, bf16[8,128,384]{2,1,0:T(8,128)(2,1)} %copy-done.4, f32[128,768]{1,0:T(8,128)} %get-tuple-element.104.e1_ref, f32[128,768]{1,0:T(8,128)} %get-tuple-element.87.h_ref, f32[1,768]{1,0:T(1,128)} %copy-done.17, ...), custom_call_target="tpu_custom_call" | custom-call | bytes 22140000 | tf_op jit(solution)/shard_map/pallas_call | solution.py:551
  300.2 10.8 %shard_map.254 = (bf16[128,3072]{1,0:T(8,128)(2,1)}, bf16[128,3072]{1,0:T(8,128)(2,1)}, f32[128,768]{1,0:T(8,128)}, bf16[8,128,128]{2,1,0:T(8,128)(2,1)}, f32[4,768]{1,0:T(4,128)}, /*index=5*/f32[1,3072]{1,0:T(1,128)}) custom-call(s32[1]{0:T(128)} %bitcast.core_ref.core, f32[128,768]{1,0:T(8,128)} %get-tuple-element.105.e_ref, ...), custom_call_target="tpu_custom_call" | custom-call | bytes 36900000 | tf_op jit(solution)/shard_map/pallas_call | solution.py:551
  311.0 5.8 %all-to-all-done.10 = bf16[8,8,9,16,128]{4,3,2,1,0:T(8,128)(2,1)S(1)} async-done(((bf16[8,8,9,16,128]{4,3,2,1,0:T(8,128)(2,1)}), bf16[8,8,9,16,128]{4,3,2,1,0:T(8,128)(2,1)S(1)}, u32[]{:S(2)}, u32[]{:S(2)}) %all-to-all-start.10) | async-done | bytes 2359328 | tf_op jit(solution)/shard_map/all_to_all | solution.py:628
  317.8 4.3 all-to-all-start.11
  322.2 8.4 %shard_map.255 = (bf16[64,18,16,128]{3,2,1,0:T(8,128)(2,1)}, bf16[64,18,16,128]{3,2,1,0:T(8,128)(2,1)}) custom-call(s32[1]{0:T(128)} %bitcast.core_ref.core, bf16[128,3072]{1,0:T(8,128)(2,1)} %get-tuple-element.112.f_ref, f32[128,768]{1,0:T(8,128)} %get-tuple-element.105.e_ref, bf16[128,768]{1,0:T(8,128)(2,1)} %get-tuple-element.113.a2_ref, ...), custom_call_target="tpu_custom_call" | custom-call | bytes 33210000 | tf_op jit(solution)/shard_map/pallas_call | solution.py:551
  330.7 5.2 %shard_map.257 = (bf16[64,9,16,128]{3,2,1,0:T(8,128)(2,1)}, bf16[64,9,16,128]{3,2,1,0:T(8,128)(2,1)}) custom-call(s32[1]{0:T(128)} %bitcast.core_ref.core, bf16[128,768]{1,0:T(8,128)(2,1)} %get-tuple-element.121.a_ref, bf16[128,2304]{1,0:T(8,128)(2,1)} %get-tuple-element.123.g_ref, bf16[128,768]{1,0:T(8,128)(2,1)} %get-tuple-element.124.o_ref, ...), custom_call_target="tpu_custom_call" | custom-call | bytes 18450000 | tf_op jit(solution)/shard_map/pallas_call | solution.py:551
  336.7 10.1 %shard_map.256 = bf16[8,128,384]{2,1,0:T(8,128)(2,1)} custom-call(s32[1]{0:T(128)} %bitcast.2.par_ref, bf16[8,128,384]{2,1,0:T(8,128)(2,1)} %copy-done.1, bf16[8,128,128]{2,1,0:T(8,128)(2,1)} %copy-done.12, s32[8,128,1]{2,1,0:T(8,128)} %subtract_select_fusion.idc, s32[1,1024]{1,0:T(1,128)} %reshape_select_fusion.idr), custom_call_target="tpu_custom_call" | custom-call | bytes 36900000 | tf_op jit(solution)/shard_map/pallas_call | solution.py:551
  346.8 10.0 %reduce-scatter.2.cloned.1.call-done = bf16[1,72,16,128]{3,2,1,0:T(8,128)(2,1)} async-done(((bf16[16,72,16,128]{3,2,1,0:T(8,128)(2,1)}), bf16[1,72,16,128]{3,2,1,0:T(8,128)(2,1)}) %reduce-scatter.2.cloned.1.call-update) | async-done | bytes 294928 | tf_op jit(solution)/shard_map/reduce_scatter | solution.py:753
  356.8 4.3 all-to-all-start.12
  361.1 1.4 copy-done.9
  362.5 10.1 %shard_map.258 = bf16[64,27,16,128]{3,2,1,0:T(8,128)(2,1)} custom-call(bf16[64,18,16,128]{3,2,1,0:T(8,128)(2,1)} %get-tuple-element.115.refs_0_, bf16[64,18,16,128]{3,2,1,0:T(8,128)(2,1)} %collective-permute-done.3.refs_1_, bf16[64,9,16,128]{3,2,1,0:T(8,128)(2,1)} %get-tuple-element.125.refs_2_, bf16[64,9,16,128]{3,2,1,0:T(8,128)(2,1)} %copy-done.9), custom_call_target="tpu_custom_call" | custom-call | flops 4194304 | bytes 21233664 | tf_op jit(solution)/shard_map/pallas_call | solution.py:611
  373.4 4.9 all-to-all-start.13
  378.4 6.0 %shard_map.259 = (bf16[128,2304]{1,0:T(8,128)(2,1)}, f32[128,768]{1,0:T(8,128)}, f32[4,768]{1,0:T(4,128)}) custom-call(s32[1]{0:T(128)} %bitcast.core_ref.core, bf16[8,128,384]{2,1,0:T(8,128)(2,1)} %copy-done.5, f32[128,768]{1,0:T(8,128)} %get-tuple-element.128.e1_ref, bf16[128,768]{1,0:T(8,128)(2,1)} %bitcast.71, f32[1,768]{1,0:T(1,128)} %copy-done.18, ...), custom_call_target="tpu_custom_call" | custom-call | bytes 22140000 | tf_op jit(solution)/shard_map/pallas_call | solution.py:551
  384.4 5.1 shard_map.260
  397.8 6.5 %shard_map.261 = bf16[64,10,16,128]{3,2,1,0:T(8,128)(2,1)} custom-call(bf16[64,9,16,128]{3,2,1,0:T(8,128)(2,1)} %get-tuple-element.132.refs_0_, bf16[64,9,16,128]{3,2,1,0:T(8,128)(2,1)} %copy-done.8, bf16[64,1,16,128]{3,2,1,0:T(8,128)(2,1)} %get-tuple-element.194.refs_2_, bf16[64,1,16,128]{3,2,1,0:T(8,128)(2,1)} %copy-done.14), custom_call_target="tpu_custom_call" | custom-call | flops 4194304 | bytes 7864320 | tf_op jit(solution)/shard_map/pallas_call | solution.py:611
  404.3 21.9 %all-to-all-done.13 = bf16[8,8,27,16,128]{4,3,2,1,0:T(8,128)(2,1)} async-done(((bf16[8,8,27,16,128]{4,3,2,1,0:T(8,128)(2,1)}), bf16[8,8,27,16,128]{4,3,2,1,0:T(8,128)(2,1)}, u32[]{:S(2)}, u32[]{:S(2)}) %all-to-all-start.13) | async-done | bytes 7077920 | tf_op jit(solution)/shard_map/all_to_all | solution.py:628
  426.3 4.2 reduce_sum.47
  430.5 26.6 %all_to_all.88 = bf16[8,8,10,16,128]{4,3,2,1,0:T(8,128)(2,1)S(1)} all-to-all(bf16[8,8,10,16,128]{4,3,2,1,0:T(8,128)(2,1)} %bitcast.67), channel_id=1, replica_groups={{0,2,1,3,32,34,33,35},{6,4,7,5,38,36,39,37},{17,19,16,18,49,51,48,50},{..., dimensions={0} | all-to-all | bytes 5242880 | tf_op jit(solution)/shard_map/all_to_all | solution.py:628
  459.5 24.8 %all_to_all.89.parts = bf16[8,46,16,128]{3,2,1,0:T(8,128)(2,1)} all-to-all(bf16[8,46,16,128]{3,2,1,0:T(8,128)(2,1)S(1)} %pad_maximum_fusion), channel_id=1, replica_groups={{0,6,17,23,96,102,113,119},{2,4,19,21,98,100,115,117},{1,7,16,22,97,103..., dimensions={0} | all-to-all | bytes 3014656 | tf_op jit(solution)/shard_map/all_to_all | solution.py:794
  484.3 2.6 shard_map.262
  486.9 3.5 all-to-all-start.16
  495.9 3.3 all-to-all-done.16.got
  500.1 6.0 %shard_map.263 = (f32[2,6,2304]{2,1,0:T(8,128)}, f32[2,6,768]{2,1,0:T(8,128)}, f32[2,6,3072]{2,1,0:T(8,128)}, f32[2,24,768]{2,1,0:T(8,128)}) custom-call(bf16[8,39,8,128]{3,2,1,0:T(8,128)(2,1)} %copy-done.6, bf16[384,384]{1,0:T(8,128)(2,1)} %constant.45.clone.order), custom_call_target="tpu_custom_call" | custom-call | bytes 11070000 | tf_op jit(solution)/shard_map/pallas_call | solution.py:551
  506.1 1.7 copy.86
  507.8 1.6 copy.84
  509.4 1.4 copy.85
  (176 shorter events, 38.2 us)
Async XLA Ops:
  8.7 11.7 %copy-start.27 = (bf16[2,2,6]{2,1,0:T(2,128)(2,1)S(1)}, bf16[2,2,6]{2,1,0:T(2,128)(2,1)}, u32[]{:S(2)}) copy-start(bf16[2,2,6]{2,1,0:T(2,128)(2,1)} %param.21) | copy-start | bytes 148
  8.7 11.8 %copy-start.28 = (bf16[2,2,6]{2,1,0:T(2,128)(2,1)S(1)}, bf16[2,2,6]{2,1,0:T(2,128)(2,1)}, u32[]{:S(2)}) copy-start(bf16[2,2,6]{2,1,0:T(2,128)(2,1)} %param.22) | copy-start | bytes 148
  8.7 11.8 %copy-start.29 = (bf16[2,2,6]{2,1,0:T(2,128)(2,1)S(1)}, bf16[2,2,6]{2,1,0:T(2,128)(2,1)}, u32[]{:S(2)}) copy-start(bf16[2,2,6]{2,1,0:T(2,128)(2,1)} %param.24) | copy-start | bytes 148
  8.7 11.9 %copy-start.30 = (bf16[2,2,6]{2,1,0:T(2,128)(2,1)S(1)}, bf16[2,2,6]{2,1,0:T(2,128)(2,1)}, u32[]{:S(2)}) copy-start(bf16[2,2,6]{2,1,0:T(2,128)(2,1)} %param.26) | copy-start | bytes 148
  8.7 12.0 %copy-start.31 = (bf16[2,24]{1,0:T(2,128)(2,1)S(1)}, bf16[2,24]{1,0:T(2,128)(2,1)}, u32[]{:S(2)}) copy-start(bf16[2,24]{1,0:T(2,128)(2,1)} %param.28) | copy-start | bytes 292
  14.6 25.9 %all-to-all-start = ((bf16[8,81,8,128]{3,2,1,0:T(8,128)(2,1)}), bf16[8,81,8,128]{3,2,1,0:T(8,128)(2,1)S(1)}, u32[]{:S(2)}, u32[]{:S(2)}) async-start(bf16[8,81,8,128]{3,2,1,0:T(8,128)(2,1)} %shard_map.239), calls=%async_computation | async-start | bytes 2654208 | tf_op jit(solution)/shard_map/all_to_all | solution.py:655
  20.3 104.8 %all-gather.5.cloned.1.call-start = ((), (), s32[]{:S(2)}) async-start(), calls=%async_computation.19 | async-start | bytes 5013504 | tf_op jit(solution)/shard_map/all_gather | solution.py:660
  40.5 1.1 copy-start.2
  44.0 173.4 %all-gather.7.cloned.1.call-start = ((), (), s32[]{:S(2)}) async-start(), calls=%async_computation.20 | async-start | bytes 10027008 | tf_op jit(solution)/shard_map/all_gather | solution.py:687
  64.9 0.9 copy-start.3
  90.4 5.0 copy-start
  90.4 5.0 collective-permute-start
  100.6 6.6 %copy-start.18 = (f32[1,768]{1,0:T(1,128)}, f32[1,768]{1,0:T(1,128)S(1)}, u32[]{:S(2)}) copy-start(f32[1,768]{1,0:T(1,128)S(1)} %get-tuple-element.202.vec) | copy-start | bytes 9220
  100.6 72.7 %copy-start.19 = (f32[1,768]{1,0:T(1,128)}, f32[1,768]{1,0:T(1,128)S(1)}, u32[]{:S(2)}) copy-start(f32[1,768]{1,0:T(1,128)S(1)} %get-tuple-element.200.vec) | copy-start | bytes 9220
  100.7 73.3 %copy-start.17 = (f32[1,768]{1,0:T(1,128)}, f32[1,768]{1,0:T(1,128)S(1)}, u32[]{:S(2)}) copy-start(f32[1,768]{1,0:T(1,128)S(1)} %get-tuple-element.198.vec) | copy-start | bytes 9220
  100.7 121.6 %copy-start.16 = (f32[1,768]{1,0:T(1,128)}, f32[1,768]{1,0:T(1,128)S(1)}, u32[]{:S(2)}) copy-start(f32[1,768]{1,0:T(1,128)S(1)} %get-tuple-element.195.vec) | copy-start | bytes 9220
  107.3 17.8 %slice-start = ((bf16[8,28,16,128]{3,2,1,0:T(8,128)(2,1)}), bf16[8,18,16,128]{3,2,1,0:T(8,128)(2,1)S(1)}, s32[]{:S(2)}) async-start(bf16[8,28,16,128]{3,2,1,0:T(8,128)(2,1)} %copy-done.3), calls=%async_computation.21 | async-start | bytes 1179648 | tf_op jit(solution)/shard_map/slice | solution.py:662
  107.3 17.8 %all-to-all-start.3 = ((bf16[8,128,384]{2,1,0:T(8,128)(2,1)}), bf16[8,128,384]{2,1,0:T(8,128)(2,1)S(1)}, u32[]{:S(2)}, u32[]{:S(2)}) async-start(bf16[8,128,384]{2,1,0:T(8,128)(2,1)} %get-tuple-element.81), calls=%async_computation.3 | async-start | bytes 1572864 | tf_op jit(solution)/shard_map/all_to_all | solution.py:689
  125.1 2.9 copy-start.1
  128.0 4.8 copy-start.26
  128.0 4.8 copy-start.32
  128.0 4.8 copy-start.33
  128.0 36.6 %all-to-all-start.4 = ((bf16[8,8,18,16,128]{4,3,2,1,0:T(8,128)(2,1)}), bf16[8,8,18,16,128]{4,3,2,1,0:T(8,128)(2,1)}, u32[]{:S(2)}, u32[]{:S(2)}) async-start(bf16[8,8,18,16,128]{4,3,2,1,0:T(8,128)(2,1)} %broadcast_in_dim.26), calls=%async_computation.4 | async-start | bytes 9437184 | tf_op jit(solution)/shard_map/all_to_all | solution.py:576
  132.8 32.6 %copy-start.15 = (f32[128,256]{1,0:T(8,128)S(1)}, f32[128,256]{1,0:T(8,128)}, u32[]{:S(2)}) copy-start(f32[128,256]{1,0:T(8,128)} %get-tuple-element.85) | copy-start | bytes 393220
  164.6 15.0 %collective-permute-start.1 = (bf16[64,18,16,128]{3,2,1,0:T(8,128)(2,1)}, bf16[64,18,16,128]{3,2,1,0:T(8,128)(2,1)}, u32[]{:S(2)}, u32[]{:S(2)}) collective-permute-start(bf16[64,18,16,128]{3,2,1,0:T(8,128)(2,1)} %bitcast.9.refs_2_.refs_0_), channel_id=1, source_target_pairs={{0,8},{8,0},{1,9},{9,1},{2,10},{10,2},{3,11},{11,3},{4,12},{12,4},... | collective-permute-start | bytes 14155784 | tf_op jit(solution)/shard_map/ppermute | solution.py:584
  165.8 13.9 %all-to-all-start.5 = ((bf16[8,128,128]{2,1,0:T(8,128)(2,1)}), bf16[8,128,128]{2,1,0:T(8,128)(2,1)S(1)}, u32[]{:S(2)}, u32[]{:S(2)}) async-start(bf16[8,128,128]{2,1,0:T(8,128)(2,1)} %shard_map.243), calls=%async_computation.5 | async-start | bytes 524288 | tf_op jit(solution)/shard_map/all_to_all | solution.py:702
  179.6 0.7 copy-start.10
  217.4 10.5 %all-to-all-start.7 = ((bf16[8,128,128]{2,1,0:T(8,128)(2,1)}), bf16[8,128,128]{2,1,0:T(8,128)(2,1)S(1)}, u32[]{:S(2)}, u32[]{:S(2)}) async-start(bf16[8,128,128]{2,1,0:T(8,128)(2,1)} %shard_map.246), calls=%async_computation.7 | async-start | bytes 524288 | tf_op jit(solution)/shard_map/all_to_all | solution.py:702
  227.9 0.7 copy-start.11
  250.8 25.4 %collective-permute-start.2 = (bf16[64,9,16,128]{3,2,1,0:T(8,128)(2,1)}, bf16[64,9,16,128]{3,2,1,0:T(8,128)(2,1)S(1)}, u32[]{:S(2)}, u32[]{:S(2)}) collective-permute-start(bf16[64,9,16,128]{3,2,1,0:T(8,128)(2,1)} %get-tuple-element.102), channel_id=1, source_target_pairs={{0,8},{8,0},{1,9},{9,1},{2,10},{10,2},{3,11},{11,3},{4,12},{12,4},... | collective-permute-start | bytes 7077896 | tf_op jit(solution)/shard_map/ppermute | solution.py:584
  250.9 11.0 %all-to-all-start.8 = ((bf16[8,128,128]{2,1,0:T(8,128)(2,1)}), bf16[8,128,128]{2,1,0:T(8,128)(2,1)S(1)}, u32[]{:S(2)}, u32[]{:S(2)}) async-start(bf16[8,128,128]{2,1,0:T(8,128)(2,1)} %get-tuple-element.96), calls=%async_computation.8 | async-start | bytes 524288 | tf_op jit(solution)/shard_map/all_to_all | solution.py:735
  254.4 102.4 %reduce-scatter.2.cloned.1.call-start = ((), (), s32[]{:S(2)}) async-start(), calls=%async_computation.18 | async-start | bytes 5013504 | tf_op jit(solution)/shard_map/reduce_scatter | solution.py:753
  261.9 0.7 copy-start.13
  272.7 16.1 %all-to-all-start.9 = ((bf16[8,128,384]{2,1,0:T(8,128)(2,1)}), bf16[8,128,384]{2,1,0:T(8,128)(2,1)S(1)}, u32[]{:S(2)}, u32[]{:S(2)}) async-start(bf16[8,128,384]{2,1,0:T(8,128)(2,1)} %shard_map.250), calls=%async_computation.9 | async-start | bytes 1572864 | tf_op jit(solution)/shard_map/all_to_all | solution.py:763
  276.3 1.4 copy-start.7
  288.8 0.9 copy-start.4
  289.7 27.0 %all-to-all-start.10 = ((bf16[8,8,9,16,128]{4,3,2,1,0:T(8,128)(2,1)}), bf16[8,8,9,16,128]{4,3,2,1,0:T(8,128)(2,1)S(1)}, u32[]{:S(2)}, u32[]{:S(2)}) async-start(bf16[8,8,9,16,128]{4,3,2,1,0:T(8,128)(2,1)} %bitcast.68), calls=%async_computation.10 | async-start | bytes 4718592 | tf_op jit(solution)/shard_map/all_to_all | solution.py:628
  317.8 12.7 %all-to-all-start.11 = ((bf16[8,128,128]{2,1,0:T(8,128)(2,1)}), bf16[8,128,128]{2,1,0:T(8,128)(2,1)S(1)}, u32[]{:S(2)}, u32[]{:S(2)}) async-start(bf16[8,128,128]{2,1,0:T(8,128)(2,1)} %get-tuple-element.110), calls=%async_computation.11 | async-start | bytes 524288 | tf_op jit(solution)/shard_map/all_to_all | solution.py:735
  330.6 6.1 %copy-start.12 = (bf16[8,128,128]{2,1,0:T(8,128)(2,1)}, bf16[8,128,128]{2,1,0:T(8,128)(2,1)S(1)}, u32[]{:S(2)}) copy-start(bf16[8,128,128]{2,1,0:T(8,128)(2,1)S(1)} %all-to-all-done.11.cot) | copy-start | bytes 786436
  330.6 30.5 %collective-permute-start.3 = (bf16[64,18,16,128]{3,2,1,0:T(8,128)(2,1)}, bf16[64,18,16,128]{3,2,1,0:T(8,128)(2,1)}, u32[]{:S(2)}, u32[]{:S(2)}) collective-permute-start(bf16[64,18,16,128]{3,2,1,0:T(8,128)(2,1)} %get-tuple-element.120), channel_id=1, source_target_pairs={{0,8},{8,0},{1,9},{9,1},{2,10},{10,2},{3,11},{11,3},{4,12},{12,4},... | collective-permute-start | bytes 14155784 | tf_op jit(solution)/shard_map/ppermute | solution.py:584
  335.9 25.2 %collective-permute-start.4 = (bf16[64,9,16,128]{3,2,1,0:T(8,128)(2,1)}, bf16[64,9,16,128]{3,2,1,0:T(8,128)(2,1)S(1)}, u32[]{:S(2)}, u32[]{:S(2)}) collective-permute-start(bf16[64,9,16,128]{3,2,1,0:T(8,128)(2,1)} %get-tuple-element.126), channel_id=1, source_target_pairs={{0,8},{8,0},{1,9},{9,1},{2,10},{10,2},{3,11},{11,3},{4,12},{12,4},... | collective-permute-start | bytes 7077896 | tf_op jit(solution)/shard_map/ppermute | solution.py:584
  356.8 15.8 %all-to-all-start.12 = ((bf16[8,128,384]{2,1,0:T(8,128)(2,1)}), bf16[8,128,384]{2,1,0:T(8,128)(2,1)S(1)}, u32[]{:S(2)}, u32[]{:S(2)}) async-start(bf16[8,128,384]{2,1,0:T(8,128)(2,1)} %shard_map.256), calls=%async_computation.13 | async-start | bytes 1572864 | tf_op jit(solution)/shard_map/all_to_all | solution.py:763
  361.1 1.4 copy-start.9
  372.6 0.9 copy-start.5
  373.4 52.8 %all-to-all-start.13 = ((bf16[8,8,27,16,128]{4,3,2,1,0:T(8,128)(2,1)}), bf16[8,8,27,16,128]{4,3,2,1,0:T(8,128)(2,1)}, u32[]{:S(2)}, u32[]{:S(2)}) async-start(bf16[8,8,27,16,128]{4,3,2,1,0:T(8,128)(2,1)} %bitcast.64), calls=%async_computation.14 | async-start | bytes 14155776 | tf_op jit(solution)/shard_map/all_to_all | solution.py:628
  378.3 11.6 %copy-start.21 = (f32[4,768]{1,0:T(4,128)S(1)}, f32[4,768]{1,0:T(4,128)}, u32[]{:S(2)}) copy-start(f32[4,768]{1,0:T(4,128)} %get-tuple-element.137) | copy-start | bytes 36868
  378.4 11.6 %copy-start.20 = (f32[1,3072]{1,0:T(1,128)S(1)}, f32[1,3072]{1,0:T(1,128)}, u32[]{:S(2)}) copy-start(f32[1,3072]{1,0:T(1,128)} %get-tuple-element.139) | copy-start | bytes 36868
  378.4 12.5 %copy-start.24 = (f32[4,768]{1,0:T(4,128)S(1)}, f32[4,768]{1,0:T(4,128)}, u32[]{:S(2)}) copy-start(f32[4,768]{1,0:T(4,128)} %get-tuple-element.135) | copy-start | bytes 36868
  378.4 12.6 %copy-start.23 = (f32[4,768]{1,0:T(4,128)S(1)}, f32[4,768]{1,0:T(4,128)}, u32[]{:S(2)}) copy-start(f32[4,768]{1,0:T(4,128)} %get-tuple-element.136) | copy-start | bytes 36868
  384.4 7.4 %copy-start.22 = (f32[1,3072]{1,0:T(1,128)S(1)}, f32[1,3072]{1,0:T(1,128)}, u32[]{:S(2)}) copy-start(f32[1,3072]{1,0:T(1,128)} %get-tuple-element.138) | copy-start | bytes 36868
  384.4 8.3 %copy-start.25 = (f32[4,768]{1,0:T(4,128)S(1)}, f32[4,768]{1,0:T(4,128)}, u32[]{:S(2)}) copy-start(f32[4,768]{1,0:T(4,128)} %get-tuple-element.134) | copy-start | bytes 36868
  384.4 9.1 %copy-start.34 = (bf16[128,128]{1,0:T(8,128)(2,1)S(1)}, bf16[128,128]{1,0:T(8,128)(2,1)}, u32[]{:S(2)}) copy-start(bf16[128,128]{1,0:T(8,128)(2,1)} %constant.46.clone) | copy-start | bytes 98308
  389.6 6.7 %collective-permute-start.5 = (bf16[64,9,16,128]{3,2,1,0:T(8,128)(2,1)}, bf16[64,9,16,128]{3,2,1,0:T(8,128)(2,1)S(1)}, u32[]{:S(2)}, u32[]{:S(2)}) collective-permute-start(bf16[64,9,16,128]{3,2,1,0:T(8,128)(2,1)} %get-tuple-element.133), channel_id=1, source_target_pairs={{0,8},{8,0},{1,9},{9,1},{2,10},{10,2},{3,11},{11,3},{4,12},{12,4},... | collective-permute-start | bytes 7077896 | tf_op jit(solution)/shard_map/ppermute | solution.py:584
  394.7 1.6 collective-permute-start.6
  396.3 0.7 copy-start.14
  396.3 1.5 copy-start.8
  486.9 12.3 %all-to-all-start.16 = ((bf16[8,39,8,128]{3,2,1,0:T(8,128)(2,1)}), bf16[8,39,8,128]{3,2,1,0:T(8,128)(2,1)S(1)}, u32[]{:S(2)}, u32[]{:S(2)}) async-start(bf16[8,39,8,128]{3,2,1,0:T(8,128)(2,1)} %get-tuple-element.142), calls=%async_computation.17 | async-start | bytes 1277952 | tf_op jit(solution)/shard_map/all_to_all | solution.py:797
  499.2 0.9 copy-start.6
Sparse Core Ops, SparseCore 0:
  44.1 64.4 all-gather.4
  111.0 100.1 all-gather.6
  262.1 94.6 reduce-scatter.1

commit v4 on v3

--- a/solution.py
+++ b/solution.py
@@ -414,62 +414,66 @@
     ship(((stage.at[0], keep), (stage.at[1], send)), sem)
 
 
-def grad_down_plain(f_ref, e_ref, out, stage, sem):
-    tall_grad(f_ref[...].T, low(e_ref), lambda u, rows: plain_store(stage, u, rows))
+def grad_mlp_plain(f_ref, e_ref, a2_ref, du_ref, out, stage, sem):
+    wide_grad(a2_ref[...].T, du_ref[...], 0, lambda u, rows: plain_store(stage, u, rows))
+    tall_grad(f_ref[...].T, low(e_ref), lambda u, rows: plain_store(stage, 24 + u, rows))
     ship(((stage, out),), sem)
 
 
-def grad_up_cube(core_ref, a2_ref, du_ref, keep, send, stage, sem):
-    core = core_ref[0]
-    wide_grad(a2_ref[...].T, du_ref[...], 0, lambda u, rows: cube_store(core, stage, 0, u // 3, u % 3, rows))
-    ship(((stage.at[0], keep), (stage.at[1], send)), sem)
-
-
 CUBE_IN, PLAIN_IN = ((0, 0), (0, 1), (1, 0)), ((0, 2), (1, 1), (1, 2))
-CUBE_OUT = ((0, 0), (0, 1), (0, 2), (1, 0), (1, 1))
+CUBE_OUT, PLAIN_OUT = ((0, 0), (1, 0), (0, 1), (0, 2)), ((1, 1), (1, 2))
+
+
+def dense(pieces, tiles):
+    left = 16 * tiles - 6 * len(pieces)
+    rows = jnp.concatenate(pieces + ([jnp.zeros((left, 128), f32)] if left else []), axis=0)
+    return rows.astype(bf16).reshape(tiles, 16, 128)
 
 
 def pack_kernel(win, wout, wup, wdown, order, pay):
+    ins = [win[...].astype(f32), wout[...].astype(f32)]
+    wide = wup[...].astype(f32)
     ups = []
     for l in range(LAYERS):
-        up = [mul(wup[l, :, 384 * m : 384 * m + 384], order[...]) for m in range(8)]
-        ups.append(jnp.concatenate(up, axis=1).astype(bf16))
+        rows = wide[:, l].astype(bf16)
+        ups.append([mul(rows[:, 384 * m : 384 * m + 384], order[...]) for m in range(8)])
+    firsts = [[v[:, l] for v in ins] for l in range(LAYERS)]
+    downs = [wdown[l].astype(f32) for l in range(LAYERS)]
 
     def get(l, group, u):
         if group == 0:
-            return win[l, :, 128 * u : 128 * u + 128] if u < 18 else wout[l, :, 128 * (u - 18) : 128 * (u - 17)]
+            wide, at = (firsts[l][0], u) if u < 18 else (firsts[l][1], u - 18)
+            return wide[:, 128 * at : 128 * at + 128]
         if group == 1:
-            return ups[l][:, 128 * u : 128 * u + 128]
+            return ups[l][u // 3][:, 128 * (u % 3) : 128 * (u % 3) + 128]
         cb, q = divmod(u, 4)
-        return wdown[l, 6 * q : 6 * q + 6, 128 * cb : 128 * cb + 128]
-
+        return downs[l][6 * q : 6 * q + 6, 128 * cb : 128 * cb + 128]
+
+    plain = dense([get(*key, u) for key in PLAIN_IN for u in range(24)], 27)
+    for d in range(8):
+        pay[d, 0:27] = plain
+        pay[d, 27:31] = dense([get(*key, 3 * d + i) for key in CUBE_IN for i in range(3)], 4)
+
+
+def regroup_kernel(got, smalls, first, third, fourth):
+    plain = [got[d, 0:27].astype(f32).reshape(432, 128) for d in range(8)]
+    cube = [got[d, 27:31].astype(f32).reshape(64, 128) for d in range(8)]
+
+    def join(rows, u):
+        return jnp.concatenate([v[6 * u : 6 * u + 6] for v in rows], axis=0).astype(bf16).reshape(3, 16, 128)
+
+    first[9] = smalls[...]
+    for u in range(9):
+        tile = 3 * u if u < 3 else 3 * u + 1
+        first[tile : tile + 3] = join(cube, u)
     for u in range(24):
-        for k, key in enumerate(CUBE_IN):
-            pay[u // 3, 3 * k + u % 3, 0:6] = get(*key, u)
-        for k, key in enumerate(PLAIN_IN):
-            rows = get(*key, u)
-            for d in range(8):
-                pay[d, 9 + 24 * k + u, 0:6] = rows
-
-
-def join_rows(got, u):
-    rows = jnp.concatenate([got[d, u].astype(f32)[0:6] for d in range(8)], axis=0)
-    return rows.astype(bf16).reshape(3, 16, 128)
-
-
-def regroup_kernel(got, smalls, first, third, fourth):
-    for u in range(3):
-        first[3 * u : 3 * u + 3] = join_rows(got, u)
-    first[9] = smalls[...]
-    for u in range(3, 9):
-        first[3 * u + 1 : 3 * u + 4] = join_rows(got, u)
-    for u in range(24):
-        third[3 * u : 3 * u + 3] = join_rows(got, 9 + u)
+        third[3 * u : 3 * u + 3] = join(plain, u)
     for u in range(48):
-        fourth[3 * u : 3 * u + 3] = join_rows(got, 33 + u)
-
-
-def smalls_kernel(core_ref, mine, theirs, vecs, few, buf, sem):
+        fourth[3 * u : 3 * u + 3] = join(plain, 24 + u)
+
+
+def smalls_kernel(core_ref, mine, theirs, *refs):
+    vecs, (few, buf, sem) = refs[:4], refs[4:]
     core = core_ref[0]
 
     def step(n, carry):
@@ -491,13 +495,11 @@
     for i in range(6):
         picked = mul(low_part, (value == i).astype(f32).astype(bf16)).astype(bf16)
         total = total + t_mul(picked, (place_in == i).astype(f32).astype(bf16))
-    vecs[...] = total
-
-
-def split_rows(out, u, rows):
-    for d in range(8):
-        part = jnp.concatenate([rows[6 * d : 6 * d + 6], jnp.zeros((2, 128), f32)], axis=0)
-        out[d, u] = part.astype(bf16)
+    for l in range(LAYERS):
+        for k, i in enumerate((2 * l, 4 + 2 * l, 8 + 2 * l, 9 + 2 * l)):
+            vecs[2 * l][k : k + 1] = total[i : i + 1]
+        for k, i in enumerate((2 * l + 1, 5 + 2 * l, 12 + 2 * l, 13 + 2 * l)):
+            vecs[2 * l + 1][k : k + 1] = total[i : i + 1]
 
 
 def finish_kernel(parts, total, out, few):
@@ -505,45 +507,50 @@
     for k in range(8):
         small = small + parts[k, 9].astype(f32)[0:2]
     few[...] = small
-    for u in range(24):
-        split_rows(out, 15 + u, total[3 * u : 3 * u + 3].reshape(48, 128).astype(f32))
-    for u in range(15):
+    units_of = []
+    for u in range(12):
         tile = 3 * u if u < 3 else 3 * u + 1
         rows = jnp.zeros((48, 128), f32)
         for k in range(8):
             rows = rows + parts[k, tile : tile + 3].reshape(48, 128).astype(f32)
-        split_rows(out, u, rows)
+        units_of.append(rows)
+    for u in range(48):
+        units_of.append(total[3 * u : 3 * u + 3].reshape(48, 128).astype(f32))
+    for d in range(8):
+        out[d] = dense([rows[6 * d : 6 * d + 6] for rows in units_of], 23)
 
 
 def unpack_kernel(got, order, g_in, g_out, g_up, g_down):
+    cube = [got[d, 0:5].reshape(80, 128).astype(f32) for d in range(8)]
+    plain = got[0].reshape(368, 128).astype(f32)
+    for d in range(1, 8):
+        plain = plain + got[d].reshape(368, 128).astype(f32)
     for l in range(LAYERS):
         for group in range(3):
-            ups = []
+            rows = []
             for u in range(24):
                 if (l, group) in CUBE_OUT:
-                    rows = got[u // 3, 3 * CUBE_OUT.index((l, group)) + u % 3].astype(f32)
+                    k = 6 * (3 * CUBE_OUT.index((l, group)) + u % 3)
+                    rows.append(cube[u // 3][k : k + 6])
                 else:
-                    rows = got[0, 15 + u].astype(f32)
-                    for d in range(1, 8):
-                        rows = rows + got[d, 15 + u].astype(f32)
-                rows = rows[0:6]
-                if group == 0 and u < 18:
-                    g_in[l, :, 128 * u : 128 * u + 128] = rows
-                elif group == 0:
-                    g_out[l, :, 128 * (u - 18) : 128 * (u - 17)] = rows
-                elif group == 1:
-                    ups.append(rows)
-                else:
+                    k = 6 * (12 + 24 * PLAIN_OUT.index((l, group)) + u)
+                    rows.append(plain[k : k + 6])
+            if group == 0:
+                g_in[:, l] = jnp.concatenate(rows[:18], axis=1)
+                g_out[:, l] = jnp.concatenate(rows[18:], axis=1)
+            elif group == 1:
+                for m in range(8):
+                    left = jnp.concatenate(rows[3 * m : 3 * m + 3], axis=1)
+                    wide = jnp.zeros((6, 384), f32)
+                    for _ in range(3):
+                        term = left.astype(bf16)
+                        left = left - term.astype(f32)
+                        wide = wide + mul_t(term, order[...])
+                    g_up[:, l, 384 * m : 384 * m + 384] = wide
+            else:
+                for u in range(24):
                     cb, q = divmod(u, 4)
-                    g_down[l, 6 * q : 6 * q + 6, 128 * cb : 128 * cb + 128] = rows
-            for m in range(len(ups) // 3):
-                left = jnp.concatenate(ups[3 * m : 3 * m + 3], axis=1)
-                wide = jnp.zeros((6, 384), f32)
-                for _ in range(3):
-                    term = left.astype(bf16)
-                    left = left - term.astype(f32)
-                    wide = wide + mul_t(term, order[...])
-                g_up[l, :, 384 * m : 384 * m + 384] = wide
+                    g_down[l, 6 * q : 6 * q + 6, 128 * cb : 128 * cb + 128] = rows[u]
 
 
 def call(kernel, outs, ins, scratch=(), us=3, out_spaces=None, aliases=None):
@@ -650,8 +657,9 @@
     order = jnp.asarray(FF_ORDER, bf16)
     smalls = jnp.concatenate([v.reshape(-1) for v in (norm_gain, norm_bias, input_bias, branch_bias, up_bias)])
     smalls = jnp.pad(smalls, (0, 2048 - 144)).reshape(16, 128)
-    (pay,) = call(pack_kernel, [((8, 81, 8, 128), bf16)],
-                  [(input_weight, "v"), (output_weight, "v"), (up_weight, "v"), (down_weight, "v"), (order, "v")])
+    (pay,) = call(pack_kernel, [((8, 31, 16, 128), bf16)],
+                  [(jnp.swapaxes(v, 0, 1), "v") for v in (input_weight, output_weight, up_weight)]
+                  + [(down_weight, "v"), (order, "v")])
     got = lax.all_to_all(pay, CTX, 0, 0)
     first, third, fourth = call(
         regroup_kernel,
@@ -662,14 +670,11 @@
     group_e, shards = spread(shards[:, :10]), shards[:, 10:]
     sources = {(0, 0): group_e, (0, 2): (down_0,)}
 
-    vecs, few = call(
-        smalls_kernel, [((16, D), f32), ((128, 256), f32)],
+    *vecs, few = call(
+        smalls_kernel, [((4, D), f32)] * 4 + [((128, 256), f32)],
         [(core, "s"), (group_e[0], "a"), (group_e[1], "a")],
         [pltpu.VMEM((128, 16, 128), bf16), DMA], us=2)
     ups = few[:, 96:144].reshape(16, 8, 2, 4, 6).transpose(2, 0, 3, 1, 4).reshape(2, 4 * D)
-
-    def vec(*index):
-        return jnp.concatenate([vecs[i : i + 1] for i in index], axis=0)
 
     def weights(l, all_groups):
         return [(w, "a") for group in range(3 if all_groups else 1) for w in sources[l, group]]
@@ -680,7 +685,7 @@
         a1, pay = call(
             functools.partial(project_kernel, l),
             [((TOK, D), bf16), ((8, TOK, 384), bf16)],
-            [(core, "s"), (hidden, "v"), (vec(2 * l, 4 + 2 * l, 8 + 2 * l, 9 + 2 * l), "v")] + weights(l, False),
+            [(core, "s"), (hidden, "v"), (vecs[2 * l], "v")] + weights(l, False),
             [w_scratch(18), DMA],
             us=5)
         if l == 0:
@@ -704,7 +709,7 @@
             functools.partial(forward_kernel, l),
             [((TOK, D), bf16), ((TOK, D), f32), ((TOK, D), bf16), ((TOK, 4 * D), f32),
              ((TOK, D), f32 if l == 0 else bf16)],
-            [(core, "s"), (hidden, "v"), (back, "v"), (vec(2 * l + 1, 5 + 2 * l, 12 + 2 * l, 13 + 2 * l), "v"),
+            [(core, "s"), (hidden, "v"), (back, "v"), (vecs[2 * l + 1], "v"),
              (ups[l : l + 1], "v")] + weights(l, True),
             [w_scratch(6), w_scratch(24), w_scratch(24), DMA((3,))],
             us=8)
@@ -718,28 +723,22 @@
             [pltpu.VMEM((2, 64, 9, 16, 128), bf16), DMA((2,))], us=5, out_spaces="aa")
 
     grad = out_grad[0]
-    few_rows, few_up = [None] * 2, [None] * 2
+    few_rows, few_up, joint = [None] * 2, [None] * 2, [None] * 2
     for l in reversed(range(LAYERS)):
         layer_in, a1, heads, o, h1, a2, u = stored[l]
         f, du, e1, pay, small_b, small_u = call(
             functools.partial(backward_kernel, l),
             [((TOK, 4 * D), bf16), ((TOK, 4 * D), bf16), ((TOK, D), f32), ((8, TOK, 128), bf16),
              ((4, D), f32), ((1, 4 * D), f32)],
-            [(core, "s"), (grad, "v"), (u, "v"), (h1, "v"), (vec(2 * l + 1), "v")] + weights(l, True),
+            [(core, "s"), (grad, "v"), (u, "v"), (h1, "v"), (vecs[2 * l + 1], "v")] + weights(l, True),
             [w_scratch(6), w_scratch(24), w_scratch(24), DMA((3,))],
             us=10)
-        if l == 0:
-            sums_up = gather_sums(after(up_1, back2))
-            pay = after(pay, sums_up)
-            f = after(f, sums_up)
         cot = lax.all_to_all(pay, CTX, 0, 0)
         if l == 1:
-            (down_1,) = call(
-                grad_down_plain, [((16, 72, 16, 128), bf16)], [(f, "v"), (grad, "v")],
-                [w_scratch(24), DMA((1,))], us=5, out_spaces="a")
-            up_1 = call(
-                grad_up_cube, [((64, 9, 16, 128), bf16)] * 2, [(core, "s"), (a2, "v"), (du, "v")],
-                [pltpu.VMEM((2, 64, 9, 16, 128), bf16), DMA((2,))], us=5, out_spaces="aa")
+            (mlp_1,) = call(
+                grad_mlp_plain, [((16, 144, 16, 128), bf16)], [(f, "v"), (grad, "v"), (a2, "v"), (du, "v")],
+                [w_scratch(48), DMA((1,))], us=9, out_spaces="a")
+            scattered = lax.psum_scatter(after(mlp_1, cot), DATA, scatter_dimension=0, tiled=False)
         else:
             keep_ud, send_ud = call(
                 grad_mlp_cube, [((64, 18, 16, 128), bf16)] * 2,
@@ -748,35 +747,27 @@
                 us=9, out_spaces="aa")
         if l == 0:
             send_ud = after(send_ud, cot)
-            joint_1 = grad_joint(after(saved[0], cot), *saved[1:])
-        else:
-            scattered = lax.psum_scatter(after(down_1, cot), DATA, scatter_dimension=0, tiled=False)
-        cot = after(cot, down_1 if l == 1 else keep_ud)
+        cot = after(cot, mlp_1 if l == 1 else keep_ud)
         (pay2,) = call(
             attend_back_kernel,
             [((8, TOK, 384), bf16)],
             [(par, "s"), (heads, "v"), (cot, "v"), (idc, "v"), (idr, "v")],
             [pltpu.VMEM((2, SLOTS, 64), f32)] * 2,
             us=10)
+        back2 = lax.all_to_all(pay2, CTX, 0, 0)
         if l == 0:
-            pay2 = after(pay2, scattered)
-        back2 = lax.all_to_all(pay2, CTX, 0, 0)
-        if l == 1:
-            up_1 = core_sums([up_1])
-            back2 = after(back2, up_1)
-        else:
-            middle = core_sums([(keep_ud, send_ud), joint_1])
+            middle = core_sums([(keep_ud, send_ud)])
             back2 = after(back2, middle)
         g, grad, small_a = call(
             functools.partial(back_project_kernel, l),
             [((TOK, 3 * D), bf16), ((TOK, D), f32), ((4, D), f32)],
-            [(core, "s"), (back2, "v"), (e1, "v"), (layer_in, "v"), (vec(2 * l), "v")] + weights(l, False),
+            [(core, "s"), (back2, "v"), (e1, "v"), (layer_in, "v"), (vecs[2 * l], "v")] + weights(l, False),
             [w_scratch(18), DMA],
             us=6)
-        if l == 1:
-            saved = (g, a1, o, e1)
-        else:
-            joint_0 = grad_joint(g, a1, o, e1)
+        joint[l] = call(
+            grad_joint_cube, [((64, 9, 16, 128), bf16)] * 2,
+            [(core, "s"), (a1, "v"), (g, "v"), (o, "v"), (e1, "v")],
+            [pltpu.VMEM((2, 64, 9, 16, 128), bf16), DMA((2,))], us=5, out_spaces="aa")
         few_rows[l] = jnp.concatenate([small_a[0:1], small_b[0:1], small_a[1:2], small_b[1:2], small_a[2:4],
                                        small_b[2:4]], axis=0)
         few_up[l] = small_u
@@ -789,15 +780,15 @@
     few = [jnp.where(core[0] == k, few[0], few[1]) for k in range(2)]
 
     middle = gather_sums(middle)
-    last = gather_sums(after(core_sums([joint_0, few]), middle))
-    sums = jnp.concatenate([last, middle, sums_up], axis=1)
+    last = gather_sums(after(core_sums([joint[0], few, joint[1]]), middle, scattered))
+    sums = jnp.concatenate([last, middle], axis=1)
     sums = lax.all_to_all(sums, ALL, 0, 0, axis_index_groups=GROUPS_A)
-    sums, few = call(finish_kernel, [((8, 39, 8, 128), bf16), ((2, 128), f32)],
+    sums, few = call(finish_kernel, [((8, 23, 16, 128), bf16), ((2, 128), f32)],
                      [(sums, "v"), (scattered, "v")])
     got = lax.all_to_all(sums, CTX, 0, 0)
     grad_in, grad_out, grad_up, grad_down = call(
         unpack_kernel,
-        [((2, 6, 3 * D), f32), ((2, 6, D), f32), ((2, 6, 4 * D), f32), ((2, 24, D), f32)],
+        [((6, 2, 3 * D), f32), ((6, 2, D), f32), ((6, 2, 4 * D), f32), ((2, 24, D), f32)],
         [(got, "v"), (order, "v")])
     few = few.reshape(256)
     few_l = [few[48 * l : 48 * l + 48].reshape(4, 2, 6) for l in range(2)]
@@ -810,11 +801,11 @@
         grad[None],
         pair(0),
         pair(1),
-        grad_in,
+        jnp.swapaxes(grad_in, 0, 1),
         pair(2),
-        grad_out,
+        jnp.swapaxes(grad_out, 0, 1),
         pair(3),
-        grad_up,
+        jnp.swapaxes(grad_up, 0, 1),
         few[96:144].reshape(2, 24),
         grad_down,
     )

time: 528 us -> 493 us (0.934)
  blocking collectives: 112 us -> 137 us
  waiting for transfers between devices: 119 us -> 96.9 us
  local copies, waits for them, and re-layouts: 37.6 us -> 21.7 us
  starting transfers between devices: 56.9 us -> 47.4 us
  Pallas kernels: 162 us -> 154 us
    all_to_all x2 -> x1, waiting for transfers between devices: 27.7 us -> 2.28 us  [gather_sums(): lax.all_to_all(part, ALL, 0, 0, axis_index_groups=GROUPS_B)]
    all_to_all x0 -> x1, blocking collectives: none -> 17.1 us  [body(): back2 = lax.all_to_all(pay2, CTX, 0, 0)]
    unnamed x76 -> x54, local copies, waits for them, and re-layouts: 20.3 us -> 6.15 us
    all_to_all x1, blocking collectives: 26.6 us -> 36.8 us  [gather_sums(): lax.all_to_all(part, ALL, 0, 0, axis_index_groups=GROUPS_B)]
    all_gather x1, waiting for transfers between devices: 0.01 us -> 7.48 us  [body(): both_1 = lax.all_gather(after(fourth, a1), DATA, axis=0, tiled=False)]
    pallas_call x3 -> x2, Pallas kernels: 23.1 us -> 16.7 us  [add_pairs(): pl.pallas_call(add_kernel, grid=(8,), out_shape=jax.ShapeDtypeStruct((64,...]
    pallas_call x22 -> x21, Pallas kernels: 139 us -> 137 us  [call(): pl.pallas_call(kernel, out_shape=[jax.ShapeDtypeStruct(*o) for o in outs]...]
  transfers between devices with their start and end apart: 22 -> 19, of which waited for: 13 -> 12; matrix products, arithmetic and copies ran while one was open for 5% -> 5% of each run, Pallas kernels for 24% -> 25%
where the time goes in v4:
time: 493 us; the launch traced here: 483 us
  Pallas kernels  154 us (31%)
  blocking collectives  137 us (28%)
  waiting for transfers between devices  96.9 us (20%)
  starting transfers between devices  47.4 us (10%)
  local copies, waits for them, and re-layouts  21.7 us (4%)
  between operations  14.9 us (3%)
  other arithmetic  11.3 us (2%)
    pallas_call x21, Pallas kernels, call(): pl.pallas_call(kernel, out_shape=[jax.ShapeDtypeStruct(*o) for o in outs]...  137 us
    all_to_all x2, blocking collectives, copies(): return lax.all_to_all(many, ALL, 0, 0, axis_index_groups=groups)  45.8 us
    all_to_all x1, blocking collectives, gather_sums(): lax.all_to_all(part, ALL, 0, 0, axis_index_groups=GROUPS_B)  36.8 us
    all_to_all x1, waiting for transfers between devices, copies(): return lax.all_to_all(many, ALL, 0, 0, axis_index_groups=groups)  25.8 us
    all_to_all x1, blocking collectives, body(): sums = lax.all_to_all(sums, ALL, 0, 0, axis_index_groups=GROUPS_A)  21 us
    all_to_all x1, blocking collectives, body(): back2 = lax.all_to_all(pay2, CTX, 0, 0)  17.1 us
    pallas_call x2, Pallas kernels, add_pairs(): pl.pallas_call(add_kernel, grid=(8,), out_shape=jax.ShapeDtypeStruct((64,...  16.7 us
    all_to_all x1, blocking collectives, body(): heads = lax.all_to_all(pay, CTX, 0, 0)  16.1 us
  transfers between devices with their start and end apart: 19, of which 12 were waited for; matrix products, arithmetic and copies ran while one was open for 5% of the time, Pallas kernels for 25%

profile of v4, /device:TPU:0, one launch (start us, length us, event | category | flops | bytes accessed | tf_op | source)
XLA Modules:
  0.0 483.1 jit_solution(9077822027339423126)
XLA Ops:
  7.2 2.9 shard_map.239
  10.2 5.7 %all-to-all-start = ((bf16[8,31,16,128]{3,2,1,0:T(8,128)(2,1)}), bf16[8,31,16,128]{3,2,1,0:T(8,128)(2,1)S(1)}, u32[]{:S(2)}, u32[]{:S(2)}) async-start(bf16[8,31,16,128]{3,2,1,0:T(8,128)(2,1)} %shard_map.239), calls=%async_computation | async-start | bytes 2031616 | tf_op jit(solution)/shard_map/all_to_all | solution.py:663
  17.1 14.2 %all-to-all-done.got = bf16[8,31,16,128]{3,2,1,0:T(8,128)(2,1)S(1)} async-done(((bf16[8,31,16,128]{3,2,1,0:T(8,128)(2,1)}), bf16[8,31,16,128]{3,2,1,0:T(8,128)(2,1)S(1)}, u32[]{:S(2)}, u32[]{:S(2)}) %all-to-all-start) | async-done | bytes 1015840 | tf_op jit(solution)/shard_map/all_to_all | solution.py:663
  31.3 1.0 copy-done.2
  32.3 2.3 shard_map.240
  34.7 1.0 broadcast_in_dim.22
  35.7 21.7 %all_to_all.80 = bf16[8,28,16,128]{3,2,1,0:T(8,128)(2,1)S(1)} all-to-all(bf16[8,28,16,128]{3,2,1,0:T(8,128)(2,1)S(1)} %broadcast_in_dim.22), channel_id=1, replica_groups={{0,6,17,23,96,102,113,119},{2,4,19,21,98,100,115,117},{1,7,16,22,97,103..., dimensions={0} | all-to-all | bytes 1835008 | tf_op jit(solution)/shard_map/all_to_all | solution.py:583
  57.9 24.1 %all_to_all.81 = bf16[8,8,10,16,128]{4,3,2,1,0:T(8,128)(2,1)S(1)} all-to-all(bf16[8,8,10,16,128]{4,3,2,1,0:T(8,128)(2,1)S(1)} %broadcast_in_dim.23), channel_id=1, replica_groups={{0,2,1,3,32,34,33,35},{6,4,7,5,38,36,39,37},{17,19,16,18,49,51,48,50},{..., dimensions={0} | all-to-all | bytes 5242880 | tf_op jit(solution)/shard_map/all_to_all | solution.py:583
  82.0 5.0 %collective-permute-done.theirs.refs_1_ = bf16[64,10,16,128]{3,2,1,0:T(8,128)(2,1)} collective-permute-done((bf16[64,10,16,128]{3,2,1,0:T(8,128)(2,1)S(1)}, bf16[64,10,16,128]{3,2,1,0:T(8,128)(2,1)}, u32[]{:S(2)}, u32[]{:S(2)}) %collective-permute-start) | collective-permute-done | bytes 2621472 | tf_op jit(solution)/shard_map/ppermute | solution.py:591
  87.0 4.2 shard_map.241
  91.2 5.0 %shard_map.242 = (bf16[128,768]{1,0:T(8,128)(2,1)}, bf16[8,128,384]{2,1,0:T(8,128)(2,1)}) custom-call(s32[1]{0:T(128)} %bitcast.core_ref.core, bf16[128,768]{1,0:T(8,128)(2,1)} %bitcast.73, f32[4,768]{1,0:T(4,128)} %get-tuple-element.75.vec, bf16[64,10,16,128]{3,2,1,0:T(8,128)(2,1)} %bitcast.65, bf16[64,10,16,128]{3,2,1,0:T(8,128)(2,1)} %collective-permute-done.theirs.refs_1_), custom_call_target="tpu_custom_call" | custom-call | bytes 18450000 | tf_op jit(solution)/shard_map/pallas_call | solution.py:558
  96.3 5.0 %all-to-all-start.3 = ((bf16[8,128,384]{2,1,0:T(8,128)(2,1)}), bf16[8,128,384]{2,1,0:T(8,128)(2,1)S(1)}, u32[]{:S(2)}, u32[]{:S(2)}) async-start(bf16[8,128,384]{2,1,0:T(8,128)(2,1)} %get-tuple-element.76), calls=%async_computation.3 | async-start | bytes 1572864 | tf_op jit(solution)/shard_map/all_to_all | solution.py:694
  101.4 12.7 %all-to-all-done.3.heads = bf16[8,128,384]{2,1,0:T(8,128)(2,1)S(1)} async-done(((bf16[8,128,384]{2,1,0:T(8,128)(2,1)}), bf16[8,128,384]{2,1,0:T(8,128)(2,1)S(1)}, u32[]{:S(2)}, u32[]{:S(2)}) %all-to-all-start.3) | async-done | bytes 786464 | tf_op jit(solution)/shard_map/all_to_all | solution.py:694
  114.1 2.9 broadcast_in_dim.26
  117.0 4.8 all-to-all-start.4
  123.2 0.9 subtract_select_fusion.idc
  124.1 7.0 %shard_map.243 = bf16[8,128,128]{2,1,0:T(8,128)(2,1)} custom-call(s32[1]{0:T(128)} %bitcast.2.par_ref, bf16[8,128,384]{2,1,0:T(8,128)(2,1)} %copy-done.1, s32[8,128,1]{2,1,0:T(8,128)} %subtract_select_fusion.idc, s32[1,1024]{1,0:T(1,128)} %reshape_select_fusion.idr), custom_call_target="tpu_custom_call" | custom-call | bytes 25830000 | tf_op jit(solution)/shard_map/pallas_call | solution.py:558
  131.1 25.8 %all-to-all-done.4 = bf16[8,8,18,16,128]{4,3,2,1,0:T(8,128)(2,1)} async-done(((bf16[8,8,18,16,128]{4,3,2,1,0:T(8,128)(2,1)}), bf16[8,8,18,16,128]{4,3,2,1,0:T(8,128)(2,1)}, u32[]{:S(2)}, u32[]{:S(2)}) %all-to-all-start.4) | async-done | bytes 4718624 | tf_op jit(solution)/shard_map/all_to_all | solution.py:583
  157.3 4.6 all-to-all-start.5
  162.4 0.8 slice.158.upb
  163.2 6.0 %all-to-all-done.5.back = bf16[8,128,128]{2,1,0:T(8,128)(2,1)S(1)} async-done(((bf16[8,128,128]{2,1,0:T(8,128)(2,1)}), bf16[8,128,128]{2,1,0:T(8,128)(2,1)S(1)}, u32[]{:S(2)}, u32[]{:S(2)}) %all-to-all-start.5) | async-done | bytes 262176 | tf_op jit(solution)/shard_map/all_to_all | solution.py:707
  169.9 8.2 %shard_map.244 = (bf16[128,768]{1,0:T(8,128)(2,1)}, f32[128,768]{1,0:T(8,128)}, bf16[128,768]{1,0:T(8,128)(2,1)}, f32[128,3072]{1,0:T(8,128)}, f32[128,768]{1,0:T(8,128)}) custom-call(s32[1]{0:T(128)} %bitcast.core_ref.core, bf16[128,768]{1,0:T(8,128)(2,1)} %bitcast.74, bf16[8,128,128]{2,1,0:T(8,128)(2,1)} %copy-done.6, f32[4,768]{1,0:T(4,128)} %get-tuple-element.80.vec, ...), custom_call_target="tpu_custom_call" | custom-call | bytes 29520000 | tf_op jit(solution)/shard_map/pallas_call | solution.py:558
  178.1 5.0 %shard_map.245 = (bf16[128,768]{1,0:T(8,128)(2,1)}, bf16[8,128,384]{2,1,0:T(8,128)(2,1)}) custom-call(s32[1]{0:T(128)} %bitcast.core_ref.core, f32[128,768]{1,0:T(8,128)} %get-tuple-element.83.h_ref, f32[4,768]{1,0:T(4,128)} %get-tuple-element.84.vec, bf16[64,18,16,128]{3,2,1,0:T(8,128)(2,1)} %bitcast.12.refs_2_.refs_0_, ...), custom_call_target="tpu_custom_call" | custom-call | bytes 18450000 | tf_op jit(solution)/shard_map/pallas_call | solution.py:558
  183.2 16.1 %all_to_all.82.heads = bf16[8,128,384]{2,1,0:T(8,128)(2,1)} all-to-all(bf16[8,128,384]{2,1,0:T(8,128)(2,1)} %get-tuple-element.85), channel_id=1, replica_groups=mesh['y'=4,'zh'=2,'c'=2,'x'=4,'zl'=2] {'x','zl'}, dimensions={0} | all-to-all | bytes 1572864 | tf_op jit(solution)/shard_map/all_to_all | solution.py:694
  199.3 7.0 %shard_map.246 = bf16[8,128,128]{2,1,0:T(8,128)(2,1)} custom-call(s32[1]{0:T(128)} %bitcast.2.par_ref, bf16[8,128,384]{2,1,0:T(8,128)(2,1)} %all_to_all.82.heads, s32[8,128,1]{2,1,0:T(8,128)} %subtract_select_fusion.idc, s32[1,1024]{1,0:T(1,128)} %reshape_select_fusion.idr), custom_call_target="tpu_custom_call" | custom-call | bytes 25830000 | tf_op jit(solution)/shard_map/pallas_call | solution.py:558
  206.3 7.5 %all-gather.7.cloned.1.call-done = bf16[2304,16,128]{2,1,0:T(8,128)(2,1)} async-done(((bf16[144,16,128]{2,1,0:T(8,128)(2,1)}), bf16[2304,16,128]{2,1,0:T(8,128)(2,1)}) %all-gather.7.cloned.1.call-update) | async-done | bytes 9437200 | tf_op jit(solution)/shard_map/all_gather | solution.py:692
  213.8 4.5 all-to-all-start.7
  218.7 0.8 slice.160.upb
  219.5 6.1 %all-to-all-done.7.back = bf16[8,128,128]{2,1,0:T(8,128)(2,1)S(1)} async-done(((bf16[8,128,128]{2,1,0:T(8,128)(2,1)}), bf16[8,128,128]{2,1,0:T(8,128)(2,1)S(1)}, u32[]{:S(2)}, u32[]{:S(2)}) %all-to-all-start.7) | async-done | bytes 262176 | tf_op jit(solution)/shard_map/all_to_all | solution.py:707
  226.3 7.6 %shard_map.247 = (bf16[128,768]{1,0:T(8,128)(2,1)}, f32[128,768]{1,0:T(8,128)}, bf16[128,768]{1,0:T(8,128)(2,1)}, f32[128,3072]{1,0:T(8,128)}, bf16[128,768]{1,0:T(8,128)(2,1)}) custom-call(s32[1]{0:T(128)} %bitcast.core_ref.core, f32[128,768]{1,0:T(8,128)} %get-tuple-element.83.h_ref, bf16[8,128,128]{2,1,0:T(8,128)(2,1)} %copy-done.7, ...), custom_call_target="tpu_custom_call" | custom-call | bytes 29520000 | tf_op jit(solution)/shard_map/pallas_call | solution.py:558
  233.9 9.5 %shard_map.248 = (bf16[128,3072]{1,0:T(8,128)(2,1)}, bf16[128,3072]{1,0:T(8,128)(2,1)}, f32[128,768]{1,0:T(8,128)}, bf16[8,128,128]{2,1,0:T(8,128)(2,1)}, f32[4,768]{1,0:T(4,128)}, /*index=5*/f32[1,3072]{1,0:T(1,128)}) custom-call(s32[1]{0:T(128)} %bitcast.core_ref.core, bf16[128,768]{1,0:T(8,128)(2,1)} %bitcast.79, f32[128,3072]{1,0:T(8,128)} %get-tuple-element.92.u_ref, ...), custom_call_target="tpu_custom_call" | custom-call | bytes 36900000 | tf_op jit(solution)/shard_map/pallas_call | solution.py:558
  243.4 3.4 all-to-all-start.8
  247.4 7.9 %shard_map.249 = bf16[16,144,16,128]{3,2,1,0:T(8,128)(2,1)} custom-call(bf16[128,3072]{1,0:T(8,128)(2,1)} %get-tuple-element.95.f_ref, bf16[128,768]{1,0:T(8,128)(2,1)} %bitcast.80, bf16[128,768]{1,0:T(8,128)(2,1)} %get-tuple-element.96.a2_ref, bf16[128,3072]{1,0:T(8,128)(2,1)} %get-tuple-element.97.du_ref), custom_call_target="tpu_custom_call" | custom-call | bytes 33210000 | tf_op jit(solution)/shard_map/pallas_call | solution.py:558
  256.0 10.1 %shard_map.250 = bf16[8,128,384]{2,1,0:T(8,128)(2,1)} custom-call(s32[1]{0:T(128)} %bitcast.2.par_ref, bf16[8,128,384]{2,1,0:T(8,128)(2,1)} %all_to_all.82.heads, bf16[8,128,128]{2,1,0:T(8,128)(2,1)} %copy-done.9, s32[8,128,1]{2,1,0:T(8,128)} %subtract_select_fusion.idc, s32[1,1024]{1,0:T(1,128)} %reshape_select_fusion.idr), custom_call_target="tpu_custom_call" | custom-call | bytes 36900000 | tf_op jit(solution)/shard_map/pallas_call | solution.py:558
  266.0 17.1 %all_to_all.83.back = bf16[8,128,384]{2,1,0:T(8,128)(2,1)} all-to-all(bf16[8,128,384]{2,1,0:T(8,128)(2,1)} %shard_map.250), channel_id=1, replica_groups=mesh['y'=4,'zh'=2,'c'=2,'x'=4,'zl'=2] {'x','zl'}, dimensions={0} | all-to-all | bytes 1572864 | tf_op jit(solution)/shard_map/all_to_all | solution.py:757
  283.1 6.0 %shard_map.251 = (bf16[128,2304]{1,0:T(8,128)(2,1)}, f32[128,768]{1,0:T(8,128)}, f32[4,768]{1,0:T(4,128)}) custom-call(s32[1]{0:T(128)} %bitcast.core_ref.core, bf16[8,128,384]{2,1,0:T(8,128)(2,1)} %all_to_all.83.back, f32[128,768]{1,0:T(8,128)} %get-tuple-element.99.e1_ref, f32[128,768]{1,0:T(8,128)} %get-tuple-element.83.h_ref, ...), custom_call_target="tpu_custom_call" | custom-call | bytes 22140000 | tf_op jit(solution)/shard_map/pallas_call | solution.py:558
  289.1 10.8 %shard_map.252 = (bf16[128,3072]{1,0:T(8,128)(2,1)}, bf16[128,3072]{1,0:T(8,128)(2,1)}, f32[128,768]{1,0:T(8,128)}, bf16[8,128,128]{2,1,0:T(8,128)(2,1)}, f32[4,768]{1,0:T(4,128)}, /*index=5*/f32[1,3072]{1,0:T(1,128)}) custom-call(s32[1]{0:T(128)} %bitcast.core_ref.core, f32[128,768]{1,0:T(8,128)} %get-tuple-element.100.e_ref, ...), custom_call_target="tpu_custom_call" | custom-call | bytes 36900000 | tf_op jit(solution)/shard_map/pallas_call | solution.py:558
  299.9 3.4 all-to-all-start.10
  303.3 8.5 %shard_map.253 = (bf16[64,18,16,128]{3,2,1,0:T(8,128)(2,1)}, bf16[64,18,16,128]{3,2,1,0:T(8,128)(2,1)}) custom-call(s32[1]{0:T(128)} %bitcast.core_ref.core, bf16[128,3072]{1,0:T(8,128)(2,1)} %get-tuple-element.104.f_ref, f32[128,768]{1,0:T(8,128)} %get-tuple-element.100.e_ref, bf16[128,768]{1,0:T(8,128)(2,1)} %get-tuple-element.105.a2_ref, ...), custom_call_target="tpu_custom_call" | custom-call | bytes 33210000 | tf_op jit(solution)/shard_map/pallas_call | solution.py:558
  312.5 10.1 %shard_map.254 = bf16[8,128,384]{2,1,0:T(8,128)(2,1)} custom-call(s32[1]{0:T(128)} %bitcast.2.par_ref, bf16[8,128,384]{2,1,0:T(8,128)(2,1)} %copy-done.1, bf16[8,128,128]{2,1,0:T(8,128)(2,1)} %copy-done.8, s32[8,128,1]{2,1,0:T(8,128)} %subtract_select_fusion.idc, s32[1,1024]{1,0:T(1,128)} %reshape_select_fusion.idr), custom_call_target="tpu_custom_call" | custom-call | bytes 36900000 | tf_op jit(solution)/shard_map/pallas_call | solution.py:558
  322.6 5.6 %all-to-all-start.11 = ((bf16[8,128,384]{2,1,0:T(8,128)(2,1)}), bf16[8,128,384]{2,1,0:T(8,128)(2,1)S(1)}, u32[]{:S(2)}, u32[]{:S(2)}) async-start(bf16[8,128,384]{2,1,0:T(8,128)(2,1)} %shard_map.254), calls=%async_computation.11 | async-start | bytes 1572864 | tf_op jit(solution)/shard_map/all_to_all | solution.py:757
  328.2 8.2 %shard_map.255 = bf16[64,18,16,128]{3,2,1,0:T(8,128)(2,1)} custom-call(bf16[64,18,16,128]{3,2,1,0:T(8,128)(2,1)} %get-tuple-element.107.refs_0_, bf16[64,18,16,128]{3,2,1,0:T(8,128)(2,1)} %collective-permute-done.2.refs_1_), custom_call_target="tpu_custom_call" | custom-call | flops 4194304 | bytes 14155776 | tf_op jit(solution)/shard_map/pallas_call | solution.py:618
  336.5 4.4 all-to-all-done.11.back
  340.9 0.9 copy-done.3
  341.8 4.6 all-to-all-start.12
  346.4 5.1 %shard_map.258 = (bf16[64,9,16,128]{3,2,1,0:T(8,128)(2,1)}, bf16[64,9,16,128]{3,2,1,0:T(8,128)(2,1)}) custom-call(s32[1]{0:T(128)} %bitcast.core_ref.core, bf16[128,768]{1,0:T(8,128)(2,1)} %get-tuple-element.124.a_ref, bf16[128,2304]{1,0:T(8,128)(2,1)} %get-tuple-element.125.g_ref, bf16[128,768]{1,0:T(8,128)(2,1)} %get-tuple-element.126.o_ref, ...), custom_call_target="tpu_custom_call" | custom-call | bytes 18450000 | tf_op jit(solution)/shard_map/pallas_call | solution.py:558
  351.7 6.0 %shard_map.256 = (bf16[128,2304]{1,0:T(8,128)(2,1)}, f32[128,768]{1,0:T(8,128)}, f32[4,768]{1,0:T(4,128)}) custom-call(s32[1]{0:T(128)} %bitcast.core_ref.core, bf16[8,128,384]{2,1,0:T(8,128)(2,1)} %copy-done.3, f32[128,768]{1,0:T(8,128)} %get-tuple-element.112.e1_ref, bf16[128,768]{1,0:T(8,128)(2,1)} %bitcast.75, f32[4,768]{1,0:T(4,128)} %get-tuple-element.75.vec, ...), custom_call_target="tpu_custom_call" | custom-call | bytes 22140000 | tf_op jit(solution)/shard_map/pallas_call | solution.py:558
  357.8 5.1 %shard_map.257 = (bf16[64,9,16,128]{3,2,1,0:T(8,128)(2,1)}, bf16[64,9,16,128]{3,2,1,0:T(8,128)(2,1)}) custom-call(s32[1]{0:T(128)} %bitcast.core_ref.core, bf16[128,768]{1,0:T(8,128)(2,1)} %get-tuple-element.87.a_ref, bf16[128,2304]{1,0:T(8,128)(2,1)} %get-tuple-element.114.g_ref, bf16[128,768]{1,0:T(8,128)(2,1)} %get-tuple-element.115.o_ref, ...), custom_call_target="tpu_custom_call" | custom-call | bytes 18450000 | tf_op jit(solution)/shard_map/pallas_call | solution.py:558
  362.9 1.2 collective-permute-start.3
  368.0 0.8 select_bitcast_fusion
  368.8 1.5 collective-permute-done.4.refs_3_
  371.0 8.5 %shard_map.259 = bf16[64,19,16,128]{3,2,1,0:T(8,128)(2,1)} custom-call(bf16[64,9,16,128]{3,2,1,0:T(8,128)(2,1)} %get-tuple-element.116.refs_0_, bf16[64,9,16,128]{3,2,1,0:T(8,128)(2,1)} %collective-permute-done.3.refs_1_, bf16[64,1,16,128]{3,2,1,0:T(8,128)(2,1)} %get-tuple-element.140.refs_2_, bf16[64,1,16,128]{3,2,1,0:T(8,128)(2,1)} %copy-done.10, ...), custom_call_target="tpu_custom_call" | custom-call | flops 4194304 | bytes 14942208 | tf_op jit(solution)/shard_map/pallas_call | solution.py:618
  379.5 2.3 all-to-all-done.12
  381.8 3.1 reduce_sum.34
  384.9 7.6 %reduce-scatter.2.cloned.1.call-done = bf16[1,144,16,128]{3,2,1,0:T(8,128)(2,1)} async-done(((bf16[16,144,16,128]{3,2,1,0:T(8,128)(2,1)}), bf16[1,144,16,128]{3,2,1,0:T(8,128)(2,1)}) %reduce-scatter.2.cloned.1.call-update) | async-done | bytes 589840 | tf_op jit(solution)/shard_map/reduce_scatter | solution.py:741
  392.5 36.8 %all_to_all.84 = bf16[8,8,19,16,128]{4,3,2,1,0:T(8,128)(2,1)} all-to-all(bf16[8,8,19,16,128]{4,3,2,1,0:T(8,128)(2,1)} %bitcast.69), channel_id=1, replica_groups={{0,2,1,3,32,34,33,35},{6,4,7,5,38,36,39,37},{17,19,16,18,49,51,48,50},{..., dimensions={0} | all-to-all | bytes 9961472 | tf_op jit(solution)/shard_map/all_to_all | solution.py:635
  429.3 3.2 reduce_sum.35
  432.7 21.0 %all_to_all.85.parts = bf16[8,37,16,128]{3,2,1,0:T(8,128)(2,1)} all-to-all(bf16[8,37,16,128]{3,2,1,0:T(8,128)(2,1)S(1)} %pad_maximum_fusion), channel_id=1, replica_groups={{0,6,17,23,96,102,113,119},{2,4,19,21,98,100,115,117},{1,7,16,22,97,103..., dimensions={0} | all-to-all | bytes 2424832 | tf_op jit(solution)/shard_map/all_to_all | solution.py:785
  453.6 2.7 shard_map.260
  456.3 3.5 all-to-all-start.15
  460.6 1.0 fusion.29
  465.3 3.8 all-to-all-done.15.got
  469.2 0.9 copy-done.4
  470.1 6.0 %shard_map.261 = (f32[6,2,2304]{2,1,0:T(2,128)}, f32[6,2,768]{2,1,0:T(2,128)}, f32[6,2,3072]{2,1,0:T(2,128)}, f32[2,24,768]{2,1,0:T(8,128)}) custom-call(bf16[8,23,16,128]{3,2,1,0:T(8,128)(2,1)} %copy-done.4, bf16[384,384]{1,0:T(8,128)(2,1)} %constant.44.clone.order), custom_call_target="tpu_custom_call" | custom-call | bytes 11070000 | tf_op jit(solution)/shard_map/pallas_call | solution.py:558
  (139 shorter events, 16.8 us)
Async XLA Ops:
  7.2 8.8 %copy-start.19 = (bf16[2,2,6]{2,1,0:T(2,128)(2,1)S(1)}, bf16[2,2,6]{2,1,0:T(2,128)(2,1)}, u32[]{:S(2)}) copy-start(bf16[2,2,6]{2,1,0:T(2,128)(2,1)} %param.21) | copy-start | bytes 148
  7.2 8.9 %copy-start.20 = (bf16[2,2,6]{2,1,0:T(2,128)(2,1)S(1)}, bf16[2,2,6]{2,1,0:T(2,128)(2,1)}, u32[]{:S(2)}) copy-start(bf16[2,2,6]{2,1,0:T(2,128)(2,1)} %param.22) | copy-start | bytes 148
  7.2 8.9 %copy-start.21 = (bf16[2,2,6]{2,1,0:T(2,128)(2,1)S(1)}, bf16[2,2,6]{2,1,0:T(2,128)(2,1)}, u32[]{:S(2)}) copy-start(bf16[2,2,6]{2,1,0:T(2,128)(2,1)} %param.24) | copy-start | bytes 148
  7.2 9.0 %copy-start.22 = (bf16[2,2,6]{2,1,0:T(2,128)(2,1)S(1)}, bf16[2,2,6]{2,1,0:T(2,128)(2,1)}, u32[]{:S(2)}) copy-start(bf16[2,2,6]{2,1,0:T(2,128)(2,1)} %param.26) | copy-start | bytes 148
  7.2 9.1 %copy-start.23 = (bf16[2,24]{1,0:T(2,128)(2,1)S(1)}, bf16[2,24]{1,0:T(2,128)(2,1)}, u32[]{:S(2)}) copy-start(bf16[2,24]{1,0:T(2,128)(2,1)} %param.28) | copy-start | bytes 292
  10.2 21.1 %all-to-all-start = ((bf16[8,31,16,128]{3,2,1,0:T(8,128)(2,1)}), bf16[8,31,16,128]{3,2,1,0:T(8,128)(2,1)S(1)}, u32[]{:S(2)}, u32[]{:S(2)}) async-start(bf16[8,31,16,128]{3,2,1,0:T(8,128)(2,1)} %shard_map.239), calls=%async_computation | async-start | bytes 2031616 | tf_op jit(solution)/shard_map/all_to_all | solution.py:663
  15.9 98.2 %all-gather.5.cloned.1.call-start = ((), (), s32[]{:S(2)}) async-start(), calls=%async_computation.18 | async-start | bytes 5013504 | tf_op jit(solution)/shard_map/all_gather | solution.py:668
  31.3 1.0 copy-start.2
  34.6 179.1 %all-gather.7.cloned.1.call-start = ((), (), s32[]{:S(2)}) async-start(), calls=%async_computation.19 | async-start | bytes 10027008 | tf_op jit(solution)/shard_map/all_gather | solution.py:692
  82.0 5.0 %copy-start = (bf16[8,8,10,16,128]{4,3,2,1,0:T(8,128)(2,1)}, bf16[8,8,10,16,128]{4,3,2,1,0:T(8,128)(2,1)S(1)}, u32[]{:S(2)}) copy-start(bf16[8,8,10,16,128]{4,3,2,1,0:T(8,128)(2,1)S(1)} %all_to_all.81) | copy-start | bytes 7864324
  82.0 5.0 %collective-permute-start = (bf16[64,10,16,128]{3,2,1,0:T(8,128)(2,1)S(1)}, bf16[64,10,16,128]{3,2,1,0:T(8,128)(2,1)}, u32[]{:S(2)}, u32[]{:S(2)}) collective-permute-start(bf16[64,10,16,128]{3,2,1,0:T(8,128)(2,1)S(1)} %bitcast.63), channel_id=1, source_target_pairs={{0,8},{8,0},{1,9},{9,1},{2,10},{10,2},{3,11},{11,3},{4,12},{12,4},... | collective-permute-start | bytes 7864328 | tf_op jit(solution)/shard_map/ppermute | solution.py:591
  96.3 17.8 %all-to-all-start.3 = ((bf16[8,128,384]{2,1,0:T(8,128)(2,1)}), bf16[8,128,384]{2,1,0:T(8,128)(2,1)S(1)}, u32[]{:S(2)}, u32[]{:S(2)}) async-start(bf16[8,128,384]{2,1,0:T(8,128)(2,1)} %get-tuple-element.76), calls=%async_computation.3 | async-start | bytes 1572864 | tf_op jit(solution)/shard_map/all_to_all | solution.py:694
  114.1 2.9 copy-start.1
  117.0 4.8 copy-start.18
  117.0 4.8 copy-start.24
  117.0 4.9 %copy-start.25 = (s32[48]{0:T(128)S(1)}, s32[48]{0:T(128)}, u32[]{:S(2)}) copy-start(s32[48]{0:T(128)} %param.18) | copy-start | bytes 580
  117.0 39.9 %all-to-all-start.4 = ((bf16[8,8,18,16,128]{4,3,2,1,0:T(8,128)(2,1)}), bf16[8,8,18,16,128]{4,3,2,1,0:T(8,128)(2,1)}, u32[]{:S(2)}, u32[]{:S(2)}) async-start(bf16[8,8,18,16,128]{4,3,2,1,0:T(8,128)(2,1)} %broadcast_in_dim.26), calls=%async_computation.4 | async-start | bytes 9437184 | tf_op jit(solution)/shard_map/all_to_all | solution.py:583
  121.8 35.1 %copy-start.11 = (f32[128,256]{1,0:T(8,128)S(1)}, f32[128,256]{1,0:T(8,128)}, u32[]{:S(2)}) copy-start(f32[128,256]{1,0:T(8,128)} %get-tuple-element.81) | copy-start | bytes 393220
  156.9 12.3 %collective-permute-start.1 = (bf16[64,18,16,128]{3,2,1,0:T(8,128)(2,1)}, bf16[64,18,16,128]{3,2,1,0:T(8,128)(2,1)}, u32[]{:S(2)}, u32[]{:S(2)}) collective-permute-start(bf16[64,18,16,128]{3,2,1,0:T(8,128)(2,1)} %bitcast.12.refs_2_.refs_0_), channel_id=1, source_target_pairs={{0,8},{8,0},{1,9},{9,1},{2,10},{10,2},{3,11},{11,3},{4,12},{12,4},... | collective-permute-start | bytes 14155784 | tf_op jit(solution)/shard_map/ppermute | solution.py:591
  157.3 11.9 %all-to-all-start.5 = ((bf16[8,128,128]{2,1,0:T(8,128)(2,1)}), bf16[8,128,128]{2,1,0:T(8,128)(2,1)S(1)}, u32[]{:S(2)}, u32[]{:S(2)}) async-start(bf16[8,128,128]{2,1,0:T(8,128)(2,1)} %shard_map.243), calls=%async_computation.5 | async-start | bytes 524288 | tf_op jit(solution)/shard_map/all_to_all | solution.py:707
  169.2 0.7 copy-start.6
  213.8 11.8 %all-to-all-start.7 = ((bf16[8,128,128]{2,1,0:T(8,128)(2,1)}), bf16[8,128,128]{2,1,0:T(8,128)(2,1)S(1)}, u32[]{:S(2)}, u32[]{:S(2)}) async-start(bf16[8,128,128]{2,1,0:T(8,128)(2,1)} %shard_map.246), calls=%async_computation.7 | async-start | bytes 524288 | tf_op jit(solution)/shard_map/all_to_all | solution.py:707
  225.6 0.7 copy-start.7
  243.4 11.8 %all-to-all-start.8 = ((bf16[8,128,128]{2,1,0:T(8,128)(2,1)}), bf16[8,128,128]{2,1,0:T(8,128)(2,1)S(1)}, u32[]{:S(2)}, u32[]{:S(2)}) async-start(bf16[8,128,128]{2,1,0:T(8,128)(2,1)} %get-tuple-element.94), calls=%async_computation.8 | async-start | bytes 524288 | tf_op jit(solution)/shard_map/all_to_all | solution.py:736
  246.9 145.7 %reduce-scatter.2.cloned.1.call-start = ((), (), s32[]{:S(2)}) async-start(), calls=%async_computation.17 | async-start | bytes 10027008 | tf_op jit(solution)/shard_map/reduce_scatter | solution.py:741
  255.3 0.7 copy-start.9
  299.9 11.9 %all-to-all-start.10 = ((bf16[8,128,128]{2,1,0:T(8,128)(2,1)}), bf16[8,128,128]{2,1,0:T(8,128)(2,1)S(1)}, u32[]{:S(2)}, u32[]{:S(2)}) async-start(bf16[8,128,128]{2,1,0:T(8,128)(2,1)} %get-tuple-element.103), calls=%async_computation.10 | async-start | bytes 524288 | tf_op jit(solution)/shard_map/all_to_all | solution.py:736
  311.8 0.7 copy-start.8
  311.8 16.4 %collective-permute-start.2 = (bf16[64,18,16,128]{3,2,1,0:T(8,128)(2,1)}, bf16[64,18,16,128]{3,2,1,0:T(8,128)(2,1)}, u32[]{:S(2)}, u32[]{:S(2)}) collective-permute-start(bf16[64,18,16,128]{3,2,1,0:T(8,128)(2,1)} %get-tuple-element.110), channel_id=1, source_target_pairs={{0,8},{8,0},{1,9},{9,1},{2,10},{10,2},{3,11},{11,3},{4,12},{12,4},... | collective-permute-start | bytes 14155784 | tf_op jit(solution)/shard_map/ppermute | solution.py:591
  322.6 18.3 %all-to-all-start.11 = ((bf16[8,128,384]{2,1,0:T(8,128)(2,1)}), bf16[8,128,384]{2,1,0:T(8,128)(2,1)S(1)}, u32[]{:S(2)}, u32[]{:S(2)}) async-start(bf16[8,128,384]{2,1,0:T(8,128)(2,1)} %shard_map.254), calls=%async_computation.11 | async-start | bytes 1572864 | tf_op jit(solution)/shard_map/all_to_all | solution.py:757
  340.9 0.9 copy-start.3
  341.8 40.0 %all-to-all-start.12 = ((bf16[8,8,18,16,128]{4,3,2,1,0:T(8,128)(2,1)}), bf16[8,8,18,16,128]{4,3,2,1,0:T(8,128)(2,1)}, u32[]{:S(2)}, u32[]{:S(2)}) async-start(bf16[8,8,18,16,128]{4,3,2,1,0:T(8,128)(2,1)} %bitcast.70), calls=%async_computation.12 | async-start | bytes 9437184 | tf_op jit(solution)/shard_map/all_to_all | solution.py:635
  351.6 17.2 %collective-permute-start.5 = (bf16[64,9,16,128]{3,2,1,0:T(8,128)(2,1)}, bf16[64,9,16,128]{3,2,1,0:T(8,128)(2,1)S(1)}, u32[]{:S(2)}, u32[]{:S(2)}) collective-permute-start(bf16[64,9,16,128]{3,2,1,0:T(8,128)(2,1)} %get-tuple-element.128), channel_id=1, source_target_pairs={{0,8},{8,0},{1,9},{9,1},{2,10},{10,2},{3,11},{11,3},{4,12},{12,4},... | collective-permute-start | bytes 7077896 | tf_op jit(solution)/shard_map/ppermute | solution.py:591
  351.6 12.4 %copy-start.13 = (f32[1,3072]{1,0:T(1,128)S(1)}, f32[1,3072]{1,0:T(1,128)}, u32[]{:S(2)}) copy-start(f32[1,3072]{1,0:T(1,128)} %get-tuple-element.123) | copy-start | bytes 36868
  351.7 13.3 %copy-start.12 = (f32[4,768]{1,0:T(4,128)S(1)}, f32[4,768]{1,0:T(4,128)}, u32[]{:S(2)}) copy-start(f32[4,768]{1,0:T(4,128)} %get-tuple-element.121) | copy-start | bytes 36868
  351.7 13.4 %copy-start.16 = (f32[1,3072]{1,0:T(1,128)S(1)}, f32[1,3072]{1,0:T(1,128)}, u32[]{:S(2)}) copy-start(f32[1,3072]{1,0:T(1,128)} %get-tuple-element.122) | copy-start | bytes 36868
  351.7 14.3 %copy-start.15 = (f32[4,768]{1,0:T(4,128)S(1)}, f32[4,768]{1,0:T(4,128)}, u32[]{:S(2)}) copy-start(f32[4,768]{1,0:T(4,128)} %get-tuple-element.120) | copy-start | bytes 36868
  357.7 9.1 %copy-start.14 = (f32[4,768]{1,0:T(4,128)S(1)}, f32[4,768]{1,0:T(4,128)}, u32[]{:S(2)}) copy-start(f32[4,768]{1,0:T(4,128)} %get-tuple-element.119) | copy-start | bytes 36868
  357.7 9.1 %copy-start.17 = (f32[4,768]{1,0:T(4,128)S(1)}, f32[4,768]{1,0:T(4,128)}, u32[]{:S(2)}) copy-start(f32[4,768]{1,0:T(4,128)} %get-tuple-element.118) | copy-start | bytes 36868
  357.7 9.9 %copy-start.26 = (bf16[128,128]{1,0:T(8,128)(2,1)S(1)}, bf16[128,128]{1,0:T(8,128)(2,1)}, u32[]{:S(2)}) copy-start(bf16[128,128]{1,0:T(8,128)(2,1)} %constant.45.clone) | copy-start | bytes 98308
  362.9 7.4 %collective-permute-start.3 = (bf16[64,9,16,128]{3,2,1,0:T(8,128)(2,1)}, bf16[64,9,16,128]{3,2,1,0:T(8,128)(2,1)}, u32[]{:S(2)}, u32[]{:S(2)}) collective-permute-start(bf16[64,9,16,128]{3,2,1,0:T(8,128)(2,1)} %get-tuple-element.117), channel_id=1, source_target_pairs={{0,8},{8,0},{1,9},{9,1},{2,10},{10,2},{3,11},{11,3},{4,12},{12,4},... | collective-permute-start | bytes 7077896 | tf_op jit(solution)/shard_map/ppermute | solution.py:591
  368.8 1.5 collective-permute-start.4
  368.8 1.5 copy-start.5
  370.3 0.7 copy-start.10
  456.3 12.8 %all-to-all-start.15 = ((bf16[8,23,16,128]{3,2,1,0:T(8,128)(2,1)}), bf16[8,23,16,128]{3,2,1,0:T(8,128)(2,1)S(1)}, u32[]{:S(2)}, u32[]{:S(2)}) async-start(bf16[8,23,16,128]{3,2,1,0:T(8,128)(2,1)} %get-tuple-element.132), calls=%async_computation.16 | async-start | bytes 1507328 | tf_op jit(solution)/shard_map/all_to_all | solution.py:788
  469.2 0.9 copy-start.4
Sparse Core Ops, SparseCore 0:
  34.8 64.7 all-gather.4
  102.0 111.7 all-gather.6
  255.4 137.0 reduce-scatter.1

commit v5 on v4

--- a/solution.py
+++ b/solution.py
@@ -206,32 +206,40 @@
             pay_ref[d, :, 128 * part : 128 * part + 128] = win.astype(bf16)
 
 
-def visible_of(block, count, idc_ref, idr_ref):
-    n = count * TOK
-    qpos = block * TOK + lax.broadcasted_iota(jnp.int32, (TOK, n), 0)
-    kpos = lax.broadcasted_iota(jnp.int32, (TOK, n), 1)
-    return (idc_ref[block] == idr_ref[:, 0:n]) & (kpos <= qpos)
-
-
-def head_blocks(par):
-    for i in range(4):
-        yield i, ((0, 2 * i, 2 * i + 1), (0, 2 * i + 1, 2 * i + 2), (1, 2 * i + par, 2 * i + 2))
+def masked(scores, first_block, second_block, idc_ref, idr_ref):
+    n = scores.shape[1]
+    ids = jnp.concatenate([idc_ref[first_block], idc_ref[second_block]], axis=0)
+    row = lax.broadcasted_iota(jnp.int32, (2 * TOK, n), 0)
+    qpos = row + jnp.where(row < TOK, first_block * TOK, (second_block - 1) * TOK)
+    seen = (ids == idr_ref[:, 0:n]) & (lax.broadcasted_iota(jnp.int32, (2 * TOK, n), 1) <= qpos)
+    return jnp.where(seen, scores, hidden_value)
+
+
+def head_pairs(par):
+    return ([(0, 2 * i, 2 * i + 1, 2 * i + 2) for i in range(4)]
+            + [(1, 4 * i + par, 4 * i + 2 + par, 4 * i + 4) for i in range(2)])
 
 
 def half(values, head):
     return values[:, 64 * head : 64 * head + 64]
 
 
-def store_pair(out, lanes, i, par, parts):
-    for k in range(2):
-        shared = jnp.where(par == k, parts[2], 0.0)
-        out[2 * i + k, :, lanes] = jnp.concatenate([parts[k], shared], axis=1).astype(bf16)
-
-
-def weights_of(q, key, seen):
-    s = jnp.where(seen, mul_t(q, key) * score_scale, hidden_value)
+def two_blocks(ref, first, second, lanes, head):
+    return jnp.concatenate([half(ref[first, :, lanes], head), half(ref[second, :, lanes], head)], axis=0)
+
+
+def store_blocks(out, par, results):
+    for b in range(8):
+        own = results[b // 2][TOK * (b % 2) : TOK * (b % 2) + TOK]
+        shared = results[4 + b // 4][TOK * (b // 2 % 2) : TOK * (b // 2 % 2) + TOK]
+        shared = jnp.where(par == b % 2, shared, 0.0)
+        out[b, :, 0:128] = jnp.concatenate([own, shared], axis=1).astype(bf16)
+
+
+def weights_of(q, key, *where):
+    s = masked(mul_t(q, key), *where)
     e = jnp.exp(s - jnp.max(s, axis=1, keepdims=True))
-    return e / jnp.sum(e, axis=1, keepdims=True)
+    return e * (1.0 / jnp.sum(e, axis=1, keepdims=True))
 
 
 def attend_kernel(par_ref, heads, idc, idr, out):
@@ -239,14 +247,13 @@
     key = heads[:, :, 128:256].reshape(SLOTS, 128)
     val = heads[:, :, 256:384].reshape(SLOTS, 128)
     keys, vals = [half(key, h) for h in range(2)], [half(val, h) for h in range(2)]
-    for i, blocks in head_blocks(par):
-        parts = []
-        for head, block, count in blocks:
-            n = count * TOK
-            q = half(heads[block, :, 0:128], head)
-            p = weights_of(q, keys[head][:n], visible_of(block, count, idc, idr)).astype(bf16)
-            parts.append(mul(p, vals[head][:n]))
-        store_pair(out, slice(0, 128), i, par, parts)
+    results = []
+    for head, first, second, count in head_pairs(par):
+        n = count * TOK
+        q = two_blocks(heads, first, second, slice(0, 128), head) * score_scale
+        p = weights_of(q, keys[head][:n], first, second, idc, idr).astype(bf16)
+        results.append(mul(p, vals[head][:n]))
+    store_blocks(out, par, results)
 
 
 def attend_back_kernel(par_ref, heads, cot, idc, idr, out, dk_acc, dv_acc):
@@ -256,20 +263,19 @@
     keys, vals = [half(key, h) for h in range(2)], [half(val, h) for h in range(2)]
     dk_acc[...] = jnp.zeros_like(dk_acc)
     dv_acc[...] = jnp.zeros_like(dv_acc)
-    for i, blocks in head_blocks(par):
-        parts = []
-        for head, block, count in blocks:
-            n = count * TOK
-            q = half(heads[block, :, 0:128], head)
-            g = half(cot[block], head)
-            p = weights_of(q, keys[head][:n], visible_of(block, count, idc, idr))
-            dp = mul_t(g, vals[head][:n])
-            ds = (p * (dp - jnp.sum(p * dp, axis=1, keepdims=True))).astype(bf16)
-            parts.append(mul(ds, keys[head][:n]) * score_scale)
-            dk_acc[head, 0:n] += t_mul(ds, q)
-            dv_acc[head, 0:n] += t_mul(p.astype(bf16), g)
-        store_pair(out, slice(0, 128), i, par, parts)
-    dk = jnp.concatenate([dk_acc[0], dk_acc[1]], axis=1) * score_scale
+    results = []
+    for head, first, second, count in head_pairs(par):
+        n = count * TOK
+        q = two_blocks(heads, first, second, slice(0, 128), head) * score_scale
+        g = two_blocks(cot, first, second, slice(0, 128), head)
+        p = weights_of(q, keys[head][:n], first, second, idc, idr)
+        dp = mul_t(g, vals[head][:n])
+        ds = (p * (dp - jnp.sum(p * dp, axis=1, keepdims=True))).astype(bf16)
+        results.append(mul(ds, keys[head][:n]) * score_scale)
+        dk_acc[head, 0:n] += t_mul(ds, q)
+        dv_acc[head, 0:n] += t_mul(p.astype(bf16), g)
+    store_blocks(out, par, results)
+    dk = jnp.concatenate([dk_acc[0], dk_acc[1]], axis=1)
     dv = jnp.concatenate([dv_acc[0], dv_acc[1]], axis=1)
     out[:, :, 128:256] = dk.astype(bf16).reshape(8, TOK, 128)
     out[:, :, 256:384] = dv.astype(bf16).reshape(8, TOK, 128)
@@ -433,10 +439,9 @@
 def pack_kernel(win, wout, wup, wdown, order, pay):
     ins = [win[...].astype(f32), wout[...].astype(f32)]
     wide = wup[...].astype(f32)
-    ups = []
-    for l in range(LAYERS):
-        rows = wide[:, l].astype(bf16)
-        ups.append([mul(rows[:, 384 * m : 384 * m + 384], order[...]) for m in range(8)])
+    stack = [wide[:, l, 384 * m : 384 * m + 384] for l in range(LAYERS) for m in range(8)]
+    stack = mul(jnp.concatenate(stack, axis=0).astype(bf16), order[...])
+    ups = [[stack[48 * l + 6 * m : 48 * l + 6 * m + 6] for m in range(8)] for l in range(LAYERS)]
     firsts = [[v[:, l] for v in ins] for l in range(LAYERS)]
     downs = [wdown[l].astype(f32) for l in range(LAYERS)]
 
@@ -525,6 +530,7 @@
     plain = got[0].reshape(368, 128).astype(f32)
     for d in range(1, 8):
         plain = plain + got[d].reshape(368, 128).astype(f32)
+    stack = []
     for l in range(LAYERS):
         for group in range(3):
             rows = []
@@ -539,18 +545,21 @@
                 g_in[:, l] = jnp.concatenate(rows[:18], axis=1)
                 g_out[:, l] = jnp.concatenate(rows[18:], axis=1)
             elif group == 1:
-                for m in range(8):
-                    left = jnp.concatenate(rows[3 * m : 3 * m + 3], axis=1)
-                    wide = jnp.zeros((6, 384), f32)
-                    for _ in range(3):
-                        term = left.astype(bf16)
-                        left = left - term.astype(f32)
-                        wide = wide + mul_t(term, order[...])
-                    g_up[:, l, 384 * m : 384 * m + 384] = wide
+                stack += [jnp.concatenate(rows[3 * m : 3 * m + 3], axis=1) for m in range(8)]
             else:
                 for u in range(24):
                     cb, q = divmod(u, 4)
                     g_down[l, 6 * q : 6 * q + 6, 128 * cb : 128 * cb + 128] = rows[u]
+    left = jnp.concatenate(stack, axis=0)
+    terms = []
+    for _ in range(3):
+        terms.append(left.astype(bf16))
+        left = left - terms[-1].astype(f32)
+    wide = mul_t(jnp.concatenate(terms, axis=0), order[...])
+    wide = wide[0:96] + wide[96:192] + wide[192:288]
+    for l in range(LAYERS):
+        for m in range(8):
+            g_up[:, l, 384 * m : 384 * m + 384] = wide[48 * l + 6 * m : 48 * l + 6 * m + 6]
 
 
 def call(kernel, outs, ins, scratch=(), us=3, out_spaces=None, aliases=None):
@@ -703,7 +712,8 @@
             theirs = swap_core(after(mine, mix))
             for key in CUBE_IN[1:]:
                 sources[key] = (mine, theirs)
-        mix = after(mix, mine if l == 0 else both_1)
+        if l == 0:
+            mix = after(mix, mine)
         back = lax.all_to_all(mix, CTX, 0, 0)
         o, h1, a2, u, following = call(
             functools.partial(forward_kernel, l),

time: 493 us -> 478 us (0.970)
  Pallas kernels: 154 us -> 143 us
    pallas_call x21, Pallas kernels: 137 us -> 126 us  [call(): pl.pallas_call(kernel, out_shape=[jax.ShapeDtypeStruct(*o) for o in outs]...]
    all_gather x1, waiting for transfers between devices: 7.48 us -> 0.01 us  [body(): both_1 = lax.all_gather(after(fourth, a1), DATA, axis=0, tiled=False)]
  transfers between devices with their start and end apart: 19 -> 19, of which waited for: 12 -> 10; matrix products, arithmetic and copies ran while one was open for 5% -> 5% of each run, Pallas kernels for 25% -> 25%
where the time goes in v5:
time: 478 us; the launch traced here: 469 us
  Pallas kernels  143 us (30%)
  blocking collectives  137 us (29%)
  waiting for transfers between devices  93.5 us (20%)
  starting transfers between devices  48 us (10%)
  local copies, waits for them, and re-layouts  21.4 us (4%)
  between operations  14.6 us (3%)
  other arithmetic  11.3 us (2%)
    pallas_call x21, Pallas kernels, call(): pl.pallas_call(kernel, out_shape=[jax.ShapeDtypeStruct(*o) for o in outs]...  126 us
    all_to_all x2, blocking collectives, copies(): return lax.all_to_all(many, ALL, 0, 0, axis_index_groups=groups)  45.8 us
    all_to_all x1, blocking collectives, gather_sums(): lax.all_to_all(part, ALL, 0, 0, axis_index_groups=GROUPS_B)  36.8 us
    all_to_all x1, waiting for transfers between devices, copies(): return lax.all_to_all(many, ALL, 0, 0, axis_index_groups=groups)  27.3 us
    all_to_all x1, blocking collectives, body(): sums = lax.all_to_all(sums, ALL, 0, 0, axis_index_groups=GROUPS_A)  21.4 us
    pallas_call x2, Pallas kernels, add_pairs(): pl.pallas_call(add_kernel, grid=(8,), out_shape=jax.ShapeDtypeStruct((64,...  16.8 us
    all_to_all x1, blocking collectives, body(): back2 = lax.all_to_all(pay2, CTX, 0, 0)  16.5 us
    all_to_all x1, blocking collectives, body(): heads = lax.all_to_all(pay, CTX, 0, 0)  16.1 us
  transfers between devices with their start and end apart: 19, of which 10 were waited for; matrix products, arithmetic and copies ran while one was open for 5% of the time, Pallas kernels for 25%

profile of v5, /device:TPU:0, one launch (start us, length us, event | category | flops | bytes accessed | tf_op | source)
XLA Modules:
  0.0 468.9 jit_solution(11696550583413149641)
XLA Ops:
  7.2 2.4 shard_map.239
  9.7 5.7 %all-to-all-start = ((bf16[8,31,16,128]{3,2,1,0:T(8,128)(2,1)}), bf16[8,31,16,128]{3,2,1,0:T(8,128)(2,1)S(1)}, u32[]{:S(2)}, u32[]{:S(2)}) async-start(bf16[8,31,16,128]{3,2,1,0:T(8,128)(2,1)} %shard_map.239), calls=%async_computation | async-start | bytes 2031616 | tf_op jit(solution)/shard_map/all_to_all | solution.py:672
  16.6 14.2 %all-to-all-done.got = bf16[8,31,16,128]{3,2,1,0:T(8,128)(2,1)S(1)} async-done(((bf16[8,31,16,128]{3,2,1,0:T(8,128)(2,1)}), bf16[8,31,16,128]{3,2,1,0:T(8,128)(2,1)S(1)}, u32[]{:S(2)}, u32[]{:S(2)}) %all-to-all-start) | async-done | bytes 1015840 | tf_op jit(solution)/shard_map/all_to_all | solution.py:672
  30.8 1.0 copy-done.2
  31.8 2.3 shard_map.240
  34.2 1.0 broadcast_in_dim.22
  35.2 21.7 %all_to_all.80 = bf16[8,28,16,128]{3,2,1,0:T(8,128)(2,1)S(1)} all-to-all(bf16[8,28,16,128]{3,2,1,0:T(8,128)(2,1)S(1)} %broadcast_in_dim.22), channel_id=1, replica_groups={{0,6,17,23,96,102,113,119},{2,4,19,21,98,100,115,117},{1,7,16,22,97,103..., dimensions={0} | all-to-all | bytes 1835008 | tf_op jit(solution)/shard_map/all_to_all | solution.py:592
  57.4 24.1 %all_to_all.81 = bf16[8,8,10,16,128]{4,3,2,1,0:T(8,128)(2,1)S(1)} all-to-all(bf16[8,8,10,16,128]{4,3,2,1,0:T(8,128)(2,1)S(1)} %broadcast_in_dim.23), channel_id=1, replica_groups={{0,2,1,3,32,34,33,35},{6,4,7,5,38,36,39,37},{17,19,16,18,49,51,48,50},{..., dimensions={0} | all-to-all | bytes 5242880 | tf_op jit(solution)/shard_map/all_to_all | solution.py:592
  81.5 5.0 %collective-permute-done.theirs.refs_1_ = bf16[64,10,16,128]{3,2,1,0:T(8,128)(2,1)} collective-permute-done((bf16[64,10,16,128]{3,2,1,0:T(8,128)(2,1)S(1)}, bf16[64,10,16,128]{3,2,1,0:T(8,128)(2,1)}, u32[]{:S(2)}, u32[]{:S(2)}) %collective-permute-start) | collective-permute-done | bytes 2621472 | tf_op jit(solution)/shard_map/ppermute | solution.py:600
  86.5 4.2 shard_map.241
  90.7 5.0 %shard_map.242 = (bf16[128,768]{1,0:T(8,128)(2,1)}, bf16[8,128,384]{2,1,0:T(8,128)(2,1)}) custom-call(s32[1]{0:T(128)} %bitcast.core_ref.core, bf16[128,768]{1,0:T(8,128)(2,1)} %bitcast.73, f32[4,768]{1,0:T(4,128)} %get-tuple-element.74.vec, bf16[64,10,16,128]{3,2,1,0:T(8,128)(2,1)} %bitcast.65, bf16[64,10,16,128]{3,2,1,0:T(8,128)(2,1)} %collective-permute-done.theirs.refs_1_), custom_call_target="tpu_custom_call" | custom-call | bytes 18450000 | tf_op jit(solution)/shard_map/pallas_call | solution.py:567
  95.8 5.0 %all-to-all-start.3 = ((bf16[8,128,384]{2,1,0:T(8,128)(2,1)}), bf16[8,128,384]{2,1,0:T(8,128)(2,1)S(1)}, u32[]{:S(2)}, u32[]{:S(2)}) async-start(bf16[8,128,384]{2,1,0:T(8,128)(2,1)} %get-tuple-element.75), calls=%async_computation.3 | async-start | bytes 1572864 | tf_op jit(solution)/shard_map/all_to_all | solution.py:703
  100.9 12.7 %all-to-all-done.3.heads = bf16[8,128,384]{2,1,0:T(8,128)(2,1)S(1)} async-done(((bf16[8,128,384]{2,1,0:T(8,128)(2,1)}), bf16[8,128,384]{2,1,0:T(8,128)(2,1)S(1)}, u32[]{:S(2)}, u32[]{:S(2)}) %all-to-all-start.3) | async-done | bytes 786464 | tf_op jit(solution)/shard_map/all_to_all | solution.py:703
  113.6 2.9 broadcast_in_dim.26
  116.5 4.8 %all-to-all-start.4 = ((bf16[8,8,18,16,128]{4,3,2,1,0:T(8,128)(2,1)}), bf16[8,8,18,16,128]{4,3,2,1,0:T(8,128)(2,1)}, u32[]{:S(2)}, u32[]{:S(2)}) async-start(bf16[8,8,18,16,128]{4,3,2,1,0:T(8,128)(2,1)} %broadcast_in_dim.26), calls=%async_computation.4 | async-start | bytes 9437184 | tf_op jit(solution)/shard_map/all_to_all | solution.py:592
  122.7 0.9 subtract_select_fusion.idc
  123.6 5.5 %shard_map.243 = bf16[8,128,128]{2,1,0:T(8,128)(2,1)} custom-call(s32[1]{0:T(128)} %bitcast.2.par_ref, bf16[8,128,384]{2,1,0:T(8,128)(2,1)} %copy-done.1, s32[8,128,1]{2,1,0:T(8,128)} %subtract_select_fusion.idc, s32[1,1024]{1,0:T(1,128)} %reshape_select_fusion.idr), custom_call_target="tpu_custom_call" | custom-call | bytes 25830000 | tf_op jit(solution)/shard_map/pallas_call | solution.py:567
  129.1 27.3 %all-to-all-done.4 = bf16[8,8,18,16,128]{4,3,2,1,0:T(8,128)(2,1)} async-done(((bf16[8,8,18,16,128]{4,3,2,1,0:T(8,128)(2,1)}), bf16[8,8,18,16,128]{4,3,2,1,0:T(8,128)(2,1)}, u32[]{:S(2)}, u32[]{:S(2)}) %all-to-all-start.4) | async-done | bytes 4718624 | tf_op jit(solution)/shard_map/all_to_all | solution.py:592
  156.8 4.9 %all-to-all-start.5 = ((bf16[8,128,128]{2,1,0:T(8,128)(2,1)}), bf16[8,128,128]{2,1,0:T(8,128)(2,1)S(1)}, u32[]{:S(2)}, u32[]{:S(2)}) async-start(bf16[8,128,128]{2,1,0:T(8,128)(2,1)} %shard_map.243), calls=%async_computation.5 | async-start | bytes 524288 | tf_op jit(solution)/shard_map/all_to_all | solution.py:717
  162.2 0.8 slice.158.upb
  163.0 6.0 %all-to-all-done.5.back = bf16[8,128,128]{2,1,0:T(8,128)(2,1)S(1)} async-done(((bf16[8,128,128]{2,1,0:T(8,128)(2,1)}), bf16[8,128,128]{2,1,0:T(8,128)(2,1)S(1)}, u32[]{:S(2)}, u32[]{:S(2)}) %all-to-all-start.5) | async-done | bytes 262176 | tf_op jit(solution)/shard_map/all_to_all | solution.py:717
  169.7 8.2 %shard_map.244 = (bf16[128,768]{1,0:T(8,128)(2,1)}, f32[128,768]{1,0:T(8,128)}, bf16[128,768]{1,0:T(8,128)(2,1)}, f32[128,3072]{1,0:T(8,128)}, f32[128,768]{1,0:T(8,128)}) custom-call(s32[1]{0:T(128)} %bitcast.core_ref.core, bf16[128,768]{1,0:T(8,128)(2,1)} %bitcast.74, bf16[8,128,128]{2,1,0:T(8,128)(2,1)} %copy-done.6, f32[4,768]{1,0:T(4,128)} %get-tuple-element.79.vec, ...), custom_call_target="tpu_custom_call" | custom-call | bytes 29520000 | tf_op jit(solution)/shard_map/pallas_call | solution.py:567
  177.9 5.0 %shard_map.245 = (bf16[128,768]{1,0:T(8,128)(2,1)}, bf16[8,128,384]{2,1,0:T(8,128)(2,1)}) custom-call(s32[1]{0:T(128)} %bitcast.core_ref.core, f32[128,768]{1,0:T(8,128)} %get-tuple-element.82.h_ref, f32[4,768]{1,0:T(4,128)} %get-tuple-element.83.vec, bf16[64,18,16,128]{3,2,1,0:T(8,128)(2,1)} %bitcast.12.refs_2_.refs_0_, ...), custom_call_target="tpu_custom_call" | custom-call | bytes 18450000 | tf_op jit(solution)/shard_map/pallas_call | solution.py:567
  183.0 16.1 %all_to_all.82.heads = bf16[8,128,384]{2,1,0:T(8,128)(2,1)} all-to-all(bf16[8,128,384]{2,1,0:T(8,128)(2,1)} %get-tuple-element.84), channel_id=1, replica_groups=mesh['y'=4,'zh'=2,'c'=2,'x'=4,'zl'=2] {'x','zl'}, dimensions={0} | all-to-all | bytes 1572864 | tf_op jit(solution)/shard_map/all_to_all | solution.py:703
  199.1 5.7 %shard_map.246 = bf16[8,128,128]{2,1,0:T(8,128)(2,1)} custom-call(s32[1]{0:T(128)} %bitcast.2.par_ref, bf16[8,128,384]{2,1,0:T(8,128)(2,1)} %all_to_all.82.heads, s32[8,128,1]{2,1,0:T(8,128)} %subtract_select_fusion.idc, s32[1,1024]{1,0:T(1,128)} %reshape_select_fusion.idr), custom_call_target="tpu_custom_call" | custom-call | bytes 25830000 | tf_op jit(solution)/shard_map/pallas_call | solution.py:567
  204.8 3.6 all-to-all-start.7
  208.8 0.8 slice.160.upb
  209.6 5.7 %all-to-all-done.7.back = bf16[8,128,128]{2,1,0:T(8,128)(2,1)S(1)} async-done(((bf16[8,128,128]{2,1,0:T(8,128)(2,1)}), bf16[8,128,128]{2,1,0:T(8,128)(2,1)S(1)}, u32[]{:S(2)}, u32[]{:S(2)}) %all-to-all-start.7) | async-done | bytes 262176 | tf_op jit(solution)/shard_map/all_to_all | solution.py:717
  215.3 0.7 copy-done.7
  216.0 7.6 %shard_map.247 = (bf16[128,768]{1,0:T(8,128)(2,1)}, f32[128,768]{1,0:T(8,128)}, bf16[128,768]{1,0:T(8,128)(2,1)}, f32[128,3072]{1,0:T(8,128)}, bf16[128,768]{1,0:T(8,128)(2,1)}) custom-call(s32[1]{0:T(128)} %bitcast.core_ref.core, f32[128,768]{1,0:T(8,128)} %get-tuple-element.82.h_ref, bf16[8,128,128]{2,1,0:T(8,128)(2,1)} %copy-done.7, ...), custom_call_target="tpu_custom_call" | custom-call | bytes 29520000 | tf_op jit(solution)/shard_map/pallas_call | solution.py:567
  223.7 9.5 %shard_map.248 = (bf16[128,3072]{1,0:T(8,128)(2,1)}, bf16[128,3072]{1,0:T(8,128)(2,1)}, f32[128,768]{1,0:T(8,128)}, bf16[8,128,128]{2,1,0:T(8,128)(2,1)}, f32[4,768]{1,0:T(4,128)}, /*index=5*/f32[1,3072]{1,0:T(1,128)}) custom-call(s32[1]{0:T(128)} %bitcast.core_ref.core, bf16[128,768]{1,0:T(8,128)(2,1)} %bitcast.79, f32[128,3072]{1,0:T(8,128)} %get-tuple-element.90.u_ref, ...), custom_call_target="tpu_custom_call" | custom-call | bytes 36900000 | tf_op jit(solution)/shard_map/pallas_call | solution.py:567
  233.2 3.4 all-to-all-start.8
  236.9 7.9 %shard_map.249 = bf16[16,144,16,128]{3,2,1,0:T(8,128)(2,1)} custom-call(bf16[128,3072]{1,0:T(8,128)(2,1)} %get-tuple-element.93.f_ref, bf16[128,768]{1,0:T(8,128)(2,1)} %bitcast.80, bf16[128,768]{1,0:T(8,128)(2,1)} %get-tuple-element.94.a2_ref, bf16[128,3072]{1,0:T(8,128)(2,1)} %get-tuple-element.95.du_ref), custom_call_target="tpu_custom_call" | custom-call | bytes 33210000 | tf_op jit(solution)/shard_map/pallas_call | solution.py:567
  245.5 8.0 %shard_map.250 = bf16[8,128,384]{2,1,0:T(8,128)(2,1)} custom-call(s32[1]{0:T(128)} %bitcast.2.par_ref, bf16[8,128,384]{2,1,0:T(8,128)(2,1)} %all_to_all.82.heads, bf16[8,128,128]{2,1,0:T(8,128)(2,1)} %copy-done.9, s32[8,128,1]{2,1,0:T(8,128)} %subtract_select_fusion.idc, s32[1,1024]{1,0:T(1,128)} %reshape_select_fusion.idr), custom_call_target="tpu_custom_call" | custom-call | bytes 36900000 | tf_op jit(solution)/shard_map/pallas_call | solution.py:567
  253.5 16.5 %all_to_all.83.back = bf16[8,128,384]{2,1,0:T(8,128)(2,1)} all-to-all(bf16[8,128,384]{2,1,0:T(8,128)(2,1)} %shard_map.250), channel_id=1, replica_groups=mesh['y'=4,'zh'=2,'c'=2,'x'=4,'zl'=2] {'x','zl'}, dimensions={0} | all-to-all | bytes 1572864 | tf_op jit(solution)/shard_map/all_to_all | solution.py:767
  270.0 6.2 %shard_map.251 = (bf16[128,2304]{1,0:T(8,128)(2,1)}, f32[128,768]{1,0:T(8,128)}, f32[4,768]{1,0:T(4,128)}) custom-call(s32[1]{0:T(128)} %bitcast.core_ref.core, bf16[8,128,384]{2,1,0:T(8,128)(2,1)} %all_to_all.83.back, f32[128,768]{1,0:T(8,128)} %get-tuple-element.97.e1_ref, f32[128,768]{1,0:T(8,128)} %get-tuple-element.82.h_ref, ...), custom_call_target="tpu_custom_call" | custom-call | bytes 22140000 | tf_op jit(solution)/shard_map/pallas_call | solution.py:567
  276.2 10.8 %shard_map.252 = (bf16[128,3072]{1,0:T(8,128)(2,1)}, bf16[128,3072]{1,0:T(8,128)(2,1)}, f32[128,768]{1,0:T(8,128)}, bf16[8,128,128]{2,1,0:T(8,128)(2,1)}, f32[4,768]{1,0:T(4,128)}, /*index=5*/f32[1,3072]{1,0:T(1,128)}) custom-call(s32[1]{0:T(128)} %bitcast.core_ref.core, f32[128,768]{1,0:T(8,128)} %get-tuple-element.98.e_ref, ...), custom_call_target="tpu_custom_call" | custom-call | bytes 36900000 | tf_op jit(solution)/shard_map/pallas_call | solution.py:567
  287.0 3.4 all-to-all-start.10
  290.4 8.4 %shard_map.253 = (bf16[64,18,16,128]{3,2,1,0:T(8,128)(2,1)}, bf16[64,18,16,128]{3,2,1,0:T(8,128)(2,1)}) custom-call(s32[1]{0:T(128)} %bitcast.core_ref.core, bf16[128,3072]{1,0:T(8,128)(2,1)} %get-tuple-element.102.f_ref, f32[128,768]{1,0:T(8,128)} %get-tuple-element.98.e_ref, bf16[128,768]{1,0:T(8,128)(2,1)} %get-tuple-element.103.a2_ref, ...), custom_call_target="tpu_custom_call" | custom-call | bytes 33210000 | tf_op jit(solution)/shard_map/pallas_call | solution.py:567
  299.6 8.0 %shard_map.254 = bf16[8,128,384]{2,1,0:T(8,128)(2,1)} custom-call(s32[1]{0:T(128)} %bitcast.2.par_ref, bf16[8,128,384]{2,1,0:T(8,128)(2,1)} %copy-done.1, bf16[8,128,128]{2,1,0:T(8,128)(2,1)} %copy-done.8, s32[8,128,1]{2,1,0:T(8,128)} %subtract_select_fusion.idc, s32[1,1024]{1,0:T(1,128)} %reshape_select_fusion.idr), custom_call_target="tpu_custom_call" | custom-call | bytes 36900000 | tf_op jit(solution)/shard_map/pallas_call | solution.py:567
  307.6 5.7 %all-to-all-start.11 = ((bf16[8,128,384]{2,1,0:T(8,128)(2,1)}), bf16[8,128,384]{2,1,0:T(8,128)(2,1)S(1)}, u32[]{:S(2)}, u32[]{:S(2)}) async-start(bf16[8,128,384]{2,1,0:T(8,128)(2,1)} %shard_map.254), calls=%async_computation.11 | async-start | bytes 1572864 | tf_op jit(solution)/shard_map/all_to_all | solution.py:767
  313.3 8.3 %shard_map.255 = bf16[64,18,16,128]{3,2,1,0:T(8,128)(2,1)} custom-call(bf16[64,18,16,128]{3,2,1,0:T(8,128)(2,1)} %get-tuple-element.105.refs_0_, bf16[64,18,16,128]{3,2,1,0:T(8,128)(2,1)} %collective-permute-done.2.refs_1_), custom_call_target="tpu_custom_call" | custom-call | flops 4194304 | bytes 14155776 | tf_op jit(solution)/shard_map/pallas_call | solution.py:627
  321.6 5.6 %all-to-all-done.11.back = bf16[8,128,384]{2,1,0:T(8,128)(2,1)S(1)} async-done(((bf16[8,128,384]{2,1,0:T(8,128)(2,1)}), bf16[8,128,384]{2,1,0:T(8,128)(2,1)S(1)}, u32[]{:S(2)}, u32[]{:S(2)}) %all-to-all-start.11) | async-done | bytes 786464 | tf_op jit(solution)/shard_map/all_to_all | solution.py:767
  327.2 0.9 copy-done.3
  328.2 4.6 all-to-all-start.12
  332.8 5.1 %shard_map.258 = (bf16[64,9,16,128]{3,2,1,0:T(8,128)(2,1)}, bf16[64,9,16,128]{3,2,1,0:T(8,128)(2,1)}) custom-call(s32[1]{0:T(128)} %bitcast.core_ref.core, bf16[128,768]{1,0:T(8,128)(2,1)} %get-tuple-element.122.a_ref, bf16[128,2304]{1,0:T(8,128)(2,1)} %get-tuple-element.123.g_ref, bf16[128,768]{1,0:T(8,128)(2,1)} %get-tuple-element.124.o_ref, ...), custom_call_target="tpu_custom_call" | custom-call | bytes 18450000 | tf_op jit(solution)/shard_map/pallas_call | solution.py:567
  337.9 1.6 collective-permute-start.5
  339.5 6.0 %shard_map.256 = (bf16[128,2304]{1,0:T(8,128)(2,1)}, f32[128,768]{1,0:T(8,128)}, f32[4,768]{1,0:T(4,128)}) custom-call(s32[1]{0:T(128)} %bitcast.core_ref.core, bf16[8,128,384]{2,1,0:T(8,128)(2,1)} %copy-done.3, f32[128,768]{1,0:T(8,128)} %get-tuple-element.110.e1_ref, bf16[128,768]{1,0:T(8,128)(2,1)} %bitcast.75, f32[4,768]{1,0:T(4,128)} %get-tuple-element.74.vec, ...), custom_call_target="tpu_custom_call" | custom-call | bytes 22140000 | tf_op jit(solution)/shard_map/pallas_call | solution.py:567
  345.6 5.4 %shard_map.257 = (bf16[64,9,16,128]{3,2,1,0:T(8,128)(2,1)}, bf16[64,9,16,128]{3,2,1,0:T(8,128)(2,1)}) custom-call(s32[1]{0:T(128)} %bitcast.core_ref.core, bf16[128,768]{1,0:T(8,128)(2,1)} %get-tuple-element.87.a_ref, bf16[128,2304]{1,0:T(8,128)(2,1)} %get-tuple-element.112.g_ref, bf16[128,768]{1,0:T(8,128)(2,1)} %get-tuple-element.113.o_ref, ...), custom_call_target="tpu_custom_call" | custom-call | bytes 18450000 | tf_op jit(solution)/shard_map/pallas_call | solution.py:567
  355.2 0.8 select_bitcast_fusion
  356.5 1.2 collective-permute-done.4.refs_3_
  358.4 8.5 %shard_map.259 = bf16[64,19,16,128]{3,2,1,0:T(8,128)(2,1)} custom-call(bf16[64,9,16,128]{3,2,1,0:T(8,128)(2,1)} %get-tuple-element.114.refs_0_, bf16[64,9,16,128]{3,2,1,0:T(8,128)(2,1)} %collective-permute-done.3.refs_1_, bf16[64,1,16,128]{3,2,1,0:T(8,128)(2,1)} %get-tuple-element.138.refs_2_, bf16[64,1,16,128]{3,2,1,0:T(8,128)(2,1)} %copy-done.10, ...), custom_call_target="tpu_custom_call" | custom-call | flops 4194304 | bytes 14942208 | tf_op jit(solution)/shard_map/pallas_call | solution.py:627
  366.9 3.1 reduce_sum.34
  370.0 12.0 %reduce-scatter.2.cloned.1.call-done = bf16[1,144,16,128]{3,2,1,0:T(8,128)(2,1)} async-done(((bf16[16,144,16,128]{3,2,1,0:T(8,128)(2,1)}), bf16[1,144,16,128]{3,2,1,0:T(8,128)(2,1)}) %reduce-scatter.2.cloned.1.call-update) | async-done | bytes 589840 | tf_op jit(solution)/shard_map/reduce_scatter | solution.py:751
  382.0 36.8 %all_to_all.84 = bf16[8,8,19,16,128]{4,3,2,1,0:T(8,128)(2,1)} all-to-all(bf16[8,8,19,16,128]{4,3,2,1,0:T(8,128)(2,1)} %bitcast.69), channel_id=1, replica_groups={{0,2,1,3,32,34,33,35},{6,4,7,5,38,36,39,37},{17,19,16,18,49,51,48,50},{..., dimensions={0} | all-to-all | bytes 9961472 | tf_op jit(solution)/shard_map/all_to_all | solution.py:644
  418.7 3.2 reduce_sum.35
  422.1 21.4 %all_to_all.85.parts = bf16[8,37,16,128]{3,2,1,0:T(8,128)(2,1)} all-to-all(bf16[8,37,16,128]{3,2,1,0:T(8,128)(2,1)S(1)} %pad_maximum_fusion), channel_id=1, replica_groups={{0,6,17,23,96,102,113,119},{2,4,19,21,98,100,115,117},{1,7,16,22,97,103..., dimensions={0} | all-to-all | bytes 2424832 | tf_op jit(solution)/shard_map/all_to_all | solution.py:795
  443.5 2.7 shard_map.260
  446.2 3.5 all-to-all-start.15
  449.7 0.8 slice.191
  450.5 1.0 fusion.29
  455.1 3.9 all-to-all-done.15.got
  459.0 0.9 copy-done.4
  459.9 2.3 shard_map.261
  (139 shorter events, 15.7 us)
Async XLA Ops:
  7.2 8.3 %copy-start.19 = (bf16[2,2,6]{2,1,0:T(2,128)(2,1)S(1)}, bf16[2,2,6]{2,1,0:T(2,128)(2,1)}, u32[]{:S(2)}) copy-start(bf16[2,2,6]{2,1,0:T(2,128)(2,1)} %param.21) | copy-start | bytes 148
  7.2 8.3 %copy-start.20 = (bf16[2,2,6]{2,1,0:T(2,128)(2,1)S(1)}, bf16[2,2,6]{2,1,0:T(2,128)(2,1)}, u32[]{:S(2)}) copy-start(bf16[2,2,6]{2,1,0:T(2,128)(2,1)} %param.22) | copy-start | bytes 148
  7.2 8.4 %copy-start.21 = (bf16[2,2,6]{2,1,0:T(2,128)(2,1)S(1)}, bf16[2,2,6]{2,1,0:T(2,128)(2,1)}, u32[]{:S(2)}) copy-start(bf16[2,2,6]{2,1,0:T(2,128)(2,1)} %param.24) | copy-start | bytes 148
  7.2 8.5 %copy-start.22 = (bf16[2,2,6]{2,1,0:T(2,128)(2,1)S(1)}, bf16[2,2,6]{2,1,0:T(2,128)(2,1)}, u32[]{:S(2)}) copy-start(bf16[2,2,6]{2,1,0:T(2,128)(2,1)} %param.26) | copy-start | bytes 148
  7.2 8.6 %copy-start.23 = (bf16[2,24]{1,0:T(2,128)(2,1)S(1)}, bf16[2,24]{1,0:T(2,128)(2,1)}, u32[]{:S(2)}) copy-start(bf16[2,24]{1,0:T(2,128)(2,1)} %param.28) | copy-start | bytes 292
  9.7 21.1 %all-to-all-start = ((bf16[8,31,16,128]{3,2,1,0:T(8,128)(2,1)}), bf16[8,31,16,128]{3,2,1,0:T(8,128)(2,1)S(1)}, u32[]{:S(2)}, u32[]{:S(2)}) async-start(bf16[8,31,16,128]{3,2,1,0:T(8,128)(2,1)} %shard_map.239), calls=%async_computation | async-start | bytes 2031616 | tf_op jit(solution)/shard_map/all_to_all | solution.py:672
  15.4 98.2 %all-gather.5.cloned.1.call-start = ((), (), s32[]{:S(2)}) async-start(), calls=%async_computation.18 | async-start | bytes 5013504 | tf_op jit(solution)/shard_map/all_gather | solution.py:677
  30.8 1.0 copy-start.2
  34.1 181.2 %all-gather.7.cloned.1.call-start = ((), (), s32[]{:S(2)}) async-start(), calls=%async_computation.19 | async-start | bytes 10027008 | tf_op jit(solution)/shard_map/all_gather | solution.py:701
  81.5 5.0 %copy-start = (bf16[8,8,10,16,128]{4,3,2,1,0:T(8,128)(2,1)}, bf16[8,8,10,16,128]{4,3,2,1,0:T(8,128)(2,1)S(1)}, u32[]{:S(2)}) copy-start(bf16[8,8,10,16,128]{4,3,2,1,0:T(8,128)(2,1)S(1)} %all_to_all.81) | copy-start | bytes 7864324
  81.5 5.0 %collective-permute-start = (bf16[64,10,16,128]{3,2,1,0:T(8,128)(2,1)S(1)}, bf16[64,10,16,128]{3,2,1,0:T(8,128)(2,1)}, u32[]{:S(2)}, u32[]{:S(2)}) collective-permute-start(bf16[64,10,16,128]{3,2,1,0:T(8,128)(2,1)S(1)} %bitcast.63), channel_id=1, source_target_pairs={{0,8},{8,0},{1,9},{9,1},{2,10},{10,2},{3,11},{11,3},{4,12},{12,4},... | collective-permute-start | bytes 7864328 | tf_op jit(solution)/shard_map/ppermute | solution.py:600
  95.8 17.8 %all-to-all-start.3 = ((bf16[8,128,384]{2,1,0:T(8,128)(2,1)}), bf16[8,128,384]{2,1,0:T(8,128)(2,1)S(1)}, u32[]{:S(2)}, u32[]{:S(2)}) async-start(bf16[8,128,384]{2,1,0:T(8,128)(2,1)} %get-tuple-element.75), calls=%async_computation.3 | async-start | bytes 1572864 | tf_op jit(solution)/shard_map/all_to_all | solution.py:703
  113.6 2.9 copy-start.1
  116.5 4.8 %copy-start.18 = (s32[48]{0:T(128)S(1)}, s32[48]{0:T(128)}, u32[]{:S(2)}) copy-start(s32[48]{0:T(128)} %param.19) | copy-start | bytes 580
  116.5 4.8 %copy-start.24 = (s32[48]{0:T(128)S(1)}, s32[48]{0:T(128)}, u32[]{:S(2)}) copy-start(s32[48]{0:T(128)} %param.20) | copy-start | bytes 580
  116.5 4.9 %copy-start.25 = (s32[48]{0:T(128)S(1)}, s32[48]{0:T(128)}, u32[]{:S(2)}) copy-start(s32[48]{0:T(128)} %param.18) | copy-start | bytes 580
  116.5 39.9 %all-to-all-start.4 = ((bf16[8,8,18,16,128]{4,3,2,1,0:T(8,128)(2,1)}), bf16[8,8,18,16,128]{4,3,2,1,0:T(8,128)(2,1)}, u32[]{:S(2)}, u32[]{:S(2)}) async-start(bf16[8,8,18,16,128]{4,3,2,1,0:T(8,128)(2,1)} %broadcast_in_dim.26), calls=%async_computation.4 | async-start | bytes 9437184 | tf_op jit(solution)/shard_map/all_to_all | solution.py:592
  121.3 35.1 %copy-start.11 = (f32[128,256]{1,0:T(8,128)S(1)}, f32[128,256]{1,0:T(8,128)}, u32[]{:S(2)}) copy-start(f32[128,256]{1,0:T(8,128)} %get-tuple-element.80) | copy-start | bytes 393220
  156.4 12.6 %collective-permute-start.1 = (bf16[64,18,16,128]{3,2,1,0:T(8,128)(2,1)}, bf16[64,18,16,128]{3,2,1,0:T(8,128)(2,1)}, u32[]{:S(2)}, u32[]{:S(2)}) collective-permute-start(bf16[64,18,16,128]{3,2,1,0:T(8,128)(2,1)} %bitcast.12.refs_2_.refs_0_), channel_id=1, source_target_pairs={{0,8},{8,0},{1,9},{9,1},{2,10},{10,2},{3,11},{11,3},{4,12},{12,4},... | collective-permute-start | bytes 14155784 | tf_op jit(solution)/shard_map/ppermute | solution.py:600
  156.8 12.2 %all-to-all-start.5 = ((bf16[8,128,128]{2,1,0:T(8,128)(2,1)}), bf16[8,128,128]{2,1,0:T(8,128)(2,1)S(1)}, u32[]{:S(2)}, u32[]{:S(2)}) async-start(bf16[8,128,128]{2,1,0:T(8,128)(2,1)} %shard_map.243), calls=%async_computation.5 | async-start | bytes 524288 | tf_op jit(solution)/shard_map/all_to_all | solution.py:717
  169.0 0.7 copy-start.6
  204.8 10.5 %all-to-all-start.7 = ((bf16[8,128,128]{2,1,0:T(8,128)(2,1)}), bf16[8,128,128]{2,1,0:T(8,128)(2,1)S(1)}, u32[]{:S(2)}, u32[]{:S(2)}) async-start(bf16[8,128,128]{2,1,0:T(8,128)(2,1)} %shard_map.246), calls=%async_computation.7 | async-start | bytes 524288 | tf_op jit(solution)/shard_map/all_to_all | solution.py:717
  215.3 0.7 copy-start.7
  233.2 11.6 %all-to-all-start.8 = ((bf16[8,128,128]{2,1,0:T(8,128)(2,1)}), bf16[8,128,128]{2,1,0:T(8,128)(2,1)S(1)}, u32[]{:S(2)}, u32[]{:S(2)}) async-start(bf16[8,128,128]{2,1,0:T(8,128)(2,1)} %get-tuple-element.92), calls=%async_computation.8 | async-start | bytes 524288 | tf_op jit(solution)/shard_map/all_to_all | solution.py:746
  236.6 145.3 %reduce-scatter.2.cloned.1.call-start = ((), (), s32[]{:S(2)}) async-start(), calls=%async_computation.17 | async-start | bytes 10027008 | tf_op jit(solution)/shard_map/reduce_scatter | solution.py:751
  244.8 0.7 copy-start.9
  287.0 11.9 %all-to-all-start.10 = ((bf16[8,128,128]{2,1,0:T(8,128)(2,1)}), bf16[8,128,128]{2,1,0:T(8,128)(2,1)S(1)}, u32[]{:S(2)}, u32[]{:S(2)}) async-start(bf16[8,128,128]{2,1,0:T(8,128)(2,1)} %get-tuple-element.101), calls=%async_computation.10 | async-start | bytes 524288 | tf_op jit(solution)/shard_map/all_to_all | solution.py:746
  298.9 0.7 copy-start.8
  298.9 14.4 %collective-permute-start.2 = (bf16[64,18,16,128]{3,2,1,0:T(8,128)(2,1)}, bf16[64,18,16,128]{3,2,1,0:T(8,128)(2,1)}, u32[]{:S(2)}, u32[]{:S(2)}) collective-permute-start(bf16[64,18,16,128]{3,2,1,0:T(8,128)(2,1)} %get-tuple-element.108), channel_id=1, source_target_pairs={{0,8},{8,0},{1,9},{9,1},{2,10},{10,2},{3,11},{11,3},{4,12},{12,4},... | collective-permute-start | bytes 14155784 | tf_op jit(solution)/shard_map/ppermute | solution.py:600
  307.6 19.6 %all-to-all-start.11 = ((bf16[8,128,384]{2,1,0:T(8,128)(2,1)}), bf16[8,128,384]{2,1,0:T(8,128)(2,1)S(1)}, u32[]{:S(2)}, u32[]{:S(2)}) async-start(bf16[8,128,384]{2,1,0:T(8,128)(2,1)} %shard_map.254), calls=%async_computation.11 | async-start | bytes 1572864 | tf_op jit(solution)/shard_map/all_to_all | solution.py:767
  327.2 0.9 copy-start.3
  328.2 38.7 %all-to-all-start.12 = ((bf16[8,8,18,16,128]{4,3,2,1,0:T(8,128)(2,1)}), bf16[8,8,18,16,128]{4,3,2,1,0:T(8,128)(2,1)}, u32[]{:S(2)}, u32[]{:S(2)}) async-start(bf16[8,8,18,16,128]{4,3,2,1,0:T(8,128)(2,1)} %bitcast.70), calls=%async_computation.12 | async-start | bytes 9437184 | tf_op jit(solution)/shard_map/all_to_all | solution.py:644
  337.9 18.6 %collective-permute-start.5 = (bf16[64,9,16,128]{3,2,1,0:T(8,128)(2,1)}, bf16[64,9,16,128]{3,2,1,0:T(8,128)(2,1)S(1)}, u32[]{:S(2)}, u32[]{:S(2)}) collective-permute-start(bf16[64,9,16,128]{3,2,1,0:T(8,128)(2,1)} %get-tuple-element.126), channel_id=1, source_target_pairs={{0,8},{8,0},{1,9},{9,1},{2,10},{10,2},{3,11},{11,3},{4,12},{12,4},... | collective-permute-start | bytes 7077896 | tf_op jit(solution)/shard_map/ppermute | solution.py:600
  339.5 11.8 %copy-start.13 = (f32[1,3072]{1,0:T(1,128)S(1)}, f32[1,3072]{1,0:T(1,128)}, u32[]{:S(2)}) copy-start(f32[1,3072]{1,0:T(1,128)} %get-tuple-element.121) | copy-start | bytes 36868
  339.5 12.7 %copy-start.12 = (f32[4,768]{1,0:T(4,128)S(1)}, f32[4,768]{1,0:T(4,128)}, u32[]{:S(2)}) copy-start(f32[4,768]{1,0:T(4,128)} %get-tuple-element.119) | copy-start | bytes 36868
  339.5 12.8 %copy-start.16 = (f32[1,3072]{1,0:T(1,128)S(1)}, f32[1,3072]{1,0:T(1,128)}, u32[]{:S(2)}) copy-start(f32[1,3072]{1,0:T(1,128)} %get-tuple-element.120) | copy-start | bytes 36868
  339.5 13.7 %copy-start.15 = (f32[4,768]{1,0:T(4,128)S(1)}, f32[4,768]{1,0:T(4,128)}, u32[]{:S(2)}) copy-start(f32[4,768]{1,0:T(4,128)} %get-tuple-element.118) | copy-start | bytes 36868
  345.6 8.5 %copy-start.14 = (f32[4,768]{1,0:T(4,128)S(1)}, f32[4,768]{1,0:T(4,128)}, u32[]{:S(2)}) copy-start(f32[4,768]{1,0:T(4,128)} %get-tuple-element.117) | copy-start | bytes 36868
  345.6 8.5 %copy-start.17 = (f32[4,768]{1,0:T(4,128)S(1)}, f32[4,768]{1,0:T(4,128)}, u32[]{:S(2)}) copy-start(f32[4,768]{1,0:T(4,128)} %get-tuple-element.116) | copy-start | bytes 36868
  345.6 9.3 %copy-start.26 = (bf16[128,128]{1,0:T(8,128)(2,1)S(1)}, bf16[128,128]{1,0:T(8,128)(2,1)}, u32[]{:S(2)}) copy-start(bf16[128,128]{1,0:T(8,128)(2,1)} %constant.45.clone) | copy-start | bytes 98308
  351.0 6.7 %collective-permute-start.3 = (bf16[64,9,16,128]{3,2,1,0:T(8,128)(2,1)}, bf16[64,9,16,128]{3,2,1,0:T(8,128)(2,1)}, u32[]{:S(2)}, u32[]{:S(2)}) collective-permute-start(bf16[64,9,16,128]{3,2,1,0:T(8,128)(2,1)} %get-tuple-element.115), channel_id=1, source_target_pairs={{0,8},{8,0},{1,9},{9,1},{2,10},{10,2},{3,11},{11,3},{4,12},{12,4},... | collective-permute-start | bytes 7077896 | tf_op jit(solution)/shard_map/ppermute | solution.py:600
  356.0 1.6 collective-permute-start.4
  356.5 1.4 copy-start.5
  357.7 0.7 copy-start.10
  446.2 12.8 %all-to-all-start.15 = ((bf16[8,23,16,128]{3,2,1,0:T(8,128)(2,1)}), bf16[8,23,16,128]{3,2,1,0:T(8,128)(2,1)S(1)}, u32[]{:S(2)}, u32[]{:S(2)}) async-start(bf16[8,23,16,128]{3,2,1,0:T(8,128)(2,1)} %get-tuple-element.130), calls=%async_computation.16 | async-start | bytes 1507328 | tf_op jit(solution)/shard_map/all_to_all | solution.py:798
  459.0 0.9 copy-start.4
Sparse Core Ops, SparseCore 0:
  34.2 64.7 all-gather.4
  101.5 111.4 all-gather.6
  244.9 136.9 reduce-scatter.1

commit v6 on v5

--- a/solution.py
+++ b/solution.py
@@ -84,21 +84,28 @@
 FF_ORDER = ff_order()
 
 
+def slot_at(y, z, x, core):
+    n = 0
+    for v, m in ((y, 4), (z, 2), (x, 1)):
+        bit_a = core * (v & 1) + (1 - core) * (v >> 1)
+        bit_b = core * (v >> 1) + (1 - core) * ((v ^ (v >> 1)) & 1)
+        n = n + m * (8 * bit_b + bit_a)
+    return n
+
+
 def fetch_cube(core_ref, mine, theirs, offset, w, sem, low, high):
     core = core_ref[0]
 
-    def step(n, carry):
+    def step(k, carry):
+        y, z, x = (k >> 2) & 3, k & 3, (low >> 1) + (k >> 4)
         for src, own in ((mine, core), (theirs, 1 - core)):
-            row, triple = place(n, own)
-
-            @pl.when((triple >= low) & (triple < high))
-            def _():
-                pltpu.make_async_copy(
-                    src.at[n, pl.ds(offset, 9)], w.at[row, pl.ds((triple - low) * 9, 9)], sem).start()
-
+            row = (y * 2 + (z >> 1)) * 2 + own
+            first = ((k >> 4) * 2 + (z & 1)) * 9
+            pltpu.make_async_copy(
+                src.at[slot_at(y, z, x, own), pl.ds(offset, 9)], w.at[row, pl.ds(first, 9)], sem).start()
         return carry
 
-    lax.fori_loop(0, 64, step, 0)
+    lax.fori_loop(0, 8 * (high - low), step, 0, unroll=4)
 
 
 COMES = {(0, 0): ("cube", 0), (0, 1): ("cube", 0), (0, 2): ("plain", 0),
@@ -192,6 +199,10 @@
 def project_kernel(layer, core, h_ref, vec, *refs):
     src, (a1_ref, pay_ref, w, sem) = sources_of(layer, (0,), refs)
     fetch(layer, 0, core, src[0], w, sem, 0, 6)
+    project(h_ref, vec, a1_ref, pay_ref, w, sem)
+
+
+def project(h_ref, vec, a1_ref, pay_ref, w, sem):
     xh, _ = norm_parts(h_ref[...].astype(f32))
     a1 = (xh * vec[0:1] + vec[1:2]).astype(bf16)
     a1_ref[...] = a1
@@ -281,11 +292,13 @@
     out[:, :, 256:384] = dv.astype(bf16).reshape(8, TOK, 128)
 
 
-def forward_kernel(layer, core, h_ref, back, vec, upb, *refs):
-    src, (o_ref, h1_ref, a2_ref, u_ref, next_ref, wo, wu, wd, sems) = sources_of(layer, (0, 1, 2), refs)
+def fetch_forward(layer, core, src, wo, wu, wd, sems):
     fetch(layer, 0, core, src[0], wo, sems.at[0], 6, 8)
     fetch(layer, 1, core, src[1], wu, sems.at[1], 0, 8)
     fetch(layer, 2, core, src[2], wd, sems.at[2], 0, 8)
+
+
+def forward(h_ref, back, vec, upb, o_ref, h1_ref, a2_ref, u_ref, next_ref, wo, wu, wd, sems):
     o = unwindow(lambda d: back[d].astype(f32)).astype(bf16)
     o_ref[...] = o
     arrived(wo, sems.at[0])
@@ -309,11 +322,29 @@
         next_ref[:, c] = (h1[:, c] + mul(f, w) + vec[3:4, c]).astype(next_ref.dtype)
 
 
-def backward_kernel(layer, core, e_ref, u_ref, h1_ref, vec, *refs):
-    src, (f_ref, du_ref, e1_ref, pay_ref, small_ref, upb_ref, wo, wu, wd, sems) = sources_of(layer, (0, 1, 2), refs)
+def forward_kernel(core, h_ref, back, vec, upb, *refs):
+    src, refs = sources_of(1, (0, 1, 2), refs)
+    fetch_forward(1, core, src, *refs[5:])
+    forward(h_ref, back, vec, upb, *refs)
+
+
+def forward_project_kernel(core, h_ref, back, vec, upb, vec_next, *refs):
+    src, refs = sources_of(0, (0, 1, 2), refs)
+    src_next, refs = sources_of(1, (0,), refs)
+    outs, (a1_ref, pay_ref), ws, (w, sem) = refs[:5], refs[5:7], refs[7:11], refs[11:]
+    fetch_forward(0, core, src, *ws)
+    fetch(1, 0, core, src_next[0], w, sem, 0, 6)
+    forward(h_ref, back, vec, upb, *outs, *ws)
+    project(outs[4], vec_next, a1_ref, pay_ref, w, sem)
+
+
+def fetch_backward(layer, core, src, wo, wu, wd, sems):
     fetch(layer, 2, core, src[2], wd, sems.at[2], 0, 8)
     fetch(layer, 1, core, src[1], wu, sems.at[1], 0, 8)
     fetch(layer, 0, core, src[0], wo, sems.at[0], 6, 8)
+
+
+def backward(e_ref, u_ref, h1_ref, vec, f_ref, du_ref, e1_ref, pay_ref, small_ref, upb_ref, wo, wu, wd, sems):
     e = e_ref[...].astype(f32)
     e2 = e.astype(bf16)
     arrived(wd, sems.at[2])
@@ -348,9 +379,13 @@
         pay_ref[d] = win.astype(bf16)
 
 
-def back_project_kernel(layer, core, back, e1_ref, h_ref, vec, *refs):
-    src, (g_ref, e_ref, small_ref, w, sem) = sources_of(layer, (0,), refs)
-    fetch(layer, 0, core, src[0], w, sem, 0, 6)
+def backward_kernel(core, e_ref, u_ref, h1_ref, vec, *refs):
+    src, refs = sources_of(1, (0, 1, 2), refs)
+    fetch_backward(1, core, src, *refs[6:])
+    backward(e_ref, u_ref, h1_ref, vec, *refs)
+
+
+def back_project(back, e1_ref, h_ref, vec, g_ref, e_ref, small_ref, w, sem):
     for part in range(3):
         got = unwindow(lambda d: back[d, :, 128 * part : 128 * part + 128].astype(f32)).astype(bf16)
         g_ref[:, D * part : D * part + D] = got
@@ -366,6 +401,22 @@
     e_ref[...] = e1_ref[...] + norm_back(cot, vec[0:1], xh, r)
 
 
+def back_project_kernel(core, back, e1_ref, h_ref, vec, *refs):
+    src, refs = sources_of(0, (0,), refs)
+    fetch(0, 0, core, src[0], *refs[3:], 0, 6)
+    back_project(back, e1_ref, h_ref, vec, *refs)
+
+
+def back_both_kernel(core, back, e1_ref, h_ref, vec, u_ref, h1_ref, vec_next, *refs):
+    src, refs = sources_of(1, (0,), refs)
+    src_next, refs = sources_of(0, (0, 1, 2), refs)
+    outs, outs_next, (w, sem), ws = refs[:3], refs[3:9], refs[9:11], refs[11:]
+    fetch(1, 0, core, src[0], w, sem, 0, 6)
+    fetch_backward(0, core, src_next, *ws)
+    back_project(back, e1_ref, h_ref, vec, *outs, w, sem)
+    backward(outs[1], u_ref, h1_ref, vec_next, *outs_next, *ws)
+
+
 def cube_store(core, stage, first_tile, triple, k, rows):
     for row in range(16):
         target = row & 1
@@ -420,14 +471,32 @@
     ship(((stage.at[0], keep), (stage.at[1], send)), sem)
 
 
-def grad_mlp_plain(f_ref, e_ref, a2_ref, du_ref, out, stage, sem):
-    wide_grad(a2_ref[...].T, du_ref[...], 0, lambda u, rows: plain_store(stage, u, rows))
-    tall_grad(f_ref[...].T, low(e_ref), lambda u, rows: plain_store(stage, 24 + u, rows))
-    ship(((stage, out),), sem)
+def grad_mlp_split(core_ref, f_ref, e_ref, a2_ref, du_ref, keep, send, plain, stage, wide, sem):
+    core = core_ref[0]
+
+    def put(u, rows):
+        triple, k = divmod(u, 3)
+        if k == 2:
+            cube_store(core, stage, 0, triple, 0, rows)
+        else:
+            plain_store(wide, 2 * triple + k, rows)
+
+    wide_grad(a2_ref[...].T, du_ref[...], 0, put)
+    tall_grad(f_ref[...].T, low(e_ref), lambda u, rows: plain_store(wide, 16 + u, rows))
+    ship(((stage.at[0], keep), (stage.at[1], send), (wide, plain)), sem)
+
+
+def out_place(l, group, u):
+    cube = ((0, 0), (1, 0), (0, 1), (0, 2))
+    triple, k = divmod(u, 3)
+    if (l, group) in cube:
+        return triple, 3 * cube.index((l, group)) + k
+    if group == 2:
+        return None, 29 + u
+    return (triple, 12) if k == 2 else (None, 13 + 2 * triple + k)
 
 
 CUBE_IN, PLAIN_IN = ((0, 0), (0, 1), (1, 0)), ((0, 2), (1, 1), (1, 2))
-CUBE_OUT, PLAIN_OUT = ((0, 0), (1, 0), (0, 1), (0, 2)), ((1, 1), (1, 2))
 
 
 def dense(pieces, tiles):
@@ -477,8 +546,15 @@
         fourth[3 * u : 3 * u + 3] = join(plain, 24 + u)
 
 
-def smalls_kernel(core_ref, mine, theirs, *refs):
-    vecs, (few, buf, sem) = refs[:4], refs[4:]
+def first_project_kernel(core, h_ref, mine, theirs, *refs):
+    outs, (w, sem, buf, small_sem) = refs[:7], refs[7:]
+    vecs = outs[2:]
+    fetch(0, 0, core, (mine, theirs), w, sem, 0, 6)
+    small_parameters(core, mine, theirs, vecs[:4], vecs[4], buf, small_sem)
+    project(h_ref, vecs[0], outs[0], outs[1], w, sem)
+
+
+def small_parameters(core_ref, mine, theirs, vecs, few, buf, sem):
     core = core_ref[0]
 
     def step(n, carry):
@@ -513,34 +589,30 @@
         small = small + parts[k, 9].astype(f32)[0:2]
     few[...] = small
     units_of = []
-    for u in range(12):
+    for u in range(13):
         tile = 3 * u if u < 3 else 3 * u + 1
         rows = jnp.zeros((48, 128), f32)
         for k in range(8):
             rows = rows + parts[k, tile : tile + 3].reshape(48, 128).astype(f32)
         units_of.append(rows)
-    for u in range(48):
+    for u in range(40):
         units_of.append(total[3 * u : 3 * u + 3].reshape(48, 128).astype(f32))
     for d in range(8):
-        out[d] = dense([rows[6 * d : 6 * d + 6] for rows in units_of], 23)
+        out[d] = dense([rows[6 * d : 6 * d + 6] for rows in units_of], 20)
 
 
 def unpack_kernel(got, order, g_in, g_out, g_up, g_down):
     cube = [got[d, 0:5].reshape(80, 128).astype(f32) for d in range(8)]
-    plain = got[0].reshape(368, 128).astype(f32)
+    plain = got[0].reshape(320, 128).astype(f32)
     for d in range(1, 8):
-        plain = plain + got[d].reshape(368, 128).astype(f32)
+        plain = plain + got[d].reshape(320, 128).astype(f32)
     stack = []
     for l in range(LAYERS):
         for group in range(3):
             rows = []
             for u in range(24):
-                if (l, group) in CUBE_OUT:
-                    k = 6 * (3 * CUBE_OUT.index((l, group)) + u % 3)
-                    rows.append(cube[u // 3][k : k + 6])
-                else:
-                    k = 6 * (12 + 24 * PLAIN_OUT.index((l, group)) + u)
-                    rows.append(plain[k : k + 6])
+                triple, k = out_place(l, group, u)
+                rows.append((plain if triple is None else cube[triple])[6 * k : 6 * k + 6])
             if group == 0:
                 g_in[:, l] = jnp.concatenate(rows[:18], axis=1)
                 g_out[:, l] = jnp.concatenate(rows[18:], axis=1)
@@ -584,11 +656,11 @@
 
 
 def after(values, *others):
-    return lax.optimization_barrier((values,) + others)[0]
-
-
-def copies(values, groups):
-    many = jnp.broadcast_to(values[None], (8,) + values.shape)
+    return lax.optimization_barrier((values,) + others)[0] if others else values
+
+
+def copies(values, groups, *others):
+    many = after(jnp.broadcast_to(values[None], (8,) + values.shape), *others)
     return lax.all_to_all(many, ALL, 0, 0, axis_index_groups=groups)
 
 
@@ -600,8 +672,8 @@
     return lax.ppermute(values, "c", [(0, 1), (1, 0)])
 
 
-def cube_copies(shards):
-    return copies(shards, GROUPS_B).reshape((64,) + shards.shape[1:])
+def cube_copies(shards, *others):
+    return copies(shards, GROUPS_B, *others).reshape((64,) + shards.shape[1:])
 
 
 def spread(shards):
@@ -677,56 +749,66 @@
     down_0 = lax.all_gather(third, DATA, axis=0, tiled=False)
     shards = copies(first, GROUPS_A)
     group_e, shards = spread(shards[:, :10]), shards[:, 10:]
+    shards = jnp.broadcast_to(shards[None], (8,) + shards.shape)
+    group_e = tuple(after(v, shards) for v in group_e)
     sources = {(0, 0): group_e, (0, 2): (down_0,)}
 
-    *vecs, few = call(
-        smalls_kernel, [((4, D), f32)] * 4 + [((128, 256), f32)],
-        [(core, "s"), (group_e[0], "a"), (group_e[1], "a")],
-        [pltpu.VMEM((128, 16, 128), bf16), DMA], us=2)
+    a1, pay, *vecs, few = call(
+        first_project_kernel,
+        [((TOK, D), bf16), ((8, TOK, 384), bf16)] + [((4, D), f32)] * 4 + [((128, 256), f32)],
+        [(core, "s"), (hidden_in[0], "v"), (group_e[0], "a"), (group_e[1], "a")],
+        [w_scratch(18), DMA, pltpu.VMEM((128, 16, 128), bf16), DMA], us=7)
     ups = few[:, 96:144].reshape(16, 8, 2, 4, 6).transpose(2, 0, 3, 1, 4).reshape(2, 4 * D)
 
     def weights(l, all_groups):
         return [(w, "a") for group in range(3 if all_groups else 1) for w in sources[l, group]]
 
-    hidden = hidden_in[0]
-    stored = []
-    for l in range(LAYERS):
-        a1, pay = call(
-            functools.partial(project_kernel, l),
-            [((TOK, D), bf16), ((8, TOK, 384), bf16)],
-            [(core, "s"), (hidden, "v"), (vecs[2 * l], "v")] + weights(l, False),
-            [w_scratch(18), DMA],
-            us=5)
-        if l == 0:
-            both_1 = lax.all_gather(after(fourth, a1), DATA, axis=0, tiled=False)
-            sources[1, 1] = sources[1, 2] = (both_1,)
-        heads = lax.all_to_all(pay, CTX, 0, 0)
-        if l == 0:
-            mine = cube_copies(after(shards, heads, down_0))
-        (mix,) = call(
-            attend_kernel,
-            [((8, TOK, 128), bf16)],
-            [(par, "s"), (heads, "v"), (idc, "v"), (idr, "v")],
-            us=7)
-        if l == 0:
-            theirs = swap_core(after(mine, mix))
-            for key in CUBE_IN[1:]:
-                sources[key] = (mine, theirs)
-        if l == 0:
-            mix = after(mix, mine)
-        back = lax.all_to_all(mix, CTX, 0, 0)
-        o, h1, a2, u, following = call(
-            functools.partial(forward_kernel, l),
-            [((TOK, D), bf16), ((TOK, D), f32), ((TOK, D), bf16), ((TOK, 4 * D), f32),
-             ((TOK, D), f32 if l == 0 else bf16)],
-            [(core, "s"), (hidden, "v"), (back, "v"), (vecs[2 * l + 1], "v"),
-             (ups[l : l + 1], "v")] + weights(l, True),
-            [w_scratch(6), w_scratch(24), w_scratch(24), DMA((3,))],
-            us=8)
-        stored.append((hidden, a1, heads, o, h1, a2, u))
-        hidden = following
-
-    def grad_joint(g, a1, o, e1):
+    def attend(heads):
+        return call(attend_kernel, [((8, TOK, 128), bf16)],
+                    [(par, "s"), (heads, "v"), (idc, "v"), (idr, "v")], us=6)[0]
+
+    def attend_back(heads, cot):
+        return call(attend_back_kernel, [((8, TOK, 384), bf16)],
+                    [(par, "s"), (heads, "v"), (cot, "v"), (idc, "v"), (idr, "v")],
+                    [pltpu.VMEM((2, SLOTS, 64), f32)] * 2, us=8)[0]
+
+    def exchange(values):
+        return lax.all_to_all(values, CTX, 0, 0)
+
+    block_scratch = [w_scratch(6), w_scratch(24), w_scratch(24), DMA((3,))]
+    project_scratch = [w_scratch(18), DMA]
+    project_outs = [((TOK, D), bf16), ((8, TOK, 384), bf16)]
+    forward_outs = [((TOK, D), bf16), ((TOK, D), f32), ((TOK, D), bf16), ((TOK, 4 * D), f32)]
+    backward_outs = [((TOK, 4 * D), bf16), ((TOK, 4 * D), bf16), ((TOK, D), f32), ((8, TOK, 128), bf16),
+                     ((4, D), f32), ((1, 4 * D), f32)]
+    back_project_outs = [((TOK, 3 * D), bf16), ((TOK, D), f32), ((4, D), f32)]
+
+    hidden_0 = hidden_in[0]
+    both_1 = lax.all_gather(after(fourth, a1), DATA, axis=0, tiled=False)
+    sources[1, 1] = sources[1, 2] = (both_1,)
+    a1 = [a1, None]
+    heads_0 = exchange(pay)
+    mine = lax.all_to_all(after(shards, heads_0, down_0), ALL, 0, 0, axis_index_groups=GROUPS_B)
+    mine = mine.reshape((64,) + mine.shape[2:])
+    mix = attend(heads_0)
+    theirs = swap_core(after(mine, mix))
+    sources[0, 1] = sources[1, 0] = (mine, theirs)
+    back = exchange(after(mix, mine))
+    o_0, h1_0, a2_0, u_0, hidden_1, a1[1], pay = call(
+        forward_project_kernel,
+        forward_outs + [((TOK, D), f32)] + project_outs,
+        [(core, "s"), (hidden_0, "v"), (back, "v"), (vecs[1], "v"), (ups[0:1], "v"), (vecs[2], "v")]
+        + weights(0, True) + weights(1, False),
+        block_scratch + project_scratch, us=12)
+    heads_1 = exchange(pay)
+    back = exchange(attend(heads_1))
+    o_1, h1_1, a2_1, u_1, hidden = call(
+        forward_kernel,
+        forward_outs + [((TOK, D), bf16)],
+        [(core, "s"), (hidden_1, "v"), (back, "v"), (vecs[3], "v"), (ups[1:2], "v")] + weights(1, True),
+        block_scratch, us=8)
+
+    def grad_joint(a1, g, o, e1):
         return call(
             grad_joint_cube, [((64, 9, 16, 128), bf16)] * 2,
             [(core, "s"), (a1, "v"), (g, "v"), (o, "v"), (e1, "v")],
@@ -734,53 +816,38 @@
 
     grad = out_grad[0]
     few_rows, few_up, joint = [None] * 2, [None] * 2, [None] * 2
-    for l in reversed(range(LAYERS)):
-        layer_in, a1, heads, o, h1, a2, u = stored[l]
-        f, du, e1, pay, small_b, small_u = call(
-            functools.partial(backward_kernel, l),
-            [((TOK, 4 * D), bf16), ((TOK, 4 * D), bf16), ((TOK, D), f32), ((8, TOK, 128), bf16),
-             ((4, D), f32), ((1, 4 * D), f32)],
-            [(core, "s"), (grad, "v"), (u, "v"), (h1, "v"), (vecs[2 * l + 1], "v")] + weights(l, True),
-            [w_scratch(6), w_scratch(24), w_scratch(24), DMA((3,))],
-            us=10)
-        cot = lax.all_to_all(pay, CTX, 0, 0)
-        if l == 1:
-            (mlp_1,) = call(
-                grad_mlp_plain, [((16, 144, 16, 128), bf16)], [(f, "v"), (grad, "v"), (a2, "v"), (du, "v")],
-                [w_scratch(48), DMA((1,))], us=9, out_spaces="a")
-            scattered = lax.psum_scatter(after(mlp_1, cot), DATA, scatter_dimension=0, tiled=False)
-        else:
-            keep_ud, send_ud = call(
-                grad_mlp_cube, [((64, 18, 16, 128), bf16)] * 2,
-                [(core, "s"), (f, "v"), (grad, "v"), (a2, "v"), (du, "v")],
-                [pltpu.VMEM((2, 64, 18, 16, 128), bf16), DMA((2,))],
-                us=9, out_spaces="aa")
-        if l == 0:
-            send_ud = after(send_ud, cot)
-        cot = after(cot, mlp_1 if l == 1 else keep_ud)
-        (pay2,) = call(
-            attend_back_kernel,
-            [((8, TOK, 384), bf16)],
-            [(par, "s"), (heads, "v"), (cot, "v"), (idc, "v"), (idr, "v")],
-            [pltpu.VMEM((2, SLOTS, 64), f32)] * 2,
-            us=10)
-        back2 = lax.all_to_all(pay2, CTX, 0, 0)
-        if l == 0:
-            middle = core_sums([(keep_ud, send_ud)])
-            back2 = after(back2, middle)
-        g, grad, small_a = call(
-            functools.partial(back_project_kernel, l),
-            [((TOK, 3 * D), bf16), ((TOK, D), f32), ((4, D), f32)],
-            [(core, "s"), (back2, "v"), (e1, "v"), (layer_in, "v"), (vecs[2 * l], "v")] + weights(l, False),
-            [w_scratch(18), DMA],
-            us=6)
-        joint[l] = call(
-            grad_joint_cube, [((64, 9, 16, 128), bf16)] * 2,
-            [(core, "s"), (a1, "v"), (g, "v"), (o, "v"), (e1, "v")],
-            [pltpu.VMEM((2, 64, 9, 16, 128), bf16), DMA((2,))], us=5, out_spaces="aa")
-        few_rows[l] = jnp.concatenate([small_a[0:1], small_b[0:1], small_a[1:2], small_b[1:2], small_a[2:4],
-                                       small_b[2:4]], axis=0)
-        few_up[l] = small_u
+    f, du, e1, pay, small_b, few_up[1] = call(
+        backward_kernel, backward_outs,
+        [(core, "s"), (grad, "v"), (u_1, "v"), (h1_1, "v"), (vecs[3], "v")] + weights(1, True),
+        block_scratch, us=10)
+    cot = exchange(pay)
+    keep_u, send_u, mlp_1 = call(
+        grad_mlp_split, [((64, 3, 16, 128), bf16)] * 2 + [((16, 120, 16, 128), bf16)],
+        [(core, "s"), (f, "v"), (grad, "v"), (a2_1, "v"), (du, "v")],
+        [pltpu.VMEM((2, 64, 3, 16, 128), bf16), w_scratch(40), DMA((3,))], us=9, out_spaces="aaa")
+    scattered = lax.psum_scatter(after(mlp_1, cot), DATA, scatter_dimension=0, tiled=False)
+    back = exchange(attend_back(heads_1, after(cot, mlp_1)))
+    e1_1, small_b1 = e1, small_b
+    g_1, grad, small_a1, f, du, e1, pay, small_b, few_up[0] = call(
+        back_both_kernel, back_project_outs + backward_outs,
+        [(core, "s"), (back, "v"), (e1_1, "v"), (hidden_1, "v"), (vecs[2], "v"), (u_0, "v"), (h1_0, "v"),
+         (vecs[1], "v")] + weights(1, False) + weights(0, True),
+        project_scratch + block_scratch, us=16)
+    cot = exchange(pay)
+    keep_ud, send_ud = call(
+        grad_mlp_cube, [((64, 18, 16, 128), bf16)] * 2,
+        [(core, "s"), (f, "v"), (grad, "v"), (a2_0, "v"), (du, "v")],
+        [pltpu.VMEM((2, 64, 18, 16, 128), bf16), DMA((2,))], us=9, out_spaces="aa")
+    send_ud = after(send_ud, cot)
+    back = exchange(attend_back(heads_0, after(cot, keep_ud)))
+    middle = core_sums([(keep_ud, send_ud), (keep_u, send_u)])
+    g_0, grad, small_a0 = call(
+        back_project_kernel, back_project_outs,
+        [(core, "s"), (after(back, middle), "v"), (e1, "v"), (hidden_0, "v"), (vecs[0], "v")] + weights(0, False),
+        project_scratch, us=6)
+    joint = [grad_joint(a1[0], g_0, o_0, e1), grad_joint(a1[1], g_1, o_1, e1_1)]
+    for l, (first, second) in enumerate(((small_a0, small_b), (small_a1, small_b1))):
+        few_rows[l] = jnp.concatenate([first[0:1], second[0:1], first[1:2], second[1:2], first[2:4], second[2:4]], axis=0)
 
     few = jnp.concatenate([r.reshape(8, 128, 6).transpose(1, 0, 2).reshape(128, 48) for r in few_rows]
                           + [r.reshape(16, 4, 8, 6).transpose(0, 2, 1, 3).reshape(128, 24) for r in few_up], axis=1)
@@ -793,7 +860,7 @@
     last = gather_sums(after(core_sums([joint[0], few, joint[1]]), middle, scattered))
     sums = jnp.concatenate([last, middle], axis=1)
     sums = lax.all_to_all(sums, ALL, 0, 0, axis_index_groups=GROUPS_A)
-    sums, few = call(finish_kernel, [((8, 23, 16, 128), bf16), ((2, 128), f32)],
+    sums, few = call(finish_kernel, [((8, 20, 16, 128), bf16), ((2, 128), f32)],
                      [(sums, "v"), (scattered, "v")])
     got = lax.all_to_all(sums, CTX, 0, 0)
     grad_in, grad_out, grad_up, grad_down = call(

time: 478 us -> 471 us (0.985)
  blocking collectives: 137 us -> 159 us
  waiting for transfers between devices: 93.5 us -> 74 us
  Pallas kernels: 143 us -> 134 us
    all_to_all x2 -> x3, blocking collectives: 32.6 us -> 54.5 us  [exchange(): return lax.all_to_all(values, CTX, 0, 0)]
    all_to_all x7 -> x6, waiting for transfers between devices: 57.2 us -> 41.7 us  [the longest x1 26.8 us: body(): lax.all_to_all(after(shards, heads_0, down_0), ALL, 0, 0, axis_index_grou...]
    reduce_scatter x1, waiting for transfers between devices: 12 us -> 0.02 us  [body(): lax.psum_scatter(after(mlp_1, cot), DATA, scatter_dimension=0, tiled=False)]
    pallas_call x21 -> x18, Pallas kernels: 126 us -> 117 us  [call(): pl.pallas_call(kernel, out_shape=[jax.ShapeDtypeStruct(*o) for o in outs]...]
    all_to_all x1, waiting for transfers between devices: 0.01 us -> 8.05 us  [gather_sums(): lax.all_to_all(part, ALL, 0, 0, axis_index_groups=GROUPS_B)]
    all_to_all x7 -> x6, starting transfers between devices: 30.9 us -> 30.4 us  [the longest x5 25.7 us: exchange(): return lax.all_to_all(values, CTX, 0, 0)]
  transfers between devices with their start and end apart: 19 -> 19, of which waited for: 10 -> 10; matrix products, arithmetic and copies ran while one was open for 5% -> 5% of each run, Pallas kernels for 25% -> 23%
where the time goes in v6:
time: 471 us; the launch traced here: 462 us
  blocking collectives  159 us (34%)
  Pallas kernels  134 us (28%)
  waiting for transfers between devices  74 us (16%)
  starting transfers between devices  46.6 us (10%)
  local copies, waits for them, and re-layouts  21.5 us (5%)
  between operations  14.7 us (3%)
  other arithmetic  11.7 us (2%)
    pallas_call x18, Pallas kernels, call(): pl.pallas_call(kernel, out_shape=[jax.ShapeDtypeStruct(*o) for o in outs]...  117 us
    all_to_all x3, blocking collectives, exchange(): return lax.all_to_all(values, CTX, 0, 0)  54.5 us
    all_to_all x2, blocking collectives, copies(): return lax.all_to_all(many, ALL, 0, 0, axis_index_groups=groups)  45.8 us
    all_to_all x1, blocking collectives, gather_sums(): lax.all_to_all(part, ALL, 0, 0, axis_index_groups=GROUPS_B)  36.8 us
    all_to_all x1, waiting for transfers between devices, body(): lax.all_to_all(after(shards, heads_0, down_0), ALL, 0, 0, axis_index_grou...  26.8 us
    all_to_all x5, starting transfers between devices, exchange(): return lax.all_to_all(values, CTX, 0, 0)  25.7 us
    all_to_all x1, blocking collectives, body(): sums = lax.all_to_all(sums, ALL, 0, 0, axis_index_groups=GROUPS_A)  22.2 us
    pallas_call x2, Pallas kernels, add_pairs(): pl.pallas_call(add_kernel, grid=(8,), out_shape=jax.ShapeDtypeStruct((64,...  17.2 us
  transfers between devices with their start and end apart: 19, of which 10 were waited for; matrix products, arithmetic and copies ran while one was open for 5% of the time, Pallas kernels for 23%

profile of v6, /device:TPU:0, one launch (start us, length us, event | category | flops | bytes accessed | tf_op | source)
XLA Modules:
  0.0 462.3 jit_solution(5562593169167055926)
XLA Ops:
  7.2 2.4 shard_map.239
  9.6 5.7 %all-to-all-start = ((bf16[8,31,16,128]{3,2,1,0:T(8,128)(2,1)}), bf16[8,31,16,128]{3,2,1,0:T(8,128)(2,1)S(1)}, u32[]{:S(2)}, u32[]{:S(2)}) async-start(bf16[8,31,16,128]{3,2,1,0:T(8,128)(2,1)} %shard_map.239), calls=%async_computation | async-start | bytes 2031616 | tf_op jit(solution)/shard_map/all_to_all | solution.py:744
  16.6 14.2 %all-to-all-done.got = bf16[8,31,16,128]{3,2,1,0:T(8,128)(2,1)S(1)} async-done(((bf16[8,31,16,128]{3,2,1,0:T(8,128)(2,1)}), bf16[8,31,16,128]{3,2,1,0:T(8,128)(2,1)S(1)}, u32[]{:S(2)}, u32[]{:S(2)}) %all-to-all-start) | async-done | bytes 1015840 | tf_op jit(solution)/shard_map/all_to_all | solution.py:744
  30.8 1.0 copy-done.1
  31.8 2.3 shard_map.240
  34.2 1.0 broadcast_in_dim.22
  35.2 21.7 %all_to_all.80 = bf16[8,28,16,128]{3,2,1,0:T(8,128)(2,1)S(1)} all-to-all(bf16[8,28,16,128]{3,2,1,0:T(8,128)(2,1)S(1)} %broadcast_in_dim.22), channel_id=1, replica_groups={{0,6,17,23,96,102,113,119},{2,4,19,21,98,100,115,117},{1,7,16,22,97,103..., dimensions={0} | all-to-all | bytes 1835008 | tf_op jit(solution)/shard_map/all_to_all | solution.py:664
  57.4 24.1 %all_to_all.81 = bf16[8,8,10,16,128]{4,3,2,1,0:T(8,128)(2,1)S(1)} all-to-all(bf16[8,8,10,16,128]{4,3,2,1,0:T(8,128)(2,1)S(1)} %broadcast_in_dim.23), channel_id=1, replica_groups={{0,2,1,3,32,34,33,35},{6,4,7,5,38,36,39,37},{17,19,16,18,49,51,48,50},{..., dimensions={0} | all-to-all | bytes 5242880 | tf_op jit(solution)/shard_map/all_to_all | solution.py:664
  81.6 3.0 broadcast_in_dim.24
  84.6 1.9 collective-permute-done.theirs.refs_1_.refs_3_
  86.5 7.5 %shard_map.241 = (bf16[128,768]{1,0:T(8,128)(2,1)}, bf16[8,128,384]{2,1,0:T(8,128)(2,1)}, f32[4,768]{1,0:T(4,128)}, f32[4,768]{1,0:T(4,128)}, f32[4,768]{1,0:T(4...) custom-call(s32[1]{0:T(128)} %bitcast.core.core_ref, bf16[128,768]{1,0:T(8,128)(2,1)} %bitcast.72, ...), custom_call_target="tpu_custom_call" | custom-call | bytes 25830000 | tf_op jit(solution)/shard_map/pallas_call | solution.py:639
  94.0 18.0 %all_to_all.82.heads = bf16[8,128,384]{2,1,0:T(8,128)(2,1)} all-to-all(bf16[8,128,384]{2,1,0:T(8,128)(2,1)} %get-tuple-element.81), channel_id=1, replica_groups=mesh['y'=4,'zh'=2,'c'=2,'x'=4,'zl'=2] {'x','zl'}, dimensions={0} | all-to-all | bytes 1572864 | tf_op jit(solution)/shard_map/all_to_all | solution.py:776
  112.0 4.8 %all-to-all-start.4 = ((bf16[8,8,18,16,128]{4,3,2,1,0:T(8,128)(2,1)}), bf16[8,8,18,16,128]{4,3,2,1,0:T(8,128)(2,1)}, u32[]{:S(2)}, u32[]{:S(2)}) async-start(bf16[8,8,18,16,128]{4,3,2,1,0:T(8,128)(2,1)} %broadcast_in_dim.24), calls=%async_computation.4 | async-start | bytes 9437184 | tf_op jit(solution)/shard_map/all_to_all | solution.py:791
  118.2 0.9 subtract_select_fusion.idc
  119.1 5.5 %shard_map.242 = bf16[8,128,128]{2,1,0:T(8,128)(2,1)} custom-call(s32[1]{0:T(128)} %bitcast.2.par_ref, bf16[8,128,384]{2,1,0:T(8,128)(2,1)} %all_to_all.82.heads, s32[8,128,1]{2,1,0:T(8,128)} %subtract_select_fusion.idc, s32[1,1024]{1,0:T(1,128)} %reshape_select_fusion.idr), custom_call_target="tpu_custom_call" | custom-call | bytes 22140000 | tf_op jit(solution)/shard_map/pallas_call | solution.py:639
  124.6 26.8 %all-to-all-done.4 = bf16[8,8,18,16,128]{4,3,2,1,0:T(8,128)(2,1)} async-done(((bf16[8,8,18,16,128]{4,3,2,1,0:T(8,128)(2,1)}), bf16[8,8,18,16,128]{4,3,2,1,0:T(8,128)(2,1)}, u32[]{:S(2)}, u32[]{:S(2)}) %all-to-all-start.4) | async-done | bytes 4718624 | tf_op jit(solution)/shard_map/all_to_all | solution.py:791
  151.8 9.3 %all-to-all-start.5 = ((bf16[8,128,128]{2,1,0:T(8,128)(2,1)}), bf16[8,128,128]{2,1,0:T(8,128)(2,1)S(1)}, u32[]{:S(2)}, u32[]{:S(2)}) async-start(bf16[8,128,128]{2,1,0:T(8,128)(2,1)} %shard_map.242), calls=%async_computation.5 | async-start | bytes 524288 | tf_op jit(solution)/shard_map/all_to_all | solution.py:776
  161.6 0.8 slice.158.upb
  162.4 6.3 %all-to-all-done.5.back = bf16[8,128,128]{2,1,0:T(8,128)(2,1)S(1)} async-done(((bf16[8,128,128]{2,1,0:T(8,128)(2,1)}), bf16[8,128,128]{2,1,0:T(8,128)(2,1)S(1)}, u32[]{:S(2)}, u32[]{:S(2)}) %all-to-all-start.5) | async-done | bytes 262176 | tf_op jit(solution)/shard_map/all_to_all | solution.py:776
  168.7 0.7 copy-done.5
  169.4 9.8 %shard_map.243 = (bf16[128,768]{1,0:T(8,128)(2,1)}, f32[128,768]{1,0:T(8,128)}, bf16[128,768]{1,0:T(8,128)(2,1)}, f32[128,3072]{1,0:T(8,128)}, f32[128,768]{1,0:...) custom-call(s32[1]{0:T(128)} %bitcast.core.core_ref, bf16[128,768]{1,0:T(8,128)(2,1)} %bitcast.73, ...), custom_call_target="tpu_custom_call" | custom-call | bytes 44280000 | tf_op jit(solution)/shard_map/pallas_call | solution.py:639
  179.2 17.9 %all_to_all.83.heads = bf16[8,128,384]{2,1,0:T(8,128)(2,1)} all-to-all(bf16[8,128,384]{2,1,0:T(8,128)(2,1)} %get-tuple-element.90), channel_id=1, replica_groups=mesh['y'=4,'zh'=2,'c'=2,'x'=4,'zl'=2] {'x','zl'}, dimensions={0} | all-to-all | bytes 1572864 | tf_op jit(solution)/shard_map/all_to_all | solution.py:776
  197.1 5.6 %shard_map.244 = bf16[8,128,128]{2,1,0:T(8,128)(2,1)} custom-call(s32[1]{0:T(128)} %bitcast.2.par_ref, bf16[8,128,384]{2,1,0:T(8,128)(2,1)} %all_to_all.83.heads, s32[8,128,1]{2,1,0:T(8,128)} %subtract_select_fusion.idc, s32[1,1024]{1,0:T(1,128)} %reshape_select_fusion.idr), custom_call_target="tpu_custom_call" | custom-call | bytes 22140000 | tf_op jit(solution)/shard_map/pallas_call | solution.py:639
  202.7 3.7 all-to-all-start.7
  206.9 0.8 slice.160.upb
  207.6 5.7 %all-to-all-done.7.back = bf16[8,128,128]{2,1,0:T(8,128)(2,1)S(1)} async-done(((bf16[8,128,128]{2,1,0:T(8,128)(2,1)}), bf16[8,128,128]{2,1,0:T(8,128)(2,1)S(1)}, u32[]{:S(2)}, u32[]{:S(2)}) %all-to-all-start.7) | async-done | bytes 262176 | tf_op jit(solution)/shard_map/all_to_all | solution.py:776
  213.3 3.2 all-gather.7.cloned.1.call-done
  216.5 7.0 %shard_map.245 = (bf16[128,768]{1,0:T(8,128)(2,1)}, f32[128,768]{1,0:T(8,128)}, bf16[128,768]{1,0:T(8,128)(2,1)}, f32[128,3072]{1,0:T(8,128)}, bf16[128,768]{1,0:T(8,128)(2,1)}) custom-call(s32[1]{0:T(128)} %bitcast.core.core_ref, f32[128,768]{1,0:T(8,128)} %get-tuple-element.89.h_ref, bf16[8,128,128]{2,1,0:T(8,128)(2,1)} %copy-done.6, ...), custom_call_target="tpu_custom_call" | custom-call | bytes 29520000 | tf_op jit(solution)/shard_map/pallas_call | solution.py:639
  223.6 9.5 %shard_map.246 = (bf16[128,3072]{1,0:T(8,128)(2,1)}, bf16[128,3072]{1,0:T(8,128)(2,1)}, f32[128,768]{1,0:T(8,128)}, bf16[8,128,128]{2,1,0:T(8,128)(2,1)}, f32[4,768]{1,0:T(4,128)}, /*index=5*/f32[1,3072]{1,0:T(1,128)}) custom-call(s32[1]{0:T(128)} %bitcast.core.core_ref, bf16[128,768]{1,0:T(8,128)(2,1)} %bitcast.78, f32[128,3072]{1,0:T(8,128)} %get-tuple-element.96.u_ref, ...), custom_call_target="tpu_custom_call" | custom-call | bytes 36900000 | tf_op jit(solution)/shard_map/pallas_call | solution.py:639
  233.1 3.4 all-to-all-start.8
  236.8 7.3 %shard_map.247 = (bf16[64,3,16,128]{3,2,1,0:T(8,128)(2,1)}, bf16[64,3,16,128]{3,2,1,0:T(8,128)(2,1)}, bf16[16,120,16,128]{3,2,1,0:T(8,128)(2,1)}) custom-call(s32[1]{0:T(128)} %bitcast.core.core_ref, bf16[128,3072]{1,0:T(8,128)(2,1)} %get-tuple-element.99.f_ref, bf16[128,768]{1,0:T(8,128)(2,1)} %bitcast.79, bf16[128,768]{1,0:T(8,128)(2,1)} %get-tuple-element.100.a2_ref, ...), custom_call_target="tpu_custom_call" | custom-call | bytes 33210000 | tf_op jit(solution)/shard_map/pallas_call | solution.py:639
  244.2 0.7 copy-done.8
  244.9 8.0 %shard_map.248 = bf16[8,128,384]{2,1,0:T(8,128)(2,1)} custom-call(s32[1]{0:T(128)} %bitcast.2.par_ref, bf16[8,128,384]{2,1,0:T(8,128)(2,1)} %all_to_all.83.heads, bf16[8,128,128]{2,1,0:T(8,128)(2,1)} %copy-done.8, s32[8,128,1]{2,1,0:T(8,128)} %subtract_select_fusion.idc, s32[1,1024]{1,0:T(1,128)} %reshape_select_fusion.idr), custom_call_target="tpu_custom_call" | custom-call | bytes 29520000 | tf_op jit(solution)/shard_map/pallas_call | solution.py:639
  252.9 18.6 %all_to_all.84.back = bf16[8,128,384]{2,1,0:T(8,128)(2,1)} all-to-all(bf16[8,128,384]{2,1,0:T(8,128)(2,1)} %shard_map.248), channel_id=1, replica_groups=mesh['y'=4,'zh'=2,'c'=2,'x'=4,'zl'=2] {'x','zl'}, dimensions={0} | all-to-all | bytes 1572864 | tf_op jit(solution)/shard_map/all_to_all | solution.py:776
  271.5 14.6 %shard_map.249 = (bf16[128,2304]{1,0:T(8,128)(2,1)}, f32[128,768]{1,0:T(8,128)}, f32[4,768]{1,0:T(4,128)}, bf16[128,3072]{1,0:T(8,128)(2,1)}, bf16[128,3072]{1,0...) custom-call(s32[1]{0:T(128)} %bitcast.core.core_ref, ...), custom_call_target="tpu_custom_call" | custom-call | bytes 59040000 | tf_op jit(solution)/shard_map/pallas_call | solution.py:639
  286.1 3.6 all-to-all-start.10
  289.7 8.4 %shard_map.250 = (bf16[64,18,16,128]{3,2,1,0:T(8,128)(2,1)}, bf16[64,18,16,128]{3,2,1,0:T(8,128)(2,1)}) custom-call(s32[1]{0:T(128)} %bitcast.core.core_ref, bf16[128,3072]{1,0:T(8,128)(2,1)} %get-tuple-element.108.f_ref, f32[128,768]{1,0:T(8,128)} %get-tuple-element.109.e_ref, bf16[128,768]{1,0:T(8,128)(2,1)} %get-tuple-element.110.a2_ref, ...), custom_call_target="tpu_custom_call" | custom-call | bytes 33210000 | tf_op jit(solution)/shard_map/pallas_call | solution.py:639
  298.2 0.9 collective-permute-start.3
  299.2 8.0 %shard_map.251 = bf16[8,128,384]{2,1,0:T(8,128)(2,1)} custom-call(s32[1]{0:T(128)} %bitcast.2.par_ref, bf16[8,128,384]{2,1,0:T(8,128)(2,1)} %all_to_all.82.heads, bf16[8,128,128]{2,1,0:T(8,128)(2,1)} %copy-done.7, s32[8,128,1]{2,1,0:T(8,128)} %subtract_select_fusion.idc, s32[1,1024]{1,0:T(1,128)} %reshape_select_fusion.idr), custom_call_target="tpu_custom_call" | custom-call | bytes 29520000 | tf_op jit(solution)/shard_map/pallas_call | solution.py:639
  307.2 5.6 %all-to-all-start.11 = ((bf16[8,128,384]{2,1,0:T(8,128)(2,1)}), bf16[8,128,384]{2,1,0:T(8,128)(2,1)S(1)}, u32[]{:S(2)}, u32[]{:S(2)}) async-start(bf16[8,128,384]{2,1,0:T(8,128)(2,1)} %shard_map.251), calls=%async_computation.11 | async-start | bytes 1572864 | tf_op jit(solution)/shard_map/all_to_all | solution.py:776
  312.8 0.9 copy-done.9
  313.7 8.8 %shard_map.252 = bf16[64,21,16,128]{3,2,1,0:T(8,128)(2,1)} custom-call(bf16[64,18,16,128]{3,2,1,0:T(8,128)(2,1)} %get-tuple-element.112.refs_0_, bf16[64,18,16,128]{3,2,1,0:T(8,128)(2,1)} %collective-permute-done.2.refs_1_, bf16[64,3,16,128]{3,2,1,0:T(8,128)(2,1)} %get-tuple-element.116.refs_2_, bf16[64,3,16,128]{3,2,1,0:T(8,128)(2,1)} %copy-done.9), custom_call_target="tpu_custom_call" | custom-call | flops 4194304 | bytes 16515072 | tf_op jit(solution)/shard_map/pallas_call | solution.py:699
  322.6 2.9 all-to-all-done.11.back
  325.5 0.9 copy-done.2
  326.4 4.7 %all-to-all-start.12 = ((bf16[8,8,21,16,128]{4,3,2,1,0:T(8,128)(2,1)}), bf16[8,8,21,16,128]{4,3,2,1,0:T(8,128)(2,1)}, u32[]{:S(2)}, u32[]{:S(2)}) async-start(bf16[8,8,21,16,128]{4,3,2,1,0:T(8,128)(2,1)} %bitcast.68), calls=%async_computation.12 | async-start | bytes 11010048 | tf_op jit(solution)/shard_map/all_to_all | solution.py:716
  331.1 5.2 %shard_map.255 = (bf16[64,9,16,128]{3,2,1,0:T(8,128)(2,1)}, bf16[64,9,16,128]{3,2,1,0:T(8,128)(2,1)}) custom-call(s32[1]{0:T(128)} %bitcast.core.core_ref, bf16[128,768]{1,0:T(8,128)(2,1)} %get-tuple-element.132.a_ref, bf16[128,2304]{1,0:T(8,128)(2,1)} %get-tuple-element.133.g_ref, bf16[128,768]{1,0:T(8,128)(2,1)} %get-tuple-element.134.o_ref, ...), custom_call_target="tpu_custom_call" | custom-call | bytes 18450000 | tf_op jit(solution)/shard_map/pallas_call | solution.py:639
  336.5 5.8 %shard_map.253 = (bf16[128,2304]{1,0:T(8,128)(2,1)}, f32[128,768]{1,0:T(8,128)}, f32[4,768]{1,0:T(4,128)}) custom-call(s32[1]{0:T(128)} %bitcast.core.core_ref, bf16[8,128,384]{2,1,0:T(8,128)(2,1)} %copy-done.2, f32[128,768]{1,0:T(8,128)} %get-tuple-element.119.e1_ref, bf16[128,768]{1,0:T(8,128)(2,1)} %bitcast.74, f32[4,768]{1,0:T(4,128)} %get-tuple-element.120.vec, ...), custom_call_target="tpu_custom_call" | custom-call | bytes 22140000 | tf_op jit(solution)/shard_map/pallas_call | solution.py:639
  342.3 5.2 %shard_map.254 = (bf16[64,9,16,128]{3,2,1,0:T(8,128)(2,1)}, bf16[64,9,16,128]{3,2,1,0:T(8,128)(2,1)}) custom-call(s32[1]{0:T(128)} %bitcast.core.core_ref, bf16[128,768]{1,0:T(8,128)(2,1)} %get-tuple-element.93.a_ref, bf16[128,2304]{1,0:T(8,128)(2,1)} %get-tuple-element.122.g_ref, bf16[128,768]{1,0:T(8,128)(2,1)} %get-tuple-element.123.o_ref, ...), custom_call_target="tpu_custom_call" | custom-call | bytes 18450000 | tf_op jit(solution)/shard_map/pallas_call | solution.py:639
  347.5 0.7 collective-permute-start.4
  352.2 0.8 select_bitcast_fusion
  353.1 1.5 collective-permute-done.5.refs_3_
  355.2 8.4 %shard_map.256 = bf16[64,19,16,128]{3,2,1,0:T(8,128)(2,1)} custom-call(bf16[64,9,16,128]{3,2,1,0:T(8,128)(2,1)} %get-tuple-element.124.refs_0_, bf16[64,9,16,128]{3,2,1,0:T(8,128)(2,1)} %collective-permute-done.4.refs_1_, bf16[64,1,16,128]{3,2,1,0:T(8,128)(2,1)} %get-tuple-element.148.refs_2_, bf16[64,1,16,128]{3,2,1,0:T(8,128)(2,1)} %copy-done.10, ...), custom_call_target="tpu_custom_call" | custom-call | flops 4194304 | bytes 14942208 | tf_op jit(solution)/shard_map/pallas_call | solution.py:699
  363.7 8.1 %all-to-all-done.12 = bf16[8,8,21,16,128]{4,3,2,1,0:T(8,128)(2,1)} async-done(((bf16[8,8,21,16,128]{4,3,2,1,0:T(8,128)(2,1)}), bf16[8,8,21,16,128]{4,3,2,1,0:T(8,128)(2,1)}, u32[]{:S(2)}, u32[]{:S(2)}) %all-to-all-start.12) | async-done | bytes 5505056 | tf_op jit(solution)/shard_map/all_to_all | solution.py:716
  371.7 3.5 reduce_sum.34
  375.2 36.8 %all_to_all.85 = bf16[8,8,19,16,128]{4,3,2,1,0:T(8,128)(2,1)} all-to-all(bf16[8,8,19,16,128]{4,3,2,1,0:T(8,128)(2,1)} %bitcast.69), channel_id=1, replica_groups={{0,2,1,3,32,34,33,35},{6,4,7,5,38,36,39,37},{17,19,16,18,49,51,48,50},{..., dimensions={0} | all-to-all | bytes 9961472 | tf_op jit(solution)/shard_map/all_to_all | solution.py:716
  412.0 3.2 reduce_sum.35
  415.3 22.2 %all_to_all.86.parts = bf16[8,40,16,128]{3,2,1,0:T(8,128)(2,1)} all-to-all(bf16[8,40,16,128]{3,2,1,0:T(8,128)(2,1)S(1)} %pad_maximum_fusion), channel_id=1, replica_groups={{0,6,17,23,96,102,113,119},{2,4,19,21,98,100,115,117},{1,7,16,22,97,103..., dimensions={0} | all-to-all | bytes 2621440 | tf_op jit(solution)/shard_map/all_to_all | solution.py:862
  437.5 2.6 shard_map.257
  440.2 3.5 all-to-all-start.15
  443.7 0.8 slice.191
  444.5 1.0 fusion.29
  449.1 3.4 all-to-all-done.15.got
  452.5 0.9 copy-done.3
  453.4 2.2 shard_map.258
  (139 shorter events, 13.1 us)
Async XLA Ops:
  7.2 8.2 %copy-start.20 = (bf16[2,2,6]{2,1,0:T(2,128)(2,1)S(1)}, bf16[2,2,6]{2,1,0:T(2,128)(2,1)}, u32[]{:S(2)}) copy-start(bf16[2,2,6]{2,1,0:T(2,128)(2,1)} %param.21) | copy-start | bytes 148
  7.2 8.3 %copy-start.21 = (bf16[2,2,6]{2,1,0:T(2,128)(2,1)S(1)}, bf16[2,2,6]{2,1,0:T(2,128)(2,1)}, u32[]{:S(2)}) copy-start(bf16[2,2,6]{2,1,0:T(2,128)(2,1)} %param.22) | copy-start | bytes 148
  7.2 8.4 %copy-start.22 = (bf16[2,2,6]{2,1,0:T(2,128)(2,1)S(1)}, bf16[2,2,6]{2,1,0:T(2,128)(2,1)}, u32[]{:S(2)}) copy-start(bf16[2,2,6]{2,1,0:T(2,128)(2,1)} %param.24) | copy-start | bytes 148
  7.2 8.5 %copy-start.23 = (bf16[2,2,6]{2,1,0:T(2,128)(2,1)S(1)}, bf16[2,2,6]{2,1,0:T(2,128)(2,1)}, u32[]{:S(2)}) copy-start(bf16[2,2,6]{2,1,0:T(2,128)(2,1)} %param.26) | copy-start | bytes 148
  7.2 8.6 %copy-start.24 = (bf16[2,24]{1,0:T(2,128)(2,1)S(1)}, bf16[2,24]{1,0:T(2,128)(2,1)}, u32[]{:S(2)}) copy-start(bf16[2,24]{1,0:T(2,128)(2,1)} %param.28) | copy-start | bytes 292
  9.6 21.1 %all-to-all-start = ((bf16[8,31,16,128]{3,2,1,0:T(8,128)(2,1)}), bf16[8,31,16,128]{3,2,1,0:T(8,128)(2,1)S(1)}, u32[]{:S(2)}, u32[]{:S(2)}) async-start(bf16[8,31,16,128]{3,2,1,0:T(8,128)(2,1)} %shard_map.239), calls=%async_computation | async-start | bytes 2031616 | tf_op jit(solution)/shard_map/all_to_all | solution.py:744
  15.4 96.6 %all-gather.5.cloned.1.call-start = ((), (), s32[]{:S(2)}) async-start(), calls=%async_computation.18 | async-start | bytes 5013504 | tf_op jit(solution)/shard_map/all_gather | solution.py:749
  30.8 1.0 copy-start.1
  34.1 182.4 %all-gather.7.cloned.1.call-start = ((), (), s32[]{:S(2)}) async-start(), calls=%async_computation.19 | async-start | bytes 10027008 | tf_op jit(solution)/shard_map/all_gather | solution.py:787
  81.5 3.1 copy-start
  81.5 5.0 %collective-permute-start = (bf16[64,10,16,128]{3,2,1,0:T(8,128)(2,1)S(1)}, bf16[64,10,16,128]{3,2,1,0:T(8,128)(2,1)}, u32[]{:S(2)}, u32[]{:S(2)}) collective-permute-start(bf16[64,10,16,128]{3,2,1,0:T(8,128)(2,1)S(1)} %bitcast.63), channel_id=1, source_target_pairs={{0,8},{8,0},{1,9},{9,1},{2,10},{10,2},{3,11},{11,3},{4,12},{12,4},... | collective-permute-start | bytes 7864328 | tf_op jit(solution)/shard_map/ppermute | solution.py:672
  112.0 4.8 %copy-start.18 = (s32[48]{0:T(128)S(1)}, s32[48]{0:T(128)}, u32[]{:S(2)}) copy-start(s32[48]{0:T(128)} %param.19) | copy-start | bytes 580
  112.0 4.8 %copy-start.25 = (s32[48]{0:T(128)S(1)}, s32[48]{0:T(128)}, u32[]{:S(2)}) copy-start(s32[48]{0:T(128)} %param.20) | copy-start | bytes 580
  112.0 4.9 %copy-start.26 = (s32[48]{0:T(128)S(1)}, s32[48]{0:T(128)}, u32[]{:S(2)}) copy-start(s32[48]{0:T(128)} %param.18) | copy-start | bytes 580
  112.0 39.4 %all-to-all-start.4 = ((bf16[8,8,18,16,128]{4,3,2,1,0:T(8,128)(2,1)}), bf16[8,8,18,16,128]{4,3,2,1,0:T(8,128)(2,1)}, u32[]{:S(2)}, u32[]{:S(2)}) async-start(bf16[8,8,18,16,128]{4,3,2,1,0:T(8,128)(2,1)} %broadcast_in_dim.24), calls=%async_computation.4 | async-start | bytes 9437184 | tf_op jit(solution)/shard_map/all_to_all | solution.py:791
  116.8 34.6 %copy-start.11 = (f32[128,256]{1,0:T(8,128)S(1)}, f32[128,256]{1,0:T(8,128)}, u32[]{:S(2)}) copy-start(f32[128,256]{1,0:T(8,128)} %get-tuple-element.86) | copy-start | bytes 393220
  151.4 17.3 %collective-permute-start.1 = (bf16[64,18,16,128]{3,2,1,0:T(8,128)(2,1)}, bf16[64,18,16,128]{3,2,1,0:T(8,128)(2,1)}, u32[]{:S(2)}, u32[]{:S(2)}) collective-permute-start(bf16[64,18,16,128]{3,2,1,0:T(8,128)(2,1)} %bitcast.12.refs_2_.refs_5_.refs_0_.refs_4_), channel_id=1, source_target_pairs={{0,8},{8,0},{1,9},{9,1},{2,10},{10,2},{3,11},{11,3},{4,12},{12,4},... | collective-permute-start | bytes 14155784 | tf_op jit(solution)/shard_map/ppermute | solution.py:672
  151.8 16.9 %all-to-all-start.5 = ((bf16[8,128,128]{2,1,0:T(8,128)(2,1)}), bf16[8,128,128]{2,1,0:T(8,128)(2,1)S(1)}, u32[]{:S(2)}, u32[]{:S(2)}) async-start(bf16[8,128,128]{2,1,0:T(8,128)(2,1)} %shard_map.242), calls=%async_computation.5 | async-start | bytes 524288 | tf_op jit(solution)/shard_map/all_to_all | solution.py:776
  168.7 0.7 copy-start.5
  202.7 10.7 %all-to-all-start.7 = ((bf16[8,128,128]{2,1,0:T(8,128)(2,1)}), bf16[8,128,128]{2,1,0:T(8,128)(2,1)S(1)}, u32[]{:S(2)}, u32[]{:S(2)}) async-start(bf16[8,128,128]{2,1,0:T(8,128)(2,1)} %shard_map.244), calls=%async_computation.7 | async-start | bytes 524288 | tf_op jit(solution)/shard_map/all_to_all | solution.py:776
  213.3 3.2 copy-start.6
  233.1 11.0 %all-to-all-start.8 = ((bf16[8,128,128]{2,1,0:T(8,128)(2,1)}), bf16[8,128,128]{2,1,0:T(8,128)(2,1)S(1)}, u32[]{:S(2)}, u32[]{:S(2)}) async-start(bf16[8,128,128]{2,1,0:T(8,128)(2,1)} %get-tuple-element.98), calls=%async_computation.8 | async-start | bytes 524288 | tf_op jit(solution)/shard_map/all_to_all | solution.py:776
  236.5 138.7 %reduce-scatter.2.cloned.1.call-start = ((), (), s32[]{:S(2)}) async-start(), calls=%async_computation.17 | async-start | bytes 8355840 | tf_op jit(solution)/shard_map/reduce_scatter | solution.py:828
  244.1 0.7 copy-start.8
  286.1 12.1 %copy-start.19 = (bf16[64,3,16,128]{3,2,1,0:T(8,128)(2,1)S(1)}, bf16[64,3,16,128]{3,2,1,0:T(8,128)(2,1)}, u32[]{:S(2)}) copy-start(bf16[64,3,16,128]{3,2,1,0:T(8,128)(2,1)} %get-tuple-element.117) | copy-start | bytes 2359300
  286.1 12.0 %all-to-all-start.10 = ((bf16[8,128,128]{2,1,0:T(8,128)(2,1)}), bf16[8,128,128]{2,1,0:T(8,128)(2,1)S(1)}, u32[]{:S(2)}, u32[]{:S(2)}) async-start(bf16[8,128,128]{2,1,0:T(8,128)(2,1)} %get-tuple-element.107), calls=%async_computation.10 | async-start | bytes 524288 | tf_op jit(solution)/shard_map/all_to_all | solution.py:776
  298.1 1.1 copy-start.7
  298.1 14.7 %collective-permute-start.2 = (bf16[64,18,16,128]{3,2,1,0:T(8,128)(2,1)}, bf16[64,18,16,128]{3,2,1,0:T(8,128)(2,1)}, u32[]{:S(2)}, u32[]{:S(2)}) collective-permute-start(bf16[64,18,16,128]{3,2,1,0:T(8,128)(2,1)} %get-tuple-element.115), channel_id=1, source_target_pairs={{0,8},{8,0},{1,9},{9,1},{2,10},{10,2},{3,11},{11,3},{4,12},{12,4},... | collective-permute-start | bytes 14155784 | tf_op jit(solution)/shard_map/ppermute | solution.py:672
  298.2 14.5 %collective-permute-start.3 = (bf16[64,3,16,128]{3,2,1,0:T(8,128)(2,1)S(1)}, bf16[64,3,16,128]{3,2,1,0:T(8,128)(2,1)S(1)}, u32[]{:S(2)}, u32[]{:S(2)}) collective-permute-start(bf16[64,3,16,128]{3,2,1,0:T(8,128)(2,1)S(1)} %copy-done.19), channel_id=1, source_target_pairs={{0,8},{8,0},{1,9},{9,1},{2,10},{10,2},{3,11},{11,3},{4,12},{12,4},... | collective-permute-start | bytes 2359304 | tf_op jit(solution)/shard_map/ppermute | solution.py:672
  307.2 18.3 %all-to-all-start.11 = ((bf16[8,128,384]{2,1,0:T(8,128)(2,1)}), bf16[8,128,384]{2,1,0:T(8,128)(2,1)S(1)}, u32[]{:S(2)}, u32[]{:S(2)}) async-start(bf16[8,128,384]{2,1,0:T(8,128)(2,1)} %shard_map.251), calls=%async_computation.11 | async-start | bytes 1572864 | tf_op jit(solution)/shard_map/all_to_all | solution.py:776
  312.8 0.9 copy-start.9
  325.5 0.9 copy-start.2
  326.4 45.3 %all-to-all-start.12 = ((bf16[8,8,21,16,128]{4,3,2,1,0:T(8,128)(2,1)}), bf16[8,8,21,16,128]{4,3,2,1,0:T(8,128)(2,1)}, u32[]{:S(2)}, u32[]{:S(2)}) async-start(bf16[8,8,21,16,128]{4,3,2,1,0:T(8,128)(2,1)} %bitcast.68), calls=%async_computation.12 | async-start | bytes 11010048 | tf_op jit(solution)/shard_map/all_to_all | solution.py:716
  336.3 16.7 %collective-permute-start.6 = (bf16[64,9,16,128]{3,2,1,0:T(8,128)(2,1)}, bf16[64,9,16,128]{3,2,1,0:T(8,128)(2,1)S(1)}, u32[]{:S(2)}, u32[]{:S(2)}) collective-permute-start(bf16[64,9,16,128]{3,2,1,0:T(8,128)(2,1)} %get-tuple-element.136), channel_id=1, source_target_pairs={{0,8},{8,0},{1,9},{9,1},{2,10},{10,2},{3,11},{11,3},{4,12},{12,4},... | collective-permute-start | bytes 7077896 | tf_op jit(solution)/shard_map/ppermute | solution.py:672
  336.4 11.9 %copy-start.13 = (f32[4,768]{1,0:T(4,128)S(1)}, f32[4,768]{1,0:T(4,128)}, u32[]{:S(2)}) copy-start(f32[4,768]{1,0:T(4,128)} %get-tuple-element.129) | copy-start | bytes 36868
  336.4 11.9 %copy-start.12 = (f32[1,3072]{1,0:T(1,128)S(1)}, f32[1,3072]{1,0:T(1,128)}, u32[]{:S(2)}) copy-start(f32[1,3072]{1,0:T(1,128)} %get-tuple-element.131) | copy-start | bytes 36868
  336.4 12.8 %copy-start.16 = (f32[4,768]{1,0:T(4,128)S(1)}, f32[4,768]{1,0:T(4,128)}, u32[]{:S(2)}) copy-start(f32[4,768]{1,0:T(4,128)} %get-tuple-element.127) | copy-start | bytes 36868
  336.4 12.9 %copy-start.15 = (f32[4,768]{1,0:T(4,128)S(1)}, f32[4,768]{1,0:T(4,128)}, u32[]{:S(2)}) copy-start(f32[4,768]{1,0:T(4,128)} %get-tuple-element.128) | copy-start | bytes 36868
  336.5 13.7 %copy-start.14 = (f32[1,3072]{1,0:T(1,128)S(1)}, f32[1,3072]{1,0:T(1,128)}, u32[]{:S(2)}) copy-start(f32[1,3072]{1,0:T(1,128)} %get-tuple-element.130) | copy-start | bytes 36868
  342.3 8.8 %copy-start.17 = (f32[4,768]{1,0:T(4,128)S(1)}, f32[4,768]{1,0:T(4,128)}, u32[]{:S(2)}) copy-start(f32[4,768]{1,0:T(4,128)} %get-tuple-element.126) | copy-start | bytes 36868
  342.3 9.6 %copy-start.27 = (bf16[128,128]{1,0:T(8,128)(2,1)S(1)}, bf16[128,128]{1,0:T(8,128)(2,1)}, u32[]{:S(2)}) copy-start(bf16[128,128]{1,0:T(8,128)(2,1)} %constant.45.clone) | copy-start | bytes 98308
  347.5 7.0 %collective-permute-start.4 = (bf16[64,9,16,128]{3,2,1,0:T(8,128)(2,1)}, bf16[64,9,16,128]{3,2,1,0:T(8,128)(2,1)}, u32[]{:S(2)}, u32[]{:S(2)}) collective-permute-start(bf16[64,9,16,128]{3,2,1,0:T(8,128)(2,1)} %get-tuple-element.125), channel_id=1, source_target_pairs={{0,8},{8,0},{1,9},{9,1},{2,10},{10,2},{3,11},{11,3},{4,12},{12,4},... | collective-permute-start | bytes 7077896 | tf_op jit(solution)/shard_map/ppermute | solution.py:672
  353.0 1.5 collective-permute-start.5
  353.1 1.5 copy-start.4
  354.5 0.7 copy-start.10
  440.2 12.4 %all-to-all-start.15 = ((bf16[8,20,16,128]{3,2,1,0:T(8,128)(2,1)}), bf16[8,20,16,128]{3,2,1,0:T(8,128)(2,1)S(1)}, u32[]{:S(2)}, u32[]{:S(2)}) async-start(bf16[8,20,16,128]{3,2,1,0:T(8,128)(2,1)} %get-tuple-element.140), calls=%async_computation.16 | async-start | bytes 1310720 | tf_op jit(solution)/shard_map/all_to_all | solution.py:865
  452.5 0.9 copy-start.3
Sparse Core Ops, SparseCore 0:
  34.3 64.8 all-gather.4
  101.5 114.9 all-gather.6
  244.3 112.6 reduce-scatter.1

commit v7 on v6

--- a/solution.py
+++ b/solution.py
@@ -298,7 +298,7 @@
     fetch(layer, 2, core, src[2], wd, sems.at[2], 0, 8)
 
 
-def forward(h_ref, back, vec, upb, o_ref, h1_ref, a2_ref, u_ref, next_ref, wo, wu, wd, sems):
+def forward(h_ref, back, vec, upb, o_ref, h1_ref, a2_ref, u_ref, f_ref, next_ref, wo, wu, wd, sems):
     o = unwindow(lambda d: back[d].astype(f32)).astype(bf16)
     o_ref[...] = o
     arrived(wo, sems.at[0])
@@ -311,9 +311,15 @@
     arrived(wu, sems.at[1])
     acts = []
     for j in range(12):
-        u = mul(a2, units(wu, 2 * j, 2)) + upb[:, 256 * j : 256 * j + 256]
-        u_ref[:, 256 * j : 256 * j + 256] = u
-        acts.append(gelu_both(u)[0].astype(bf16))
+        c = slice(256 * j, 256 * j + 256)
+        u = mul(a2, units(wu, 2 * j, 2)) + upb[:, c]
+        act, slope = gelu_both(u)
+        acts.append(act.astype(bf16))
+        if f_ref is None:
+            u_ref[:, c] = u
+        else:
+            u_ref[:, c] = slope
+            f_ref[:, c] = acts[-1]
     f = jnp.concatenate(acts, axis=1)
     arrived(wd, sems.at[2])
     for j in range(3):
@@ -322,10 +328,12 @@
         next_ref[:, c] = (h1[:, c] + mul(f, w) + vec[3:4, c]).astype(next_ref.dtype)
 
 
-def forward_kernel(core, h_ref, back, vec, upb, *refs):
+def last_kernel(core, h_ref, back, vec, upb, e_ref, *refs):
     src, refs = sources_of(1, (0, 1, 2), refs)
-    fetch_forward(1, core, src, *refs[5:])
-    forward(h_ref, back, vec, upb, *refs)
+    o_ref, a2_ref, next_ref, f_ref, outs, h1, slope, ws = refs[0], refs[1], refs[2], refs[3], refs[4:9], refs[9], refs[10], refs[11:]
+    fetch_forward(1, core, src, *ws)
+    forward(h_ref, back, vec, upb, o_ref, h1, a2_ref, slope, f_ref, next_ref, *ws)
+    backward(e_ref, slope, h1, vec, None, *outs, *ws[:3], None)
 
 
 def forward_project_kernel(core, h_ref, back, vec, upb, vec_next, *refs):
@@ -334,7 +342,7 @@
     outs, (a1_ref, pay_ref), ws, (w, sem) = refs[:5], refs[5:7], refs[7:11], refs[11:]
     fetch_forward(0, core, src, *ws)
     fetch(1, 0, core, src_next[0], w, sem, 0, 6)
-    forward(h_ref, back, vec, upb, *outs, *ws)
+    forward(h_ref, back, vec, upb, *outs[:4], None, outs[4], *ws)
     project(outs[4], vec_next, a1_ref, pay_ref, w, sem)
 
 
@@ -345,19 +353,25 @@
 
 
 def backward(e_ref, u_ref, h1_ref, vec, f_ref, du_ref, e1_ref, pay_ref, small_ref, upb_ref, wo, wu, wd, sems):
+    def arrive(w, k):
+        if sems is not None:
+            arrived(w, sems.at[k])
+
     e = e_ref[...].astype(f32)
     e2 = e.astype(bf16)
-    arrived(wd, sems.at[2])
+    arrive(wd, 2)
     df = jnp.zeros((TOK, 4 * D), f32)
     for j in range(3):
         w = jnp.concatenate([tall_units(wd, 2 * j), tall_units(wd, 2 * j + 1)], axis=1)
         df = df + mul_t(e2[:, 256 * j : 256 * j + 256], w)
-    arrived(wu, sems.at[1])
+    arrive(wu, 1)
     cot = jnp.zeros((TOK, D), f32)
     for j in range(12):
         c = slice(256 * j, 256 * j + 256)
-        f, slope = gelu_both(u_ref[:, c])
-        f_ref[:, c] = f.astype(bf16)
+        slope = u_ref[:, c]
+        if f_ref is not None:
+            f, slope = gelu_both(slope)
+            f_ref[:, c] = f.astype(bf16)
         du = (df[:, c] * slope).astype(bf16)
         du_ref[:, c] = du
         upb_ref[:, c] = rows_sum(du.astype(f32))
@@ -370,19 +384,13 @@
     small_ref[1:2] = rows_sum(cot)
     small_ref[2:3] = rows_sum(b1.astype(f32))
     small_ref[3:4] = rows_sum(e2.astype(f32))
-    arrived(wo, sems.at[0])
+    arrive(wo, 0)
     do = jnp.zeros((TOK, D), f32)
     for j in range(3):
         do = do + mul_t(b1[:, 256 * j : 256 * j + 256], units(wo, 2 * j, 2))
     do = do.astype(bf16).astype(f32)
     for d, win in enumerate(windows(do)):
         pay_ref[d] = win.astype(bf16)
-
-
-def backward_kernel(core, e_ref, u_ref, h1_ref, vec, *refs):
-    src, refs = sources_of(1, (0, 1, 2), refs)
-    fetch_backward(1, core, src, *refs[6:])
-    backward(e_ref, u_ref, h1_ref, vec, *refs)
 
 
 def back_project(back, e1_ref, h_ref, vec, g_ref, e_ref, small_ref, w, sem):
@@ -711,9 +719,8 @@
     return add_pairs([(keep, swap_core(send)) for keep, send in pairs])
 
 
-def gather_sums(part):
-    part = part.reshape((8, 8) + part.shape[1:])
-    return sum_first(lax.all_to_all(part, ALL, 0, 0, axis_index_groups=GROUPS_B)).astype(bf16)
+def to_cube(part):
+    return lax.all_to_all(part.reshape((8, 8) + part.shape[1:]), ALL, 0, 0, axis_index_groups=GROUPS_B)
 
 
 def token_ids(group_index, positions, sequence_group, sequence_start, sequence_length):
@@ -779,8 +786,7 @@
     project_scratch = [w_scratch(18), DMA]
     project_outs = [((TOK, D), bf16), ((8, TOK, 384), bf16)]
     forward_outs = [((TOK, D), bf16), ((TOK, D), f32), ((TOK, D), bf16), ((TOK, 4 * D), f32)]
-    backward_outs = [((TOK, 4 * D), bf16), ((TOK, 4 * D), bf16), ((TOK, D), f32), ((8, TOK, 128), bf16),
-                     ((4, D), f32), ((1, 4 * D), f32)]
+    backward_outs = [((TOK, 4 * D), bf16), ((TOK, D), f32), ((8, TOK, 128), bf16), ((4, D), f32), ((1, 4 * D), f32)]
     back_project_outs = [((TOK, 3 * D), bf16), ((TOK, D), f32), ((4, D), f32)]
 
     hidden_0 = hidden_in[0]
@@ -802,12 +808,6 @@
         block_scratch + project_scratch, us=12)
     heads_1 = exchange(pay)
     back = exchange(attend(heads_1))
-    o_1, h1_1, a2_1, u_1, hidden = call(
-        forward_kernel,
-        forward_outs + [((TOK, D), bf16)],
-        [(core, "s"), (hidden_1, "v"), (back, "v"), (vecs[3], "v"), (ups[1:2], "v")] + weights(1, True),
-        block_scratch, us=8)
-
     def grad_joint(a1, g, o, e1):
         return call(
             grad_joint_cube, [((64, 9, 16, 128), bf16)] * 2,
@@ -816,10 +816,11 @@
 
     grad = out_grad[0]
     few_rows, few_up, joint = [None] * 2, [None] * 2, [None] * 2
-    f, du, e1, pay, small_b, few_up[1] = call(
-        backward_kernel, backward_outs,
-        [(core, "s"), (grad, "v"), (u_1, "v"), (h1_1, "v"), (vecs[3], "v")] + weights(1, True),
-        block_scratch, us=10)
+    o_1, a2_1, hidden, f, du, e1, pay, small_b, few_up[1] = call(
+        last_kernel,
+        [((TOK, D), bf16), ((TOK, D), bf16), ((TOK, D), bf16), ((TOK, 4 * D), bf16)] + backward_outs,
+        [(core, "s"), (hidden_1, "v"), (back, "v"), (vecs[3], "v"), (ups[1:2], "v"), (grad, "v")] + weights(1, True),
+        [pltpu.VMEM((TOK, D), f32), pltpu.VMEM((TOK, 4 * D), f32)] + block_scratch, us=16)
     cot = exchange(pay)
     keep_u, send_u, mlp_1 = call(
         grad_mlp_split, [((64, 3, 16, 128), bf16)] * 2 + [((16, 120, 16, 128), bf16)],
@@ -828,15 +829,15 @@
     scattered = lax.psum_scatter(after(mlp_1, cot), DATA, scatter_dimension=0, tiled=False)
     back = exchange(attend_back(heads_1, after(cot, mlp_1)))
     e1_1, small_b1 = e1, small_b
-    g_1, grad, small_a1, f, du, e1, pay, small_b, few_up[0] = call(
-        back_both_kernel, back_project_outs + backward_outs,
+    g_1, grad, small_a1, f_0, du, e1, pay, small_b, few_up[0] = call(
+        back_both_kernel, back_project_outs + [((TOK, 4 * D), bf16)] + backward_outs,
         [(core, "s"), (back, "v"), (e1_1, "v"), (hidden_1, "v"), (vecs[2], "v"), (u_0, "v"), (h1_0, "v"),
          (vecs[1], "v")] + weights(1, False) + weights(0, True),
         project_scratch + block_scratch, us=16)
     cot = exchange(pay)
     keep_ud, send_ud = call(
         grad_mlp_cube, [((64, 18, 16, 128), bf16)] * 2,
-        [(core, "s"), (f, "v"), (grad, "v"), (a2_0, "v"), (du, "v")],
+        [(core, "s"), (f_0, "v"), (grad, "v"), (a2_0, "v"), (du, "v")],
         [pltpu.VMEM((2, 64, 18, 16, 128), bf16), DMA((2,))], us=9, out_spaces="aa")
     send_ud = after(send_ud, cot)
     back = exchange(attend_back(heads_0, after(cot, keep_ud)))
@@ -856,9 +857,9 @@
     few = jnp.pad(few.reshape(2, 64, 1, 2, 128), ((0, 0),) * 3 + ((0, 14), (0, 0)))
     few = [jnp.where(core[0] == k, few[0], few[1]) for k in range(2)]
 
-    middle = gather_sums(middle)
-    last = gather_sums(after(core_sums([joint[0], few, joint[1]]), middle, scattered))
-    sums = jnp.concatenate([last, middle], axis=1)
+    middle = to_cube(middle)
+    last = to_cube(after(core_sums([joint[0], few, joint[1]]), middle, scattered))
+    sums = jnp.concatenate([sum_first(last).astype(bf16), sum_first(middle).astype(bf16)], axis=1)
     sums = lax.all_to_all(sums, ALL, 0, 0, axis_index_groups=GROUPS_A)
     sums, few = call(finish_kernel, [((8, 20, 16, 128), bf16), ((2, 128), f32)],
                      [(sums, "v"), (scattered, "v")])

time: 471 us -> 466 us (0.989)
  blocking collectives: 159 us -> 121 us
  waiting for transfers between devices: 74 us -> 106 us
  starting transfers between devices: 46.6 us -> 51.7 us
    all_to_all x1 -> x0, blocking collectives: 36.8 us -> none  [gather_sums(): lax.all_to_all(part, ALL, 0, 0, axis_index_groups=GROUPS_B)]
    all_to_all x1 -> x2, waiting for transfers between devices: 8.05 us -> 38.6 us  [to_cube(): lax.all_to_all(part.reshape((8, 8) + part.shape[1:]), ALL, 0, 0, axis_ind...]
    pallas_call x18 -> x17, Pallas kernels: 117 us -> 113 us  [call(): pl.pallas_call(kernel, out_shape=[jax.ShapeDtypeStruct(*o) for o in outs]...]
  transfers between devices with their start and end apart: 19 -> 20, of which waited for: 10 -> 11; matrix products, arithmetic and copies ran while one was open for 5% -> 5% of each run, Pallas kernels for 23% -> 24%
where the time goes in v7:
time: 466 us; the launch traced here: 457 us
  Pallas kernels  130 us (28%)
  blocking collectives  121 us (26%)
  waiting for transfers between devices  106 us (23%)
  starting transfers between devices  51.7 us (11%)
  local copies, waits for them, and re-layouts  21.5 us (5%)
  between operations  14.7 us (3%)
  other arithmetic  11.7 us (3%)
    pallas_call x17, Pallas kernels, call(): pl.pallas_call(kernel, out_shape=[jax.ShapeDtypeStruct(*o) for o in outs]...  113 us
    all_to_all x3, blocking collectives, exchange(): return lax.all_to_all(values, CTX, 0, 0)  54.5 us
    all_to_all x2, blocking collectives, copies(): return lax.all_to_all(many, ALL, 0, 0, axis_index_groups=groups)  45.8 us
    all_to_all x2, waiting for transfers between devices, to_cube(): lax.all_to_all(part.reshape((8, 8) + part.shape[1:]), ALL, 0, 0, axis_ind...  38.6 us
    all_to_all x1, waiting for transfers between devices, body(): lax.all_to_all(after(shards, heads_0, down_0), ALL, 0, 0, axis_index_grou...  26.8 us
    all_to_all x5, starting transfers between devices, exchange(): return lax.all_to_all(values, CTX, 0, 0)  25.7 us
    all_to_all x1, blocking collectives, body(): sums = lax.all_to_all(sums, ALL, 0, 0, axis_index_groups=GROUPS_A)  21.1 us
    pallas_call x2, Pallas kernels, add_pairs(): pl.pallas_call(add_kernel, grid=(8,), out_shape=jax.ShapeDtypeStruct((64,...  17.2 us
  transfers between devices with their start and end apart: 20, of which 11 were waited for; matrix products, arithmetic and copies ran while one was open for 5% of the time, Pallas kernels for 24%

profile of v7, /device:TPU:0, one launch (start us, length us, event | category | flops | bytes accessed | tf_op | source)
XLA Modules:
  0.0 457.1 jit_solution(11561213679209177155)
XLA Ops:
  7.2 2.4 shard_map.239
  9.7 5.7 %all-to-all-start = ((bf16[8,31,16,128]{3,2,1,0:T(8,128)(2,1)}), bf16[8,31,16,128]{3,2,1,0:T(8,128)(2,1)S(1)}, u32[]{:S(2)}, u32[]{:S(2)}) async-start(bf16[8,31,16,128]{3,2,1,0:T(8,128)(2,1)} %shard_map.239), calls=%async_computation | async-start | bytes 2031616 | tf_op jit(solution)/shard_map/all_to_all | solution.py:751
  16.6 14.2 %all-to-all-done.got = bf16[8,31,16,128]{3,2,1,0:T(8,128)(2,1)S(1)} async-done(((bf16[8,31,16,128]{3,2,1,0:T(8,128)(2,1)}), bf16[8,31,16,128]{3,2,1,0:T(8,128)(2,1)S(1)}, u32[]{:S(2)}, u32[]{:S(2)}) %all-to-all-start) | async-done | bytes 1015840 | tf_op jit(solution)/shard_map/all_to_all | solution.py:751
  30.8 1.0 copy-done.1
  31.8 2.3 shard_map.240
  34.2 1.0 broadcast_in_dim.22
  35.2 21.7 %all_to_all.80 = bf16[8,28,16,128]{3,2,1,0:T(8,128)(2,1)S(1)} all-to-all(bf16[8,28,16,128]{3,2,1,0:T(8,128)(2,1)S(1)} %broadcast_in_dim.22), channel_id=1, replica_groups={{0,6,17,23,96,102,113,119},{2,4,19,21,98,100,115,117},{1,7,16,22,97,103..., dimensions={0} | all-to-all | bytes 1835008 | tf_op jit(solution)/shard_map/all_to_all | solution.py:672
  57.4 24.1 %all_to_all.81 = bf16[8,8,10,16,128]{4,3,2,1,0:T(8,128)(2,1)S(1)} all-to-all(bf16[8,8,10,16,128]{4,3,2,1,0:T(8,128)(2,1)S(1)} %broadcast_in_dim.23), channel_id=1, replica_groups={{0,2,1,3,32,34,33,35},{6,4,7,5,38,36,39,37},{17,19,16,18,49,51,48,50},{..., dimensions={0} | all-to-all | bytes 5242880 | tf_op jit(solution)/shard_map/all_to_all | solution.py:672
  81.6 3.0 broadcast_in_dim.24
  84.6 2.0 collective-permute-done.theirs.refs_1_.refs_3_
  86.5 7.4 %shard_map.241 = (bf16[128,768]{1,0:T(8,128)(2,1)}, bf16[8,128,384]{2,1,0:T(8,128)(2,1)}, f32[4,768]{1,0:T(4,128)}, f32[4,768]{1,0:T(4,128)}, f32[4,768]{1,0:T(4...) custom-call(s32[1]{0:T(128)} %bitcast.core.core_ref, bf16[128,768]{1,0:T(8,128)(2,1)} %bitcast.70, ...), custom_call_target="tpu_custom_call" | custom-call | bytes 25830000 | tf_op jit(solution)/shard_map/pallas_call | solution.py:647
  94.0 18.0 %all_to_all.82.heads = bf16[8,128,384]{2,1,0:T(8,128)(2,1)} all-to-all(bf16[8,128,384]{2,1,0:T(8,128)(2,1)} %get-tuple-element.79), channel_id=1, replica_groups=mesh['y'=4,'zh'=2,'c'=2,'x'=4,'zl'=2] {'x','zl'}, dimensions={0} | all-to-all | bytes 1572864 | tf_op jit(solution)/shard_map/all_to_all | solution.py:783
  112.0 4.8 %all-to-all-start.4 = ((bf16[8,8,18,16,128]{4,3,2,1,0:T(8,128)(2,1)}), bf16[8,8,18,16,128]{4,3,2,1,0:T(8,128)(2,1)}, u32[]{:S(2)}, u32[]{:S(2)}) async-start(bf16[8,8,18,16,128]{4,3,2,1,0:T(8,128)(2,1)} %broadcast_in_dim.24), calls=%async_computation.4 | async-start | bytes 9437184 | tf_op jit(solution)/shard_map/all_to_all | solution.py:797
  118.2 0.9 subtract_select_fusion.idc
  119.0 5.5 %shard_map.242 = bf16[8,128,128]{2,1,0:T(8,128)(2,1)} custom-call(s32[1]{0:T(128)} %bitcast.2.par_ref, bf16[8,128,384]{2,1,0:T(8,128)(2,1)} %all_to_all.82.heads, s32[8,128,1]{2,1,0:T(8,128)} %subtract_select_fusion.idc, s32[1,1024]{1,0:T(1,128)} %reshape_select_fusion.idr), custom_call_target="tpu_custom_call" | custom-call | bytes 22140000 | tf_op jit(solution)/shard_map/pallas_call | solution.py:647
  124.6 26.8 %all-to-all-done.4 = bf16[8,8,18,16,128]{4,3,2,1,0:T(8,128)(2,1)} async-done(((bf16[8,8,18,16,128]{4,3,2,1,0:T(8,128)(2,1)}), bf16[8,8,18,16,128]{4,3,2,1,0:T(8,128)(2,1)}, u32[]{:S(2)}, u32[]{:S(2)}) %all-to-all-start.4) | async-done | bytes 4718624 | tf_op jit(solution)/shard_map/all_to_all | solution.py:797
  151.8 9.3 %all-to-all-start.5 = ((bf16[8,128,128]{2,1,0:T(8,128)(2,1)}), bf16[8,128,128]{2,1,0:T(8,128)(2,1)S(1)}, u32[]{:S(2)}, u32[]{:S(2)}) async-start(bf16[8,128,128]{2,1,0:T(8,128)(2,1)} %shard_map.242), calls=%async_computation.5 | async-start | bytes 524288 | tf_op jit(solution)/shard_map/all_to_all | solution.py:783
  161.6 0.8 slice.158.upb
  162.4 6.3 %all-to-all-done.5.back = bf16[8,128,128]{2,1,0:T(8,128)(2,1)S(1)} async-done(((bf16[8,128,128]{2,1,0:T(8,128)(2,1)}), bf16[8,128,128]{2,1,0:T(8,128)(2,1)S(1)}, u32[]{:S(2)}, u32[]{:S(2)}) %all-to-all-start.5) | async-done | bytes 262176 | tf_op jit(solution)/shard_map/all_to_all | solution.py:783
  168.7 0.7 copy-done.6
  169.3 9.8 %shard_map.243 = (bf16[128,768]{1,0:T(8,128)(2,1)}, f32[128,768]{1,0:T(8,128)}, bf16[128,768]{1,0:T(8,128)(2,1)}, f32[128,3072]{1,0:T(8,128)}, f32[128,768]{1,0:...) custom-call(s32[1]{0:T(128)} %bitcast.core.core_ref, bf16[128,768]{1,0:T(8,128)(2,1)} %bitcast.71, ...), custom_call_target="tpu_custom_call" | custom-call | bytes 44280000 | tf_op jit(solution)/shard_map/pallas_call | solution.py:647
  179.1 17.9 %all_to_all.83.heads = bf16[8,128,384]{2,1,0:T(8,128)(2,1)} all-to-all(bf16[8,128,384]{2,1,0:T(8,128)(2,1)} %get-tuple-element.88), channel_id=1, replica_groups=mesh['y'=4,'zh'=2,'c'=2,'x'=4,'zl'=2] {'x','zl'}, dimensions={0} | all-to-all | bytes 1572864 | tf_op jit(solution)/shard_map/all_to_all | solution.py:783
  197.0 5.6 %shard_map.244 = bf16[8,128,128]{2,1,0:T(8,128)(2,1)} custom-call(s32[1]{0:T(128)} %bitcast.2.par_ref, bf16[8,128,384]{2,1,0:T(8,128)(2,1)} %all_to_all.83.heads, s32[8,128,1]{2,1,0:T(8,128)} %subtract_select_fusion.idc, s32[1,1024]{1,0:T(1,128)} %reshape_select_fusion.idr), custom_call_target="tpu_custom_call" | custom-call | bytes 22140000 | tf_op jit(solution)/shard_map/pallas_call | solution.py:647
  202.6 3.7 all-to-all-start.7
  206.8 0.8 slice.160.upb
  207.6 5.7 %all-to-all-done.7.back = bf16[8,128,128]{2,1,0:T(8,128)(2,1)S(1)} async-done(((bf16[8,128,128]{2,1,0:T(8,128)(2,1)}), bf16[8,128,128]{2,1,0:T(8,128)(2,1)S(1)}, u32[]{:S(2)}, u32[]{:S(2)}) %all-to-all-start.7) | async-done | bytes 262176 | tf_op jit(solution)/shard_map/all_to_all | solution.py:783
  213.3 3.1 all-gather.7.cloned.1.call-done
  216.4 12.2 %shard_map.245 = (bf16[128,768]{1,0:T(8,128)(2,1)}, bf16[128,768]{1,0:T(8,128)(2,1)}, bf16[128,768]{1,0:T(8,128)(2,1)}, bf16[128,3072]{1,0:T(8,128)(2,1)}, bf16[...) custom-call(s32[1]{0:T(128)} %bitcast.core.core_ref, ...), custom_call_target="tpu_custom_call" | custom-call | bytes 59040000 | tf_op jit(solution)/shard_map/pallas_call | solution.py:647
  228.6 3.4 all-to-all-start.8
  232.3 7.3 %shard_map.246 = (bf16[64,3,16,128]{3,2,1,0:T(8,128)(2,1)}, bf16[64,3,16,128]{3,2,1,0:T(8,128)(2,1)}, bf16[16,120,16,128]{3,2,1,0:T(8,128)(2,1)}) custom-call(s32[1]{0:T(128)} %bitcast.core.core_ref, bf16[128,3072]{1,0:T(8,128)(2,1)} %get-tuple-element.95.f_ref, bf16[128,768]{1,0:T(8,128)(2,1)} %bitcast.77, bf16[128,768]{1,0:T(8,128)(2,1)} %get-tuple-element.96.a2_ref, ...), custom_call_target="tpu_custom_call" | custom-call | bytes 33210000 | tf_op jit(solution)/shard_map/pallas_call | solution.py:647
  239.7 0.7 copy-done.8
  240.4 8.0 %shard_map.247 = bf16[8,128,384]{2,1,0:T(8,128)(2,1)} custom-call(s32[1]{0:T(128)} %bitcast.2.par_ref, bf16[8,128,384]{2,1,0:T(8,128)(2,1)} %all_to_all.83.heads, bf16[8,128,128]{2,1,0:T(8,128)(2,1)} %copy-done.8, s32[8,128,1]{2,1,0:T(8,128)} %subtract_select_fusion.idc, s32[1,1024]{1,0:T(1,128)} %reshape_select_fusion.idr), custom_call_target="tpu_custom_call" | custom-call | bytes 29520000 | tf_op jit(solution)/shard_map/pallas_call | solution.py:647
  248.4 18.6 %all_to_all.84.back = bf16[8,128,384]{2,1,0:T(8,128)(2,1)} all-to-all(bf16[8,128,384]{2,1,0:T(8,128)(2,1)} %shard_map.247), channel_id=1, replica_groups=mesh['y'=4,'zh'=2,'c'=2,'x'=4,'zl'=2] {'x','zl'}, dimensions={0} | all-to-all | bytes 1572864 | tf_op jit(solution)/shard_map/all_to_all | solution.py:783
  267.0 14.6 %shard_map.248 = (bf16[128,2304]{1,0:T(8,128)(2,1)}, f32[128,768]{1,0:T(8,128)}, f32[4,768]{1,0:T(4,128)}, bf16[128,3072]{1,0:T(8,128)(2,1)}, bf16[128,3072]{1,0...) custom-call(s32[1]{0:T(128)} %bitcast.core.core_ref, ...), custom_call_target="tpu_custom_call" | custom-call | bytes 59040000 | tf_op jit(solution)/shard_map/pallas_call | solution.py:647
  281.6 3.6 all-to-all-start.10
  285.2 8.4 %shard_map.249 = (bf16[64,18,16,128]{3,2,1,0:T(8,128)(2,1)}, bf16[64,18,16,128]{3,2,1,0:T(8,128)(2,1)}) custom-call(s32[1]{0:T(128)} %bitcast.core.core_ref, bf16[128,3072]{1,0:T(8,128)(2,1)} %get-tuple-element.104.f_ref, f32[128,768]{1,0:T(8,128)} %get-tuple-element.105.e_ref, bf16[128,768]{1,0:T(8,128)(2,1)} %get-tuple-element.106.a2_ref, ...), custom_call_target="tpu_custom_call" | custom-call | bytes 33210000 | tf_op jit(solution)/shard_map/pallas_call | solution.py:647
  293.8 0.9 collective-permute-start.3
  294.7 8.0 %shard_map.250 = bf16[8,128,384]{2,1,0:T(8,128)(2,1)} custom-call(s32[1]{0:T(128)} %bitcast.2.par_ref, bf16[8,128,384]{2,1,0:T(8,128)(2,1)} %all_to_all.82.heads, bf16[8,128,128]{2,1,0:T(8,128)(2,1)} %copy-done.7, s32[8,128,1]{2,1,0:T(8,128)} %subtract_select_fusion.idc, s32[1,1024]{1,0:T(1,128)} %reshape_select_fusion.idr), custom_call_target="tpu_custom_call" | custom-call | bytes 29520000 | tf_op jit(solution)/shard_map/pallas_call | solution.py:647
  302.7 5.6 %all-to-all-start.11 = ((bf16[8,128,384]{2,1,0:T(8,128)(2,1)}), bf16[8,128,384]{2,1,0:T(8,128)(2,1)S(1)}, u32[]{:S(2)}, u32[]{:S(2)}) async-start(bf16[8,128,384]{2,1,0:T(8,128)(2,1)} %shard_map.250), calls=%async_computation.11 | async-start | bytes 1572864 | tf_op jit(solution)/shard_map/all_to_all | solution.py:783
  308.4 0.9 copy-done.9
  309.3 8.8 %shard_map.251 = bf16[64,21,16,128]{3,2,1,0:T(8,128)(2,1)} custom-call(bf16[64,18,16,128]{3,2,1,0:T(8,128)(2,1)} %get-tuple-element.108.refs_0_, bf16[64,18,16,128]{3,2,1,0:T(8,128)(2,1)} %collective-permute-done.2.refs_1_, bf16[64,3,16,128]{3,2,1,0:T(8,128)(2,1)} %get-tuple-element.112.refs_2_, bf16[64,3,16,128]{3,2,1,0:T(8,128)(2,1)} %copy-done.9), custom_call_target="tpu_custom_call" | custom-call | flops 4194304 | bytes 16515072 | tf_op jit(solution)/shard_map/pallas_call | solution.py:707
  318.1 2.9 all-to-all-done.11.back
  321.0 0.9 copy-done.2
  322.0 4.7 %all-to-all-start.12 = ((bf16[8,8,21,16,128]{4,3,2,1,0:T(8,128)(2,1)}), bf16[8,8,21,16,128]{4,3,2,1,0:T(8,128)(2,1)}, u32[]{:S(2)}, u32[]{:S(2)}) async-start(bf16[8,8,21,16,128]{4,3,2,1,0:T(8,128)(2,1)} %bitcast.66), calls=%async_computation.12 | async-start | bytes 11010048 | tf_op jit(solution)/shard_map/all_to_all | solution.py:723
  326.7 5.2 %shard_map.254 = (bf16[64,9,16,128]{3,2,1,0:T(8,128)(2,1)}, bf16[64,9,16,128]{3,2,1,0:T(8,128)(2,1)}) custom-call(s32[1]{0:T(128)} %bitcast.core.core_ref, bf16[128,768]{1,0:T(8,128)(2,1)} %get-tuple-element.128.a_ref, bf16[128,2304]{1,0:T(8,128)(2,1)} %get-tuple-element.129.g_ref, bf16[128,768]{1,0:T(8,128)(2,1)} %get-tuple-element.130.o_ref, ...), custom_call_target="tpu_custom_call" | custom-call | bytes 18450000 | tf_op jit(solution)/shard_map/pallas_call | solution.py:647
  332.0 5.8 %shard_map.252 = (bf16[128,2304]{1,0:T(8,128)(2,1)}, f32[128,768]{1,0:T(8,128)}, f32[4,768]{1,0:T(4,128)}) custom-call(s32[1]{0:T(128)} %bitcast.core.core_ref, bf16[8,128,384]{2,1,0:T(8,128)(2,1)} %copy-done.2, f32[128,768]{1,0:T(8,128)} %get-tuple-element.115.e1_ref, bf16[128,768]{1,0:T(8,128)(2,1)} %bitcast.72, f32[4,768]{1,0:T(4,128)} %get-tuple-element.116.vec, ...), custom_call_target="tpu_custom_call" | custom-call | bytes 22140000 | tf_op jit(solution)/shard_map/pallas_call | solution.py:647
  337.9 5.2 %shard_map.253 = (bf16[64,9,16,128]{3,2,1,0:T(8,128)(2,1)}, bf16[64,9,16,128]{3,2,1,0:T(8,128)(2,1)}) custom-call(s32[1]{0:T(128)} %bitcast.core.core_ref, bf16[128,768]{1,0:T(8,128)(2,1)} %get-tuple-element.91.a_ref, bf16[128,2304]{1,0:T(8,128)(2,1)} %get-tuple-element.118.g_ref, bf16[128,768]{1,0:T(8,128)(2,1)} %get-tuple-element.119.o_ref, ...), custom_call_target="tpu_custom_call" | custom-call | bytes 18450000 | tf_op jit(solution)/shard_map/pallas_call | solution.py:647
  343.1 0.7 collective-permute-start.4
  347.7 0.8 select_bitcast_fusion
  348.6 1.5 collective-permute-done.5.refs_3_
  350.8 8.4 %shard_map.255 = bf16[64,19,16,128]{3,2,1,0:T(8,128)(2,1)} custom-call(bf16[64,9,16,128]{3,2,1,0:T(8,128)(2,1)} %get-tuple-element.120.refs_0_, bf16[64,9,16,128]{3,2,1,0:T(8,128)(2,1)} %collective-permute-done.4.refs_1_, bf16[64,1,16,128]{3,2,1,0:T(8,128)(2,1)} %get-tuple-element.144.refs_2_, bf16[64,1,16,128]{3,2,1,0:T(8,128)(2,1)} %copy-done.10, ...), custom_call_target="tpu_custom_call" | custom-call | flops 4194304 | bytes 14942208 | tf_op jit(solution)/shard_map/pallas_call | solution.py:707
  359.2 8.2 %all-to-all-done.12 = bf16[8,8,21,16,128]{4,3,2,1,0:T(8,128)(2,1)} async-done(((bf16[8,8,21,16,128]{4,3,2,1,0:T(8,128)(2,1)}), bf16[8,8,21,16,128]{4,3,2,1,0:T(8,128)(2,1)}, u32[]{:S(2)}, u32[]{:S(2)}) %all-to-all-start.12) | async-done | bytes 5505056 | tf_op jit(solution)/shard_map/all_to_all | solution.py:723
  367.4 4.6 %all-to-all-start.13 = ((bf16[8,8,19,16,128]{4,3,2,1,0:T(8,128)(2,1)}), bf16[8,8,19,16,128]{4,3,2,1,0:T(8,128)(2,1)}, u32[]{:S(2)}, u32[]{:S(2)}) async-start(bf16[8,8,19,16,128]{4,3,2,1,0:T(8,128)(2,1)} %bitcast.67), calls=%async_computation.14 | async-start | bytes 9961472 | tf_op jit(solution)/shard_map/all_to_all | solution.py:723
  372.1 3.5 reduce_sum.35
  375.5 30.4 %all-to-all-done.13 = bf16[8,8,19,16,128]{4,3,2,1,0:T(8,128)(2,1)} async-done(((bf16[8,8,19,16,128]{4,3,2,1,0:T(8,128)(2,1)}), bf16[8,8,19,16,128]{4,3,2,1,0:T(8,128)(2,1)}, u32[]{:S(2)}, u32[]{:S(2)}) %all-to-all-start.13) | async-done | bytes 4980768 | tf_op jit(solution)/shard_map/all_to_all | solution.py:723
  405.9 3.2 reduce_sum.34
  409.3 21.1 %all_to_all.85.parts = bf16[8,40,16,128]{3,2,1,0:T(8,128)(2,1)} all-to-all(bf16[8,40,16,128]{3,2,1,0:T(8,128)(2,1)S(1)} %pad_maximum_fusion), channel_id=1, replica_groups={{0,6,17,23,96,102,113,119},{2,4,19,21,98,100,115,117},{1,7,16,22,97,103..., dimensions={0} | all-to-all | bytes 2621440 | tf_op jit(solution)/shard_map/all_to_all | solution.py:863
  430.4 2.6 shard_map.256
  433.0 0.8 slice.191
  434.4 4.0 all-to-all-start.15
  438.4 1.0 fusion.29
  442.4 4.9 %all-to-all-done.15.got = bf16[8,20,16,128]{3,2,1,0:T(8,128)(2,1)S(1)} async-done(((bf16[8,20,16,128]{3,2,1,0:T(8,128)(2,1)}), bf16[8,20,16,128]{3,2,1,0:T(8,128)(2,1)S(1)}, u32[]{:S(2)}, u32[]{:S(2)}) %all-to-all-start.15) | async-done | bytes 655392 | tf_op jit(solution)/shard_map/all_to_all | solution.py:866
  447.3 0.8 copy-done.3
  448.2 2.2 shard_map.257
  (139 shorter events, 13.1 us)
Async XLA Ops:
  7.2 8.3 %copy-start.20 = (bf16[2,2,6]{2,1,0:T(2,128)(2,1)S(1)}, bf16[2,2,6]{2,1,0:T(2,128)(2,1)}, u32[]{:S(2)}) copy-start(bf16[2,2,6]{2,1,0:T(2,128)(2,1)} %param.21) | copy-start | bytes 148
  7.2 8.3 %copy-start.21 = (bf16[2,2,6]{2,1,0:T(2,128)(2,1)S(1)}, bf16[2,2,6]{2,1,0:T(2,128)(2,1)}, u32[]{:S(2)}) copy-start(bf16[2,2,6]{2,1,0:T(2,128)(2,1)} %param.22) | copy-start | bytes 148
  7.2 8.4 %copy-start.22 = (bf16[2,2,6]{2,1,0:T(2,128)(2,1)S(1)}, bf16[2,2,6]{2,1,0:T(2,128)(2,1)}, u32[]{:S(2)}) copy-start(bf16[2,2,6]{2,1,0:T(2,128)(2,1)} %param.24) | copy-start | bytes 148
  7.2 8.5 %copy-start.23 = (bf16[2,2,6]{2,1,0:T(2,128)(2,1)S(1)}, bf16[2,2,6]{2,1,0:T(2,128)(2,1)}, u32[]{:S(2)}) copy-start(bf16[2,2,6]{2,1,0:T(2,128)(2,1)} %param.26) | copy-start | bytes 148
  7.2 8.6 %copy-start.24 = (bf16[2,24]{1,0:T(2,128)(2,1)S(1)}, bf16[2,24]{1,0:T(2,128)(2,1)}, u32[]{:S(2)}) copy-start(bf16[2,24]{1,0:T(2,128)(2,1)} %param.28) | copy-start | bytes 292
  9.7 21.1 %all-to-all-start = ((bf16[8,31,16,128]{3,2,1,0:T(8,128)(2,1)}), bf16[8,31,16,128]{3,2,1,0:T(8,128)(2,1)S(1)}, u32[]{:S(2)}, u32[]{:S(2)}) async-start(bf16[8,31,16,128]{3,2,1,0:T(8,128)(2,1)} %shard_map.239), calls=%async_computation | async-start | bytes 2031616 | tf_op jit(solution)/shard_map/all_to_all | solution.py:751
  15.4 96.6 %all-gather.5.cloned.1.call-start = ((), (), s32[]{:S(2)}) async-start(), calls=%async_computation.18 | async-start | bytes 5013504 | tf_op jit(solution)/shard_map/all_gather | solution.py:756
  30.8 1.0 copy-start.1
  34.1 182.3 %all-gather.7.cloned.1.call-start = ((), (), s32[]{:S(2)}) async-start(), calls=%async_computation.19 | async-start | bytes 10027008 | tf_op jit(solution)/shard_map/all_gather | solution.py:793
  81.5 3.1 copy-start
  81.5 5.0 %collective-permute-start = (bf16[64,10,16,128]{3,2,1,0:T(8,128)(2,1)S(1)}, bf16[64,10,16,128]{3,2,1,0:T(8,128)(2,1)}, u32[]{:S(2)}, u32[]{:S(2)}) collective-permute-start(bf16[64,10,16,128]{3,2,1,0:T(8,128)(2,1)S(1)} %bitcast.59), channel_id=1, source_target_pairs={{0,8},{8,0},{1,9},{9,1},{2,10},{10,2},{3,11},{11,3},{4,12},{12,4},... | collective-permute-start | bytes 7864328 | tf_op jit(solution)/shard_map/ppermute | solution.py:680
  112.0 4.8 %copy-start.18 = (s32[48]{0:T(128)S(1)}, s32[48]{0:T(128)}, u32[]{:S(2)}) copy-start(s32[48]{0:T(128)} %param.19) | copy-start | bytes 580
  112.0 4.8 %copy-start.25 = (s32[48]{0:T(128)S(1)}, s32[48]{0:T(128)}, u32[]{:S(2)}) copy-start(s32[48]{0:T(128)} %param.20) | copy-start | bytes 580
  112.0 4.9 %copy-start.26 = (s32[48]{0:T(128)S(1)}, s32[48]{0:T(128)}, u32[]{:S(2)}) copy-start(s32[48]{0:T(128)} %param.18) | copy-start | bytes 580
  112.0 39.4 %all-to-all-start.4 = ((bf16[8,8,18,16,128]{4,3,2,1,0:T(8,128)(2,1)}), bf16[8,8,18,16,128]{4,3,2,1,0:T(8,128)(2,1)}, u32[]{:S(2)}, u32[]{:S(2)}) async-start(bf16[8,8,18,16,128]{4,3,2,1,0:T(8,128)(2,1)} %broadcast_in_dim.24), calls=%async_computation.4 | async-start | bytes 9437184 | tf_op jit(solution)/shard_map/all_to_all | solution.py:797
  116.8 34.6 %copy-start.11 = (f32[128,256]{1,0:T(8,128)S(1)}, f32[128,256]{1,0:T(8,128)}, u32[]{:S(2)}) copy-start(f32[128,256]{1,0:T(8,128)} %get-tuple-element.84) | copy-start | bytes 393220
  151.3 17.3 %collective-permute-start.1 = (bf16[64,18,16,128]{3,2,1,0:T(8,128)(2,1)}, bf16[64,18,16,128]{3,2,1,0:T(8,128)(2,1)}, u32[]{:S(2)}, u32[]{:S(2)}) collective-permute-start(bf16[64,18,16,128]{3,2,1,0:T(8,128)(2,1)} %bitcast.12.refs_2_.refs_5_.refs_0_.refs_4_), channel_id=1, source_target_pairs={{0,8},{8,0},{1,9},{9,1},{2,10},{10,2},{3,11},{11,3},{4,12},{12,4},... | collective-permute-start | bytes 14155784 | tf_op jit(solution)/shard_map/ppermute | solution.py:680
  151.8 16.9 %all-to-all-start.5 = ((bf16[8,128,128]{2,1,0:T(8,128)(2,1)}), bf16[8,128,128]{2,1,0:T(8,128)(2,1)S(1)}, u32[]{:S(2)}, u32[]{:S(2)}) async-start(bf16[8,128,128]{2,1,0:T(8,128)(2,1)} %shard_map.242), calls=%async_computation.5 | async-start | bytes 524288 | tf_op jit(solution)/shard_map/all_to_all | solution.py:783
  168.7 0.7 copy-start.6
  202.6 10.6 %all-to-all-start.7 = ((bf16[8,128,128]{2,1,0:T(8,128)(2,1)}), bf16[8,128,128]{2,1,0:T(8,128)(2,1)S(1)}, u32[]{:S(2)}, u32[]{:S(2)}) async-start(bf16[8,128,128]{2,1,0:T(8,128)(2,1)} %shard_map.244), calls=%async_computation.7 | async-start | bytes 524288 | tf_op jit(solution)/shard_map/all_to_all | solution.py:783
  213.3 3.1 copy-start.5
  228.6 11.0 %all-to-all-start.8 = ((bf16[8,128,128]{2,1,0:T(8,128)(2,1)}), bf16[8,128,128]{2,1,0:T(8,128)(2,1)S(1)}, u32[]{:S(2)}, u32[]{:S(2)}) async-start(bf16[8,128,128]{2,1,0:T(8,128)(2,1)} %get-tuple-element.94), calls=%async_computation.8 | async-start | bytes 524288 | tf_op jit(solution)/shard_map/all_to_all | solution.py:783
  232.1 135.4 %reduce-scatter.2.cloned.1.call-start = ((), (), s32[]{:S(2)}) async-start(), calls=%async_computation.17 | async-start | bytes 8355840 | tf_op jit(solution)/shard_map/reduce_scatter | solution.py:829
  239.7 0.7 copy-start.8
  281.6 12.1 %copy-start.19 = (bf16[64,3,16,128]{3,2,1,0:T(8,128)(2,1)S(1)}, bf16[64,3,16,128]{3,2,1,0:T(8,128)(2,1)}, u32[]{:S(2)}) copy-start(bf16[64,3,16,128]{3,2,1,0:T(8,128)(2,1)} %get-tuple-element.113) | copy-start | bytes 2359300
  281.6 12.0 %all-to-all-start.10 = ((bf16[8,128,128]{2,1,0:T(8,128)(2,1)}), bf16[8,128,128]{2,1,0:T(8,128)(2,1)S(1)}, u32[]{:S(2)}, u32[]{:S(2)}) async-start(bf16[8,128,128]{2,1,0:T(8,128)(2,1)} %get-tuple-element.103), calls=%async_computation.10 | async-start | bytes 524288 | tf_op jit(solution)/shard_map/all_to_all | solution.py:783
  293.7 1.1 copy-start.7
  293.7 14.7 %collective-permute-start.2 = (bf16[64,18,16,128]{3,2,1,0:T(8,128)(2,1)}, bf16[64,18,16,128]{3,2,1,0:T(8,128)(2,1)}, u32[]{:S(2)}, u32[]{:S(2)}) collective-permute-start(bf16[64,18,16,128]{3,2,1,0:T(8,128)(2,1)} %get-tuple-element.111), channel_id=1, source_target_pairs={{0,8},{8,0},{1,9},{9,1},{2,10},{10,2},{3,11},{11,3},{4,12},{12,4},... | collective-permute-start | bytes 14155784 | tf_op jit(solution)/shard_map/ppermute | solution.py:680
  293.8 14.6 %collective-permute-start.3 = (bf16[64,3,16,128]{3,2,1,0:T(8,128)(2,1)S(1)}, bf16[64,3,16,128]{3,2,1,0:T(8,128)(2,1)S(1)}, u32[]{:S(2)}, u32[]{:S(2)}) collective-permute-start(bf16[64,3,16,128]{3,2,1,0:T(8,128)(2,1)S(1)} %copy-done.19), channel_id=1, source_target_pairs={{0,8},{8,0},{1,9},{9,1},{2,10},{10,2},{3,11},{11,3},{4,12},{12,4},... | collective-permute-start | bytes 2359304 | tf_op jit(solution)/shard_map/ppermute | solution.py:680
  302.7 18.3 %all-to-all-start.11 = ((bf16[8,128,384]{2,1,0:T(8,128)(2,1)}), bf16[8,128,384]{2,1,0:T(8,128)(2,1)S(1)}, u32[]{:S(2)}, u32[]{:S(2)}) async-start(bf16[8,128,384]{2,1,0:T(8,128)(2,1)} %shard_map.250), calls=%async_computation.11 | async-start | bytes 1572864 | tf_op jit(solution)/shard_map/all_to_all | solution.py:783
  308.3 0.9 copy-start.9
  321.0 0.9 copy-start.2
  322.0 45.4 %all-to-all-start.12 = ((bf16[8,8,21,16,128]{4,3,2,1,0:T(8,128)(2,1)}), bf16[8,8,21,16,128]{4,3,2,1,0:T(8,128)(2,1)}, u32[]{:S(2)}, u32[]{:S(2)}) async-start(bf16[8,8,21,16,128]{4,3,2,1,0:T(8,128)(2,1)} %bitcast.66), calls=%async_computation.12 | async-start | bytes 11010048 | tf_op jit(solution)/shard_map/all_to_all | solution.py:723
  331.9 16.7 %collective-permute-start.6 = (bf16[64,9,16,128]{3,2,1,0:T(8,128)(2,1)}, bf16[64,9,16,128]{3,2,1,0:T(8,128)(2,1)S(1)}, u32[]{:S(2)}, u32[]{:S(2)}) collective-permute-start(bf16[64,9,16,128]{3,2,1,0:T(8,128)(2,1)} %get-tuple-element.132), channel_id=1, source_target_pairs={{0,8},{8,0},{1,9},{9,1},{2,10},{10,2},{3,11},{11,3},{4,12},{12,4},... | collective-permute-start | bytes 7077896 | tf_op jit(solution)/shard_map/ppermute | solution.py:680
  332.0 11.9 %copy-start.13 = (f32[4,768]{1,0:T(4,128)S(1)}, f32[4,768]{1,0:T(4,128)}, u32[]{:S(2)}) copy-start(f32[4,768]{1,0:T(4,128)} %get-tuple-element.125) | copy-start | bytes 36868
  332.0 11.9 %copy-start.12 = (f32[1,3072]{1,0:T(1,128)S(1)}, f32[1,3072]{1,0:T(1,128)}, u32[]{:S(2)}) copy-start(f32[1,3072]{1,0:T(1,128)} %get-tuple-element.127) | copy-start | bytes 36868
  332.0 12.8 %copy-start.16 = (f32[4,768]{1,0:T(4,128)S(1)}, f32[4,768]{1,0:T(4,128)}, u32[]{:S(2)}) copy-start(f32[4,768]{1,0:T(4,128)} %get-tuple-element.123) | copy-start | bytes 36868
  332.0 12.9 %copy-start.15 = (f32[4,768]{1,0:T(4,128)S(1)}, f32[4,768]{1,0:T(4,128)}, u32[]{:S(2)}) copy-start(f32[4,768]{1,0:T(4,128)} %get-tuple-element.124) | copy-start | bytes 36868
  332.0 12.9 %copy-start.14 = (f32[1,3072]{1,0:T(1,128)S(1)}, f32[1,3072]{1,0:T(1,128)}, u32[]{:S(2)}) copy-start(f32[1,3072]{1,0:T(1,128)} %get-tuple-element.126) | copy-start | bytes 36868
  337.9 8.8 %copy-start.17 = (f32[4,768]{1,0:T(4,128)S(1)}, f32[4,768]{1,0:T(4,128)}, u32[]{:S(2)}) copy-start(f32[4,768]{1,0:T(4,128)} %get-tuple-element.122) | copy-start | bytes 36868
  337.9 9.6 %copy-start.27 = (bf16[128,128]{1,0:T(8,128)(2,1)S(1)}, bf16[128,128]{1,0:T(8,128)(2,1)}, u32[]{:S(2)}) copy-start(bf16[128,128]{1,0:T(8,128)(2,1)} %constant.45.clone) | copy-start | bytes 98308
  343.1 7.0 %collective-permute-start.4 = (bf16[64,9,16,128]{3,2,1,0:T(8,128)(2,1)}, bf16[64,9,16,128]{3,2,1,0:T(8,128)(2,1)}, u32[]{:S(2)}, u32[]{:S(2)}) collective-permute-start(bf16[64,9,16,128]{3,2,1,0:T(8,128)(2,1)} %get-tuple-element.121), channel_id=1, source_target_pairs={{0,8},{8,0},{1,9},{9,1},{2,10},{10,2},{3,11},{11,3},{4,12},{12,4},... | collective-permute-start | bytes 7077896 | tf_op jit(solution)/shard_map/ppermute | solution.py:680
  348.6 1.5 collective-permute-start.5
  348.6 1.5 copy-start.4
  350.1 0.7 copy-start.10
  367.4 38.5 %all-to-all-start.13 = ((bf16[8,8,19,16,128]{4,3,2,1,0:T(8,128)(2,1)}), bf16[8,8,19,16,128]{4,3,2,1,0:T(8,128)(2,1)}, u32[]{:S(2)}, u32[]{:S(2)}) async-start(bf16[8,8,19,16,128]{4,3,2,1,0:T(8,128)(2,1)} %bitcast.67), calls=%async_computation.14 | async-start | bytes 9961472 | tf_op jit(solution)/shard_map/all_to_all | solution.py:723
  434.4 12.9 %all-to-all-start.15 = ((bf16[8,20,16,128]{3,2,1,0:T(8,128)(2,1)}), bf16[8,20,16,128]{3,2,1,0:T(8,128)(2,1)S(1)}, u32[]{:S(2)}, u32[]{:S(2)}) async-start(bf16[8,20,16,128]{3,2,1,0:T(8,128)(2,1)} %get-tuple-element.136), calls=%async_computation.16 | async-start | bytes 1310720 | tf_op jit(solution)/shard_map/all_to_all | solution.py:866
  447.3 0.9 copy-start.3
Sparse Core Ops, SparseCore 0:
  34.3 64.7 all-gather.4
  101.5 114.8 all-gather.6
  239.8 112.6 reduce-scatter.1

commit v8 on v7

--- a/solution.py
+++ b/solution.py
@@ -360,10 +360,11 @@
     e = e_ref[...].astype(f32)
     e2 = e.astype(bf16)
     arrive(wd, 2)
-    df = jnp.zeros((TOK, 4 * D), f32)
+    df = None
     for j in range(3):
         w = jnp.concatenate([tall_units(wd, 2 * j), tall_units(wd, 2 * j + 1)], axis=1)
-        df = df + mul_t(e2[:, 256 * j : 256 * j + 256], w)
+        part = mul_t(e2[:, 256 * j : 256 * j + 256], w)
+        df = part if df is None else df + part
     arrive(wu, 1)
     cot = jnp.zeros((TOK, D), f32)
     for j in range(12):
@@ -375,7 +376,8 @@
         du = (df[:, c] * slope).astype(bf16)
         du_ref[:, c] = du
         upb_ref[:, c] = rows_sum(du.astype(f32))
-        cot = cot + mul_t(du, units(wu, 2 * j, 2))
+        if j % 3 == 2:
+            cot = cot + mul_t(du_ref[:, D * (j // 3) : D * (j // 3) + D], units(wu, 2 * j - 4, 6))
     xh, r = norm_parts(h1_ref[...])
     e1 = e + norm_back(cot, vec[0:1], xh, r)
     e1_ref[...] = e1
@@ -385,10 +387,7 @@
     small_ref[2:3] = rows_sum(b1.astype(f32))
     small_ref[3:4] = rows_sum(e2.astype(f32))
     arrive(wo, 0)
-    do = jnp.zeros((TOK, D), f32)
-    for j in range(3):
-        do = do + mul_t(b1[:, 256 * j : 256 * j + 256], units(wo, 2 * j, 2))
-    do = do.astype(bf16).astype(f32)
+    do = mul_t(b1, units(wo, 0, 6)).astype(bf16).astype(f32)
     for d, win in enumerate(windows(do)):
         pay_ref[d] = win.astype(bf16)
 
@@ -401,8 +400,8 @@
             small_ref[2 + part // 2 : 3 + part // 2] = rows_sum(got.astype(f32))
     arrived(w, sem)
     cot = jnp.zeros((TOK, D), f32)
-    for j in range(9):
-        cot = cot + mul_t(g_ref[:, 256 * j : 256 * j + 256], units(w, 2 * j, 2))
+    for j in range(3):
+        cot = cot + mul_t(g_ref[:, D * j : D * j + D], units(w, 6 * j, 6))
     xh, r = norm_parts(h_ref[...].astype(f32))
     small_ref[0:1] = rows_sum(cot * xh)
     small_ref[1:2] = rows_sum(cot)

time: 466 us -> 467 us (level)
  no operation moved by 1% of the time
where the time goes in v8:
time: 467 us; the launch traced here: 458 us
  Pallas kernels  130 us (28%)
  blocking collectives  122 us (26%)
  waiting for transfers between devices  106 us (23%)
  starting transfers between devices  51.7 us (11%)
  local copies, waits for them, and re-layouts  21.5 us (5%)
  between operations  14.7 us (3%)
  other arithmetic  11.7 us (3%)
    pallas_call x17, Pallas kernels, call(): pl.pallas_call(kernel, out_shape=[jax.ShapeDtypeStruct(*o) for o in outs]...  113 us
    all_to_all x3, blocking collectives, exchange(): return lax.all_to_all(values, CTX, 0, 0)  54.5 us
    all_to_all x2, blocking collectives, copies(): return lax.all_to_all(many, ALL, 0, 0, axis_index_groups=groups)  45.8 us
    all_to_all x2, waiting for transfers between devices, to_cube(): lax.all_to_all(part.reshape((8, 8) + part.shape[1:]), ALL, 0, 0, axis_ind...  38.2 us
    all_to_all x1, waiting for transfers between devices, body(): lax.all_to_all(after(shards, heads_0, down_0), ALL, 0, 0, axis_index_grou...  26.8 us
    all_to_all x5, starting transfers between devices, exchange(): return lax.all_to_all(values, CTX, 0, 0)  25.7 us
    all_to_all x1, blocking collectives, body(): sums = lax.all_to_all(sums, ALL, 0, 0, axis_index_groups=GROUPS_A)  21.5 us
    pallas_call x2, Pallas kernels, add_pairs(): pl.pallas_call(add_kernel, grid=(8,), out_shape=jax.ShapeDtypeStruct((64,...  17.2 us
  transfers between devices with their start and end apart: 20, of which 11 were waited for; matrix products, arithmetic and copies ran while one was open for 5% of the time, Pallas kernels for 24%

profile of v8, /device:TPU:0, one launch (start us, length us, event | category | flops | bytes accessed | tf_op | source)
XLA Modules:
  0.0 457.5 jit_solution(13129924337996315193)
XLA Ops:
  7.2 2.4 shard_map.239
  9.7 5.7 %all-to-all-start = ((bf16[8,31,16,128]{3,2,1,0:T(8,128)(2,1)}), bf16[8,31,16,128]{3,2,1,0:T(8,128)(2,1)S(1)}, u32[]{:S(2)}, u32[]{:S(2)}) async-start(bf16[8,31,16,128]{3,2,1,0:T(8,128)(2,1)} %shard_map.239), calls=%async_computation | async-start | bytes 2031616 | tf_op jit(solution)/shard_map/all_to_all | solution.py:750
  16.6 14.2 %all-to-all-done.got = bf16[8,31,16,128]{3,2,1,0:T(8,128)(2,1)S(1)} async-done(((bf16[8,31,16,128]{3,2,1,0:T(8,128)(2,1)}), bf16[8,31,16,128]{3,2,1,0:T(8,128)(2,1)S(1)}, u32[]{:S(2)}, u32[]{:S(2)}) %all-to-all-start) | async-done | bytes 1015840 | tf_op jit(solution)/shard_map/all_to_all | solution.py:750
  30.8 1.0 copy-done.1
  31.8 2.3 shard_map.240
  34.2 1.0 broadcast_in_dim.22
  35.2 21.7 %all_to_all.80 = bf16[8,28,16,128]{3,2,1,0:T(8,128)(2,1)S(1)} all-to-all(bf16[8,28,16,128]{3,2,1,0:T(8,128)(2,1)S(1)} %broadcast_in_dim.22), channel_id=1, replica_groups={{0,6,17,23,96,102,113,119},{2,4,19,21,98,100,115,117},{1,7,16,22,97,103..., dimensions={0} | all-to-all | bytes 1835008 | tf_op jit(solution)/shard_map/all_to_all | solution.py:671
  57.4 24.1 %all_to_all.81 = bf16[8,8,10,16,128]{4,3,2,1,0:T(8,128)(2,1)S(1)} all-to-all(bf16[8,8,10,16,128]{4,3,2,1,0:T(8,128)(2,1)S(1)} %broadcast_in_dim.23), channel_id=1, replica_groups={{0,2,1,3,32,34,33,35},{6,4,7,5,38,36,39,37},{17,19,16,18,49,51,48,50},{..., dimensions={0} | all-to-all | bytes 5242880 | tf_op jit(solution)/shard_map/all_to_all | solution.py:671
  81.6 3.0 broadcast_in_dim.24
  84.6 2.0 collective-permute-done.theirs.refs_1_.refs_3_
  86.5 7.4 %shard_map.241 = (bf16[128,768]{1,0:T(8,128)(2,1)}, bf16[8,128,384]{2,1,0:T(8,128)(2,1)}, f32[4,768]{1,0:T(4,128)}, f32[4,768]{1,0:T(4,128)}, f32[4,768]{1,0:T(4...) custom-call(s32[1]{0:T(128)} %bitcast.core.core_ref, bf16[128,768]{1,0:T(8,128)(2,1)} %bitcast.70, ...), custom_call_target="tpu_custom_call" | custom-call | bytes 25830000 | tf_op jit(solution)/shard_map/pallas_call | solution.py:646
  94.0 18.0 %all_to_all.82.heads = bf16[8,128,384]{2,1,0:T(8,128)(2,1)} all-to-all(bf16[8,128,384]{2,1,0:T(8,128)(2,1)} %get-tuple-element.79), channel_id=1, replica_groups=mesh['y'=4,'zh'=2,'c'=2,'x'=4,'zl'=2] {'x','zl'}, dimensions={0} | all-to-all | bytes 1572864 | tf_op jit(solution)/shard_map/all_to_all | solution.py:782
  112.0 4.8 %all-to-all-start.4 = ((bf16[8,8,18,16,128]{4,3,2,1,0:T(8,128)(2,1)}), bf16[8,8,18,16,128]{4,3,2,1,0:T(8,128)(2,1)}, u32[]{:S(2)}, u32[]{:S(2)}) async-start(bf16[8,8,18,16,128]{4,3,2,1,0:T(8,128)(2,1)} %broadcast_in_dim.24), calls=%async_computation.4 | async-start | bytes 9437184 | tf_op jit(solution)/shard_map/all_to_all | solution.py:796
  118.2 0.9 subtract_select_fusion.idc
  119.0 5.5 %shard_map.242 = bf16[8,128,128]{2,1,0:T(8,128)(2,1)} custom-call(s32[1]{0:T(128)} %bitcast.2.par_ref, bf16[8,128,384]{2,1,0:T(8,128)(2,1)} %all_to_all.82.heads, s32[8,128,1]{2,1,0:T(8,128)} %subtract_select_fusion.idc, s32[1,1024]{1,0:T(1,128)} %reshape_select_fusion.idr), custom_call_target="tpu_custom_call" | custom-call | bytes 22140000 | tf_op jit(solution)/shard_map/pallas_call | solution.py:646
  124.6 26.8 %all-to-all-done.4 = bf16[8,8,18,16,128]{4,3,2,1,0:T(8,128)(2,1)} async-done(((bf16[8,8,18,16,128]{4,3,2,1,0:T(8,128)(2,1)}), bf16[8,8,18,16,128]{4,3,2,1,0:T(8,128)(2,1)}, u32[]{:S(2)}, u32[]{:S(2)}) %all-to-all-start.4) | async-done | bytes 4718624 | tf_op jit(solution)/shard_map/all_to_all | solution.py:796
  151.8 9.3 %all-to-all-start.5 = ((bf16[8,128,128]{2,1,0:T(8,128)(2,1)}), bf16[8,128,128]{2,1,0:T(8,128)(2,1)S(1)}, u32[]{:S(2)}, u32[]{:S(2)}) async-start(bf16[8,128,128]{2,1,0:T(8,128)(2,1)} %shard_map.242), calls=%async_computation.5 | async-start | bytes 524288 | tf_op jit(solution)/shard_map/all_to_all | solution.py:782
  161.6 0.8 slice.158.upb
  162.4 6.3 %all-to-all-done.5.back = bf16[8,128,128]{2,1,0:T(8,128)(2,1)S(1)} async-done(((bf16[8,128,128]{2,1,0:T(8,128)(2,1)}), bf16[8,128,128]{2,1,0:T(8,128)(2,1)S(1)}, u32[]{:S(2)}, u32[]{:S(2)}) %all-to-all-start.5) | async-done | bytes 262176 | tf_op jit(solution)/shard_map/all_to_all | solution.py:782
  168.7 0.7 copy-done.6
  169.3 9.8 %shard_map.243 = (bf16[128,768]{1,0:T(8,128)(2,1)}, f32[128,768]{1,0:T(8,128)}, bf16[128,768]{1,0:T(8,128)(2,1)}, f32[128,3072]{1,0:T(8,128)}, f32[128,768]{1,0:...) custom-call(s32[1]{0:T(128)} %bitcast.core.core_ref, bf16[128,768]{1,0:T(8,128)(2,1)} %bitcast.71, ...), custom_call_target="tpu_custom_call" | custom-call | bytes 44280000 | tf_op jit(solution)/shard_map/pallas_call | solution.py:646
  179.1 17.9 %all_to_all.83.heads = bf16[8,128,384]{2,1,0:T(8,128)(2,1)} all-to-all(bf16[8,128,384]{2,1,0:T(8,128)(2,1)} %get-tuple-element.88), channel_id=1, replica_groups=mesh['y'=4,'zh'=2,'c'=2,'x'=4,'zl'=2] {'x','zl'}, dimensions={0} | all-to-all | bytes 1572864 | tf_op jit(solution)/shard_map/all_to_all | solution.py:782
  197.0 5.6 %shard_map.244 = bf16[8,128,128]{2,1,0:T(8,128)(2,1)} custom-call(s32[1]{0:T(128)} %bitcast.2.par_ref, bf16[8,128,384]{2,1,0:T(8,128)(2,1)} %all_to_all.83.heads, s32[8,128,1]{2,1,0:T(8,128)} %subtract_select_fusion.idc, s32[1,1024]{1,0:T(1,128)} %reshape_select_fusion.idr), custom_call_target="tpu_custom_call" | custom-call | bytes 22140000 | tf_op jit(solution)/shard_map/pallas_call | solution.py:646
  202.6 3.7 all-to-all-start.7
  206.8 0.8 slice.160.upb
  207.6 5.7 %all-to-all-done.7.back = bf16[8,128,128]{2,1,0:T(8,128)(2,1)S(1)} async-done(((bf16[8,128,128]{2,1,0:T(8,128)(2,1)}), bf16[8,128,128]{2,1,0:T(8,128)(2,1)S(1)}, u32[]{:S(2)}, u32[]{:S(2)}) %all-to-all-start.7) | async-done | bytes 262176 | tf_op jit(solution)/shard_map/all_to_all | solution.py:782
  213.3 3.1 all-gather.7.cloned.1.call-done
  216.4 12.4 %shard_map.245 = (bf16[128,768]{1,0:T(8,128)(2,1)}, bf16[128,768]{1,0:T(8,128)(2,1)}, bf16[128,768]{1,0:T(8,128)(2,1)}, bf16[128,3072]{1,0:T(8,128)(2,1)}, bf16[...) custom-call(s32[1]{0:T(128)} %bitcast.core.core_ref, ...), custom_call_target="tpu_custom_call" | custom-call | bytes 59040000 | tf_op jit(solution)/shard_map/pallas_call | solution.py:646
  228.8 3.4 all-to-all-start.8
  232.5 7.3 %shard_map.246 = (bf16[64,3,16,128]{3,2,1,0:T(8,128)(2,1)}, bf16[64,3,16,128]{3,2,1,0:T(8,128)(2,1)}, bf16[16,120,16,128]{3,2,1,0:T(8,128)(2,1)}) custom-call(s32[1]{0:T(128)} %bitcast.core.core_ref, bf16[128,3072]{1,0:T(8,128)(2,1)} %get-tuple-element.95.f_ref, bf16[128,768]{1,0:T(8,128)(2,1)} %bitcast.77, bf16[128,768]{1,0:T(8,128)(2,1)} %get-tuple-element.96.a2_ref, ...), custom_call_target="tpu_custom_call" | custom-call | bytes 33210000 | tf_op jit(solution)/shard_map/pallas_call | solution.py:646
  239.8 0.7 copy-done.8
  240.5 8.0 %shard_map.247 = bf16[8,128,384]{2,1,0:T(8,128)(2,1)} custom-call(s32[1]{0:T(128)} %bitcast.2.par_ref, bf16[8,128,384]{2,1,0:T(8,128)(2,1)} %all_to_all.83.heads, bf16[8,128,128]{2,1,0:T(8,128)(2,1)} %copy-done.8, s32[8,128,1]{2,1,0:T(8,128)} %subtract_select_fusion.idc, s32[1,1024]{1,0:T(1,128)} %reshape_select_fusion.idr), custom_call_target="tpu_custom_call" | custom-call | bytes 29520000 | tf_op jit(solution)/shard_map/pallas_call | solution.py:646
  248.5 18.6 %all_to_all.84.back = bf16[8,128,384]{2,1,0:T(8,128)(2,1)} all-to-all(bf16[8,128,384]{2,1,0:T(8,128)(2,1)} %shard_map.247), channel_id=1, replica_groups=mesh['y'=4,'zh'=2,'c'=2,'x'=4,'zl'=2] {'x','zl'}, dimensions={0} | all-to-all | bytes 1572864 | tf_op jit(solution)/shard_map/all_to_all | solution.py:782
  267.2 14.8 %shard_map.248 = (bf16[128,2304]{1,0:T(8,128)(2,1)}, f32[128,768]{1,0:T(8,128)}, f32[4,768]{1,0:T(4,128)}, bf16[128,3072]{1,0:T(8,128)(2,1)}, bf16[128,3072]{1,0...) custom-call(s32[1]{0:T(128)} %bitcast.core.core_ref, ...), custom_call_target="tpu_custom_call" | custom-call | bytes 59040000 | tf_op jit(solution)/shard_map/pallas_call | solution.py:646
  282.0 3.6 all-to-all-start.10
  285.6 8.4 %shard_map.249 = (bf16[64,18,16,128]{3,2,1,0:T(8,128)(2,1)}, bf16[64,18,16,128]{3,2,1,0:T(8,128)(2,1)}) custom-call(s32[1]{0:T(128)} %bitcast.core.core_ref, bf16[128,3072]{1,0:T(8,128)(2,1)} %get-tuple-element.104.f_ref, f32[128,768]{1,0:T(8,128)} %get-tuple-element.105.e_ref, bf16[128,768]{1,0:T(8,128)(2,1)} %get-tuple-element.106.a2_ref, ...), custom_call_target="tpu_custom_call" | custom-call | bytes 33210000 | tf_op jit(solution)/shard_map/pallas_call | solution.py:646
  294.2 0.9 collective-permute-start.3
  295.1 8.0 %shard_map.250 = bf16[8,128,384]{2,1,0:T(8,128)(2,1)} custom-call(s32[1]{0:T(128)} %bitcast.2.par_ref, bf16[8,128,384]{2,1,0:T(8,128)(2,1)} %all_to_all.82.heads, bf16[8,128,128]{2,1,0:T(8,128)(2,1)} %copy-done.7, s32[8,128,1]{2,1,0:T(8,128)} %subtract_select_fusion.idc, s32[1,1024]{1,0:T(1,128)} %reshape_select_fusion.idr), custom_call_target="tpu_custom_call" | custom-call | bytes 29520000 | tf_op jit(solution)/shard_map/pallas_call | solution.py:646
  303.1 5.6 %all-to-all-start.11 = ((bf16[8,128,384]{2,1,0:T(8,128)(2,1)}), bf16[8,128,384]{2,1,0:T(8,128)(2,1)S(1)}, u32[]{:S(2)}, u32[]{:S(2)}) async-start(bf16[8,128,384]{2,1,0:T(8,128)(2,1)} %shard_map.250), calls=%async_computation.11 | async-start | bytes 1572864 | tf_op jit(solution)/shard_map/all_to_all | solution.py:782
  308.7 0.9 copy-done.9
  309.6 8.8 %shard_map.251 = bf16[64,21,16,128]{3,2,1,0:T(8,128)(2,1)} custom-call(bf16[64,18,16,128]{3,2,1,0:T(8,128)(2,1)} %get-tuple-element.108.refs_0_, bf16[64,18,16,128]{3,2,1,0:T(8,128)(2,1)} %collective-permute-done.2.refs_1_, bf16[64,3,16,128]{3,2,1,0:T(8,128)(2,1)} %get-tuple-element.112.refs_2_, bf16[64,3,16,128]{3,2,1,0:T(8,128)(2,1)} %copy-done.9), custom_call_target="tpu_custom_call" | custom-call | flops 4194304 | bytes 16515072 | tf_op jit(solution)/shard_map/pallas_call | solution.py:706
  318.5 3.0 all-to-all-done.11.back
  321.4 0.9 copy-done.2
  322.4 4.7 %all-to-all-start.12 = ((bf16[8,8,21,16,128]{4,3,2,1,0:T(8,128)(2,1)}), bf16[8,8,21,16,128]{4,3,2,1,0:T(8,128)(2,1)}, u32[]{:S(2)}, u32[]{:S(2)}) async-start(bf16[8,8,21,16,128]{4,3,2,1,0:T(8,128)(2,1)} %bitcast.66), calls=%async_computation.12 | async-start | bytes 11010048 | tf_op jit(solution)/shard_map/all_to_all | solution.py:722
  327.0 5.2 %shard_map.254 = (bf16[64,9,16,128]{3,2,1,0:T(8,128)(2,1)}, bf16[64,9,16,128]{3,2,1,0:T(8,128)(2,1)}) custom-call(s32[1]{0:T(128)} %bitcast.core.core_ref, bf16[128,768]{1,0:T(8,128)(2,1)} %get-tuple-element.128.a_ref, bf16[128,2304]{1,0:T(8,128)(2,1)} %get-tuple-element.129.g_ref, bf16[128,768]{1,0:T(8,128)(2,1)} %get-tuple-element.130.o_ref, ...), custom_call_target="tpu_custom_call" | custom-call | bytes 18450000 | tf_op jit(solution)/shard_map/pallas_call | solution.py:646
  332.4 5.8 %shard_map.252 = (bf16[128,2304]{1,0:T(8,128)(2,1)}, f32[128,768]{1,0:T(8,128)}, f32[4,768]{1,0:T(4,128)}) custom-call(s32[1]{0:T(128)} %bitcast.core.core_ref, bf16[8,128,384]{2,1,0:T(8,128)(2,1)} %copy-done.2, f32[128,768]{1,0:T(8,128)} %get-tuple-element.115.e1_ref, bf16[128,768]{1,0:T(8,128)(2,1)} %bitcast.72, f32[4,768]{1,0:T(4,128)} %get-tuple-element.116.vec, ...), custom_call_target="tpu_custom_call" | custom-call | bytes 22140000 | tf_op jit(solution)/shard_map/pallas_call | solution.py:646
  338.2 5.2 %shard_map.253 = (bf16[64,9,16,128]{3,2,1,0:T(8,128)(2,1)}, bf16[64,9,16,128]{3,2,1,0:T(8,128)(2,1)}) custom-call(s32[1]{0:T(128)} %bitcast.core.core_ref, bf16[128,768]{1,0:T(8,128)(2,1)} %get-tuple-element.91.a_ref, bf16[128,2304]{1,0:T(8,128)(2,1)} %get-tuple-element.118.g_ref, bf16[128,768]{1,0:T(8,128)(2,1)} %get-tuple-element.119.o_ref, ...), custom_call_target="tpu_custom_call" | custom-call | bytes 18450000 | tf_op jit(solution)/shard_map/pallas_call | solution.py:646
  343.5 0.7 collective-permute-start.4
  348.1 0.8 select_bitcast_fusion
  349.0 1.5 collective-permute-done.5.refs_3_
  351.2 8.4 %shard_map.255 = bf16[64,19,16,128]{3,2,1,0:T(8,128)(2,1)} custom-call(bf16[64,9,16,128]{3,2,1,0:T(8,128)(2,1)} %get-tuple-element.120.refs_0_, bf16[64,9,16,128]{3,2,1,0:T(8,128)(2,1)} %collective-permute-done.4.refs_1_, bf16[64,1,16,128]{3,2,1,0:T(8,128)(2,1)} %get-tuple-element.144.refs_2_, bf16[64,1,16,128]{3,2,1,0:T(8,128)(2,1)} %copy-done.10, ...), custom_call_target="tpu_custom_call" | custom-call | flops 4194304 | bytes 14942208 | tf_op jit(solution)/shard_map/pallas_call | solution.py:706
  359.6 7.8 %all-to-all-done.12 = bf16[8,8,21,16,128]{4,3,2,1,0:T(8,128)(2,1)} async-done(((bf16[8,8,21,16,128]{4,3,2,1,0:T(8,128)(2,1)}), bf16[8,8,21,16,128]{4,3,2,1,0:T(8,128)(2,1)}, u32[]{:S(2)}, u32[]{:S(2)}) %all-to-all-start.12) | async-done | bytes 5505056 | tf_op jit(solution)/shard_map/all_to_all | solution.py:722
  367.4 4.6 %all-to-all-start.13 = ((bf16[8,8,19,16,128]{4,3,2,1,0:T(8,128)(2,1)}), bf16[8,8,19,16,128]{4,3,2,1,0:T(8,128)(2,1)}, u32[]{:S(2)}, u32[]{:S(2)}) async-start(bf16[8,8,19,16,128]{4,3,2,1,0:T(8,128)(2,1)} %bitcast.67), calls=%async_computation.14 | async-start | bytes 9961472 | tf_op jit(solution)/shard_map/all_to_all | solution.py:722
  372.0 3.5 reduce_sum.35
  375.5 30.4 %all-to-all-done.13 = bf16[8,8,19,16,128]{4,3,2,1,0:T(8,128)(2,1)} async-done(((bf16[8,8,19,16,128]{4,3,2,1,0:T(8,128)(2,1)}), bf16[8,8,19,16,128]{4,3,2,1,0:T(8,128)(2,1)}, u32[]{:S(2)}, u32[]{:S(2)}) %all-to-all-start.13) | async-done | bytes 4980768 | tf_op jit(solution)/shard_map/all_to_all | solution.py:722
  405.9 3.2 reduce_sum.34
  409.2 21.5 %all_to_all.85.parts = bf16[8,40,16,128]{3,2,1,0:T(8,128)(2,1)} all-to-all(bf16[8,40,16,128]{3,2,1,0:T(8,128)(2,1)S(1)} %pad_maximum_fusion), channel_id=1, replica_groups={{0,6,17,23,96,102,113,119},{2,4,19,21,98,100,115,117},{1,7,16,22,97,103..., dimensions={0} | all-to-all | bytes 2621440 | tf_op jit(solution)/shard_map/all_to_all | solution.py:862
  430.7 2.6 shard_map.256
  433.4 0.8 slice.191
  434.8 4.0 all-to-all-start.15
  438.8 1.0 fusion.29
  442.8 4.9 %all-to-all-done.15.got = bf16[8,20,16,128]{3,2,1,0:T(8,128)(2,1)S(1)} async-done(((bf16[8,20,16,128]{3,2,1,0:T(8,128)(2,1)}), bf16[8,20,16,128]{3,2,1,0:T(8,128)(2,1)S(1)}, u32[]{:S(2)}, u32[]{:S(2)}) %all-to-all-start.15) | async-done | bytes 655392 | tf_op jit(solution)/shard_map/all_to_all | solution.py:865
  447.7 0.8 copy-done.3
  448.6 2.2 shard_map.257
  (139 shorter events, 13.1 us)
Async XLA Ops:
  7.2 8.3 %copy-start.20 = (bf16[2,2,6]{2,1,0:T(2,128)(2,1)S(1)}, bf16[2,2,6]{2,1,0:T(2,128)(2,1)}, u32[]{:S(2)}) copy-start(bf16[2,2,6]{2,1,0:T(2,128)(2,1)} %param.21) | copy-start | bytes 148
  7.2 8.3 %copy-start.21 = (bf16[2,2,6]{2,1,0:T(2,128)(2,1)S(1)}, bf16[2,2,6]{2,1,0:T(2,128)(2,1)}, u32[]{:S(2)}) copy-start(bf16[2,2,6]{2,1,0:T(2,128)(2,1)} %param.22) | copy-start | bytes 148
  7.2 8.4 %copy-start.22 = (bf16[2,2,6]{2,1,0:T(2,128)(2,1)S(1)}, bf16[2,2,6]{2,1,0:T(2,128)(2,1)}, u32[]{:S(2)}) copy-start(bf16[2,2,6]{2,1,0:T(2,128)(2,1)} %param.24) | copy-start | bytes 148
  7.2 8.5 %copy-start.23 = (bf16[2,2,6]{2,1,0:T(2,128)(2,1)S(1)}, bf16[2,2,6]{2,1,0:T(2,128)(2,1)}, u32[]{:S(2)}) copy-start(bf16[2,2,6]{2,1,0:T(2,128)(2,1)} %param.26) | copy-start | bytes 148
  7.2 8.6 %copy-start.24 = (bf16[2,24]{1,0:T(2,128)(2,1)S(1)}, bf16[2,24]{1,0:T(2,128)(2,1)}, u32[]{:S(2)}) copy-start(bf16[2,24]{1,0:T(2,128)(2,1)} %param.28) | copy-start | bytes 292
  9.7 21.1 %all-to-all-start = ((bf16[8,31,16,128]{3,2,1,0:T(8,128)(2,1)}), bf16[8,31,16,128]{3,2,1,0:T(8,128)(2,1)S(1)}, u32[]{:S(2)}, u32[]{:S(2)}) async-start(bf16[8,31,16,128]{3,2,1,0:T(8,128)(2,1)} %shard_map.239), calls=%async_computation | async-start | bytes 2031616 | tf_op jit(solution)/shard_map/all_to_all | solution.py:750
  15.4 96.6 %all-gather.5.cloned.1.call-start = ((), (), s32[]{:S(2)}) async-start(), calls=%async_computation.18 | async-start | bytes 5013504 | tf_op jit(solution)/shard_map/all_gather | solution.py:755
  30.8 1.0 copy-start.1
  34.1 182.3 %all-gather.7.cloned.1.call-start = ((), (), s32[]{:S(2)}) async-start(), calls=%async_computation.19 | async-start | bytes 10027008 | tf_op jit(solution)/shard_map/all_gather | solution.py:792
  81.5 3.1 copy-start
  81.5 5.0 %collective-permute-start = (bf16[64,10,16,128]{3,2,1,0:T(8,128)(2,1)S(1)}, bf16[64,10,16,128]{3,2,1,0:T(8,128)(2,1)}, u32[]{:S(2)}, u32[]{:S(2)}) collective-permute-start(bf16[64,10,16,128]{3,2,1,0:T(8,128)(2,1)S(1)} %bitcast.59), channel_id=1, source_target_pairs={{0,8},{8,0},{1,9},{9,1},{2,10},{10,2},{3,11},{11,3},{4,12},{12,4},... | collective-permute-start | bytes 7864328 | tf_op jit(solution)/shard_map/ppermute | solution.py:679
  112.0 4.8 %copy-start.18 = (s32[48]{0:T(128)S(1)}, s32[48]{0:T(128)}, u32[]{:S(2)}) copy-start(s32[48]{0:T(128)} %param.19) | copy-start | bytes 580
  112.0 4.8 %copy-start.25 = (s32[48]{0:T(128)S(1)}, s32[48]{0:T(128)}, u32[]{:S(2)}) copy-start(s32[48]{0:T(128)} %param.20) | copy-start | bytes 580
  112.0 4.9 %copy-start.26 = (s32[48]{0:T(128)S(1)}, s32[48]{0:T(128)}, u32[]{:S(2)}) copy-start(s32[48]{0:T(128)} %param.18) | copy-start | bytes 580
  112.0 39.4 %all-to-all-start.4 = ((bf16[8,8,18,16,128]{4,3,2,1,0:T(8,128)(2,1)}), bf16[8,8,18,16,128]{4,3,2,1,0:T(8,128)(2,1)}, u32[]{:S(2)}, u32[]{:S(2)}) async-start(bf16[8,8,18,16,128]{4,3,2,1,0:T(8,128)(2,1)} %broadcast_in_dim.24), calls=%async_computation.4 | async-start | bytes 9437184 | tf_op jit(solution)/shard_map/all_to_all | solution.py:796
  116.8 34.6 %copy-start.11 = (f32[128,256]{1,0:T(8,128)S(1)}, f32[128,256]{1,0:T(8,128)}, u32[]{:S(2)}) copy-start(f32[128,256]{1,0:T(8,128)} %get-tuple-element.84) | copy-start | bytes 393220
  151.3 17.3 %collective-permute-start.1 = (bf16[64,18,16,128]{3,2,1,0:T(8,128)(2,1)}, bf16[64,18,16,128]{3,2,1,0:T(8,128)(2,1)}, u32[]{:S(2)}, u32[]{:S(2)}) collective-permute-start(bf16[64,18,16,128]{3,2,1,0:T(8,128)(2,1)} %bitcast.12.refs_2_.refs_5_.refs_0_.refs_4_), channel_id=1, source_target_pairs={{0,8},{8,0},{1,9},{9,1},{2,10},{10,2},{3,11},{11,3},{4,12},{12,4},... | collective-permute-start | bytes 14155784 | tf_op jit(solution)/shard_map/ppermute | solution.py:679
  151.8 16.9 %all-to-all-start.5 = ((bf16[8,128,128]{2,1,0:T(8,128)(2,1)}), bf16[8,128,128]{2,1,0:T(8,128)(2,1)S(1)}, u32[]{:S(2)}, u32[]{:S(2)}) async-start(bf16[8,128,128]{2,1,0:T(8,128)(2,1)} %shard_map.242), calls=%async_computation.5 | async-start | bytes 524288 | tf_op jit(solution)/shard_map/all_to_all | solution.py:782
  168.7 0.7 copy-start.6
  202.6 10.6 %all-to-all-start.7 = ((bf16[8,128,128]{2,1,0:T(8,128)(2,1)}), bf16[8,128,128]{2,1,0:T(8,128)(2,1)S(1)}, u32[]{:S(2)}, u32[]{:S(2)}) async-start(bf16[8,128,128]{2,1,0:T(8,128)(2,1)} %shard_map.244), calls=%async_computation.7 | async-start | bytes 524288 | tf_op jit(solution)/shard_map/all_to_all | solution.py:782
  213.3 3.1 copy-start.5
  228.8 11.0 %all-to-all-start.8 = ((bf16[8,128,128]{2,1,0:T(8,128)(2,1)}), bf16[8,128,128]{2,1,0:T(8,128)(2,1)S(1)}, u32[]{:S(2)}, u32[]{:S(2)}) async-start(bf16[8,128,128]{2,1,0:T(8,128)(2,1)} %get-tuple-element.94), calls=%async_computation.8 | async-start | bytes 524288 | tf_op jit(solution)/shard_map/all_to_all | solution.py:782
  232.2 135.2 %reduce-scatter.2.cloned.1.call-start = ((), (), s32[]{:S(2)}) async-start(), calls=%async_computation.17 | async-start | bytes 8355840 | tf_op jit(solution)/shard_map/reduce_scatter | solution.py:828
  239.8 0.7 copy-start.8
  282.0 12.1 %copy-start.19 = (bf16[64,3,16,128]{3,2,1,0:T(8,128)(2,1)S(1)}, bf16[64,3,16,128]{3,2,1,0:T(8,128)(2,1)}, u32[]{:S(2)}) copy-start(bf16[64,3,16,128]{3,2,1,0:T(8,128)(2,1)} %get-tuple-element.113) | copy-start | bytes 2359300
  282.0 12.0 %all-to-all-start.10 = ((bf16[8,128,128]{2,1,0:T(8,128)(2,1)}), bf16[8,128,128]{2,1,0:T(8,128)(2,1)S(1)}, u32[]{:S(2)}, u32[]{:S(2)}) async-start(bf16[8,128,128]{2,1,0:T(8,128)(2,1)} %get-tuple-element.103), calls=%async_computation.10 | async-start | bytes 524288 | tf_op jit(solution)/shard_map/all_to_all | solution.py:782
  294.0 1.1 copy-start.7
  294.1 14.7 %collective-permute-start.2 = (bf16[64,18,16,128]{3,2,1,0:T(8,128)(2,1)}, bf16[64,18,16,128]{3,2,1,0:T(8,128)(2,1)}, u32[]{:S(2)}, u32[]{:S(2)}) collective-permute-start(bf16[64,18,16,128]{3,2,1,0:T(8,128)(2,1)} %get-tuple-element.111), channel_id=1, source_target_pairs={{0,8},{8,0},{1,9},{9,1},{2,10},{10,2},{3,11},{11,3},{4,12},{12,4},... | collective-permute-start | bytes 14155784 | tf_op jit(solution)/shard_map/ppermute | solution.py:679
  294.2 14.6 %collective-permute-start.3 = (bf16[64,3,16,128]{3,2,1,0:T(8,128)(2,1)S(1)}, bf16[64,3,16,128]{3,2,1,0:T(8,128)(2,1)S(1)}, u32[]{:S(2)}, u32[]{:S(2)}) collective-permute-start(bf16[64,3,16,128]{3,2,1,0:T(8,128)(2,1)S(1)} %copy-done.19), channel_id=1, source_target_pairs={{0,8},{8,0},{1,9},{9,1},{2,10},{10,2},{3,11},{11,3},{4,12},{12,4},... | collective-permute-start | bytes 2359304 | tf_op jit(solution)/shard_map/ppermute | solution.py:679
  303.1 18.3 %all-to-all-start.11 = ((bf16[8,128,384]{2,1,0:T(8,128)(2,1)}), bf16[8,128,384]{2,1,0:T(8,128)(2,1)S(1)}, u32[]{:S(2)}, u32[]{:S(2)}) async-start(bf16[8,128,384]{2,1,0:T(8,128)(2,1)} %shard_map.250), calls=%async_computation.11 | async-start | bytes 1572864 | tf_op jit(solution)/shard_map/all_to_all | solution.py:782
  308.7 0.9 copy-start.9
  321.4 0.9 copy-start.2
  322.4 45.0 %all-to-all-start.12 = ((bf16[8,8,21,16,128]{4,3,2,1,0:T(8,128)(2,1)}), bf16[8,8,21,16,128]{4,3,2,1,0:T(8,128)(2,1)}, u32[]{:S(2)}, u32[]{:S(2)}) async-start(bf16[8,8,21,16,128]{4,3,2,1,0:T(8,128)(2,1)} %bitcast.66), calls=%async_computation.12 | async-start | bytes 11010048 | tf_op jit(solution)/shard_map/all_to_all | solution.py:722
  332.3 16.7 %collective-permute-start.6 = (bf16[64,9,16,128]{3,2,1,0:T(8,128)(2,1)}, bf16[64,9,16,128]{3,2,1,0:T(8,128)(2,1)S(1)}, u32[]{:S(2)}, u32[]{:S(2)}) collective-permute-start(bf16[64,9,16,128]{3,2,1,0:T(8,128)(2,1)} %get-tuple-element.132), channel_id=1, source_target_pairs={{0,8},{8,0},{1,9},{9,1},{2,10},{10,2},{3,11},{11,3},{4,12},{12,4},... | collective-permute-start | bytes 7077896 | tf_op jit(solution)/shard_map/ppermute | solution.py:679
  332.3 11.8 %copy-start.13 = (f32[4,768]{1,0:T(4,128)S(1)}, f32[4,768]{1,0:T(4,128)}, u32[]{:S(2)}) copy-start(f32[4,768]{1,0:T(4,128)} %get-tuple-element.125) | copy-start | bytes 36868
  332.4 11.9 %copy-start.12 = (f32[1,3072]{1,0:T(1,128)S(1)}, f32[1,3072]{1,0:T(1,128)}, u32[]{:S(2)}) copy-start(f32[1,3072]{1,0:T(1,128)} %get-tuple-element.127) | copy-start | bytes 36868
  332.4 12.8 %copy-start.16 = (f32[4,768]{1,0:T(4,128)S(1)}, f32[4,768]{1,0:T(4,128)}, u32[]{:S(2)}) copy-start(f32[4,768]{1,0:T(4,128)} %get-tuple-element.123) | copy-start | bytes 36868
  332.4 12.8 %copy-start.15 = (f32[4,768]{1,0:T(4,128)S(1)}, f32[4,768]{1,0:T(4,128)}, u32[]{:S(2)}) copy-start(f32[4,768]{1,0:T(4,128)} %get-tuple-element.124) | copy-start | bytes 36868
  332.4 12.9 %copy-start.14 = (f32[1,3072]{1,0:T(1,128)S(1)}, f32[1,3072]{1,0:T(1,128)}, u32[]{:S(2)}) copy-start(f32[1,3072]{1,0:T(1,128)} %get-tuple-element.126) | copy-start | bytes 36868
  338.2 8.8 %copy-start.17 = (f32[4,768]{1,0:T(4,128)S(1)}, f32[4,768]{1,0:T(4,128)}, u32[]{:S(2)}) copy-start(f32[4,768]{1,0:T(4,128)} %get-tuple-element.122) | copy-start | bytes 36868
  338.2 9.6 %copy-start.27 = (bf16[128,128]{1,0:T(8,128)(2,1)S(1)}, bf16[128,128]{1,0:T(8,128)(2,1)}, u32[]{:S(2)}) copy-start(bf16[128,128]{1,0:T(8,128)(2,1)} %constant.45.clone) | copy-start | bytes 98308
  343.5 7.0 %collective-permute-start.4 = (bf16[64,9,16,128]{3,2,1,0:T(8,128)(2,1)}, bf16[64,9,16,128]{3,2,1,0:T(8,128)(2,1)}, u32[]{:S(2)}, u32[]{:S(2)}) collective-permute-start(bf16[64,9,16,128]{3,2,1,0:T(8,128)(2,1)} %get-tuple-element.121), channel_id=1, source_target_pairs={{0,8},{8,0},{1,9},{9,1},{2,10},{10,2},{3,11},{11,3},{4,12},{12,4},... | collective-permute-start | bytes 7077896 | tf_op jit(solution)/shard_map/ppermute | solution.py:679
  348.9 1.5 collective-permute-start.5
  349.0 1.5 copy-start.4
  350.5 0.7 copy-start.10
  367.4 38.5 %all-to-all-start.13 = ((bf16[8,8,19,16,128]{4,3,2,1,0:T(8,128)(2,1)}), bf16[8,8,19,16,128]{4,3,2,1,0:T(8,128)(2,1)}, u32[]{:S(2)}, u32[]{:S(2)}) async-start(bf16[8,8,19,16,128]{4,3,2,1,0:T(8,128)(2,1)} %bitcast.67), calls=%async_computation.14 | async-start | bytes 9961472 | tf_op jit(solution)/shard_map/all_to_all | solution.py:722
  434.8 12.9 %all-to-all-start.15 = ((bf16[8,20,16,128]{3,2,1,0:T(8,128)(2,1)}), bf16[8,20,16,128]{3,2,1,0:T(8,128)(2,1)S(1)}, u32[]{:S(2)}, u32[]{:S(2)}) async-start(bf16[8,20,16,128]{3,2,1,0:T(8,128)(2,1)} %get-tuple-element.136), calls=%async_computation.16 | async-start | bytes 1310720 | tf_op jit(solution)/shard_map/all_to_all | solution.py:865
  447.7 0.9 copy-start.3
Sparse Core Ops, SparseCore 0:
  34.3 64.7 all-gather.4
  101.5 114.8 all-gather.6
  240.0 112.9 reduce-scatter.1
